TPU v7x, 32 devices: a whole 2x2x4 slice. The times are simulated.
32 devices in a mesh: grp: 2 (over core), row: 4 (over y, x), col: 4 (over z).
Axes of the slice: x: 2, y: 2, z: 4, core: 2. Of those that a mesh axis runs over, the one named last changes fastest.
Arguments:
- global_state: bfloat16 [64, 1440, 384], P(('grp', 'row'), 'col'), may hold values from -6 to 6
- spec_filter: float32 [2, 720, 384], P(None, None, 'col'), may hold values from -4 to 4
- w_skip: bfloat16 [384, 384], replicated, may hold values from -0.3125 to 0.3125
- w_mix: bfloat16 [384, 384], replicated, may hold values from -0.3125 to 0.3125
- w_decode: bfloat16 [384, 26], replicated, may hold values from -0.3125 to 0.3125
- regional_state: bfloat16 [99, 128, 512], P(None, ('grp', 'row'), 'col'), may hold values from -6 to 6
- noise_draws: bfloat16 [2, 99, 128, 512], P(None, None, ('grp', 'row'), 'col'), may hold values from -6 to 6
- w_first: bfloat16 [128, 9, 125], replicated, may hold values from -0.1875 to 0.1875
- w_down: bfloat16 [256, 9, 128], replicated, may hold values from -0.1875 to 0.1875
- w_up: bfloat16 [128, 256], replicated, may hold values from -0.375 to 0.375
- w_bridge: bfloat16 [128, 128], replicated, may hold values from -0.5 to 0.5
- w_last: bfloat16 [99, 9, 128], replicated, may hold values from -0.1875 to 0.1875
- box_lat0: int32 [1], replicated, may hold values from 0 to 46
- box_lon0: int32 [1], replicated, may hold values from 0 to 1374
- stencil_lat: int32 [128, 512], P(('grp', 'row'), 'col'), may hold values from 0 to 16, as said below
- stencil_lon: int32 [128, 512], P(('grp', 'row'), 'col'), may hold values from 0 to 64, as said below
Outputs:
- global_final: bfloat16 [64, 1440, 384], P(('grp', 'row'), 'col')
- regional_final: bfloat16 [99, 128, 512], P(None, ('grp', 'row'), 'col')
Inputs may be any that keep to these rules, and one draw needn't show every extreme that they name: stencil_lat[r, q] is r // 8 or r // 8 + 1. stencil_lon[r, q] is q // 8 or q // 8 + 1.
All inputs are finite; a program needn't handle non-finite values.
Results may differ from a plain program's by a relative error of at most 0.012.
Values may be sent and summed in bfloat16 or wider, within the bound.
No kernel may reach another device: no remote copies, remote signals or barrier semaphores. Data moves between devices by JAX's collectives and lax.ppermute only.
A program may use at most 128 MiB of HBM per device.

v0:
```python
import functools
import math

import jax
import jax.numpy as jnp
import ml_dtypes
import numpy as np
from jax import lax
from jax.experimental import pallas as pl
from jax.experimental.pallas import tpu as pltpu
from jax.sharding import PartitionSpec as P

RATIO = 8
noise_level = 0.5
PLANE = ("grp", "row")
RIM = 9
RIM_USED = 4
LANES = 128
RIM_COLS = 16


def fourier_tables(length, num_modes):
    position = np.arange(length, dtype=np.int64)[:, None]
    frequency = np.arange(num_modes, dtype=np.int64)[None, :]
    angle = (position * frequency % length).astype(np.float64) * (2.0 * math.pi / length)
    cosine = np.cos(angle)
    sine = np.sin(angle)
    factor = np.where(frequency == 0, 1.0, 2.0) / length
    forward = np.concatenate([cosine, -sine], axis=1).T.astype(ml_dtypes.bfloat16)
    inverse = np.concatenate([cosine * factor, -sine * factor], axis=1).astype(ml_dtypes.bfloat16)
    return jnp.asarray(forward), jnp.asarray(inverse)


def shift_pairs(count, step):
    return [(source, (source + step) % count) for source in range(count)]


def exchange(blocks, axis):
    count = lax.axis_size(axis)
    me = lax.axis_index(axis)
    pieces = []
    for step in range(1, count):
        piece = lax.dynamic_index_in_dim(blocks, (me + step) % count, 0, keepdims=True)
        pieces.append(lax.ppermute(piece, axis, shift_pairs(count, step)))
    result = blocks
    for step, piece in enumerate(pieces, 1):
        result = lax.dynamic_update_slice_in_dim(result, piece, (me - step) % count, 0)
    return result


def collect(block, axis):
    count = lax.axis_size(axis)
    me = lax.axis_index(axis)
    pieces = [
        lax.ppermute(block, axis, shift_pairs(count, step)) for step in range(1, count)
    ]
    result = jnp.broadcast_to(block[None], (count,) + block.shape)
    for step, piece in enumerate(pieces, 1):
        result = lax.dynamic_update_slice_in_dim(result, piece[None], (me - step) % count, 0)
    return result


def collect_filter(spec_filter):
    rows = 2 * spec_filter.shape[1]
    flat = spec_filter.reshape(rows, spec_filter.shape[2]).astype(jnp.bfloat16)
    grp, row = lax.axis_size("grp"), lax.axis_size("row")
    share = rows // (grp * row)
    place = lax.axis_index("row") * grp + lax.axis_index("grp")
    mine = lax.dynamic_slice_in_dim(flat, place * share, share, 0)
    wide = collect(mine, "col")
    wide = jnp.swapaxes(wide, 0, 1).reshape(share, -1)
    pair = collect(wide, "grp").reshape(grp * share, -1)
    return collect(pair, "row").reshape(rows, -1)


def latitude_kernel(
    hours, block, state_ref, forward_ref, inverse_ref, filter_ref, skip_ref, mix_ref, decode_ref,
    out_ref, coarse_ref, filtered_ref,
):
    length = state_ref.shape[0]
    modes = filter_ref.shape[0] // 2
    for hour in range(hours):
        source_ref = state_ref if hour == 0 else out_ref

        def analyse(index, carry):
            low = pl.ds(pl.multiple_of(index * block, 16), block)
            high = pl.ds(pl.multiple_of(modes + index * block, 16), block)
            state = source_ref[...]
            real = jnp.dot(forward_ref[low, :], state, preferred_element_type=jnp.float32)
            imag = jnp.dot(forward_ref[high, :], state, preferred_element_type=jnp.float32)
            gain_real = filter_ref[low, :].astype(jnp.float32)
            gain_imag = filter_ref[high, :].astype(jnp.float32)
            filtered_ref[low, :] = (real * gain_real - imag * gain_imag).astype(jnp.bfloat16)
            filtered_ref[high, :] = (real * gain_imag + imag * gain_real).astype(jnp.bfloat16)
            return carry

        lax.fori_loop(0, modes // block, analyse, 0)

        def synthesise(index, carry):
            here = pl.ds(pl.multiple_of(index * block, 16), block)
            spectral = jnp.dot(
                inverse_ref[here, :], filtered_ref[...], preferred_element_type=jnp.float32
            ).astype(jnp.bfloat16)
            state = source_ref[here, :]
            skipped = jnp.dot(state, skip_ref[...], preferred_element_type=jnp.float32)
            activated = jax.nn.gelu(spectral.astype(jnp.float32) + skipped).astype(jnp.bfloat16)
            update = jnp.dot(activated, mix_ref[...], preferred_element_type=jnp.float32)
            fresh = (state.astype(jnp.float32) + update).astype(jnp.bfloat16)
            out_ref[here, :] = fresh
            coarse_ref[hour, here, :] = jnp.dot(
                fresh, decode_ref[...], preferred_element_type=jnp.float32
            ).astype(jnp.bfloat16)
            return carry

        lax.fori_loop(0, length // block, synthesise, 0)


def advance_latitude(hours, state, forward, inverse, gains, w_skip, w_mix, decode):
    length, channels = state.shape
    modes = gains.shape[0] // 2
    block = next(b for b in (720, 240, 144, 48, 16) if modes % b == 0)
    flops = hours * 2 * length * channels * (4 * modes + 2 * channels + LANES)
    return pl.pallas_call(
        functools.partial(latitude_kernel, hours, block),
        out_shape=(
            jax.ShapeDtypeStruct((length, channels), jnp.bfloat16),
            jax.ShapeDtypeStruct((hours, length, LANES), jnp.bfloat16),
        ),
        scratch_shapes=[pltpu.VMEM((2 * modes, channels), jnp.bfloat16)],
        compiler_params=pltpu.CompilerParams(vmem_limit_bytes=40 * 2**20),
        cost_estimate=pl.CostEstimate(
            flops=flops, bytes_accessed=12 * 2**20, transcendentals=hours * length * channels
        ),
        name="advance_latitude",
    )(state, forward, inverse, gains, w_skip, w_mix, decode)


def global_hour(current, spec_filter, w_skip, w_mix, forward, inverse):
    longitude = lax.all_to_all(current, "col", split_axis=2, concat_axis=1, tiled=True)
    spectrum = jnp.einsum("alc,ml->amc", longitude, forward, preferred_element_type=jnp.float32)
    num_modes = spec_filter.shape[1]
    real_part = spectrum[:, :num_modes, :]
    imag_part = spectrum[:, num_modes:, :]
    filt_real = spec_filter[0][None]
    filt_imag = spec_filter[1][None]
    mixed = jnp.concatenate(
        [
            real_part * filt_real - imag_part * filt_imag,
            real_part * filt_imag + imag_part * filt_real,
        ],
        axis=1,
    ).astype(jnp.bfloat16)
    filtered = jnp.einsum("amc,lm->alc", mixed, inverse, preferred_element_type=jnp.float32).astype(
        jnp.bfloat16
    )
    spectral = lax.all_to_all(filtered, "col", split_axis=1, concat_axis=2, tiled=True)
    skipped = jnp.einsum("alc,cd->ald", current, w_skip, preferred_element_type=jnp.float32)
    activated = jax.nn.gelu(spectral.astype(jnp.float32) + skipped).astype(jnp.bfloat16)
    update = jnp.einsum("ald,de->ale", activated, w_mix, preferred_element_type=jnp.float32)
    return (current.astype(jnp.float32) + update).astype(jnp.bfloat16)


def window_extent(cells):
    return (cells + RIM - 1) // RATIO + 3 - (-RIM // RATIO)


def window_stride(cells):
    return -(-window_extent(cells) // 32) * 32


def window_base():
    return -(-RIM // RATIO)


def pad_windows(windows, cols_here):
    spare = window_stride(cols_here) - windows.shape[2]
    return jnp.pad(windows, ((0, 0), (0, 0), (0, spare), (0, 0)))


def global_by_latitude(
    hours, global_state, spec_filter, w_skip, w_mix, w_decode, box_lat0, box_lon0, rows_here, cols_here
):
    count = lax.axis_size("col")
    lats_here, _, channels = global_state.shape
    lon_total = global_state.shape[1] * count
    turns = lats_here // count
    forward, inverse = fourier_tables(lon_total, spec_filter.shape[1])
    conds = w_decode.shape[1]
    decode = jnp.pad(w_decode, ((0, 0), (0, LANES - conds)))
    gathered = [
        exchange(global_state[turn * count : (turn + 1) * count], "col") for turn in range(turns)
    ]
    gains = collect_filter(spec_filter)
    finals, coarses = [], []
    for turn in range(turns):
        state = gathered[turn].reshape(lon_total, channels)
        state, coarse = advance_latitude(
            hours, state, forward, inverse, gains, w_skip, w_mix, decode
        )
        finals.append(exchange(state.reshape((count, -1, channels)), "col"))
        coarses.append(coarse)
    global_final = jnp.concatenate(finals, axis=0)
    base = window_base()
    high, wide = window_extent(rows_here), window_extent(cols_here)
    coarse = jnp.stack(coarses, axis=1)[..., :conds]
    step = cols_here // RATIO
    span = (count - 1) * step + wide
    coarse = jnp.pad(coarse, ((0, 0), (0, 0), (base, span), (0, 0)))
    zero = jnp.zeros((), jnp.int32)
    strip = lax.dynamic_slice(
        coarse, (zero, zero, box_lon0[0], zero), (hours, turns, span, conds)
    )
    packed = jnp.stack(
        [strip[:, :, col * step : col * step + wide].reshape(-1) for col in range(count)]
    )
    size = packed.shape[1]
    packed = jnp.pad(packed, ((0, 0), (0, -size % 1024))).reshape(count, -1, LANES)
    plane = lax.axis_size(PLANE)
    sent = jnp.broadcast_to(packed[None], (plane,) + packed.shape).reshape(
        (plane * count,) + packed.shape[1:]
    )
    got = lax.all_to_all(sent, PLANE + ("col",), split_axis=0, concat_axis=0, tiled=True)
    got = got.reshape(plane, count, -1)[..., :size].reshape(plane, count, hours, turns, wide, conds)
    got = jnp.transpose(got, (2, 0, 3, 1, 4, 5)).reshape(hours, plane * lats_here, wide, conds)
    got = jnp.pad(got, ((0, 0), (base, high), (0, 0), (0, 0)))
    start = box_lat0[0] + lax.axis_index(PLANE) * (rows_here // RATIO)
    windows = lax.dynamic_slice_in_dim(got, start, high, 1)
    return global_final, pad_windows(windows, cols_here)


def global_by_channel(
    hours, global_state, spec_filter, w_skip, w_mix, w_decode, box_lat0, box_lon0, rows_here, cols_here
):
    count = lax.axis_size("col")
    forward, inverse = fourier_tables(global_state.shape[1] * count, spec_filter.shape[1])
    base = window_base()
    high, wide = window_extent(rows_here), window_extent(cols_here)
    span = (count - 1) * (cols_here // RATIO) + wide
    lat_start = box_lat0[0] + lax.axis_index(PLANE) * (rows_here // RATIO)
    lon_start = box_lon0[0] + lax.axis_index("col") * (cols_here // RATIO)
    windows = []
    for _ in range(hours):
        global_state = global_hour(global_state, spec_filter, w_skip, w_mix, forward, inverse)
        coarse = jnp.einsum(
            "alc,ck->alk", global_state, w_decode, preferred_element_type=jnp.float32
        ).astype(jnp.bfloat16)
        coarse = lax.all_gather(coarse, "col", axis=1, tiled=True)
        coarse = jnp.pad(coarse, ((0, 0), (base, span), (0, 0)))
        coarse = lax.dynamic_slice_in_dim(coarse, box_lon0[0], base + span, 1)
        coarse = lax.all_gather(coarse, PLANE, axis=0, tiled=True)
        coarse = lax.dynamic_slice_in_dim(coarse, lon_start - box_lon0[0], wide, 1)
        coarse = jnp.pad(coarse, ((base, high), (0, 0), (0, 0)))
        coarse = lax.dynamic_slice_in_dim(coarse, lat_start, high, 0)
        windows.append(coarse)
    return global_state, pad_windows(jnp.stack(windows), cols_here)


def next_to(low, high, axis):
    count = lax.axis_size(axis)
    forward = [(i, i + 1) for i in range(count - 1)]
    backward = [(target, source) for source, target in forward]
    return lax.ppermute(low, axis, forward), lax.ppermute(high, axis, backward)


def grid_place(start_ref, total, base, extent):
    place = start_ref + base + lax.broadcasted_iota(jnp.int32, (extent, 1), 0)
    return (place >= 0) & (place < total)


def assemble_kernel(
    rows, cols, totals, high, wide, lanes, place_ref, mid0_ref, mid1_ref, above_ref, below_ref,
    left_ref, right_ref, noisy_ref, noise_ref, blend_ref,
):
    inner = RIM - RIM_USED
    pad = (noisy_ref.shape[1] - cols) // 2
    width = noisy_ref.shape[1]
    for ref, mid_ref, rim, part in ((noisy_ref, mid0_ref, RIM, 0), (noise_ref, mid1_ref, inner, RIM)):
        ref[0:rim, pad : pad + cols, :] = above_ref[part : part + rim]
        ref[rim : rim + rows, pad : pad + cols, :] = mid_ref[...]
        ref[rim + rows :, pad : pad + cols, :] = below_ref[part : part + rim]
        first = 0 if rim == RIM else rows + 2 * RIM
        ref[:, 0:pad, :] = left_ref[first : first + rows + 2 * rim]
        ref[:, pad + cols :, :] = right_ref[first : first + rows + 2 * rim]

    base = window_base()
    col = lax.broadcasted_iota(jnp.int32, (width, 1), 0) - pad
    col_in = grid_place(place_ref[1], totals[1], -pad, width)
    frac_col = ((col % RATIO).astype(jnp.float32) + 0.5) / RATIO
    col_base = jnp.where(col_in, (col + pad) // RATIO - pad // RATIO + base, -4 * high * wide)
    point = lax.broadcasted_iota(jnp.int32, (width, high * wide), 1)
    point_lat = (point // wide).astype(jnp.float32)
    point_lon = (point % wide).astype(jnp.float32)

    def weigh(index, carry):
        row = index - RIM
        whole = (row + 2 * RATIO) // RATIO - 2
        frac_row = ((row - whole * RATIO).astype(jnp.float32) + 0.5) / RATIO
        there = place_ref[0] + row
        row_base = jnp.where((there >= 0) & (there < totals[0]), whole + base, -4 * high * wide)
        shifts = noisy_ref[index, :, :].astype(jnp.float32)
        lat = row_base.astype(jnp.float32) + shifts[:, lanes : lanes + 1]
        lon = col_base.astype(jnp.float32) + shifts[:, lanes + 1 : lanes + 2]
        from_lat = point_lat - lat
        from_lon = point_lon - lon
        weight_lat = jnp.where(
            from_lat == 0.0, 1.0 - frac_row, jnp.where(from_lat == 1.0, frac_row, 0.0)
        )
        weight_lon = jnp.where(
            from_lon == 0.0, 1.0 - frac_col, jnp.where(from_lon == 1.0, frac_col, 0.0)
        )
        blend_ref[index, :, :] = (weight_lat * weight_lon).astype(jnp.bfloat16)
        return carry

    lax.fori_loop(0, rows + 2 * RIM, weigh, 0)


def assemble(rows, cols, totals, high, wide, lanes, place, mid0, mid1, above, below, left, right):
    inner = RIM - RIM_USED
    width = cols + 2 * left.shape[1]
    channels = mid0.shape[2]
    return pl.pallas_call(
        functools.partial(assemble_kernel, rows, cols, totals, high, wide, lanes),
        out_shape=(
            jax.ShapeDtypeStruct((rows + 2 * RIM, width, channels), jnp.bfloat16),
            jax.ShapeDtypeStruct((rows + 2 * inner, width, channels), jnp.bfloat16),
            jax.ShapeDtypeStruct((rows + 2 * RIM, width, high * wide), jnp.bfloat16),
        ),
        in_specs=[pl.BlockSpec(memory_space=pltpu.SMEM)]
        + [pl.BlockSpec(memory_space=pltpu.VMEM)] * 6,
        compiler_params=pltpu.CompilerParams(vmem_limit_bytes=40 * 2**20),
        cost_estimate=pl.CostEstimate(flops=2 * 10**8, bytes_accessed=10**7, transcendentals=0),
        name="assemble",
    )(place, mid0, mid1, above, below, left, right)


def silu(x):
    return x / (1.0 + jnp.exp(-x))


def denoise_kernel(
    rows, cols, totals, variables, place_ref, noisy_ref, noise_ref, blend_ref, window_ref, first_w_ref,
    down_w_ref, up_w_ref, bridge_w_ref, last_w_ref, out_ref, stack_ref, first_ref, pooled_ref,
    lifted_ref, third_ref, pair_ref, spread_ref,
):
    width = noisy_ref.shape[1]
    half = width // 2
    pad = (width - cols) // 2
    channels = noisy_ref.shape[2]
    f32, bf16 = jnp.float32, jnp.bfloat16
    col_in = grid_place(place_ref[1], totals[1], -pad, width).astype(f32)
    lane = lax.broadcasted_iota(jnp.int32, (1, channels), 1)
    is_state = lane < variables

    def flat(start, count, unit):
        return pl.ds(pl.multiple_of(start * unit, 16), count * unit)

    def inside(row, count):
        marks = []
        for step in range(count):
            there = place_ref[0] + row + step
            marks.append(col_in * jnp.where((there >= 0) & (there < totals[0]), 1.0, 0.0))
        return jnp.concatenate(marks, axis=0)

    def conv(source_ref, row, count, unit, weight_ref):
        lhs = jnp.concatenate(
            [source_ref[flat(row + step, count, unit), :] for step in range(3)], axis=1
        )
        wide = jnp.dot(lhs, weight_ref[...], preferred_element_type=f32)
        size = weight_ref.shape[1] // 3
        span = count * unit
        return (
            pltpu.roll(wide[:, :size], 1, 0)
            + wide[:, size : 2 * size]
            + pltpu.roll(wide[:, 2 * size :], span - 1, 0)
        )

    for hour in range(2):
        rim = RIM - RIM_USED * hour
        tall = rows + 2 * rim

        def stack(index, carry, hour=hour, rim=rim):
            here = flat(index * 2, 2, width)
            weights = blend_ref[pl.ds(index * 2 + RIM - rim, 2)].reshape(2 * width, -1)
            cond = jnp.dot(weights, window_ref[hour], preferred_element_type=f32).astype(bf16)
            if hour == 0:
                own = noisy_ref[pl.ds(index * 2, 2)].reshape(2 * width, channels)
            else:
                own = stack_ref[here, :]
            stack_ref[here, :] = jnp.where(is_state, own, cond)
            return carry

        lax.fori_loop(0, tall // 2, stack, 0)

        def make_first(index, carry, rim=rim):
            row = index * 4
            value = silu(conv(stack_ref, row, 4, width, first_w_ref)) * inside(row - rim + 1, 4)
            value = value.astype(bf16)
            first_ref[flat(row, 4, width), :] = value
            value = value.astype(f32)
            for step in range(2):
                at = 2 * step * width
                pair_ref[...] = value[at : at + width] + value[at + width : at + 2 * width]
                even = pair_ref[pl.ds(0, half, stride=2), :]
                odd = pair_ref[pl.ds(1, half, stride=2), :]
                pooled_ref[flat(index * 2 + step, 1, half), :] = ((even + odd) * 0.25).astype(bf16)
            return carry

        lax.fori_loop(0, (tall - 2) // 4, make_first, 0)

        half_rows = (tall - 2) // 2 - 2

        def make_lifted(index, carry):
            value = silu(conv(pooled_ref, index * 2, 2, half, down_w_ref)).astype(bf16)
            lifted_ref[flat(index * 2, 2, half), :] = jnp.dot(
                value, up_w_ref[...], preferred_element_type=f32
            )
            return carry

        lax.fori_loop(0, half_rows // 2, make_lifted, 0)

        def make_third(index, carry, rim=rim):
            row = index * 2
            lifted = lifted_ref[flat(index, 1, half), :]
            spread_ref[pl.ds(0, half, stride=2), :] = lifted
            spread_ref[pl.ds(1, half, stride=2), :] = lifted
            bridged = jnp.dot(
                first_ref[flat(row + 2, 2, width), :], bridge_w_ref[...], preferred_element_type=f32
            )
            spread = spread_ref[...]
            value = silu(bridged + jnp.concatenate([spread, spread], axis=0))
            value = value * inside(row - rim + 3, 2)
            third_ref[flat(row, 2, width), :] = value.astype(bf16)
            return carry

        lax.fori_loop(0, half_rows, make_third, 0)

        def finish(index, carry, hour=hour, rim=rim):
            row = index * 2
            skip = 1 if hour == 1 else 0
            fresh = conv(third_ref, row + skip, 2, width, last_w_ref)
            own = stack_ref[flat(row + RIM_USED + skip, 2, width), :].astype(f32)
            fresh = (own + fresh).astype(bf16)
            if hour == 0:
                noise = noise_ref[pl.ds(row, 2)].reshape(2 * width, channels).astype(f32)
                fresh = (fresh.astype(f32) + noise_level * noise) * inside(row - rim + RIM_USED, 2)
                stack_ref[flat(row, 2, width), :] = fresh.astype(bf16)
            else:
                for step in range(2):
                    at = step * width + pad
                    out_ref[row + step] = fresh[at : at + cols]
            return carry

        lax.fori_loop(0, (tall - 2 * RIM_USED) // 2 if hour == 0 else rows // 2, finish, 0)


def denoise(rows, cols, totals, variables, place, noisy, noise, blend, windows, weights):
    width, channels = noisy.shape[1:]
    tall = rows + 2 * RIM
    bf16, f32 = jnp.bfloat16, jnp.float32
    return pl.pallas_call(
        functools.partial(denoise_kernel, rows, cols, totals, variables),
        out_shape=jax.ShapeDtypeStruct((rows, cols, channels), bf16),
        in_specs=[pl.BlockSpec(memory_space=pltpu.SMEM)]
        + [pl.BlockSpec(memory_space=pltpu.VMEM)] * 9,
        scratch_shapes=[
            pltpu.VMEM((tall * width, channels), bf16),
            pltpu.VMEM((tall * width, channels), bf16),
            pltpu.VMEM((tall // 2 * width // 2, channels), bf16),
            pltpu.VMEM((tall // 2 * width // 2, channels), f32),
            pltpu.VMEM((tall * width, channels), bf16),
            pltpu.VMEM((width, channels), f32),
            pltpu.VMEM((width, channels), f32),
        ],
        compiler_params=pltpu.CompilerParams(vmem_limit_bytes=40 * 2**20),
        cost_estimate=pl.CostEstimate(
            flops=10**10, bytes_accessed=10**7, transcendentals=4 * 10**6
        ),
        name="denoise",
    )(place, noisy, noise, blend, windows, *weights)


def conv_weight(weight, depth, width):
    out, _, given = weight.shape
    weight = weight.reshape(out, 3, 3, given)
    weight = jnp.pad(weight, ((0, width - out), (0, 0), (0, 0), (0, depth - given)))
    return jnp.transpose(weight, (1, 3, 2, 0)).reshape(3 * depth, 3 * width)


def shards(
    global_state,
    spec_filter,
    w_skip,
    w_mix,
    w_decode,
    regional_state,
    noise_draws,
    w_first,
    w_down,
    w_up,
    w_bridge,
    w_last,
    box_lat0,
    box_lon0,
    stencil_lat,
    stencil_lon,
):
    hours = noise_draws.shape[0]
    rows_here, cols_here = regional_state.shape[1:]
    row_start = lax.axis_index(PLANE) * rows_here
    col_start = lax.axis_index("col") * cols_here
    total_rows = rows_here * lax.axis_size(PLANE)
    total_cols = cols_here * lax.axis_size("col")
    assert hours == 2

    by_latitude = global_state.shape[0] % lax.axis_size("col") == 0
    global_steps = global_by_latitude if by_latitude else global_by_channel
    global_final, windows = global_steps(
        hours, global_state, spec_filter, w_skip, w_mix, w_decode, box_lat0, box_lon0,
        rows_here, cols_here,
    )

    variables = regional_state.shape[0]
    conds = w_decode.shape[1]
    lanes = variables + conds
    noisy = (
        regional_state.astype(jnp.float32) + noise_level * noise_draws[0].astype(jnp.float32)
    ).astype(jnp.bfloat16)
    lat_shift = stencil_lat - (row_start + jnp.arange(rows_here, dtype=jnp.int32))[:, None] // RATIO
    lon_shift = stencil_lon - (col_start + jnp.arange(cols_here, dtype=jnp.int32))[None, :] // RATIO
    mid0 = jnp.concatenate(
        [
            jnp.transpose(noisy, (1, 2, 0)),
            jnp.zeros((rows_here, cols_here, conds), jnp.bfloat16),
            lat_shift.astype(jnp.bfloat16)[..., None],
            lon_shift.astype(jnp.bfloat16)[..., None],
            jnp.zeros((rows_here, cols_here, LANES - lanes - 2), jnp.bfloat16),
        ],
        axis=2,
    )
    mid1 = jnp.pad(
        jnp.transpose(noise_draws[1], (1, 2, 0)), ((0, 0), (0, 0), (0, LANES - variables))
    )
    inner = RIM - RIM_USED
    above, below = next_to(
        jnp.concatenate([mid0[rows_here - RIM :], mid1[rows_here - inner :]], axis=0),
        jnp.concatenate([mid0[:RIM], mid1[:inner]], axis=0),
        PLANE,
    )

    def rim_cols(part):
        return jnp.concatenate(
            [
                above[:RIM, part], mid0[:, part], below[:RIM, part],
                above[RIM:, part], mid1[:, part], below[RIM:, part],
            ],
            axis=0,
        )

    left, right = next_to(
        rim_cols(slice(cols_here - RIM_COLS, cols_here)), rim_cols(slice(0, RIM_COLS)), "col"
    )
    high, wide = window_extent(rows_here), window_stride(cols_here)
    place = jnp.stack([row_start, col_start]).astype(jnp.int32)
    totals = (total_rows, total_cols)
    noisy, noise, blend = assemble(
        rows_here, cols_here, totals, high, wide, lanes, place, mid0, mid1, above, below, left, right
    )
    weights = (
        conv_weight(w_first, LANES, w_first.shape[0]),
        conv_weight(w_down, w_down.shape[2], w_down.shape[0]),
        w_up.T,
        w_bridge.T,
        conv_weight(w_last, w_last.shape[2], LANES),
    )
    windows = jnp.pad(windows, ((0, 0), (0, 0), (0, 0), (variables, LANES - lanes))).reshape(
        hours, high * wide, LANES
    )
    regional_final = denoise(
        rows_here, cols_here, totals, variables, place, noisy, noise, blend, windows, weights
    )
    return global_final, jnp.transpose(regional_final[:, :, :variables], (2, 0, 1))


def solution(mesh):
    return jax.shard_map(
        shards,
        mesh=mesh,
        in_specs=(
            P(PLANE, "col", None),
            P(None, None, "col"),
            P(),
            P(),
            P(),
            P(None, PLANE, "col"),
            P(None, None, PLANE, "col"),
            P(),
            P(),
            P(),
            P(),
            P(),
            P(),
            P(),
            P(PLANE, "col"),
            P(PLANE, "col"),
        ),
        out_specs=(P(PLANE, "col", None), P(None, PLANE, "col")),
        check_vma=False,
    )
```

profile of v0, /device:TPU:8, one launch (start us, length us, event | category | flops | bytes accessed | tf_op | source)
XLA Modules:
  0.0 231.9 jit_solution(3086462472244663359)
XLA Ops:
  5.6 2.0 collective-permute-start.5
  14.1 2.0 fusion.19
  20.8 3.0 %concatenate.19.mid0_ref = bf16[16,128,128]{2,1,0:T(8,128)(2,1)S(1)} concatenate(bf16[16,128,99]{2,1,0:T(8,128)(2,1)S(1)} %copy-done.21, bf16[16,128,26]{2,1,0:T(8,128)(2,1)} %broadcast_in_dim.74, bf16[16,128,1]{2,1,0:T(8,128)(2,1)} %copy.61, bf16[16,128,1]{2,1,0:T(8,128)(2,1)} %copy.62, bf16[16,128,1]{2,1,0:T(8,128)(2,1)} %broadcast_in_dim.77), dimensions={2} | concatenate | bytes 1048576 | tf_op jit(solution)/shard_map/concatenate | solution.py:530
  34.7 3.6 %dynamic_update_slice.61 = bf16[4,180,96]{2,0,1:T(4,128)(2,1)} dynamic-update-slice(bf16[4,180,96]{2,0,1:T(4,128)(2,1)} %copy.54, bf16[1,180,96]{2,0,1:T(2,128)(2,1)} %copy.55, s32[]{:T(128)S(6)} %select_n.173, s32[]{:T(128)} %constant.173.clone.1, s32[]{:T(128)} %constant.173.clone.1) | dynamic-update-slice | bytes 69124 | tf_op jit(solution)/shard_map/dynamic_update_slice | solution.py:59
  38.4 3.6 %dynamic_update_slice.62 = bf16[4,180,96]{2,0,1:T(4,128)(2,1)} dynamic-update-slice(bf16[4,180,96]{2,0,1:T(4,128)(2,1)} %dynamic_update_slice.61, bf16[1,180,96]{2,0,1:T(2,128)(2,1)} %copy.57, s32[]{:T(128)S(6)} %select_n.177, s32[]{:T(128)} %constant.173.clone.1, s32[]{:T(128)} %constant.173.clone.1) | dynamic-update-slice | bytes 69124 | tf_op jit(solution)/shard_map/dynamic_update_slice | solution.py:59
  42.0 1.8 broadcast_in_dim.66
  43.8 1.9 pad_maximum_fusion.1
  45.7 4.2 %collective-permute-start.19 = (bf16[14,128,128]{2,1,0:T(8,128)(2,1)}, bf16[14,128,128]{2,1,0:T(8,128)(2,1)}, u32[]{:S(2)}, u32[]{:S(2)}) collective-permute-start(bf16[14,128,128]{2,1,0:T(8,128)(2,1)} %pad_maximum_fusion.1), channel_id=1, source_target_pairs={{0,4},{4,8},{8,12},{12,16},{16,20},{20,24},{24,28},{1,5},{5,9},{9,... | collective-permute-start | bytes 1376264 | tf_op jit(solution)/shard_map/ppermute | solution.py:262
  55.3 1.9 pad.43
  59.9 2.6 %collective-permute-start.7 = (bf16[360,384]{1,0:T(8,128)(2,1)}, bf16[360,384]{1,0:T(8,128)(2,1)}, u32[]{:S(2)}, u32[]{:S(2)}) collective-permute-start(bf16[360,384]{1,0:T(8,128)(2,1)} %broadcast_in_dim.69), channel_id=1, source_target_pairs={{0,4},{4,8},{8,12},{12,0},{1,5},{5,9},{9,13},{13,1},{2,6},{6,10},{... | collective-permute-start | bytes 829448 | tf_op jit(solution)/shard_map/ppermute | solution.py:55
  69.9 2.2 copy.72
  72.1 2.1 copy.85
  79.1 2.4 %collective-permute-start.9 = (bf16[360,384]{1,0:T(8,128)(2,1)S(1)}, bf16[360,384]{1,0:T(8,128)(2,1)S(1)}, u32[]{:S(2)}, u32[]{:S(2)}) collective-permute-start(bf16[360,384]{1,0:T(8,128)(2,1)S(1)} %copy-done.23), channel_id=1, source_target_pairs={{0,12},{4,0},{8,4},{12,8},{1,13},{5,1},{9,5},{13,9},{2,14},{6,2},{... | collective-permute-start | bytes 829448 | tf_op jit(solution)/shard_map/ppermute | solution.py:55
  82.5 3.5 %collective-permute-start.1 = (bf16[1,360,384]{2,1,0:T(8,128)(2,1)S(1)}, bf16[1,360,384]{2,1,0:T(8,128)(2,1)S(1)}, u32[]{:S(2)}, u32[]{:S(2)}) collective-permute-start(bf16[1,360,384]{2,1,0:T(8,128)(2,1)S(1)} %get-tuple-element.28), channel_id=1, source_target_pairs={{0,2},{1,3},{2,0},{3,1},{4,6},{5,7},{6,4},{7,5},{8,10},{9,11},{10,... | collective-permute-start | bytes 829448 | tf_op jit(solution)/shard_map/ppermute | solution.py:44
  88.7 2.5 %collective-permute-start.14 = (bf16[1,360,384]{2,1,0:T(8,128)(2,1)S(1)}, bf16[1,360,384]{2,1,0:T(8,128)(2,1)S(1)}, u32[]{:S(2)}, u32[]{:S(2)}) collective-permute-start(bf16[1,360,384]{2,1,0:T(8,128)(2,1)S(1)} %get-tuple-element.34), channel_id=1, source_target_pairs={{0,2},{1,3},{2,0},{3,1},{4,6},{5,7},{6,4},{7,5},{8,10},{9,11},{10,... | collective-permute-start | bytes 829448 | tf_op jit(solution)/shard_map/ppermute | solution.py:44
  99.6 2.6 %collective-permute-start.21 = (bf16[60,16,128]{2,1,0:T(8,128)(2,1)}, bf16[60,16,128]{2,1,0:T(8,128)(2,1)}, u32[]{:S(2)}, u32[]{:S(2)}) collective-permute-start(bf16[60,16,128]{2,1,0:T(8,128)(2,1)} %get-tuple-element.47), channel_id=1, source_target_pairs={{0,1},{1,2},{2,3},{4,5},{5,6},{6,7},{8,9},{9,10},{10,11},{12,13},{... | collective-permute-start | bytes 737288 | tf_op jit(solution)/shard_map/ppermute | solution.py:262
  102.2 13.7 %collective-permute-done.1 = bf16[1,360,384]{2,1,0:T(8,128)(2,1)S(1)} collective-permute-done((bf16[1,360,384]{2,1,0:T(8,128)(2,1)S(1)}, bf16[1,360,384]{2,1,0:T(8,128)(2,1)S(1)}, u32[]{:S(2)}, u32[]{:S(2)}) %collective-permute-start.1) | collective-permute-done | bytes 276512 | tf_op jit(solution)/shard_map/ppermute | solution.py:44
  115.9 1.9 collective-permute-start.22
  117.9 3.9 %collective-permute-done.14 = bf16[1,360,384]{2,1,0:T(8,128)(2,1)S(1)} collective-permute-done((bf16[1,360,384]{2,1,0:T(8,128)(2,1)S(1)}, bf16[1,360,384]{2,1,0:T(8,128)(2,1)S(1)}, u32[]{:S(2)}, u32[]{:S(2)}) %collective-permute-start.14) | collective-permute-done | bytes 276512 | tf_op jit(solution)/shard_map/ppermute | solution.py:44
  122.0 2.2 copy-done.17
  124.3 2.3 copy-done.18
  126.5 15.3 %advance_latitude.2 = (bf16[1440,384]{1,0:T(8,128)(2,1)S(1)}, bf16[2,1440,128]{2,1,0:T(8,128)(2,1)S(1)}) custom-call(bf16[1440,384]{1,0:T(8,128)(2,1)S(1)} %bitcast.78, bf16[1440,1440]{1,0:T(8,128)(2,1)S(1)} %copy-done.17, bf16[1440,1440]{1,0:T(8,128)(2,1)S(1)} %copy-done.18, bf16[1440,384]{1,0:T(8,128)(2,1)S(1)} %bitcast.83, ...), custom_call_target="tpu_custom_call" | custom-call | flops 8351907840 | bytes 12582912 | tf_op jit(solution)/shard_map/advance_latitude/pallas_call | solution.py:123
  141.9 15.4 %advance_latitude.3 = (bf16[1440,384]{1,0:T(8,128)(2,1)S(1)}, bf16[2,1440,128]{2,1,0:T(8,128)(2,1)S(1)}) custom-call(bf16[1440,384]{1,0:T(8,128)(2,1)S(1)} %bitcast.77, bf16[1440,1440]{1,0:T(8,128)(2,1)S(1)} %copy-done.17, bf16[1440,1440]{1,0:T(8,128)(2,1)S(1)} %copy-done.18, bf16[1440,384]{1,0:T(8,128)(2,1)S(1)} %bitcast.84, ...), custom_call_target="tpu_custom_call" | custom-call | flops 8351907840 | bytes 12582912 | tf_op jit(solution)/shard_map/advance_latitude/pallas_call | solution.py:123
  159.5 4.0 %collective-permute-start.16 = (bf16[1,360,384]{2,1,0:T(8,128)(2,1)}, bf16[1,360,384]{2,1,0:T(8,128)(2,1)}, u32[]{:S(2)}, u32[]{:S(2)}) collective-permute-start(bf16[1,360,384]{2,1,0:T(8,128)(2,1)} %constant_dynamic-slice_fusion.2), channel_id=1, source_target_pairs={{0,1},{1,2},{2,3},{3,0},{4,5},{5,6},{6,7},{7,4},{8,9},{9,10},{10,1... | collective-permute-start | bytes 829448 | tf_op jit(solution)/shard_map/ppermute | solution.py:44
  164.3 3.0 %all-to-all-start = ((bf16[32,24,128]{2,1,0:T(8,128)(2,1)}), bf16[32,24,128]{2,1,0:T(8,128)(2,1)}, u32[]{:S(2)}, u32[]{:S(2)}) async-start(bf16[32,24,128]{2,1,0:T(8,128)(2,1)} %bitcast.24), calls=%async_computation | async-start | bytes 393216 | tf_op jit(solution)/shard_map/all_to_all | solution.py:222
  167.4 6.5 %assemble.1 = (bf16[34,160,128]{2,1,0:T(8,128)(2,1)S(1)}, bf16[26,160,128]{2,1,0:T(8,128)(2,1)S(1)}, bf16[34,160,256]{2,1,0:T(8,128)(2,1)S(1)}) custom-call(s32[2]{0:T(128)S(1)} %pad_add_fusion.place_ref, bf16[16,128,128]{2,1,0:T(8,128)(2,1)S(1)} %concatenate.19.mid0_ref, bf16[16,128,128]{2,1,0:T(8,128)(2,1)S(1)} %pad.37.mid1_ref, ...), custom_call_target="tpu_custom_call" | custom-call | flops 200000000 | bytes 10000000 | tf_op jit(solution)/shard_map/assemble/pallas_call | solution.py:321
  176.0 2.1 constant_dynamic-slice_fusion.6
  180.3 1.9 constant_dynamic-slice_fusion
  182.8 2.3 collective-permute-start.18
  186.2 2.4 %reshape.144 = bf16[8,4,2,2,22,26]{5,4,3,2,0,1:T(8,128)(2,1)} reshape(bf16[8,4,2288]{2,0,1:T(8,128)(2,1)S(1)} %copy.68) | data formatting | bytes 292864 | tf_op jit(solution)/shard_map/reshape | solution.py:223
  188.6 1.8 copy.69
  193.7 32.2 %denoise.1 = bf16[16,128,128]{2,1,0:T(8,128)(2,1)S(1)} custom-call(s32[2]{0:T(128)S(1)} %copy-done.8, bf16[34,160,128]{2,1,0:T(8,128)(2,1)S(1)} %copy-done.12, bf16[26,160,128]{2,1,0:T(8,128)(2,1)S(1)} %copy-done.14, bf16[34,160,256]{2,1,0:T(8,128)(2,1)S(1)} %copy-done.10, bf16[2,256,128]{2,1,0:T(8,128)(2,1)S(1)} %bitcast.88, ...), custom_call_target="tpu_custom_call" | custom-call | flops 10000000000 | bytes 10000000 | tf_op jit(solution)/shard_map/denoise/pallas_call | solution.py:460
  (172 shorter events, 76.3 us)
Async XLA Ops:
  3.0 24.0 %collective-permute-start.3 = (bf16[180,96]{0,1:T(8,128)(2,1)}, bf16[180,96]{0,1:T(8,128)(2,1)}, u32[]{:S(2)}, u32[]{:S(2)}) collective-permute-start(bf16[180,96]{0,1:T(8,128)(2,1)} %constant_dynamic-slice_fusion.9), channel_id=1, source_target_pairs={{0,1},{1,2},{2,3},{3,0},{4,5},{5,6},{6,7},{7,4},{8,9},{9,10},{10,1... | collective-permute-start | bytes 103688 | tf_op jit(solution)/shard_map/ppermute | solution.py:55
  4.6 27.0 %collective-permute-start.4 = (bf16[180,96]{0,1:T(8,128)(2,1)}, bf16[180,96]{0,1:T(8,128)(2,1)}, u32[]{:S(2)}, u32[]{:S(2)}) collective-permute-start(bf16[180,96]{0,1:T(8,128)(2,1)} %constant_dynamic-slice_fusion.9), channel_id=1, source_target_pairs={{0,2},{1,3},{2,0},{3,1},{4,6},{5,7},{6,4},{7,5},{8,10},{9,11},{10,... | collective-permute-start | bytes 103688 | tf_op jit(solution)/shard_map/ppermute | solution.py:55
  5.6 27.6 %collective-permute-start.5 = (bf16[180,96]{0,1:T(8,128)(2,1)}, bf16[180,96]{0,1:T(8,128)(2,1)}, u32[]{:S(2)}, u32[]{:S(2)}) collective-permute-start(bf16[180,96]{0,1:T(8,128)(2,1)} %constant_dynamic-slice_fusion.9), channel_id=1, source_target_pairs={{0,3},{1,0},{2,1},{3,2},{4,7},{5,4},{6,5},{7,6},{8,11},{9,8},{10,9... | collective-permute-start | bytes 103688 | tf_op jit(solution)/shard_map/ppermute | solution.py:55
  10.2 67.0 %collective-permute-start = (bf16[1,360,384]{2,1,0:T(8,128)(2,1)}, bf16[1,360,384]{2,1,0:T(8,128)(2,1)}, u32[]{:S(2)}, u32[]{:S(2)}) collective-permute-start(bf16[1,360,384]{2,1,0:T(8,128)(2,1)} %constant_dynamic-slice_fusion.12), channel_id=1, source_target_pairs={{0,1},{1,2},{2,3},{3,0},{4,5},{5,6},{6,7},{7,4},{8,9},{9,10},{10,1... | collective-permute-start | bytes 829448 | tf_op jit(solution)/shard_map/ppermute | solution.py:44
  11.0 68.1 %collective-permute-start.13 = (bf16[1,360,384]{2,1,0:T(8,128)(2,1)}, bf16[1,360,384]{2,1,0:T(8,128)(2,1)}, u32[]{:S(2)}, u32[]{:S(2)}) collective-permute-start(bf16[1,360,384]{2,1,0:T(8,128)(2,1)} %constant_dynamic-slice_fusion.5), channel_id=1, source_target_pairs={{0,1},{1,2},{2,3},{3,0},{4,5},{5,6},{6,7},{7,4},{8,9},{9,10},{10,1... | collective-permute-start | bytes 829448 | tf_op jit(solution)/shard_map/ppermute | solution.py:44
  26.0 16.0 %copy-start.19 = (bf16[1,99,16,128]{1,3,2,0:T(8,128)(2,1)}, bf16[1,99,16,128]{1,3,2,0:T(8,128)(2,1)S(1)}, u32[]{:S(2)}) copy-start(bf16[1,99,16,128]{1,3,2,0:T(8,128)(2,1)S(1)} %copy.80) | copy-start | bytes 1216516
  42.0 7.9 %copy-start.24 = (bf16[5,128,128]{2,1,0:T(8,128)(2,1)S(1)}, bf16[5,128,128]{2,1,0:T(8,128)(2,1)}, u32[]{:S(2)}) copy-start(bf16[5,128,128]{2,1,0:T(8,128)(2,1)} %get-tuple-element.44) | copy-start | bytes 491524
  43.8 13.4 %collective-permute-start.6 = (bf16[180,384]{1,0:T(8,128)(2,1)}, bf16[180,384]{1,0:T(8,128)(2,1)}, u32[]{:S(2)}, u32[]{:S(2)}) collective-permute-start(bf16[180,384]{1,0:T(8,128)(2,1)} %broadcast_in_dim.66), channel_id=1, source_target_pairs={{0,16},{16,0},{1,17},{17,1},{2,18},{18,2},{3,19},{19,3},{4,20},{20... | collective-permute-start | bytes 414728 | tf_op jit(solution)/shard_map/ppermute | solution.py:55
  45.7 45.6 %collective-permute-start.19 = (bf16[14,128,128]{2,1,0:T(8,128)(2,1)}, bf16[14,128,128]{2,1,0:T(8,128)(2,1)}, u32[]{:S(2)}, u32[]{:S(2)}) collective-permute-start(bf16[14,128,128]{2,1,0:T(8,128)(2,1)} %pad_maximum_fusion.1), channel_id=1, source_target_pairs={{0,4},{4,8},{8,12},{12,16},{16,20},{20,24},{24,28},{1,5},{5,9},{9,... | collective-permute-start | bytes 1376264 | tf_op jit(solution)/shard_map/ppermute | solution.py:262
  50.7 44.1 %collective-permute-start.20 = (bf16[14,128,128]{2,1,0:T(8,128)(2,1)}, bf16[14,128,128]{2,1,0:T(8,128)(2,1)}, u32[]{:S(2)}, u32[]{:S(2)}) collective-permute-start(bf16[14,128,128]{2,1,0:T(8,128)(2,1)} %pad_maximum_fusion.2), channel_id=1, source_target_pairs={{4,0},{8,4},{12,8},{16,12},{20,16},{24,20},{28,24},{5,1},{9,5},{13... | collective-permute-start | bytes 1376264 | tf_op jit(solution)/shard_map/ppermute | solution.py:262
  55.3 7.3 %copy-start.22 = (bf16[128,3,3,128]{0,2,3,1:T(4,128)(2,1)S(1)}, bf16[128,3,3,128]{0,2,3,1:T(4,128)(2,1)}, u32[]{:S(2)}) copy-start(bf16[128,3,3,128]{0,2,3,1:T(4,128)(2,1)} %pad.44) | copy-start | bytes 884740
  59.9 22.6 %collective-permute-start.7 = (bf16[360,384]{1,0:T(8,128)(2,1)}, bf16[360,384]{1,0:T(8,128)(2,1)}, u32[]{:S(2)}, u32[]{:S(2)}) collective-permute-start(bf16[360,384]{1,0:T(8,128)(2,1)} %broadcast_in_dim.69), channel_id=1, source_target_pairs={{0,4},{4,8},{8,12},{12,0},{1,5},{5,9},{9,13},{13,1},{2,6},{6,10},{... | collective-permute-start | bytes 829448 | tf_op jit(solution)/shard_map/ppermute | solution.py:55
  77.2 10.0 %collective-permute-start.8 = (bf16[360,384]{1,0:T(8,128)(2,1)}, bf16[360,384]{1,0:T(8,128)(2,1)S(1)}, u32[]{:S(2)}, u32[]{:S(2)}) collective-permute-start(bf16[360,384]{1,0:T(8,128)(2,1)} %broadcast_in_dim.69), channel_id=1, source_target_pairs={{0,8},{4,12},{8,0},{12,4},{1,9},{5,13},{9,1},{13,5},{2,10},{6,14},... | collective-permute-start | bytes 829448 | tf_op jit(solution)/shard_map/ppermute | solution.py:55
  79.1 9.6 %collective-permute-start.9 = (bf16[360,384]{1,0:T(8,128)(2,1)S(1)}, bf16[360,384]{1,0:T(8,128)(2,1)S(1)}, u32[]{:S(2)}, u32[]{:S(2)}) collective-permute-start(bf16[360,384]{1,0:T(8,128)(2,1)S(1)} %copy-done.23), channel_id=1, source_target_pairs={{0,12},{4,0},{8,4},{12,8},{1,13},{5,1},{9,5},{13,9},{2,14},{6,2},{... | collective-permute-start | bytes 829448 | tf_op jit(solution)/shard_map/ppermute | solution.py:55
  82.5 33.4 %collective-permute-start.1 = (bf16[1,360,384]{2,1,0:T(8,128)(2,1)S(1)}, bf16[1,360,384]{2,1,0:T(8,128)(2,1)S(1)}, u32[]{:S(2)}, u32[]{:S(2)}) collective-permute-start(bf16[1,360,384]{2,1,0:T(8,128)(2,1)S(1)} %get-tuple-element.28), channel_id=1, source_target_pairs={{0,2},{1,3},{2,0},{3,1},{4,6},{5,7},{6,4},{7,5},{8,10},{9,11},{10,... | collective-permute-start | bytes 829448 | tf_op jit(solution)/shard_map/ppermute | solution.py:44
  86.2 11.4 %copy-start.20 = (bf16[1,99,16,128]{1,3,2,0:T(8,128)(2,1)S(1)}, bf16[1,99,16,128]{1,3,2,0:T(8,128)(2,1)}, u32[]{:S(2)}) copy-start(bf16[1,99,16,128]{1,3,2,0:T(8,128)(2,1)} %copy-done.19) | copy-start | bytes 1216516
  87.2 34.6 %collective-permute-start.2 = (bf16[1,360,384]{2,1,0:T(8,128)(2,1)S(1)}, bf16[1,360,384]{2,1,0:T(8,128)(2,1)S(1)}, u32[]{:S(2)}, u32[]{:S(2)}) collective-permute-start(bf16[1,360,384]{2,1,0:T(8,128)(2,1)S(1)} %get-tuple-element.27), channel_id=1, source_target_pairs={{0,3},{1,0},{2,1},{3,2},{4,7},{5,4},{6,5},{7,6},{8,11},{9,8},{10,9... | collective-permute-start | bytes 829448 | tf_op jit(solution)/shard_map/ppermute | solution.py:44
  88.7 33.1 %collective-permute-start.14 = (bf16[1,360,384]{2,1,0:T(8,128)(2,1)S(1)}, bf16[1,360,384]{2,1,0:T(8,128)(2,1)S(1)}, u32[]{:S(2)}, u32[]{:S(2)}) collective-permute-start(bf16[1,360,384]{2,1,0:T(8,128)(2,1)S(1)} %get-tuple-element.34), channel_id=1, source_target_pairs={{0,2},{1,3},{2,0},{3,1},{4,6},{5,7},{6,4},{7,5},{8,10},{9,11},{10,... | collective-permute-start | bytes 829448 | tf_op jit(solution)/shard_map/ppermute | solution.py:44
  91.3 30.6 %collective-permute-start.15 = (bf16[1,360,384]{2,1,0:T(8,128)(2,1)S(1)}, bf16[1,360,384]{2,1,0:T(8,128)(2,1)S(1)}, u32[]{:S(2)}, u32[]{:S(2)}) collective-permute-start(bf16[1,360,384]{2,1,0:T(8,128)(2,1)S(1)} %get-tuple-element.33), channel_id=1, source_target_pairs={{0,3},{1,0},{2,1},{3,2},{4,7},{5,4},{6,5},{7,6},{8,11},{9,8},{10,9... | collective-permute-start | bytes 829448 | tf_op jit(solution)/shard_map/ppermute | solution.py:44
  99.6 67.8 %collective-permute-start.21 = (bf16[60,16,128]{2,1,0:T(8,128)(2,1)}, bf16[60,16,128]{2,1,0:T(8,128)(2,1)}, u32[]{:S(2)}, u32[]{:S(2)}) collective-permute-start(bf16[60,16,128]{2,1,0:T(8,128)(2,1)} %get-tuple-element.47), channel_id=1, source_target_pairs={{0,1},{1,2},{2,3},{4,5},{5,6},{6,7},{8,9},{9,10},{10,11},{12,13},{... | collective-permute-start | bytes 737288 | tf_op jit(solution)/shard_map/ppermute | solution.py:262
  115.9 51.5 %collective-permute-start.22 = (bf16[60,16,128]{2,1,0:T(8,128)(2,1)}, bf16[60,16,128]{2,1,0:T(8,128)(2,1)}, u32[]{:S(2)}, u32[]{:S(2)}) collective-permute-start(bf16[60,16,128]{2,1,0:T(8,128)(2,1)} %get-tuple-element.46), channel_id=1, source_target_pairs={{1,0},{2,1},{3,2},{5,4},{6,5},{7,6},{9,8},{10,9},{11,10},{13,12},{... | collective-permute-start | bytes 737288 | tf_op jit(solution)/shard_map/ppermute | solution.py:262
  141.9 15.5 %copy-start = (bf16[1440,384]{1,0:T(8,128)(2,1)}, bf16[1440,384]{1,0:T(8,128)(2,1)S(1)}, u32[]{:S(2)}) copy-start(bf16[1440,384]{1,0:T(8,128)(2,1)S(1)} %get-tuple-element.9) | copy-start | bytes 3317764
  158.1 17.9 %collective-permute-start.10 = (bf16[1,360,384]{2,1,0:T(8,128)(2,1)}, bf16[1,360,384]{2,1,0:T(8,128)(2,1)}, u32[]{:S(2)}, u32[]{:S(2)}) collective-permute-start(bf16[1,360,384]{2,1,0:T(8,128)(2,1)} %constant_dynamic-slice_fusion.8), channel_id=1, source_target_pairs={{0,1},{1,2},{2,3},{3,0},{4,5},{5,6},{6,7},{7,4},{8,9},{9,10},{10,1... | collective-permute-start | bytes 829448 | tf_op jit(solution)/shard_map/ppermute | solution.py:44
  159.5 20.8 %collective-permute-start.16 = (bf16[1,360,384]{2,1,0:T(8,128)(2,1)}, bf16[1,360,384]{2,1,0:T(8,128)(2,1)}, u32[]{:S(2)}, u32[]{:S(2)}) collective-permute-start(bf16[1,360,384]{2,1,0:T(8,128)(2,1)} %constant_dynamic-slice_fusion.2), channel_id=1, source_target_pairs={{0,1},{1,2},{2,3},{3,0},{4,5},{5,6},{6,7},{7,4},{8,9},{9,10},{10,1... | collective-permute-start | bytes 829448 | tf_op jit(solution)/shard_map/ppermute | solution.py:44
  164.3 20.8 %all-to-all-start = ((bf16[32,24,128]{2,1,0:T(8,128)(2,1)}), bf16[32,24,128]{2,1,0:T(8,128)(2,1)}, u32[]{:S(2)}, u32[]{:S(2)}) async-start(bf16[32,24,128]{2,1,0:T(8,128)(2,1)} %bitcast.24), calls=%async_computation | async-start | bytes 393216 | tf_op jit(solution)/shard_map/all_to_all | solution.py:222
  167.4 6.5 %copy-start.7 = (s32[2]{0:T(128)}, s32[2]{0:T(128)S(1)}, u32[]{:S(2)}) copy-start(s32[2]{0:T(128)S(1)} %pad_add_fusion.place_ref) | copy-start | bytes 28
  167.4 8.6 %copy-start.1 = (bf16[1440,384]{1,0:T(8,128)(2,1)S(1)}, bf16[1440,384]{1,0:T(8,128)(2,1)}, u32[]{:S(2)}) copy-start(bf16[1440,384]{1,0:T(8,128)(2,1)} %copy-done) | copy-start | bytes 3317764
  176.0 6.2 %copy-start.9 = (bf16[34,160,256]{2,1,0:T(8,128)(2,1)}, bf16[34,160,256]{2,1,0:T(8,128)(2,1)S(1)}, u32[]{:S(2)}) copy-start(bf16[34,160,256]{2,1,0:T(8,128)(2,1)S(1)} %get-tuple-element.13.blend_ref) | copy-start | bytes 8355844
  178.0 49.1 %collective-permute-start.11 = (bf16[1,360,384]{2,1,0:T(8,128)(2,1)}, bf16[1,360,384]{2,1,0:T(8,128)(2,1)}, u32[]{:S(2)}, u32[]{:S(2)}) collective-permute-start(bf16[1,360,384]{2,1,0:T(8,128)(2,1)} %get-tuple-element.25), channel_id=1, source_target_pairs={{0,2},{1,3},{2,0},{3,1},{4,6},{5,7},{6,4},{7,5},{8,10},{9,11},{10,... | collective-permute-start | bytes 829448 | tf_op jit(solution)/shard_map/ppermute | solution.py:44
  179.8 48.4 %collective-permute-start.12 = (bf16[1,360,384]{2,1,0:T(8,128)(2,1)}, bf16[1,360,384]{2,1,0:T(8,128)(2,1)S(1)}, u32[]{:S(2)}, u32[]{:S(2)}) collective-permute-start(bf16[1,360,384]{2,1,0:T(8,128)(2,1)} %get-tuple-element.24), channel_id=1, source_target_pairs={{0,3},{1,0},{2,1},{3,2},{4,7},{5,4},{6,5},{7,6},{8,11},{9,8},{10,9... | collective-permute-start | bytes 829448 | tf_op jit(solution)/shard_map/ppermute | solution.py:44
  182.2 46.0 %collective-permute-start.17 = (bf16[1,360,384]{2,1,0:T(8,128)(2,1)}, bf16[1,360,384]{2,1,0:T(8,128)(2,1)}, u32[]{:S(2)}, u32[]{:S(2)}) collective-permute-start(bf16[1,360,384]{2,1,0:T(8,128)(2,1)} %get-tuple-element.31), channel_id=1, source_target_pairs={{0,2},{1,3},{2,0},{3,1},{4,6},{5,7},{6,4},{7,5},{8,10},{9,11},{10,... | collective-permute-start | bytes 829448 | tf_op jit(solution)/shard_map/ppermute | solution.py:44
  182.8 46.4 %collective-permute-start.18 = (bf16[1,360,384]{2,1,0:T(8,128)(2,1)}, bf16[1,360,384]{2,1,0:T(8,128)(2,1)}, u32[]{:S(2)}, u32[]{:S(2)}) collective-permute-start(bf16[1,360,384]{2,1,0:T(8,128)(2,1)} %get-tuple-element.30), channel_id=1, source_target_pairs={{0,3},{1,0},{2,1},{3,2},{4,7},{5,4},{6,5},{7,6},{8,11},{9,8},{10,9... | collective-permute-start | bytes 829448 | tf_op jit(solution)/shard_map/ppermute | solution.py:44
  (20 other events, 48.1 us)
where the time goes:
time: 236 us; the launch traced here: 232 us
  local copies, waits for them, and re-layouts  93 us (39%)
  Pallas kernels  69.4 us (29%)
  starting transfers between devices  42.5 us (18%)
  waiting for transfers between devices  17.7 us (8%)
  other arithmetic  6.65 us (3%)
  between operations  2.63 us (1%)
    pallas_call x1, Pallas kernels, denoise(): pl.pallas_call(functools.partial(denoise_kernel, rows, cols, totals, vari...  32.2 us
    pallas_call x2, Pallas kernels, advance_latitude(): pl.pallas_call(functools.partial(latitude_kernel, hours, block), out_shap...  30.7 us
    unnamed x71, local copies, waits for them, and re-layouts  26.2 us
    ppermute x12, starting transfers between devices, exchange(): pieces.append(lax.ppermute(piece, axis, shift_pairs(count, step)))  19 us
    ppermute x12, waiting for transfers between devices, exchange(): pieces.append(lax.ppermute(piece, axis, shift_pairs(count, step)))  17.7 us
    dynamic_update_slice x8, local copies, waits for them, and re-layouts, collect(): lax.dynamic_update_slice_in_dim(result, piece[None], (me - step) % count, 0)  12.5 us
    ppermute x7, starting transfers between devices, collect(): lax.ppermute(block, axis, shift_pairs(count, step))  10.4 us
    dynamic_slice x8, local copies, waits for them, and re-layouts, exchange(): lax.dynamic_index_in_dim(blocks, (me + step) % count, 0, keepdims=True)  9.03 us
  transfers between devices with their start and end apart: 24, of which 2 were waited for; matrix products, arithmetic and copies ran while one was open for 37% of the time, Pallas kernels for 30%

commit v1 on v0

--- a/solution.py
+++ b/solution.py
@@ -31,46 +31,22 @@
     return jnp.asarray(forward), jnp.asarray(inverse)
 
 
-def shift_pairs(count, step):
-    return [(source, (source + step) % count) for source in range(count)]
-
-
 def exchange(blocks, axis):
-    count = lax.axis_size(axis)
-    me = lax.axis_index(axis)
-    pieces = []
-    for step in range(1, count):
-        piece = lax.dynamic_index_in_dim(blocks, (me + step) % count, 0, keepdims=True)
-        pieces.append(lax.ppermute(piece, axis, shift_pairs(count, step)))
-    result = blocks
-    for step, piece in enumerate(pieces, 1):
-        result = lax.dynamic_update_slice_in_dim(result, piece, (me - step) % count, 0)
-    return result
-
-
-def collect(block, axis):
-    count = lax.axis_size(axis)
-    me = lax.axis_index(axis)
-    pieces = [
-        lax.ppermute(block, axis, shift_pairs(count, step)) for step in range(1, count)
-    ]
-    result = jnp.broadcast_to(block[None], (count,) + block.shape)
-    for step, piece in enumerate(pieces, 1):
-        result = lax.dynamic_update_slice_in_dim(result, piece[None], (me - step) % count, 0)
-    return result
+    return lax.all_to_all(blocks, axis, split_axis=0, concat_axis=0, tiled=True)
+
+
+def spread(block, axis):
+    return exchange(jnp.broadcast_to(block[None], (lax.axis_size(axis),) + block.shape), axis)
 
 
 def collect_filter(spec_filter):
     rows = 2 * spec_filter.shape[1]
-    flat = spec_filter.reshape(rows, spec_filter.shape[2]).astype(jnp.bfloat16)
-    grp, row = lax.axis_size("grp"), lax.axis_size("row")
-    share = rows // (grp * row)
-    place = lax.axis_index("row") * grp + lax.axis_index("grp")
-    mine = lax.dynamic_slice_in_dim(flat, place * share, share, 0)
-    wide = collect(mine, "col")
+    flat = spec_filter.reshape(rows, spec_filter.shape[2])
+    share = rows // lax.axis_size(PLANE)
+    mine = lax.dynamic_slice_in_dim(flat, lax.axis_index(PLANE) * share, share, 0)
+    wide = spread(mine.astype(jnp.bfloat16), "col")
     wide = jnp.swapaxes(wide, 0, 1).reshape(share, -1)
-    pair = collect(wide, "grp").reshape(grp * share, -1)
-    return collect(pair, "row").reshape(rows, -1)
+    return spread(wide, PLANE).reshape(rows, -1)
 
 
 def latitude_kernel(
@@ -527,19 +503,21 @@
     ).astype(jnp.bfloat16)
     lat_shift = stencil_lat - (row_start + jnp.arange(rows_here, dtype=jnp.int32))[:, None] // RATIO
     lon_shift = stencil_lon - (col_start + jnp.arange(cols_here, dtype=jnp.int32))[None, :] // RATIO
-    mid0 = jnp.concatenate(
+    cells = (rows_here, cols_here)
+    mids = jnp.concatenate(
         [
-            jnp.transpose(noisy, (1, 2, 0)),
-            jnp.zeros((rows_here, cols_here, conds), jnp.bfloat16),
-            lat_shift.astype(jnp.bfloat16)[..., None],
-            lon_shift.astype(jnp.bfloat16)[..., None],
-            jnp.zeros((rows_here, cols_here, LANES - lanes - 2), jnp.bfloat16),
+            noisy,
+            jnp.zeros((conds,) + cells, jnp.bfloat16),
+            lat_shift.astype(jnp.bfloat16)[None],
+            lon_shift.astype(jnp.bfloat16)[None],
+            jnp.zeros((LANES - lanes - 2,) + cells, jnp.bfloat16),
+            noise_draws[1],
+            jnp.zeros((LANES - variables,) + cells, jnp.bfloat16),
         ],
-        axis=2,
-    )
-    mid1 = jnp.pad(
-        jnp.transpose(noise_draws[1], (1, 2, 0)), ((0, 0), (0, 0), (0, LANES - variables))
-    )
+        axis=0,
+    )
+    mids = jnp.transpose(mids.reshape((2, LANES) + cells), (0, 2, 3, 1))
+    mid0, mid1 = mids[0], mids[1]
     inner = RIM - RIM_USED
     above, below = next_to(
         jnp.concatenate([mid0[rows_here - RIM :], mid1[rows_here - inner :]], axis=0),

time: 236 us -> 254 us (1.076); the launches traced: 232 us -> 253 us
  waiting for transfers between devices: 17.7 us -> 77.2 us
  local copies, waits for them, and re-layouts: 93 us -> 44.7 us
  blocking collectives: 0 us -> 10.9 us
    all_to_all x0 -> x5, waiting for transfers between devices: none -> 36.6 us  [exchange(): return lax.all_to_all(blocks, axis, split_axis=0, concat_axis=0, tiled=True)]
    ppermute x19 -> x0, starting transfers between devices: 29.4 us -> none  [the longest x12 19 us: exchange(): pieces.append(lax.ppermute(piece, axis, shift_pairs(count, step)))]
    all_to_all x0 -> x5, starting transfers between devices: none -> 27.2 us  [exchange(): return lax.all_to_all(blocks, axis, split_axis=0, concat_axis=0, tiled=True)]
    ppermute x2, waiting for transfers between devices: 0.01 us -> 22.3 us  [next_to(): lax.ppermute(low, axis, forward)]
    ppermute x19 -> x0, waiting for transfers between devices: 17.7 us -> none  [the longest x12 17.7 us: exchange(): pieces.append(lax.ppermute(piece, axis, shift_pairs(count, step)))]
    dynamic_update_slice x15 -> x0, local copies, waits for them, and re-layouts: 15.8 us -> none  [the longest x8 12.5 us: collect(): lax.dynamic_update_slice_in_dim(result, piece[None], (me - step) % count, 0)]
    broadcast_in_dim x11 -> x3, local copies, waits for them, and re-layouts: 12.2 us -> 1.29 us  [spread(): jnp.broadcast_to(block[None], (lax.axis_size(axis),) + block.shape)]
    all_to_all x0 -> x1, blocking collectives: none -> 10.9 us  [exchange(): return lax.all_to_all(blocks, axis, split_axis=0, concat_axis=0, tiled=True)]
  transfers between devices with their start and end apart: 24 -> 10, of which waited for: 2 -> 7; matrix products, arithmetic and copies ran while one was open for 37% -> 9% of each run, Pallas kernels for 30% -> 21%
where the time goes in v1:
time: 254 us; the launch traced here: 253 us
  waiting for transfers between devices  77.2 us (30%)
  Pallas kernels  70 us (28%)
  local copies, waits for them, and re-layouts  44.7 us (18%)
  starting transfers between devices  41.3 us (16%)
  blocking collectives  10.9 us (4%)
  other arithmetic  6.25 us (2%)
    all_to_all x5, waiting for transfers between devices, exchange(): return lax.all_to_all(blocks, axis, split_axis=0, concat_axis=0, tiled=True)  36.6 us
    pallas_call x1, Pallas kernels, denoise(): pl.pallas_call(functools.partial(denoise_kernel, rows, cols, totals, vari...  32.2 us
    pallas_call x2, Pallas kernels, advance_latitude(): pl.pallas_call(functools.partial(latitude_kernel, hours, block), out_shap...  32.2 us
    all_to_all x5, starting transfers between devices, exchange(): return lax.all_to_all(blocks, axis, split_axis=0, concat_axis=0, tiled=True)  27.2 us
    unnamed x67, local copies, waits for them, and re-layouts  27.1 us
    ppermute x2, waiting for transfers between devices, next_to(): lax.ppermute(low, axis, forward)  22.3 us
    all_to_all x1, blocking collectives, exchange(): return lax.all_to_all(blocks, axis, split_axis=0, concat_axis=0, tiled=True)  10.9 us
    ppermute x2, waiting for transfers between devices, next_to(): lax.ppermute(high, axis, backward)  10.3 us
  transfers between devices with their start and end apart: 10, of which 7 were waited for; matrix products, arithmetic and copies ran while one was open for 9% of the time, Pallas kernels for 21%

profile of v1, /device:TPU:8, one launch (start us, length us, event | category | flops | bytes accessed | tf_op | source)
XLA Modules:
  0.0 252.8 jit_solution(11362968312221495281)
XLA Ops:
  2.0 10.9 %all_to_all.35 = bf16[4,180,96]{2,1,0:T(8,128)(2,1)S(1)} all-to-all(bf16[4,180,96]{2,1,0:T(8,128)(2,1)S(1)} %broadcast_in_dim.37), channel_id=1, replica_groups=mesh['grp'=2,'row'=4,'col'=4] {'col'}, dimensions={0} | all-to-all | bytes 276480 | tf_op jit(solution)/shard_map/all_to_all | solution.py:35
  14.2 4.4 %all-to-all-start.2 = ((bf16[8,180,384]{2,1,0:T(8,128)(2,1)}), bf16[8,180,384]{2,1,0:T(8,128)(2,1)}, u32[]{:S(2)}, u32[]{:S(2)}) async-start(bf16[8,180,384]{2,1,0:T(8,128)(2,1)} %broadcast_in_dim.39), calls=%async_computation.2 | async-start | bytes 2260992 | tf_op jit(solution)/shard_map/all_to_all | solution.py:35
  18.6 1.6 fusion.18
  20.2 14.2 %all-to-all-done.2 = bf16[8,180,384]{2,1,0:T(8,128)(2,1)} async-done(((bf16[8,180,384]{2,1,0:T(8,128)(2,1)}), bf16[8,180,384]{2,1,0:T(8,128)(2,1)}, u32[]{:S(2)}, u32[]{:S(2)}) %all-to-all-start.2) | async-done | bytes 1105952 | tf_op jit(solution)/shard_map/all_to_all | solution.py:35
  34.4 5.2 %all-to-all-start = ((bf16[4,360,384]{2,1,0:T(8,128)(2,1)}), bf16[4,360,384]{2,1,0:T(8,128)(2,1)S(1)}, u32[]{:S(2)}, u32[]{:S(2)}) async-start(bf16[4,360,384]{2,1,0:T(8,128)(2,1)} %get-tuple-element.28), calls=%async_computation | async-start | bytes 2211840 | tf_op jit(solution)/shard_map/all_to_all | solution.py:35
  41.6 22.4 %all-to-all-done = bf16[4,360,384]{2,1,0:T(8,128)(2,1)S(1)} async-done(((bf16[4,360,384]{2,1,0:T(8,128)(2,1)}), bf16[4,360,384]{2,1,0:T(8,128)(2,1)S(1)}, u32[]{:S(2)}, u32[]{:S(2)}) %all-to-all-start) | async-done | bytes 1105952 | tf_op jit(solution)/shard_map/all_to_all | solution.py:35
  64.0 6.8 %all-to-all-start.4 = ((bf16[4,360,384]{2,1,0:T(8,128)(2,1)}), bf16[4,360,384]{2,1,0:T(8,128)(2,1)S(1)}, u32[]{:S(2)}, u32[]{:S(2)}) async-start(bf16[4,360,384]{2,1,0:T(8,128)(2,1)} %get-tuple-element.29), calls=%async_computation.4 | async-start | bytes 2211840 | tf_op jit(solution)/shard_map/all_to_all | solution.py:35
  72.0 1.7 copy.97
  73.7 1.3 reshape.144.filter_ref
  77.0 2.3 copy-done.12
  79.3 2.3 copy-done.14
  81.5 16.0 %advance_latitude.2 = (bf16[1440,384]{1,0:T(8,128)(2,1)}, bf16[2,1440,128]{2,1,0:T(8,128)(2,1)S(1)}) custom-call(bf16[1440,384]{1,0:T(8,128)(2,1)S(1)} %bitcast.78, bf16[1440,1440]{1,0:T(8,128)(2,1)S(1)} %copy-done.12, bf16[1440,1440]{1,0:T(8,128)(2,1)S(1)} %copy-done.14, bf16[1440,384]{1,0:T(8,128)(2,1)S(1)} %reshape.144.filter_ref, ...), custom_call_target="tpu_custom_call" | custom-call | flops 8351907840 | bytes 12582912 | tf_op jit(solution)/shard_map/advance_latitude/pallas_call | solution.py:99
  100.3 2.3 copy-done.13
  102.6 2.3 copy-done.15
  104.8 16.2 %advance_latitude.3 = (bf16[1440,384]{1,0:T(8,128)(2,1)}, bf16[2,1440,128]{2,1,0:T(8,128)(2,1)S(1)}) custom-call(bf16[1440,384]{1,0:T(8,128)(2,1)S(1)} %bitcast.79, bf16[1440,1440]{1,0:T(8,128)(2,1)S(1)} %copy-done.13, bf16[1440,1440]{1,0:T(8,128)(2,1)S(1)} %copy-done.15, bf16[1440,384]{1,0:T(8,128)(2,1)S(1)} %reshape.144.filter_ref, ...), custom_call_target="tpu_custom_call" | custom-call | flops 8351907840 | bytes 12582912 | tf_op jit(solution)/shard_map/advance_latitude/pallas_call | solution.py:99
  122.5 4.2 %all-to-all-start.6 = ((bf16[32,24,128]{2,1,0:T(8,128)(2,1)}), bf16[32,24,128]{2,1,0:T(8,128)(2,1)S(1)}, u32[]{:S(2)}, u32[]{:S(2)}) async-start(bf16[32,24,128]{2,1,0:T(8,128)(2,1)} %bitcast.23), calls=%async_computation.6 | async-start | bytes 393216 | tf_op jit(solution)/shard_map/all_to_all | solution.py:198
  126.8 8.1 %all-to-all-done.6 = bf16[32,24,128]{2,1,0:T(8,128)(2,1)S(1)} async-done(((bf16[32,24,128]{2,1,0:T(8,128)(2,1)}), bf16[32,24,128]{2,1,0:T(8,128)(2,1)S(1)}, u32[]{:S(2)}, u32[]{:S(2)}) %all-to-all-start.6) | async-done | bytes 196640 | tf_op jit(solution)/shard_map/all_to_all | solution.py:198
  134.9 5.7 %all-to-all-start.3 = ((bf16[4,360,384]{2,1,0:T(8,128)(2,1)}), bf16[4,360,384]{2,1,0:T(8,128)(2,1)}, u32[]{:S(2)}, u32[]{:S(2)}) async-start(bf16[4,360,384]{2,1,0:T(8,128)(2,1)} %bitcast.3), calls=%async_computation.3 | async-start | bytes 2211840 | tf_op jit(solution)/shard_map/all_to_all | solution.py:35
  141.4 2.8 %collective-permute-start = (bf16[14,128,128]{2,1,0:T(8,128)(2,1)}, bf16[14,128,128]{2,1,0:T(8,128)(2,1)S(1)}, u32[]{:S(2)}, u32[]{:S(2)}) collective-permute-start(bf16[14,128,128]{2,1,0:T(8,128)(2,1)} %pad_maximum_fusion.1), channel_id=1, source_target_pairs={{0,4},{4,8},{8,12},{12,16},{16,20},{20,24},{24,28},{1,5},{5,9},{9,... | collective-permute-start | bytes 1376264 | tf_op jit(solution)/shard_map/ppermute | solution.py:238
  153.4 2.1 collective-permute-done.above_ref
  156.8 8.5 %collective-permute-done.1.below_ref = bf16[14,128,128]{2,1,0:T(8,128)(2,1)S(1)} collective-permute-done((bf16[14,128,128]{2,1,0:T(8,128)(2,1)}, bf16[14,128,128]{2,1,0:T(8,128)(2,1)S(1)}, u32[]{:S(2)}, u32[]{:S(2)}) %collective-permute-start.1) | collective-permute-done | bytes 458784 | tf_op jit(solution)/shard_map/ppermute | solution.py:238
  167.2 5.1 %all-to-all-start.5 = ((bf16[4,360,384]{2,1,0:T(8,128)(2,1)}), bf16[4,360,384]{2,1,0:T(8,128)(2,1)}, u32[]{:S(2)}, u32[]{:S(2)}) async-start(bf16[4,360,384]{2,1,0:T(8,128)(2,1)} %bitcast.5), calls=%async_computation.5 | async-start | bytes 2211840 | tf_op jit(solution)/shard_map/all_to_all | solution.py:35
  172.9 3.4 %collective-permute-start.2 = (bf16[60,16,128]{2,1,0:T(8,128)(2,1)}, bf16[60,16,128]{2,1,0:T(8,128)(2,1)S(1)}, u32[]{:S(2)}, u32[]{:S(2)}) collective-permute-start(bf16[60,16,128]{2,1,0:T(8,128)(2,1)} %get-tuple-element.41), channel_id=1, source_target_pairs={{0,1},{1,2},{2,3},{4,5},{5,6},{6,7},{8,9},{9,10},{10,11},{12,13},{... | collective-permute-start | bytes 737288 | tf_op jit(solution)/shard_map/ppermute | solution.py:238
  176.3 2.5 collective-permute-start.3
  180.0 20.2 %collective-permute-done.2.left_ref = bf16[60,16,128]{2,1,0:T(8,128)(2,1)S(1)} collective-permute-done((bf16[60,16,128]{2,1,0:T(8,128)(2,1)}, bf16[60,16,128]{2,1,0:T(8,128)(2,1)S(1)}, u32[]{:S(2)}, u32[]{:S(2)}) %collective-permute-start.2) | collective-permute-done | bytes 245792 | tf_op jit(solution)/shard_map/ppermute | solution.py:238
  200.2 1.8 collective-permute-done.3.right_ref
  202.0 5.6 %assemble.1 = (bf16[34,160,128]{2,1,0:T(8,128)(2,1)S(1)}, bf16[26,160,128]{2,1,0:T(8,128)(2,1)S(1)}, bf16[34,160,256]{2,1,0:T(8,128)(2,1)S(1)}) custom-call(s32[2]{0:T(128)S(1)} %pad_add_fusion.place_ref, bf16[16,128,128]{2,1,0:T(8,128)(2,1)S(1)} %get-tuple-element.35.mid0_ref, bf16[16,128,128]{2,1,0:T(8,128)(2,1)S(1)} %get-tuple-element.34.mid1_ref, ...), custom_call_target="tpu_custom_call" | custom-call | flops 200000000 | bytes 10000000 | tf_op jit(solution)/shard_map/assemble/pallas_call | solution.py:297
  207.6 1.5 copy-done.2
  211.4 1.4 reshape.151
  214.4 1.8 copy-done.3
  216.2 32.2 %denoise.1 = bf16[16,128,128]{2,1,0:T(8,128)(2,1)S(1)} custom-call(s32[2]{0:T(128)S(1)} %pad_add_fusion.place_ref, bf16[34,160,128]{2,1,0:T(8,128)(2,1)S(1)} %copy-done.5, bf16[26,160,128]{2,1,0:T(8,128)(2,1)S(1)} %copy-done.7, bf16[34,160,256]{2,1,0:T(8,128)(2,1)S(1)} %copy-done.3, bf16[2,256,128]{2,1,0:T(8,128)(2,1)S(1)} %bitcast.83, ...), custom_call_target="tpu_custom_call" | custom-call | flops 10000000000 | bytes 10000000 | tf_op jit(solution)/shard_map/denoise/pallas_call | solution.py:436
  249.6 3.2 %pad_maximum_fusion = bf16[8,360,384]{2,1,0:T(8,128)(2,1)} fusion(bf16[4,360,384]{2,1,0:T(8,128)(2,1)} %all-to-all-done.5, bf16[4,360,384]{2,1,0:T(8,128)(2,1)} %all-to-all-done.3), kind=kLoop, calls=%fused_computation | loop fusion | flops 1105920 | bytes 4423680 | tf_op jit(solution)/shard_map/concatenate | solution.py:178
  (110 shorter events, 30.7 us)
Async XLA Ops:
  14.2 4.4 %copy-start.17 = (bf16[8,360,384]{2,1,0:T(8,128)(2,1)S(1)}, bf16[8,360,384]{2,1,0:T(8,128)(2,1)}, u32[]{:S(2)}) copy-start(bf16[8,360,384]{2,1,0:T(8,128)(2,1)} %param.18) | copy-start | bytes 6635524
  14.2 20.2 %all-to-all-start.2 = ((bf16[8,180,384]{2,1,0:T(8,128)(2,1)}), bf16[8,180,384]{2,1,0:T(8,128)(2,1)}, u32[]{:S(2)}, u32[]{:S(2)}) async-start(bf16[8,180,384]{2,1,0:T(8,128)(2,1)} %broadcast_in_dim.39), calls=%async_computation.2 | async-start | bytes 2260992 | tf_op jit(solution)/shard_map/all_to_all | solution.py:35
  20.2 19.4 %copy-start.23 = (bf16[384,26]{0,1:T(8,128)(2,1)S(1)}, bf16[384,26]{0,1:T(8,128)(2,1)}, u32[]{:S(2)}) copy-start(bf16[384,26]{0,1:T(8,128)(2,1)} %param.22) | copy-start | bytes 59908
  34.4 6.1 %copy-start.18 = (bf16[2,99,16,128]{3,2,1,0:T(8,128)(2,1)S(1)}, bf16[2,99,16,128]{3,2,1,0:T(8,128)(2,1)}, u32[]{:S(2)}) copy-start(bf16[2,99,16,128]{3,2,1,0:T(8,128)(2,1)} %param.24) | copy-start | bytes 2433028
  34.4 29.7 %all-to-all-start = ((bf16[4,360,384]{2,1,0:T(8,128)(2,1)}), bf16[4,360,384]{2,1,0:T(8,128)(2,1)S(1)}, u32[]{:S(2)}, u32[]{:S(2)}) async-start(bf16[4,360,384]{2,1,0:T(8,128)(2,1)} %get-tuple-element.28), calls=%async_computation | async-start | bytes 2211840 | tf_op jit(solution)/shard_map/all_to_all | solution.py:35
  41.6 29.2 %copy-start.24 = (s32[16,128]{1,0:T(8,128)S(1)}, s32[16,128]{1,0:T(8,128)}, u32[]{:S(2)}) copy-start(s32[16,128]{1,0:T(8,128)} %param.32) | copy-start | bytes 24580
  41.6 29.2 %copy-start.25 = (s32[16,128]{1,0:T(8,128)S(1)}, s32[16,128]{1,0:T(8,128)}, u32[]{:S(2)}) copy-start(s32[16,128]{1,0:T(8,128)} %param.33) | copy-start | bytes 24580
  64.0 34.4 %all-to-all-start.4 = ((bf16[4,360,384]{2,1,0:T(8,128)(2,1)}), bf16[4,360,384]{2,1,0:T(8,128)(2,1)S(1)}, u32[]{:S(2)}, u32[]{:S(2)}) async-start(bf16[4,360,384]{2,1,0:T(8,128)(2,1)} %get-tuple-element.29), calls=%async_computation.4 | async-start | bytes 2211840 | tf_op jit(solution)/shard_map/all_to_all | solution.py:35
  75.1 1.0 copy-start.8
  77.0 2.3 copy-start.12
  79.3 2.3 copy-start.14
  100.3 2.3 copy-start.13
  102.6 2.3 copy-start.15
  104.8 16.2 %copy-start.1 = (bf16[2,1440,128]{2,1,0:T(8,128)(2,1)S(1)}, bf16[2,1440,128]{2,1,0:T(8,128)(2,1)}, u32[]{:S(2)}) copy-start(bf16[2,1440,128]{2,1,0:T(8,128)(2,1)} %copy-done) | copy-start | bytes 2211844
  121.0 5.7 %copy-start.16 = (bf16[2,128,16,128]{1,3,2,0:T(8,128)(2,1)S(1)}, bf16[2,128,16,128]{1,3,2,0:T(8,128)(2,1)}, u32[]{:S(2)}) copy-start(bf16[2,128,16,128]{1,3,2,0:T(8,128)(2,1)} %copy.97) | copy-start | bytes 3145732
  122.5 12.4 %all-to-all-start.6 = ((bf16[32,24,128]{2,1,0:T(8,128)(2,1)}), bf16[32,24,128]{2,1,0:T(8,128)(2,1)S(1)}, u32[]{:S(2)}, u32[]{:S(2)}) async-start(bf16[32,24,128]{2,1,0:T(8,128)(2,1)} %bitcast.23), calls=%async_computation.6 | async-start | bytes 393216 | tf_op jit(solution)/shard_map/all_to_all | solution.py:198
  134.9 32.3 %all-to-all-start.3 = ((bf16[4,360,384]{2,1,0:T(8,128)(2,1)}), bf16[4,360,384]{2,1,0:T(8,128)(2,1)}, u32[]{:S(2)}, u32[]{:S(2)}) async-start(bf16[4,360,384]{2,1,0:T(8,128)(2,1)} %bitcast.3), calls=%async_computation.3 | async-start | bytes 2211840 | tf_op jit(solution)/shard_map/all_to_all | solution.py:35
  141.4 14.1 %collective-permute-start = (bf16[14,128,128]{2,1,0:T(8,128)(2,1)}, bf16[14,128,128]{2,1,0:T(8,128)(2,1)S(1)}, u32[]{:S(2)}, u32[]{:S(2)}) collective-permute-start(bf16[14,128,128]{2,1,0:T(8,128)(2,1)} %pad_maximum_fusion.1), channel_id=1, source_target_pairs={{0,4},{4,8},{8,12},{12,16},{16,20},{20,24},{24,28},{1,5},{5,9},{9,... | collective-permute-start | bytes 1376264 | tf_op jit(solution)/shard_map/ppermute | solution.py:238
  145.1 20.2 %collective-permute-start.1 = (bf16[14,128,128]{2,1,0:T(8,128)(2,1)}, bf16[14,128,128]{2,1,0:T(8,128)(2,1)S(1)}, u32[]{:S(2)}, u32[]{:S(2)}) collective-permute-start(bf16[14,128,128]{2,1,0:T(8,128)(2,1)} %pad_maximum_fusion.2), channel_id=1, source_target_pairs={{4,0},{8,4},{12,8},{16,12},{20,16},{24,20},{28,24},{5,1},{9,5},{13... | collective-permute-start | bytes 1376264 | tf_op jit(solution)/shard_map/ppermute | solution.py:238
  146.5 2.9 %copy-start.20 = (bf16[128,9,125]{2,0,1:T(8,128)(2,1)S(1)}, bf16[128,9,125]{2,0,1:T(8,128)(2,1)}, u32[]{:S(2)}) copy-start(bf16[128,9,125]{2,0,1:T(8,128)(2,1)} %param.25) | copy-start | bytes 864004
  148.4 2.2 copy-start.19
  150.6 2.6 %copy-start.21 = (bf16[128,256]{1,0:T(8,128)(2,1)S(1)}, bf16[128,256]{1,0:T(8,128)(2,1)}, u32[]{:S(2)}) copy-start(bf16[128,256]{1,0:T(8,128)(2,1)} %param.27) | copy-start | bytes 196612
  150.6 2.7 %copy-start.22 = (bf16[128,128]{1,0:T(8,128)(2,1)S(1)}, bf16[128,128]{1,0:T(8,128)(2,1)}, u32[]{:S(2)}) copy-start(bf16[128,128]{1,0:T(8,128)(2,1)} %param.28) | copy-start | bytes 98308
  167.2 82.4 %all-to-all-start.5 = ((bf16[4,360,384]{2,1,0:T(8,128)(2,1)}), bf16[4,360,384]{2,1,0:T(8,128)(2,1)}, u32[]{:S(2)}, u32[]{:S(2)}) async-start(bf16[4,360,384]{2,1,0:T(8,128)(2,1)} %bitcast.5), calls=%async_computation.5 | async-start | bytes 2211840 | tf_op jit(solution)/shard_map/all_to_all | solution.py:35
  172.9 27.2 %collective-permute-start.2 = (bf16[60,16,128]{2,1,0:T(8,128)(2,1)}, bf16[60,16,128]{2,1,0:T(8,128)(2,1)S(1)}, u32[]{:S(2)}, u32[]{:S(2)}) collective-permute-start(bf16[60,16,128]{2,1,0:T(8,128)(2,1)} %get-tuple-element.41), channel_id=1, source_target_pairs={{0,1},{1,2},{2,3},{4,5},{5,6},{6,7},{8,9},{9,10},{10,11},{12,13},{... | collective-permute-start | bytes 737288 | tf_op jit(solution)/shard_map/ppermute | solution.py:238
  176.3 25.7 %collective-permute-start.3 = (bf16[60,16,128]{2,1,0:T(8,128)(2,1)}, bf16[60,16,128]{2,1,0:T(8,128)(2,1)S(1)}, u32[]{:S(2)}, u32[]{:S(2)}) collective-permute-start(bf16[60,16,128]{2,1,0:T(8,128)(2,1)} %get-tuple-element.40), channel_id=1, source_target_pairs={{1,0},{2,1},{3,2},{5,4},{6,5},{7,6},{9,8},{10,9},{11,10},{13,12},{... | collective-permute-start | bytes 737288 | tf_op jit(solution)/shard_map/ppermute | solution.py:238
  207.6 1.5 copy-start.2
  209.2 1.1 copy-start.4
  210.2 1.0 copy-start.6
  212.8 1.3 copy-start.5
  212.8 1.6 copy-start.7
  214.4 1.8 copy-start.3
  (4 other events, 3.8 us)

commit v2 on v1

--- a/solution.py
+++ b/solution.py
@@ -16,6 +16,9 @@
 RIM = 9
 RIM_USED = 4
 LANES = 128
+PACKED = 32
+STRIP = 8
+FAR = -4096
 RIM_COLS = 16
 
 
@@ -28,7 +31,23 @@
     factor = np.where(frequency == 0, 1.0, 2.0) / length
     forward = np.concatenate([cosine, -sine], axis=1).T.astype(ml_dtypes.bfloat16)
     inverse = np.concatenate([cosine * factor, -sine * factor], axis=1).astype(ml_dtypes.bfloat16)
-    return jnp.asarray(forward), jnp.asarray(inverse)
+    return forward, inverse
+
+
+def round_up(size, unit):
+    return -(-size // unit) * unit
+
+
+def pieced_tables(length, num_modes, count):
+    forward, inverse = fourier_tables(length, num_modes)
+    piece = length // count
+    spare = round_up(piece, LANES) - piece
+    forward = np.pad(forward.reshape(2 * num_modes, count, piece), ((0, 0), (0, 0), (0, spare)))
+    inverse = np.pad(inverse.reshape(count, piece, 2 * num_modes), ((0, 0), (0, spare), (0, 0)))
+    return (
+        jnp.asarray(forward.reshape(2 * num_modes, -1)),
+        jnp.asarray(inverse.reshape(-1, 2 * num_modes)),
+    )
 
 
 def exchange(blocks, axis):
@@ -49,66 +68,129 @@
     return spread(wide, PLANE).reshape(rows, -1)
 
 
-def latitude_kernel(
-    hours, block, state_ref, forward_ref, inverse_ref, filter_ref, skip_ref, mix_ref, decode_ref,
-    out_ref, coarse_ref, filtered_ref,
-):
-    length = state_ref.shape[0]
+def latitude_kernel(hours, count, block, targets, step, place_ref, *refs):
+    piece_refs, refs = refs[:count], refs[count:]
+    forward_ref, inverse_ref, filter_ref, skip_ref, mix_ref, decode_ref = refs[:6]
+    out_refs, strip_ref = refs[6 : 6 + count], refs[6 + count]
+    state_ref, filtered_ref, coarse_ref, near_ref, packed_ref = refs[7 + count :]
+    piece = piece_refs[0].shape[1]
+    padded = state_ref.shape[0] // count
+    length = piece * count
     modes = filter_ref.shape[0] // 2
+    group = LANES // PACKED
+    for index in range(count):
+        own = piece_refs[index][0]
+        spare = jnp.zeros((padded - piece, own.shape[1]), own.dtype)
+        state_ref[index * padded : (index + 1) * padded, :] = jnp.concatenate([own, spare], axis=0)
+
     for hour in range(hours):
-        source_ref = state_ref if hour == 0 else out_ref
-
-        def analyse(index, carry):
-            low = pl.ds(pl.multiple_of(index * block, 16), block)
-            high = pl.ds(pl.multiple_of(modes + index * block, 16), block)
-            state = source_ref[...]
-            real = jnp.dot(forward_ref[low, :], state, preferred_element_type=jnp.float32)
-            imag = jnp.dot(forward_ref[high, :], state, preferred_element_type=jnp.float32)
-            gain_real = filter_ref[low, :].astype(jnp.float32)
-            gain_imag = filter_ref[high, :].astype(jnp.float32)
-            filtered_ref[low, :] = (real * gain_real - imag * gain_imag).astype(jnp.bfloat16)
-            filtered_ref[high, :] = (real * gain_imag + imag * gain_real).astype(jnp.bfloat16)
-            return carry
-
-        lax.fori_loop(0, modes // block, analyse, 0)
+        state = state_ref[...]
+        real = jnp.dot(forward_ref[:modes, :], state, preferred_element_type=jnp.float32)
+        imag = jnp.dot(forward_ref[modes:, :], state, preferred_element_type=jnp.float32)
+        gain_real = filter_ref[:modes, :].astype(jnp.float32)
+        gain_imag = filter_ref[modes:, :].astype(jnp.float32)
+        filtered_ref[:modes, :] = (real * gain_real - imag * gain_imag).astype(jnp.bfloat16)
+        filtered_ref[modes:, :] = (real * gain_imag + imag * gain_real).astype(jnp.bfloat16)
 
         def synthesise(index, carry):
-            here = pl.ds(pl.multiple_of(index * block, 16), block)
+            here = pl.ds(pl.multiple_of(index * block, LANES), block)
             spectral = jnp.dot(
                 inverse_ref[here, :], filtered_ref[...], preferred_element_type=jnp.float32
             ).astype(jnp.bfloat16)
-            state = source_ref[here, :]
+            state = state_ref[here, :]
             skipped = jnp.dot(state, skip_ref[...], preferred_element_type=jnp.float32)
             activated = jax.nn.gelu(spectral.astype(jnp.float32) + skipped).astype(jnp.bfloat16)
             update = jnp.dot(activated, mix_ref[...], preferred_element_type=jnp.float32)
-            fresh = (state.astype(jnp.float32) + update).astype(jnp.bfloat16)
-            out_ref[here, :] = fresh
-            coarse_ref[hour, here, :] = jnp.dot(
-                fresh, decode_ref[...], preferred_element_type=jnp.float32
-            ).astype(jnp.bfloat16)
+            state_ref[here, :] = (state.astype(jnp.float32) + update).astype(jnp.bfloat16)
             return carry
 
-        lax.fori_loop(0, length // block, synthesise, 0)
-
-
-def advance_latitude(hours, state, forward, inverse, gains, w_skip, w_mix, decode):
-    length, channels = state.shape
+        lax.fori_loop(0, count * padded // block, synthesise, 0)
+
+        for index in range(count):
+            coarse_ref[index * piece : (index + 1) * piece, :] = jnp.dot(
+                state_ref[index * padded : (index + 1) * padded, :],
+                decode_ref[...],
+                preferred_element_type=jnp.float32,
+            )[:piece]
+        span = near_ref.shape[0]
+        coarse_ref[length : length + span, :] = coarse_ref[:span, :]
+        near_ref[...] = coarse_ref[pl.ds(place_ref[0], span), :]
+        rows = span // group
+        packed = near_ref[pl.ds(0, rows, stride=group), :]
+        for turn in range(1, group):
+            packed += pltpu.roll(near_ref[pl.ds(turn, rows, stride=group), :], turn * PACKED, 1)
+        packed_ref[hour * rows : (hour + 1) * rows, :] = packed
+
+    for index in range(count):
+        out_refs[index][0] = state_ref[index * padded : index * padded + piece, :]
+    rows = near_ref.shape[0] // group
+    for target in range(targets):
+        low = target * step // group
+        strip = [
+            packed_ref[hour * rows + low : hour * rows + low + STRIP, :] for hour in range(hours)
+        ]
+        strip_ref[target] = jnp.concatenate(strip, axis=0).astype(jnp.bfloat16)
+
+
+def advance_latitude(hours, step, place, pieces, forward, inverse, gains, w_skip, w_mix, decode):
+    count = len(pieces)
+    _, piece, channels = pieces[0].shape
+    padded = round_up(piece, LANES)
     modes = gains.shape[0] // 2
-    block = next(b for b in (720, 240, 144, 48, 16) if modes % b == 0)
-    flops = hours * 2 * length * channels * (4 * modes + 2 * channels + LANES)
-    return pl.pallas_call(
-        functools.partial(latitude_kernel, hours, block),
-        out_shape=(
-            jax.ShapeDtypeStruct((length, channels), jnp.bfloat16),
-            jax.ShapeDtypeStruct((hours, length, LANES), jnp.bfloat16),
-        ),
-        scratch_shapes=[pltpu.VMEM((2 * modes, channels), jnp.bfloat16)],
-        compiler_params=pltpu.CompilerParams(vmem_limit_bytes=40 * 2**20),
+    group = LANES // PACKED
+    span = round_up((count - 1) * step + STRIP * group, 8 * group)
+    flops = hours * 2 * count * padded * channels * (4 * modes + 2 * channels + LANES)
+    block = 2 * padded if count % 2 == 0 else padded
+    results = pl.pallas_call(
+        functools.partial(latitude_kernel, hours, count, block, count, step),
+        out_shape=tuple(jax.ShapeDtypeStruct((1, piece, channels), jnp.bfloat16) for _ in pieces)
+        + (jax.ShapeDtypeStruct((count, hours * STRIP, LANES), jnp.bfloat16),),
+        in_specs=[pl.BlockSpec(memory_space=pltpu.SMEM)]
+        + [pl.BlockSpec(memory_space=pltpu.VMEM)] * (count + 6),
+        scratch_shapes=[
+            pltpu.VMEM((count * padded, channels), jnp.bfloat16),
+            pltpu.VMEM((2 * modes, channels), jnp.bfloat16),
+            pltpu.VMEM((count * piece + span, LANES), jnp.float32),
+            pltpu.VMEM((span, LANES), jnp.float32),
+            pltpu.VMEM((hours * span // group, LANES), jnp.float32),
+        ],
+        compiler_params=pltpu.CompilerParams(vmem_limit_bytes=48 * 2**20),
         cost_estimate=pl.CostEstimate(
-            flops=flops, bytes_accessed=12 * 2**20, transcendentals=hours * length * channels
+            flops=flops, bytes_accessed=14 * 2**20, transcendentals=hours * count * piece * channels
         ),
         name="advance_latitude",
-    )(state, forward, inverse, gains, w_skip, w_mix, decode)
+    )(place, *pieces, forward, inverse, gains, w_skip, w_mix, decode)
+    return results[:count], results[count]
+
+
+def collate_kernel(count, place_ref, *refs):
+    pieces, out_ref, sems = refs[:-2], refs[-2], refs[-1]
+    copies = [
+        pltpu.make_async_copy(piece, out_ref.at[pl.ds(place_ref[index], 1)], sems.at[index])
+        for index, piece in enumerate(pieces)
+    ]
+    for copy in copies:
+        copy.start()
+    for copy in copies:
+        copy.wait()
+
+
+def collate(place, pieces):
+    count = len(pieces)
+    return pl.pallas_call(
+        functools.partial(collate_kernel, count),
+        out_shape=jax.ShapeDtypeStruct((count,) + pieces[0].shape[1:], pieces[0].dtype),
+        in_specs=[pl.BlockSpec(memory_space=pltpu.SMEM)]
+        + [pl.BlockSpec(memory_space=pl.ANY)] * count,
+        out_specs=pl.BlockSpec(memory_space=pl.ANY),
+        scratch_shapes=[pltpu.SemaphoreType.DMA((count,))],
+        name="collate",
+    )(place, *pieces)
+
+
+def shift(block, axis, step):
+    count = lax.axis_size(axis)
+    return lax.ppermute(block, axis, [(source, (source + step) % count) for source in range(count)])
 
 
 def global_hour(current, spec_filter, w_skip, w_mix, forward, inverse):
@@ -140,74 +222,63 @@
     return (cells + RIM - 1) // RATIO + 3 - (-RIM // RATIO)
 
 
-def window_stride(cells):
-    return -(-window_extent(cells) // 32) * 32
-
-
 def window_base():
     return -(-RIM // RATIO)
 
 
-def pad_windows(windows, cols_here):
-    spare = window_stride(cols_here) - windows.shape[2]
-    return jnp.pad(windows, ((0, 0), (0, 0), (0, spare), (0, 0)))
-
-
 def global_by_latitude(
-    hours, global_state, spec_filter, w_skip, w_mix, w_decode, box_lat0, box_lon0, rows_here, cols_here
+    hours, global_state, spec_filter, w_skip, w_mix, w_decode, box_lat0, box_lon0, rows_here,
+    cols_here, prepare,
 ):
     count = lax.axis_size("col")
-    lats_here, _, channels = global_state.shape
-    lon_total = global_state.shape[1] * count
+    me = lax.axis_index("col")
+    lats_here, piece, _ = global_state.shape
+    length = piece * count
     turns = lats_here // count
-    forward, inverse = fourier_tables(lon_total, spec_filter.shape[1])
-    conds = w_decode.shape[1]
-    decode = jnp.pad(w_decode, ((0, 0), (0, LANES - conds)))
-    gathered = [
-        exchange(global_state[turn * count : (turn + 1) * count], "col") for turn in range(turns)
-    ]
+    forward, inverse = pieced_tables(length, spec_filter.shape[1], count)
+    decode = jnp.pad(w_decode, ((0, 0), (0, LANES - w_decode.shape[1])))
+    received = []
+    for turn in range(turns):
+        pieces = []
+        for step in range(count):
+            lat = turn * count + (me - step) % count
+            own = lax.dynamic_slice_in_dim(global_state, lat, 1, 0)
+            pieces.append(shift(own, "col", -step) if step else own)
+        received.append(pieces)
     gains = collect_filter(spec_filter)
-    finals, coarses = [], []
+    prepared = prepare(received[0][1])
+    tied = lax.optimization_barrier((received[0], gains, decode, prepared))
+    received[0], gains, decode, prepared = tied
+    start = ((box_lon0 - window_base() - me * piece) % length).astype(jnp.int32)
+    places, finals, strips = [], [], []
     for turn in range(turns):
-        state = gathered[turn].reshape(lon_total, channels)
-        state, coarse = advance_latitude(
-            hours, state, forward, inverse, gains, w_skip, w_mix, decode
+        pieces, strip = advance_latitude(
+            hours, cols_here // RATIO, start, received[turn], forward, inverse, gains, w_skip, w_mix,
+            decode,
         )
-        finals.append(exchange(state.reshape((count, -1, channels)), "col"))
-        coarses.append(coarse)
-    global_final = jnp.concatenate(finals, axis=0)
-    base = window_base()
-    high, wide = window_extent(rows_here), window_extent(cols_here)
-    coarse = jnp.stack(coarses, axis=1)[..., :conds]
-    step = cols_here // RATIO
-    span = (count - 1) * step + wide
-    coarse = jnp.pad(coarse, ((0, 0), (0, 0), (base, span), (0, 0)))
-    zero = jnp.zeros((), jnp.int32)
-    strip = lax.dynamic_slice(
-        coarse, (zero, zero, box_lon0[0], zero), (hours, turns, span, conds)
-    )
-    packed = jnp.stack(
-        [strip[:, :, col * step : col * step + wide].reshape(-1) for col in range(count)]
-    )
-    size = packed.shape[1]
-    packed = jnp.pad(packed, ((0, 0), (0, -size % 1024))).reshape(count, -1, LANES)
+        strips.append(strip)
+        for step in range(count):
+            places.append(turn * count + (me - step) % count)
+            finals.append(shift(pieces[step], "col", step) if step else pieces[step])
+    global_final = collate(jnp.stack(places).astype(jnp.int32), finals)
     plane = lax.axis_size(PLANE)
-    sent = jnp.broadcast_to(packed[None], (plane,) + packed.shape).reshape(
-        (plane * count,) + packed.shape[1:]
-    )
-    got = lax.all_to_all(sent, PLANE + ("col",), split_axis=0, concat_axis=0, tiled=True)
-    got = got.reshape(plane, count, -1)[..., :size].reshape(plane, count, hours, turns, wide, conds)
-    got = jnp.transpose(got, (2, 0, 3, 1, 4, 5)).reshape(hours, plane * lats_here, wide, conds)
-    got = jnp.pad(got, ((0, 0), (base, high), (0, 0), (0, 0)))
-    start = box_lat0[0] + lax.axis_index(PLANE) * (rows_here // RATIO)
-    windows = lax.dynamic_slice_in_dim(got, start, high, 1)
-    return global_final, pad_windows(windows, cols_here)
+    strips = jnp.concatenate(strips, axis=1)
+    sent = jnp.broadcast_to(strips[None], (plane,) + strips.shape)
+    got = exchange(sent.reshape((plane * count,) + strips.shape[1:]), PLANE + ("col",))
+    got = got.reshape((plane * lats_here, -1, LANES))
+    lat = box_lat0[0] - window_base() + lax.axis_index(PLANE) * (rows_here // RATIO)
+    lat = jnp.clip(lat + jnp.arange(window_extent(rows_here), dtype=jnp.int32), 0, plane * lats_here - 1)
+    band, lat = lat // lats_here, lat % lats_here
+    pick = (band * count + lat % count) * turns + lat // count
+    return global_final, got, pick.astype(jnp.int32), prepared
 
 
 def global_by_channel(
-    hours, global_state, spec_filter, w_skip, w_mix, w_decode, box_lat0, box_lon0, rows_here, cols_here
+    hours, global_state, spec_filter, w_skip, w_mix, w_decode, box_lat0, box_lon0, rows_here,
+    cols_here, prepare,
 ):
     count = lax.axis_size("col")
+    prepared = prepare(global_state)
     forward, inverse = fourier_tables(global_state.shape[1] * count, spec_filter.shape[1])
     base = window_base()
     high, wide = window_extent(rows_here), window_extent(cols_here)
@@ -228,7 +299,13 @@
         coarse = jnp.pad(coarse, ((base, high), (0, 0), (0, 0)))
         coarse = lax.dynamic_slice_in_dim(coarse, lat_start, high, 0)
         windows.append(coarse)
-    return global_state, pad_windows(jnp.stack(windows), cols_here)
+    group = LANES // PACKED
+    windows = jnp.stack(windows, axis=1)
+    windows = jnp.pad(
+        windows, ((0, 0), (0, 0), (0, STRIP * group - wide), (0, PACKED - windows.shape[3]))
+    )
+    windows = windows.reshape(high, hours * STRIP, LANES)
+    return global_state, windows, jnp.arange(high, dtype=jnp.int32), prepared
 
 
 def next_to(low, high, axis):
@@ -244,7 +321,7 @@
 
 
 def assemble_kernel(
-    rows, cols, totals, high, wide, lanes, place_ref, mid0_ref, mid1_ref, above_ref, below_ref,
+    rows, cols, totals, high, lanes, place_ref, mid0_ref, mid1_ref, above_ref, below_ref,
     left_ref, right_ref, noisy_ref, noise_ref, blend_ref,
 ):
     inner = RIM - RIM_USED
@@ -262,17 +339,18 @@
     col = lax.broadcasted_iota(jnp.int32, (width, 1), 0) - pad
     col_in = grid_place(place_ref[1], totals[1], -pad, width)
     frac_col = ((col % RATIO).astype(jnp.float32) + 0.5) / RATIO
-    col_base = jnp.where(col_in, (col + pad) // RATIO - pad // RATIO + base, -4 * high * wide)
-    point = lax.broadcasted_iota(jnp.int32, (width, high * wide), 1)
-    point_lat = (point // wide).astype(jnp.float32)
-    point_lon = (point % wide).astype(jnp.float32)
+    col_base = jnp.where(col_in, (col + pad) // RATIO - pad // RATIO + base, FAR)
+    group = LANES // PACKED
+    point = lax.broadcasted_iota(jnp.int32, (width, group * high * STRIP), 1)
+    point_lat = (point // STRIP % high).astype(jnp.float32)
+    point_lon = (point % STRIP * group + point // (STRIP * high)).astype(jnp.float32)
 
     def weigh(index, carry):
         row = index - RIM
         whole = (row + 2 * RATIO) // RATIO - 2
         frac_row = ((row - whole * RATIO).astype(jnp.float32) + 0.5) / RATIO
         there = place_ref[0] + row
-        row_base = jnp.where((there >= 0) & (there < totals[0]), whole + base, -4 * high * wide)
+        row_base = jnp.where((there >= 0) & (there < totals[0]), whole + base, FAR)
         shifts = noisy_ref[index, :, :].astype(jnp.float32)
         lat = row_base.astype(jnp.float32) + shifts[:, lanes : lanes + 1]
         lon = col_base.astype(jnp.float32) + shifts[:, lanes + 1 : lanes + 2]
@@ -290,16 +368,18 @@
     lax.fori_loop(0, rows + 2 * RIM, weigh, 0)
 
 
-def assemble(rows, cols, totals, high, wide, lanes, place, mid0, mid1, above, below, left, right):
+def assemble(rows, cols, totals, high, lanes, place, mid0, mid1, above, below, left, right):
     inner = RIM - RIM_USED
     width = cols + 2 * left.shape[1]
     channels = mid0.shape[2]
     return pl.pallas_call(
-        functools.partial(assemble_kernel, rows, cols, totals, high, wide, lanes),
+        functools.partial(assemble_kernel, rows, cols, totals, high, lanes),
         out_shape=(
             jax.ShapeDtypeStruct((rows + 2 * RIM, width, channels), jnp.bfloat16),
             jax.ShapeDtypeStruct((rows + 2 * inner, width, channels), jnp.bfloat16),
-            jax.ShapeDtypeStruct((rows + 2 * RIM, width, high * wide), jnp.bfloat16),
+            jax.ShapeDtypeStruct(
+                (rows + 2 * RIM, width, LANES // PACKED * high * STRIP), jnp.bfloat16
+            ),
         ),
         in_specs=[pl.BlockSpec(memory_space=pltpu.SMEM)]
         + [pl.BlockSpec(memory_space=pltpu.VMEM)] * 6,
@@ -314,9 +394,9 @@
 
 
 def denoise_kernel(
-    rows, cols, totals, variables, place_ref, noisy_ref, noise_ref, blend_ref, window_ref, first_w_ref,
-    down_w_ref, up_w_ref, bridge_w_ref, last_w_ref, out_ref, stack_ref, first_ref, pooled_ref,
-    lifted_ref, third_ref, pair_ref, spread_ref,
+    rows, cols, totals, variables, conds, place_ref, pick_ref, noisy_ref, noise_ref, blend_ref,
+    strip_ref, first_w_ref, down_w_ref, up_w_ref, bridge_w_ref, last_w_ref, out_ref, stack_ref, first_ref, pooled_ref,
+    lifted_ref, third_ref, pair_ref, spread_ref, window_ref,
 ):
     width = noisy_ref.shape[1]
     half = width // 2
@@ -326,6 +406,16 @@
     col_in = grid_place(place_ref[1], totals[1], -pad, width).astype(f32)
     lane = lax.broadcasted_iota(jnp.int32, (1, channels), 1)
     is_state = lane < variables
+    is_cond = (lane >= variables) & (lane < variables + conds)
+    high = pick_ref.shape[0]
+    strips = [strip_ref[pick_ref[index]].astype(f32) for index in range(high)]
+    for hour in range(2):
+        near = jnp.concatenate([s[hour * STRIP : (hour + 1) * STRIP] for s in strips], axis=0)
+        for turn in range(LANES // PACKED):
+            moved = pltpu.roll(near, (variables - turn * PACKED) % LANES, 1)
+            window_ref[hour, turn * high * STRIP : (turn + 1) * high * STRIP, :] = jnp.where(
+                is_cond, moved, 0.0
+            ).astype(bf16)
 
     def flat(start, count, unit):
         return pl.ds(pl.multiple_of(start * unit, 16), count * unit)
@@ -429,14 +519,14 @@
         lax.fori_loop(0, (tall - 2 * RIM_USED) // 2 if hour == 0 else rows // 2, finish, 0)
 
 
-def denoise(rows, cols, totals, variables, place, noisy, noise, blend, windows, weights):
+def denoise(rows, cols, totals, variables, conds, place, pick, noisy, noise, blend, strips, weights):
     width, channels = noisy.shape[1:]
     tall = rows + 2 * RIM
     bf16, f32 = jnp.bfloat16, jnp.float32
     return pl.pallas_call(
-        functools.partial(denoise_kernel, rows, cols, totals, variables),
+        functools.partial(denoise_kernel, rows, cols, totals, variables, conds),
         out_shape=jax.ShapeDtypeStruct((rows, cols, channels), bf16),
-        in_specs=[pl.BlockSpec(memory_space=pltpu.SMEM)]
+        in_specs=[pl.BlockSpec(memory_space=pltpu.SMEM)] * 2
         + [pl.BlockSpec(memory_space=pltpu.VMEM)] * 9,
         scratch_shapes=[
             pltpu.VMEM((tall * width, channels), bf16),
@@ -446,13 +536,14 @@
             pltpu.VMEM((tall * width, channels), bf16),
             pltpu.VMEM((width, channels), f32),
             pltpu.VMEM((width, channels), f32),
+            pltpu.VMEM((2, blend.shape[2], channels), bf16),
         ],
         compiler_params=pltpu.CompilerParams(vmem_limit_bytes=40 * 2**20),
         cost_estimate=pl.CostEstimate(
             flops=10**10, bytes_accessed=10**7, transcendentals=4 * 10**6
         ),
         name="denoise",
-    )(place, noisy, noise, blend, windows, *weights)
+    )(place, pick, noisy, noise, blend, strips, *weights)
 
 
 def conv_weight(weight, depth, width):
@@ -488,13 +579,6 @@
     total_cols = cols_here * lax.axis_size("col")
     assert hours == 2
 
-    by_latitude = global_state.shape[0] % lax.axis_size("col") == 0
-    global_steps = global_by_latitude if by_latitude else global_by_channel
-    global_final, windows = global_steps(
-        hours, global_state, spec_filter, w_skip, w_mix, w_decode, box_lat0, box_lon0,
-        rows_here, cols_here,
-    )
-
     variables = regional_state.shape[0]
     conds = w_decode.shape[1]
     lanes = variables + conds
@@ -519,10 +603,29 @@
     mids = jnp.transpose(mids.reshape((2, LANES) + cells), (0, 2, 3, 1))
     mid0, mid1 = mids[0], mids[1]
     inner = RIM - RIM_USED
-    above, below = next_to(
-        jnp.concatenate([mid0[rows_here - RIM :], mid1[rows_here - inner :]], axis=0),
-        jnp.concatenate([mid0[:RIM], mid1[:inner]], axis=0),
-        PLANE,
+    high = window_extent(rows_here)
+    place = jnp.stack([row_start, col_start]).astype(jnp.int32)
+    totals = (total_rows, total_cols)
+
+    def prepare(after):
+        lows = jnp.concatenate([mid0[rows_here - RIM :], mid1[rows_here - inner :]], axis=0)
+        highs = jnp.concatenate([mid0[:RIM], mid1[:inner]], axis=0)
+        lows, highs, _ = lax.optimization_barrier((lows, highs, after))
+        above, below = next_to(lows, highs, PLANE)
+        weights = (
+            conv_weight(w_first, LANES, w_first.shape[0]),
+            conv_weight(w_down, w_down.shape[2], w_down.shape[0]),
+            w_up.T,
+            w_bridge.T,
+            conv_weight(w_last, w_last.shape[2], LANES),
+        )
+        return above, below, weights
+
+    by_latitude = global_state.shape[0] % lax.axis_size("col") == 0
+    global_steps = global_by_latitude if by_latitude else global_by_channel
+    global_final, strips, pick, (above, below, weights) = global_steps(
+        hours, global_state, spec_filter, w_skip, w_mix, w_decode, box_lat0, box_lon0,
+        rows_here, cols_here, prepare,
     )
 
     def rim_cols(part):
@@ -537,24 +640,11 @@
     left, right = next_to(
         rim_cols(slice(cols_here - RIM_COLS, cols_here)), rim_cols(slice(0, RIM_COLS)), "col"
     )
-    high, wide = window_extent(rows_here), window_stride(cols_here)
-    place = jnp.stack([row_start, col_start]).astype(jnp.int32)
-    totals = (total_rows, total_cols)
     noisy, noise, blend = assemble(
-        rows_here, cols_here, totals, high, wide, lanes, place, mid0, mid1, above, below, left, right
-    )
-    weights = (
-        conv_weight(w_first, LANES, w_first.shape[0]),
-        conv_weight(w_down, w_down.shape[2], w_down.shape[0]),
-        w_up.T,
-        w_bridge.T,
-        conv_weight(w_last, w_last.shape[2], LANES),
-    )
-    windows = jnp.pad(windows, ((0, 0), (0, 0), (0, 0), (variables, LANES - lanes))).reshape(
-        hours, high * wide, LANES
+        rows_here, cols_here, totals, high, lanes, place, mid0, mid1, above, below, left, right
     )
     regional_final = denoise(
-        rows_here, cols_here, totals, variables, place, noisy, noise, blend, windows, weights
+        rows_here, cols_here, totals, variables, conds, place, pick, noisy, noise, blend, strips, weights
     )
     return global_final, jnp.transpose(regional_final[:, :, :variables], (2, 0, 1))
 

time: 254 us -> 302 us (1.19)
  Pallas kernels: 70 us -> 147 us
  blocking collectives: 10.9 us -> 0 us
  local copies, waits for them, and re-layouts: 44.7 us -> 35.4 us
  waiting for transfers between devices: 77.2 us -> 72.1 us
  other arithmetic: 6.25 us -> 2.36 us
    pallas_call x2 -> x3, Pallas kernels: 32.2 us -> 109 us  [the longest x1 69 us: collate(): pl.pallas_call(functools.partial(collate_kernel, count), out_shape=jax.Sh...]
    ppermute x0 -> x12, waiting for transfers between devices: none -> 31.8 us  [shift(): lax.ppermute(block, axis, [(source, (source + step) % count) for source i...]
    ppermute x2, waiting for transfers between devices: 22.3 us -> 2.84 us  [next_to(): lax.ppermute(low, axis, forward)]
    ppermute x0 -> x12, starting transfers between devices: none -> 17.6 us  [shift(): lax.ppermute(block, axis, [(source, (source + step) % count) for source i...]
    all_to_all x5 -> x3, starting transfers between devices: 27.2 us -> 11.8 us  [exchange(): return lax.all_to_all(blocks, axis, split_axis=0, concat_axis=0, tiled=True)]
    all_to_all x1 -> x0, blocking collectives: 10.9 us -> none  [exchange(): return lax.all_to_all(blocks, axis, split_axis=0, concat_axis=0, tiled=True)]
    all_to_all x5 -> x3, waiting for transfers between devices: 36.6 us -> 25.9 us  [exchange(): return lax.all_to_all(blocks, axis, split_axis=0, concat_axis=0, tiled=True)]
    all_to_all x1 -> x0, waiting for transfers between devices: 8.07 us -> none  [global_by_latitude(): lax.all_to_all(sent, PLANE + ('col',), split_axis=0, concat_axis=0, tiled...]
  transfers between devices with their start and end apart: 10 -> 19, of which waited for: 7 -> 9; matrix products, arithmetic and copies ran while one was open for 9% -> 6% of each run, Pallas kernels for 21% -> 38%
where the time goes in v2:
time: 302 us; the launch traced here: 301 us
  Pallas kernels  147 us (49%)
  waiting for transfers between devices  72.1 us (24%)
  starting transfers between devices  41.3 us (14%)
  local copies, waits for them, and re-layouts  35.4 us (12%)
    pallas_call x1, Pallas kernels, collate(): pl.pallas_call(functools.partial(collate_kernel, count), out_shape=jax.Sh...  69 us
    pallas_call x2, Pallas kernels, advance_latitude(): pl.pallas_call(functools.partial(latitude_kernel, hours, count, block, co...  40 us
    pallas_call x1, Pallas kernels, denoise(): pl.pallas_call(functools.partial(denoise_kernel, rows, cols, totals, vari...  32.3 us
    ppermute x12, waiting for transfers between devices, shift(): lax.ppermute(block, axis, [(source, (source + step) % count) for source i...  31.8 us
    all_to_all x3, waiting for transfers between devices, exchange(): return lax.all_to_all(blocks, axis, split_axis=0, concat_axis=0, tiled=True)  25.9 us
    unnamed x85, local copies, waits for them, and re-layouts  21.6 us
    ppermute x12, starting transfers between devices, shift(): lax.ppermute(block, axis, [(source, (source + step) % count) for source i...  17.6 us
    all_to_all x3, starting transfers between devices, exchange(): return lax.all_to_all(blocks, axis, split_axis=0, concat_axis=0, tiled=True)  11.8 us
  transfers between devices with their start and end apart: 19, of which 9 were waited for; matrix products, arithmetic and copies ran while one was open for 6% of the time, Pallas kernels for 38%

profile of v2, /device:TPU:8, one launch (start us, length us, event | category | flops | bytes accessed | tf_op | source)
XLA Modules:
  0.0 301.1 jit_solution(14093384955758386917)
XLA Ops:
  0.7 3.0 %constant_dynamic-slice_fusion = (bf16[1,360,384]{2,1,0:T(8,128)(2,1)}, bf16[1,360,384]{2,1,0:T(8,128)(2,1)}, bf16[1,360,384]{2,1,0:T(8,128)(2,1)}, bf16[1,360,3...) fusion(bf16[8,360,384]{2,1,0:T(8,128)(2,1)} %param.18, ...), kind=kLoop, calls=%fused_computation.38 | loop fusion | bytes 4423712 | tf_op jit(solution)/shard_map/dynamic_slice | solution.py:245
  3.9 3.0 %collective-permute-start.1 = (bf16[1,360,384]{2,1,0:T(8,128)(2,1)}, bf16[1,360,384]{2,1,0:T(8,128)(2,1)}, u32[]{:S(2)}, u32[]{:S(2)}) collective-permute-start(bf16[1,360,384]{2,1,0:T(8,128)(2,1)} %get-tuple-element.72), channel_id=1, source_target_pairs={{0,2},{1,3},{2,0},{3,1},{4,6},{5,7},{6,4},{7,5},{8,10},{9,11},{10,... | collective-permute-start | bytes 829448 | tf_op jit(solution)/shard_map/ppermute | solution.py:193
  6.9 2.5 collective-permute-start.2
  10.3 3.6 %all-to-all-start = ((bf16[4,180,96]{2,1,0:T(8,128)(2,1)}), bf16[4,180,96]{2,1,0:T(8,128)(2,1)S(1)}, u32[]{:S(2)}, u32[]{:S(2)}) async-start(bf16[4,180,96]{2,1,0:T(8,128)(2,1)} %broadcast_in_dim.36), calls=%async_computation | async-start | bytes 376832 | tf_op jit(solution)/shard_map/all_to_all | solution.py:54
  16.4 24.2 %all-to-all-done = bf16[4,180,96]{2,1,0:T(8,128)(2,1)S(1)} async-done(((bf16[4,180,96]{2,1,0:T(8,128)(2,1)}), bf16[4,180,96]{2,1,0:T(8,128)(2,1)S(1)}, u32[]{:S(2)}, u32[]{:S(2)}) %all-to-all-start) | async-done | bytes 138272 | tf_op jit(solution)/shard_map/all_to_all | solution.py:54
  42.0 4.4 %all-to-all-start.1 = ((bf16[8,180,384]{2,1,0:T(8,128)(2,1)}), bf16[8,180,384]{2,1,0:T(8,128)(2,1)}, u32[]{:S(2)}, u32[]{:S(2)}) async-start(bf16[8,180,384]{2,1,0:T(8,128)(2,1)} %broadcast_in_dim.38), calls=%async_computation.1 | async-start | bytes 2260992 | tf_op jit(solution)/shard_map/all_to_all | solution.py:54
  48.4 3.8 %collective-permute-start.3 = (bf16[14,128,128]{2,1,0:T(8,128)(2,1)}, bf16[14,128,128]{2,1,0:T(8,128)(2,1)S(1)}, u32[]{:S(2)}, u32[]{:S(2)}) collective-permute-start(bf16[14,128,128]{2,1,0:T(8,128)(2,1)} %get-tuple-element.30), channel_id=1, source_target_pairs={{0,4},{4,8},{8,12},{12,16},{16,20},{20,24},{24,28},{1,5},{5,9},{9,... | collective-permute-start | bytes 1376264 | tf_op jit(solution)/shard_map/ppermute | solution.py:315
  55.2 2.2 copy.64
  57.4 2.1 copy.72
  60.5 1.7 all-to-all-done.1
  63.5 3.3 %collective-permute-start.9 = (bf16[1,360,384]{2,1,0:T(8,128)(2,1)}, bf16[1,360,384]{2,1,0:T(8,128)(2,1)S(1)}, u32[]{:S(2)}, u32[]{:S(2)}) collective-permute-start(bf16[1,360,384]{2,1,0:T(8,128)(2,1)} %get-tuple-element.75), channel_id=1, source_target_pairs={{0,2},{1,3},{2,0},{3,1},{4,6},{5,7},{6,4},{7,5},{8,10},{9,11},{10,... | collective-permute-start | bytes 829448 | tf_op jit(solution)/shard_map/ppermute | solution.py:193
  66.8 2.8 collective-permute-done.3.above_ref
  69.7 11.6 %collective-permute-done.4.below_ref = bf16[14,128,128]{2,1,0:T(8,128)(2,1)S(1)} collective-permute-done((bf16[14,128,128]{2,1,0:T(8,128)(2,1)}, bf16[14,128,128]{2,1,0:T(8,128)(2,1)S(1)}, u32[]{:S(2)}, u32[]{:S(2)}) %collective-permute-start.4) | collective-permute-done | bytes 458784 | tf_op jit(solution)/shard_map/ppermute | solution.py:315
  85.1 20.4 %advance_latitude.2 = (bf16[1,360,384]{2,1,0:T(8,128)(2,1)S(1)}, bf16[1,360,384]{2,1,0:T(8,128)(2,1)}, bf16[1,360,384]{2,1,0:T(8,128)(2,1)S(1)}, bf16[1,360,384]{2,1,0:T(8,128)(2,1)S(1)}, bf16[4,16,128]{2,1,0:T(8,128)(2,1)S(1)}) custom-call(s32[1]{0:T(128)S(6)} %select_n.118.place_ref, bf16[1,360,384]{2,1,0:T(8,128)(2,1)S(1)} %copy-done.3, ...), custom_call_target="tpu_custom_call" | custom-call | flops 8908701696 | bytes 14680064 | tf_op jit(solution)/shard_map/advance_latitude/pallas_call | solution.py:144
  106.2 1.9 collective-permute-start.5
  111.9 3.9 %collective-permute-start.14 = (bf16[60,16,128]{2,1,0:T(8,128)(2,1)}, bf16[60,16,128]{2,1,0:T(8,128)(2,1)}, u32[]{:S(2)}, u32[]{:S(2)}) collective-permute-start(bf16[60,16,128]{2,1,0:T(8,128)(2,1)} %get-tuple-element.87), channel_id=1, source_target_pairs={{0,1},{1,2},{2,3},{4,5},{5,6},{6,7},{8,9},{9,10},{10,11},{12,13},{... | collective-permute-start | bytes 737288 | tf_op jit(solution)/shard_map/ppermute | solution.py:315
  115.8 2.9 collective-permute-start.15
  118.8 19.6 %advance_latitude.3 = (bf16[1,360,384]{2,1,0:T(8,128)(2,1)S(1)}, bf16[1,360,384]{2,1,0:T(8,128)(2,1)S(1)}, bf16[1,360,384]{2,1,0:T(8,128)(2,1)S(1)}, bf16[1,360,...) custom-call(s32[1]{0:T(128)S(6)} %select_n.118.place_ref, bf16[1,360,384]{2,1,0:T(8,128)(2,1)S(1)} %copy-done.2, ...), custom_call_target="tpu_custom_call" | custom-call | flops 8908701696 | bytes 14680064 | tf_op jit(solution)/shard_map/advance_latitude/pallas_call | solution.py:144
  142.0 3.8 %all-to-all-start.2 = ((bf16[32,32,128]{2,1,0:T(8,128)(2,1)}), bf16[32,32,128]{2,1,0:T(8,128)(2,1)S(1)}, u32[]{:S(2)}, u32[]{:S(2)}) async-start(bf16[32,32,128]{2,1,0:T(8,128)(2,1)} %bitcast.34), calls=%async_computation.2 | async-start | bytes 524288 | tf_op jit(solution)/shard_map/all_to_all | solution.py:54
  145.8 2.5 collective-permute-start.6
  148.8 1.5 collective-permute-start.11
  150.3 2.3 collective-permute-start.12
  154.0 6.2 %assemble.1 = (bf16[34,160,128]{2,1,0:T(8,128)(2,1)S(1)}, bf16[26,160,128]{2,1,0:T(8,128)(2,1)S(1)}, bf16[34,160,256]{2,1,0:T(8,128)(2,1)S(1)}) custom-call(s32[2]{0:T(128)S(1)} %pad_add_fusion.place_ref, bf16[16,128,128]{2,1,0:T(8,128)(2,1)S(1)} %get-tuple-element.77.mid0_ref, bf16[16,128,128]{2,1,0:T(8,128)(2,1)S(1)} %get-tuple-element.76.mid1_ref, ...), custom_call_target="tpu_custom_call" | custom-call | flops 200000000 | bytes 10000000 | tf_op jit(solution)/shard_map/assemble/pallas_call | solution.py:375
  160.2 1.5 copy-done.7
  163.8 18.1 %collective-permute-done.6.refs_2_ = bf16[1,360,384]{2,1,0:T(8,128)(2,1)S(1)} collective-permute-done((bf16[1,360,384]{2,1,0:T(8,128)(2,1)}, bf16[1,360,384]{2,1,0:T(8,128)(2,1)S(1)}, u32[]{:S(2)}, u32[]{:S(2)}) %collective-permute-start.6) | collective-permute-done | bytes 276512 | tf_op jit(solution)/shard_map/ppermute | solution.py:193
  181.8 2.2 collective-permute-done.7.refs_3_
  184.0 3.7 %collective-permute-done.11.refs_5_ = bf16[1,360,384]{2,1,0:T(8,128)(2,1)S(1)} collective-permute-done((bf16[1,360,384]{2,1,0:T(8,128)(2,1)}, bf16[1,360,384]{2,1,0:T(8,128)(2,1)S(1)}, u32[]{:S(2)}, u32[]{:S(2)}) %collective-permute-start.11) | collective-permute-done | bytes 276512 | tf_op jit(solution)/shard_map/ppermute | solution.py:193
  187.7 5.7 %collective-permute-done.12.refs_6_ = bf16[1,360,384]{2,1,0:T(8,128)(2,1)} collective-permute-done((bf16[1,360,384]{2,1,0:T(8,128)(2,1)}, bf16[1,360,384]{2,1,0:T(8,128)(2,1)}, u32[]{:S(2)}, u32[]{:S(2)}) %collective-permute-start.12) | collective-permute-done | bytes 276512 | tf_op jit(solution)/shard_map/ppermute | solution.py:193
  193.5 2.0 collective-permute-done.13.refs_7_
  195.6 69.0 %collate.1 = bf16[8,360,384]{2,1,0:T(8,128)(2,1)} custom-call(s32[8]{0:T(128)} %stack.44.place_ref, bf16[1,360,384]{2,1,0:T(8,128)(2,1)} %copy-done.4, bf16[1,360,384]{2,1,0:T(8,128)(2,1)} %collective-permute-done.5.refs_1_, bf16[1,360,384]{2,1,0:T(8,128)(2,1)} %copy-done.27, bf16[1,360,384]{2,1,0:T(8,128)(2,1)} %copy-done.28, ...), custom_call_target="tpu_custom_call" | custom-call | tf_op jit(solution)/shard_map/collate/pallas_call | solution.py:180
  264.6 1.8 copy-done.8
  267.6 32.3 %denoise.1 = bf16[16,128,128]{2,1,0:T(8,128)(2,1)S(1)} custom-call(s32[2]{0:T(128)S(1)} %pad_add_fusion.place_ref, s32[8]{0:T(128)S(1)} %multiply_add_fusion.pick_ref, bf16[34,160,128]{2,1,0:T(8,128)(2,1)S(1)} %copy-done.10, bf16[26,160,128]{2,1,0:T(8,128)(2,1)S(1)} %copy-done.12, bf16[34,160,256]{2,1,0:T(8,128)(2,1)S(1)} %copy-done.8, ...), custom_call_target="tpu_custom_call" | custom-call | flops 10000000000 | bytes 10000000 | tf_op jit(solution)/shard_map/denoise/pallas_call | solution.py:526
  (129 shorter events, 29.1 us)
Async XLA Ops:
  0.7 13.3 %copy-start.24 = (bf16[2,99,16,128]{3,2,1,0:T(8,128)(2,1)S(1)}, bf16[2,99,16,128]{3,2,1,0:T(8,128)(2,1)}, u32[]{:S(2)}) copy-start(bf16[2,99,16,128]{3,2,1,0:T(8,128)(2,1)} %param.24) | copy-start | bytes 2433028
  3.8 11.5 %copy-start.35 = (s32[16,128]{1,0:T(8,128)S(1)}, s32[16,128]{1,0:T(8,128)}, u32[]{:S(2)}) copy-start(s32[16,128]{1,0:T(8,128)} %param.33) | copy-start | bytes 24580
  3.8 44.6 %collective-permute-start = (bf16[1,360,384]{2,1,0:T(8,128)(2,1)}, bf16[1,360,384]{2,1,0:T(8,128)(2,1)S(1)}, u32[]{:S(2)}, u32[]{:S(2)}) collective-permute-start(bf16[1,360,384]{2,1,0:T(8,128)(2,1)} %get-tuple-element.73), channel_id=1, source_target_pairs={{0,3},{1,0},{2,1},{3,2},{4,7},{5,4},{6,5},{7,6},{8,11},{9,8},{10,9... | collective-permute-start | bytes 829448 | tf_op jit(solution)/shard_map/ppermute | solution.py:193
  3.9 59.6 %collective-permute-start.1 = (bf16[1,360,384]{2,1,0:T(8,128)(2,1)}, bf16[1,360,384]{2,1,0:T(8,128)(2,1)}, u32[]{:S(2)}, u32[]{:S(2)}) collective-permute-start(bf16[1,360,384]{2,1,0:T(8,128)(2,1)} %get-tuple-element.72), channel_id=1, source_target_pairs={{0,2},{1,3},{2,0},{3,1},{4,6},{5,7},{6,4},{7,5},{8,10},{9,11},{10,... | collective-permute-start | bytes 829448 | tf_op jit(solution)/shard_map/ppermute | solution.py:193
  6.9 60.0 %collective-permute-start.2 = (bf16[1,360,384]{2,1,0:T(8,128)(2,1)}, bf16[1,360,384]{2,1,0:T(8,128)(2,1)}, u32[]{:S(2)}, u32[]{:S(2)}) collective-permute-start(bf16[1,360,384]{2,1,0:T(8,128)(2,1)} %get-tuple-element.71), channel_id=1, source_target_pairs={{0,1},{1,2},{2,3},{3,0},{4,5},{5,6},{6,7},{7,4},{8,9},{9,10},{10,1... | collective-permute-start | bytes 829448 | tf_op jit(solution)/shard_map/ppermute | solution.py:193
  10.3 30.3 %all-to-all-start = ((bf16[4,180,96]{2,1,0:T(8,128)(2,1)}), bf16[4,180,96]{2,1,0:T(8,128)(2,1)S(1)}, u32[]{:S(2)}, u32[]{:S(2)}) async-start(bf16[4,180,96]{2,1,0:T(8,128)(2,1)} %broadcast_in_dim.36), calls=%async_computation | async-start | bytes 376832 | tf_op jit(solution)/shard_map/all_to_all | solution.py:54
  13.9 101.9 %collective-permute-start.8 = (bf16[1,360,384]{2,1,0:T(8,128)(2,1)}, bf16[1,360,384]{2,1,0:T(8,128)(2,1)}, u32[]{:S(2)}, u32[]{:S(2)}) collective-permute-start(bf16[1,360,384]{2,1,0:T(8,128)(2,1)} %get-tuple-element.69), channel_id=1, source_target_pairs={{0,3},{1,0},{2,1},{3,2},{4,7},{5,4},{6,5},{7,6},{8,11},{9,8},{10,9... | collective-permute-start | bytes 829448 | tf_op jit(solution)/shard_map/ppermute | solution.py:193
  42.0 20.2 %all-to-all-start.1 = ((bf16[8,180,384]{2,1,0:T(8,128)(2,1)}), bf16[8,180,384]{2,1,0:T(8,128)(2,1)}, u32[]{:S(2)}, u32[]{:S(2)}) async-start(bf16[8,180,384]{2,1,0:T(8,128)(2,1)} %broadcast_in_dim.38), calls=%async_computation.1 | async-start | bytes 2260992 | tf_op jit(solution)/shard_map/all_to_all | solution.py:54
  48.4 21.2 %collective-permute-start.3 = (bf16[14,128,128]{2,1,0:T(8,128)(2,1)}, bf16[14,128,128]{2,1,0:T(8,128)(2,1)S(1)}, u32[]{:S(2)}, u32[]{:S(2)}) collective-permute-start(bf16[14,128,128]{2,1,0:T(8,128)(2,1)} %get-tuple-element.30), channel_id=1, source_target_pairs={{0,4},{4,8},{8,12},{12,16},{16,20},{20,24},{24,28},{1,5},{5,9},{9,... | collective-permute-start | bytes 1376264 | tf_op jit(solution)/shard_map/ppermute | solution.py:315
  52.2 29.0 %collective-permute-start.4 = (bf16[14,128,128]{2,1,0:T(8,128)(2,1)}, bf16[14,128,128]{2,1,0:T(8,128)(2,1)S(1)}, u32[]{:S(2)}, u32[]{:S(2)}) collective-permute-start(bf16[14,128,128]{2,1,0:T(8,128)(2,1)} %get-tuple-element.31), channel_id=1, source_target_pairs={{4,0},{8,4},{12,8},{16,12},{20,16},{24,20},{28,24},{5,1},{9,5},{13... | collective-permute-start | bytes 1376264 | tf_op jit(solution)/shard_map/ppermute | solution.py:315
  63.5 55.2 %collective-permute-start.9 = (bf16[1,360,384]{2,1,0:T(8,128)(2,1)}, bf16[1,360,384]{2,1,0:T(8,128)(2,1)S(1)}, u32[]{:S(2)}, u32[]{:S(2)}) collective-permute-start(bf16[1,360,384]{2,1,0:T(8,128)(2,1)} %get-tuple-element.75), channel_id=1, source_target_pairs={{0,2},{1,3},{2,0},{3,1},{4,6},{5,7},{6,4},{7,5},{8,10},{9,11},{10,... | collective-permute-start | bytes 829448 | tf_op jit(solution)/shard_map/ppermute | solution.py:193
  66.8 51.9 %collective-permute-start.10 = (bf16[1,360,384]{2,1,0:T(8,128)(2,1)}, bf16[1,360,384]{2,1,0:T(8,128)(2,1)S(1)}, u32[]{:S(2)}, u32[]{:S(2)}) collective-permute-start(bf16[1,360,384]{2,1,0:T(8,128)(2,1)} %get-tuple-element.68), channel_id=1, source_target_pairs={{0,1},{1,2},{2,3},{3,0},{4,5},{5,6},{6,7},{7,4},{8,9},{9,10},{10,1... | collective-permute-start | bytes 829448 | tf_op jit(solution)/shard_map/ppermute | solution.py:193
  85.1 33.7 %copy-start.2 = (bf16[1,360,384]{2,1,0:T(8,128)(2,1)S(1)}, bf16[1,360,384]{2,1,0:T(8,128)(2,1)}, u32[]{:S(2)}) copy-start(bf16[1,360,384]{2,1,0:T(8,128)(2,1)} %get-tuple-element.70.refs_0_) | copy-start | bytes 829444
  85.1 33.7 %copy-start.14 = (bf16[384,384]{1,0:T(8,128)(2,1)S(1)}, bf16[384,384]{1,0:T(8,128)(2,1)}, u32[]{:S(2)}) copy-start(bf16[384,384]{1,0:T(8,128)(2,1)} %refs_7_.3) | copy-start | bytes 884740
  85.1 33.7 %copy-start.16 = (bf16[384,384]{1,0:T(8,128)(2,1)S(1)}, bf16[384,384]{1,0:T(8,128)(2,1)}, u32[]{:S(2)}) copy-start(bf16[384,384]{1,0:T(8,128)(2,1)} %refs_8_.3) | copy-start | bytes 884740
  106.2 12.6 %copy-start.19 = (bf16[1,360,384]{2,1,0:T(8,128)(2,1)}, bf16[1,360,384]{2,1,0:T(8,128)(2,1)S(1)}, u32[]{:S(2)}) copy-start(bf16[1,360,384]{2,1,0:T(8,128)(2,1)S(1)} %get-tuple-element.41) | copy-start | bytes 829444
  106.2 12.6 %copy-start.20 = (bf16[1,360,384]{2,1,0:T(8,128)(2,1)}, bf16[1,360,384]{2,1,0:T(8,128)(2,1)S(1)}, u32[]{:S(2)}) copy-start(bf16[1,360,384]{2,1,0:T(8,128)(2,1)S(1)} %get-tuple-element.40) | copy-start | bytes 829444
  106.2 46.4 %collective-permute-start.5 = (bf16[1,360,384]{2,1,0:T(8,128)(2,1)}, bf16[1,360,384]{2,1,0:T(8,128)(2,1)}, u32[]{:S(2)}, u32[]{:S(2)}) collective-permute-start(bf16[1,360,384]{2,1,0:T(8,128)(2,1)} %get-tuple-element.39), channel_id=1, source_target_pairs={{0,1},{1,2},{2,3},{3,0},{4,5},{5,6},{6,7},{7,4},{8,9},{9,10},{10,1... | collective-permute-start | bytes 829448 | tf_op jit(solution)/shard_map/ppermute | solution.py:193
  111.9 36.8 %collective-permute-start.14 = (bf16[60,16,128]{2,1,0:T(8,128)(2,1)}, bf16[60,16,128]{2,1,0:T(8,128)(2,1)}, u32[]{:S(2)}, u32[]{:S(2)}) collective-permute-start(bf16[60,16,128]{2,1,0:T(8,128)(2,1)} %get-tuple-element.87), channel_id=1, source_target_pairs={{0,1},{1,2},{2,3},{4,5},{5,6},{6,7},{8,9},{9,10},{10,11},{12,13},{... | collective-permute-start | bytes 737288 | tf_op jit(solution)/shard_map/ppermute | solution.py:315
  115.8 34.5 %collective-permute-start.15 = (bf16[60,16,128]{2,1,0:T(8,128)(2,1)}, bf16[60,16,128]{2,1,0:T(8,128)(2,1)}, u32[]{:S(2)}, u32[]{:S(2)}) collective-permute-start(bf16[60,16,128]{2,1,0:T(8,128)(2,1)} %get-tuple-element.86), channel_id=1, source_target_pairs={{1,0},{2,1},{3,2},{5,4},{6,5},{7,6},{9,8},{10,9},{11,10},{13,12},{... | collective-permute-start | bytes 737288 | tf_op jit(solution)/shard_map/ppermute | solution.py:315
  142.0 122.6 %all-to-all-start.2 = ((bf16[32,32,128]{2,1,0:T(8,128)(2,1)}), bf16[32,32,128]{2,1,0:T(8,128)(2,1)S(1)}, u32[]{:S(2)}, u32[]{:S(2)}) async-start(bf16[32,32,128]{2,1,0:T(8,128)(2,1)} %bitcast.34), calls=%async_computation.2 | async-start | bytes 524288 | tf_op jit(solution)/shard_map/all_to_all | solution.py:54
  145.8 36.1 %collective-permute-start.6 = (bf16[1,360,384]{2,1,0:T(8,128)(2,1)}, bf16[1,360,384]{2,1,0:T(8,128)(2,1)S(1)}, u32[]{:S(2)}, u32[]{:S(2)}) collective-permute-start(bf16[1,360,384]{2,1,0:T(8,128)(2,1)} %copy-done.20), channel_id=1, source_target_pairs={{0,2},{1,3},{2,0},{3,1},{4,6},{5,7},{6,4},{7,5},{8,10},{9,11},{10,... | collective-permute-start | bytes 829448 | tf_op jit(solution)/shard_map/ppermute | solution.py:193
  148.2 35.8 %collective-permute-start.7 = (bf16[1,360,384]{2,1,0:T(8,128)(2,1)}, bf16[1,360,384]{2,1,0:T(8,128)(2,1)S(1)}, u32[]{:S(2)}, u32[]{:S(2)}) collective-permute-start(bf16[1,360,384]{2,1,0:T(8,128)(2,1)} %copy-done.19), channel_id=1, source_target_pairs={{0,3},{1,0},{2,1},{3,2},{4,7},{5,4},{6,5},{7,6},{8,11},{9,8},{10,9... | collective-permute-start | bytes 829448 | tf_op jit(solution)/shard_map/ppermute | solution.py:193
  148.8 39.0 %collective-permute-start.11 = (bf16[1,360,384]{2,1,0:T(8,128)(2,1)}, bf16[1,360,384]{2,1,0:T(8,128)(2,1)S(1)}, u32[]{:S(2)}, u32[]{:S(2)}) collective-permute-start(bf16[1,360,384]{2,1,0:T(8,128)(2,1)} %copy-done.23), channel_id=1, source_target_pairs={{0,1},{1,2},{2,3},{3,0},{4,5},{5,6},{6,7},{7,4},{8,9},{9,10},{10,1... | collective-permute-start | bytes 829448 | tf_op jit(solution)/shard_map/ppermute | solution.py:193
  150.3 43.2 %collective-permute-start.12 = (bf16[1,360,384]{2,1,0:T(8,128)(2,1)}, bf16[1,360,384]{2,1,0:T(8,128)(2,1)}, u32[]{:S(2)}, u32[]{:S(2)}) collective-permute-start(bf16[1,360,384]{2,1,0:T(8,128)(2,1)} %copy-done.22), channel_id=1, source_target_pairs={{0,2},{1,3},{2,0},{3,1},{4,6},{5,7},{6,4},{7,5},{8,10},{9,11},{10,... | collective-permute-start | bytes 829448 | tf_op jit(solution)/shard_map/ppermute | solution.py:193
  152.6 42.9 %collective-permute-start.13 = (bf16[1,360,384]{2,1,0:T(8,128)(2,1)}, bf16[1,360,384]{2,1,0:T(8,128)(2,1)}, u32[]{:S(2)}, u32[]{:S(2)}) collective-permute-start(bf16[1,360,384]{2,1,0:T(8,128)(2,1)} %copy-done.21), channel_id=1, source_target_pairs={{0,3},{1,0},{2,1},{3,2},{4,7},{5,4},{6,5},{7,6},{8,11},{9,8},{10,9... | collective-permute-start | bytes 829448 | tf_op jit(solution)/shard_map/ppermute | solution.py:193
  181.8 13.7 %copy-start.27 = (bf16[1,360,384]{2,1,0:T(8,128)(2,1)}, bf16[1,360,384]{2,1,0:T(8,128)(2,1)S(1)}, u32[]{:S(2)}) copy-start(bf16[1,360,384]{2,1,0:T(8,128)(2,1)S(1)} %collective-permute-done.6.refs_2_) | copy-start | bytes 829444
  184.0 11.5 %copy-start.28 = (bf16[1,360,384]{2,1,0:T(8,128)(2,1)}, bf16[1,360,384]{2,1,0:T(8,128)(2,1)S(1)}, u32[]{:S(2)}) copy-start(bf16[1,360,384]{2,1,0:T(8,128)(2,1)S(1)} %collective-permute-done.7.refs_3_) | copy-start | bytes 829444
  195.5 69.0 %copy-start = (bf16[48,8,3,256]{3,1,2,0:T(8,128)(2,1)S(1)}, bf16[48,8,3,256]{3,1,2,0:T(8,128)(2,1)}, u32[]{:S(2)}) copy-start(bf16[48,8,3,256]{3,1,2,0:T(8,128)(2,1)} %copy.72) | copy-start | bytes 1769476
  195.5 69.0 %copy-start.1 = (bf16[384,384]{1,0:T(8,128)(2,1)S(1)}, bf16[384,384]{1,0:T(8,128)(2,1)}, u32[]{:S(2)}) copy-start(bf16[384,384]{1,0:T(8,128)(2,1)} %get-tuple-element.53.first_w_ref) | copy-start | bytes 884740
  195.6 69.0 %copy-start.6 = (bf16[128,128]{0,1:T(8,128)(2,1)S(1)}, bf16[128,128]{0,1:T(8,128)(2,1)}, u32[]{:S(2)}) copy-start(bf16[128,128]{0,1:T(8,128)(2,1)} %copy.66) | copy-start | bytes 98308
  195.6 69.0 %copy-start.10 = (bf16[34,160,128]{2,1,0:T(8,128)(2,1)S(1)}, bf16[34,160,128]{2,1,0:T(8,128)(2,1)}, u32[]{:S(2)}) copy-start(bf16[34,160,128]{2,1,0:T(8,128)(2,1)} %copy-done.9) | copy-start | bytes 4177924
  (23 other events, 83.1 us)

commit v3 on v2

--- a/solution.py
+++ b/solution.py
@@ -17,6 +17,7 @@
 RIM_USED = 4
 LANES = 128
 PACKED = 32
+MODE_TILE = 64
 STRIP = 8
 FAR = -4096
 RIM_COLS = 16
@@ -38,16 +39,56 @@
     return -(-size // unit) * unit
 
 
-def pieced_tables(length, num_modes, count):
-    forward, inverse = fourier_tables(length, num_modes)
-    piece = length // count
-    spare = round_up(piece, LANES) - piece
-    forward = np.pad(forward.reshape(2 * num_modes, count, piece), ((0, 0), (0, 0), (0, spare)))
-    inverse = np.pad(inverse.reshape(count, piece, 2 * num_modes), ((0, 0), (0, spare), (0, 0)))
-    return (
-        jnp.asarray(forward.reshape(2 * num_modes, -1)),
-        jnp.asarray(inverse.reshape(-1, 2 * num_modes)),
-    )
+def split_tables(length, num_modes):
+    piece = length // 4
+    place = np.arange(piece, dtype=np.int64)[:, None]
+
+    def waves(mode):
+        angle = (place * mode[None, :] % length).astype(np.float64) * (2.0 * math.pi / length)
+        return np.cos(angle), np.sin(angle), np.where(mode == 0, 1.0, 2.0)[None, :] / length
+
+    def padded(blocks, unit_rows, unit_cols):
+        rows = []
+        for row in blocks:
+            cols = []
+            for block in row:
+                spare = [(0, -block.shape[0] % unit_rows), (0, -block.shape[1] % unit_cols)]
+                cols.append(np.pad(block, spare))
+            rows.append(np.concatenate(cols, axis=1))
+        return np.concatenate(rows, axis=0).astype(ml_dtypes.bfloat16)
+
+    forward, inverse = [], []
+    for residue in (0, 2):
+        cosine, sine, factor = waves(np.arange(residue, num_modes, 4))
+        forward.append(padded([[cosine.T], [-sine.T]], MODE_TILE, LANES))
+        inverse.append(padded([[cosine * factor, -sine * factor]], LANES, MODE_TILE))
+    mode = np.arange(1, num_modes, 2)
+    cosine, sine, factor = waves(mode)
+    sign = np.where(mode % 4 == 1, 1.0, -1.0)[None, :]
+    odd_forward = padded(
+        [[cosine.T, (-sign * sine).T], [-sine.T, (-sign * cosine).T]], 2 * MODE_TILE, LANES
+    )
+    odd_inverse = padded(
+        [
+            [cosine * factor, -sine * factor],
+            [-sign * sine * factor, -sign * cosine * factor],
+        ],
+        LANES,
+        2 * MODE_TILE,
+    )
+    return tuple(
+        jnp.asarray(table)
+        for table in (np.stack(forward), odd_forward, np.stack(inverse), odd_inverse)
+    )
+
+
+def sort_modes(spec_filter):
+    parts = []
+    for low, step, unit in ((0, 4, MODE_TILE), (2, 4, MODE_TILE), (1, 2, 2 * MODE_TILE)):
+        part = spec_filter[:, low::step].astype(jnp.bfloat16)
+        part = jnp.pad(part, ((0, 0), (0, -part.shape[1] % unit), (0, 0)))
+        parts.append(part.reshape(-1, part.shape[2]))
+    return jnp.concatenate(parts, axis=0)
 
 
 def exchange(blocks, axis):
@@ -59,114 +100,161 @@
 
 
 def collect_filter(spec_filter):
-    rows = 2 * spec_filter.shape[1]
-    flat = spec_filter.reshape(rows, spec_filter.shape[2])
+    flat = sort_modes(spec_filter)
+    rows = flat.shape[0]
     share = rows // lax.axis_size(PLANE)
     mine = lax.dynamic_slice_in_dim(flat, lax.axis_index(PLANE) * share, share, 0)
-    wide = spread(mine.astype(jnp.bfloat16), "col")
+    wide = spread(mine, "col")
     wide = jnp.swapaxes(wide, 0, 1).reshape(share, -1)
     return spread(wide, PLANE).reshape(rows, -1)
 
 
-def latitude_kernel(hours, count, block, targets, step, place_ref, *refs):
-    piece_refs, refs = refs[:count], refs[count:]
-    forward_ref, inverse_ref, filter_ref, skip_ref, mix_ref, decode_ref = refs[:6]
-    out_refs, strip_ref = refs[6 : 6 + count], refs[6 + count]
-    state_ref, filtered_ref, coarse_ref, near_ref, packed_ref = refs[7 + count :]
-    piece = piece_refs[0].shape[1]
-    padded = state_ref.shape[0] // count
-    length = piece * count
-    modes = filter_ref.shape[0] // 2
+def latitude_kernel(hours, turns, step, place_ref, *refs):
+    piece_refs, refs = refs[:4], refs[4:]
+    even_forward_ref, odd_forward_ref, even_inverse_ref, odd_inverse_ref = refs[:4]
+    filter_ref, skip_ref, mix_ref, decode_ref = refs[4:8]
+    out_refs, strip_ref = refs[8:12], refs[12]
+    state_ref, spectral_ref, coarse_ref, near_ref, packed_ref = refs[13:]
+    f32, bf16 = jnp.float32, jnp.bfloat16
+    piece, channels = piece_refs[0].shape[1:]
+    padded = state_ref.shape[0] // 4
     group = LANES // PACKED
-    for index in range(count):
-        own = piece_refs[index][0]
-        spare = jnp.zeros((padded - piece, own.shape[1]), own.dtype)
-        state_ref[index * padded : (index + 1) * padded, :] = jnp.concatenate([own, spare], axis=0)
-
-    for hour in range(hours):
-        state = state_ref[...]
-        real = jnp.dot(forward_ref[:modes, :], state, preferred_element_type=jnp.float32)
-        imag = jnp.dot(forward_ref[modes:, :], state, preferred_element_type=jnp.float32)
-        gain_real = filter_ref[:modes, :].astype(jnp.float32)
-        gain_imag = filter_ref[modes:, :].astype(jnp.float32)
-        filtered_ref[:modes, :] = (real * gain_real - imag * gain_imag).astype(jnp.bfloat16)
-        filtered_ref[modes:, :] = (real * gain_imag + imag * gain_real).astype(jnp.bfloat16)
-
-        def synthesise(index, carry):
-            here = pl.ds(pl.multiple_of(index * block, LANES), block)
-            spectral = jnp.dot(
-                inverse_ref[here, :], filtered_ref[...], preferred_element_type=jnp.float32
-            ).astype(jnp.bfloat16)
-            state = state_ref[here, :]
-            skipped = jnp.dot(state, skip_ref[...], preferred_element_type=jnp.float32)
-            activated = jax.nn.gelu(spectral.astype(jnp.float32) + skipped).astype(jnp.bfloat16)
-            update = jnp.dot(activated, mix_ref[...], preferred_element_type=jnp.float32)
-            state_ref[here, :] = (state.astype(jnp.float32) + update).astype(jnp.bfloat16)
+    span = near_ref.shape[0]
+    rows = span // group
+    spare = jnp.zeros((padded - piece, channels), bf16)
+    for index in range(4):
+        for turn in range(turns):
+            state_ref[
+                index * padded : (index + 1) * padded, turn * channels : (turn + 1) * channels
+            ] = jnp.concatenate([piece_refs[index][turn], spare], axis=0)
+
+    def gain(spectrum, low):
+        half = spectrum.shape[0] // 2
+        real, imag = spectrum[:half], spectrum[half:]
+        gain_real = filter_ref[low : low + half, :].astype(f32)
+        gain_imag = filter_ref[low + half : low + 2 * half, :].astype(f32)
+        gain_real = jnp.concatenate([gain_real] * turns, axis=1)
+        gain_imag = jnp.concatenate([gain_imag] * turns, axis=1)
+        return jnp.concatenate(
+            [
+                (real * gain_real - imag * gain_imag).astype(bf16),
+                (real * gain_imag + imag * gain_real).astype(bf16),
+            ],
+            axis=0,
+        )
+
+    def dot(left, right):
+        return jnp.dot(left, right, preferred_element_type=f32)
+
+    def advance(hour, carry):
+        pieces = [
+            state_ref[index * padded : (index + 1) * padded, :].astype(f32) for index in range(4)
+        ]
+        both, other = pieces[0] + pieces[2], pieces[1] + pieces[3]
+        low = 0
+        shares = []
+        for index, mixed in enumerate((both + other, both - other)):
+            spectrum = dot(even_forward_ref[index], mixed.astype(bf16))
+            shares.append(dot(even_inverse_ref[index], gain(spectrum, low)))
+            low += spectrum.shape[0]
+        mixed = jnp.concatenate([pieces[0] - pieces[2], pieces[1] - pieces[3]], axis=0)
+        odd = gain(dot(odd_forward_ref[...], mixed.astype(bf16)), low)
+        odd = dot(odd_inverse_ref[...], odd)
+        for index in range(4):
+            even = shares[0] + shares[1] if index % 2 == 0 else shares[0] - shares[1]
+            part = odd[:padded] if index % 2 == 0 else odd[padded:]
+            total = even + part if index < 2 else even - part
+            spectral_ref[index * padded : (index + 1) * padded, :] = total.astype(bf16)
+
+        def mix(index, carry):
+            here = pl.ds(pl.multiple_of(index * padded, LANES), padded)
+            for turn in range(turns):
+                lanes = slice(turn * channels, (turn + 1) * channels)
+                state = state_ref[here, lanes]
+                summed = spectral_ref[here, lanes].astype(f32) + dot(state, skip_ref[...])
+                activated = jax.nn.gelu(summed).astype(bf16)
+                update = dot(activated, mix_ref[...])
+                state_ref[here, lanes] = (state.astype(f32) + update).astype(bf16)
             return carry
 
-        lax.fori_loop(0, count * padded // block, synthesise, 0)
-
-        for index in range(count):
-            coarse_ref[index * piece : (index + 1) * piece, :] = jnp.dot(
-                state_ref[index * padded : (index + 1) * padded, :],
-                decode_ref[...],
-                preferred_element_type=jnp.float32,
-            )[:piece]
-        span = near_ref.shape[0]
-        coarse_ref[length : length + span, :] = coarse_ref[:span, :]
-        near_ref[...] = coarse_ref[pl.ds(place_ref[0], span), :]
-        rows = span // group
-        packed = near_ref[pl.ds(0, rows, stride=group), :]
-        for turn in range(1, group):
-            packed += pltpu.roll(near_ref[pl.ds(turn, rows, stride=group), :], turn * PACKED, 1)
-        packed_ref[hour * rows : (hour + 1) * rows, :] = packed
-
-    for index in range(count):
-        out_refs[index][0] = state_ref[index * padded : index * padded + piece, :]
-    rows = near_ref.shape[0] // group
-    for target in range(targets):
+        lax.fori_loop(0, 4, mix, 0)
+
+        for index in range(2):
+            here = pl.ds(pl.multiple_of(place_ref[index] * padded, LANES), padded)
+            coarse = dot(state_ref[here, :], decode_ref[...])
+            for turn in range(turns):
+                coarse_ref[turn, index * piece : (index + 1) * piece, :] = coarse[
+                    :piece, turn * LANES : (turn + 1) * LANES
+                ]
+        for turn in range(turns):
+            near_ref[...] = coarse_ref[turn, pl.ds(place_ref[2], span), :]
+            packed = near_ref[pl.ds(0, rows, stride=group), :]
+            for sub in range(1, group):
+                packed += pltpu.roll(near_ref[pl.ds(sub, rows, stride=group), :], sub * PACKED, 1)
+            packed_ref[turn, pl.ds(pl.multiple_of(hour * rows, 8), rows), :] = packed
+        return carry
+
+    lax.fori_loop(0, hours, advance, 0)
+    for index in range(4):
+        for turn in range(turns):
+            out_refs[index][turn] = state_ref[
+                index * padded : index * padded + piece, turn * channels : (turn + 1) * channels
+            ]
+    for target in range(4):
         low = target * step // group
-        strip = [
-            packed_ref[hour * rows + low : hour * rows + low + STRIP, :] for hour in range(hours)
-        ]
-        strip_ref[target] = jnp.concatenate(strip, axis=0).astype(jnp.bfloat16)
-
-
-def advance_latitude(hours, step, place, pieces, forward, inverse, gains, w_skip, w_mix, decode):
-    count = len(pieces)
-    _, piece, channels = pieces[0].shape
+        for turn in range(turns):
+            strip = [
+                packed_ref[turn, hour * rows + low : hour * rows + low + STRIP, :]
+                for hour in range(hours)
+            ]
+            strip_ref[target, turn * hours * STRIP : (turn + 1) * hours * STRIP, :] = jnp.concatenate(
+                strip, axis=0
+            ).astype(bf16)
+
+
+def advance_latitudes(hours, step, place, pieces, tables, gains, w_skip, w_mix, w_decode):
+    turns, piece, channels = pieces[0].shape
     padded = round_up(piece, LANES)
+    group = LANES // PACKED
+    span = round_up(3 * step + STRIP * group, 8 * group)
+    decode = jnp.pad(w_decode, ((0, 0), (0, LANES - w_decode.shape[1])))
+    decode = jnp.concatenate(
+        [jnp.pad(decode, ((0, 0), (t * LANES, (turns - 1 - t) * LANES))) for t in range(turns)], axis=0
+    )
     modes = gains.shape[0] // 2
-    group = LANES // PACKED
-    span = round_up((count - 1) * step + STRIP * group, 8 * group)
-    flops = hours * 2 * count * padded * channels * (4 * modes + 2 * channels + LANES)
-    block = 2 * padded if count % 2 == 0 else padded
+    flops = hours * turns * 8 * padded * channels * (3 * modes // 4 + 2 * channels)
     results = pl.pallas_call(
-        functools.partial(latitude_kernel, hours, count, block, count, step),
-        out_shape=tuple(jax.ShapeDtypeStruct((1, piece, channels), jnp.bfloat16) for _ in pieces)
-        + (jax.ShapeDtypeStruct((count, hours * STRIP, LANES), jnp.bfloat16),),
+        functools.partial(latitude_kernel, hours, turns, step),
+        out_shape=tuple(
+            jax.ShapeDtypeStruct((turns, piece, channels), jnp.bfloat16) for _ in pieces
+        )
+        + (jax.ShapeDtypeStruct((4, turns * hours * STRIP, LANES), jnp.bfloat16),),
         in_specs=[pl.BlockSpec(memory_space=pltpu.SMEM)]
-        + [pl.BlockSpec(memory_space=pltpu.VMEM)] * (count + 6),
+        + [pl.BlockSpec(memory_space=pltpu.VMEM)] * 12,
         scratch_shapes=[
-            pltpu.VMEM((count * padded, channels), jnp.bfloat16),
-            pltpu.VMEM((2 * modes, channels), jnp.bfloat16),
-            pltpu.VMEM((count * piece + span, LANES), jnp.float32),
+            pltpu.VMEM((4 * padded, turns * channels), jnp.bfloat16),
+            pltpu.VMEM((4 * padded, turns * channels), jnp.bfloat16),
+            pltpu.VMEM((turns, 2 * piece, LANES), jnp.float32),
             pltpu.VMEM((span, LANES), jnp.float32),
-            pltpu.VMEM((hours * span // group, LANES), jnp.float32),
+            pltpu.VMEM((turns, hours * span // group, LANES), jnp.float32),
         ],
         compiler_params=pltpu.CompilerParams(vmem_limit_bytes=48 * 2**20),
         cost_estimate=pl.CostEstimate(
-            flops=flops, bytes_accessed=14 * 2**20, transcendentals=hours * count * piece * channels
+            flops=flops,
+            bytes_accessed=12 * 2**20,
+            transcendentals=hours * turns * 4 * piece * channels,
         ),
-        name="advance_latitude",
-    )(place, *pieces, forward, inverse, gains, w_skip, w_mix, decode)
-    return results[:count], results[count]
+        name="advance_latitudes",
+    )(place, *pieces, *tables, gains, w_skip, w_mix, decode)
+    return results[:4], results[4]
 
 
 def collate_kernel(count, place_ref, *refs):
-    pieces, out_ref, sems = refs[:-2], refs[-2], refs[-1]
+    pieces, out_ref, sems = refs[:count], refs[count], refs[count + 1]
     copies = [
-        pltpu.make_async_copy(piece, out_ref.at[pl.ds(place_ref[index], 1)], sems.at[index])
+        pltpu.make_async_copy(
+            piece, out_ref.at[pl.ds(place_ref[index], piece.shape[0])], sems.at[index]
+        )
         for index, piece in enumerate(pieces)
     ]
     for copy in copies:
@@ -177,11 +265,12 @@
 
 def collate(place, pieces):
     count = len(pieces)
+    turns, piece, channels = pieces[0].shape
     return pl.pallas_call(
         functools.partial(collate_kernel, count),
-        out_shape=jax.ShapeDtypeStruct((count,) + pieces[0].shape[1:], pieces[0].dtype),
+        out_shape=jax.ShapeDtypeStruct((count * turns, piece, channels), pieces[0].dtype),
         in_specs=[pl.BlockSpec(memory_space=pltpu.SMEM)]
-        + [pl.BlockSpec(memory_space=pl.ANY)] * count,
+        + [pl.BlockSpec(memory_space=pltpu.VMEM)] * count,
         out_specs=pl.BlockSpec(memory_space=pl.ANY),
         scratch_shapes=[pltpu.SemaphoreType.DMA((count,))],
         name="collate",
@@ -233,44 +322,35 @@
     count = lax.axis_size("col")
     me = lax.axis_index("col")
     lats_here, piece, _ = global_state.shape
-    length = piece * count
     turns = lats_here // count
-    forward, inverse = pieced_tables(length, spec_filter.shape[1], count)
-    decode = jnp.pad(w_decode, ((0, 0), (0, LANES - w_decode.shape[1])))
+    tables = split_tables(piece * count, spec_filter.shape[1])
+    owners = [(me - step) % count * turns for step in range(count)]
     received = []
-    for turn in range(turns):
-        pieces = []
-        for step in range(count):
-            lat = turn * count + (me - step) % count
-            own = lax.dynamic_slice_in_dim(global_state, lat, 1, 0)
-            pieces.append(shift(own, "col", -step) if step else own)
-        received.append(pieces)
+    for step, owner in enumerate(owners):
+        own = lax.dynamic_slice_in_dim(global_state, owner, turns, 0)
+        received.append(shift(own, "col", -step) if step else own)
     gains = collect_filter(spec_filter)
-    prepared = prepare(received[0][1])
-    tied = lax.optimization_barrier((received[0], gains, decode, prepared))
-    received[0], gains, decode, prepared = tied
-    start = ((box_lon0 - window_base() - me * piece) % length).astype(jnp.int32)
-    places, finals, strips = [], [], []
-    for turn in range(turns):
-        pieces, strip = advance_latitude(
-            hours, cols_here // RATIO, start, received[turn], forward, inverse, gains, w_skip, w_mix,
-            decode,
-        )
-        strips.append(strip)
-        for step in range(count):
-            places.append(turn * count + (me - step) % count)
-            finals.append(shift(pieces[step], "col", step) if step else pieces[step])
-    global_final = collate(jnp.stack(places).astype(jnp.int32), finals)
+    prepared = prepare(received[1])
+    received, gains, prepared = lax.optimization_barrier((received, gains, prepared))
+    start = (box_lon0[0] - window_base() - me * piece) % (piece * count)
+    place = jnp.stack([start // piece, (start // piece + 1) % count, start % piece])
+    pieces, strips = advance_latitudes(
+        hours, cols_here // RATIO, place.astype(jnp.int32), received, tables, gains, w_skip, w_mix,
+        w_decode,
+    )
     plane = lax.axis_size(PLANE)
-    strips = jnp.concatenate(strips, axis=1)
     sent = jnp.broadcast_to(strips[None], (plane,) + strips.shape)
     got = exchange(sent.reshape((plane * count,) + strips.shape[1:]), PLANE + ("col",))
     got = got.reshape((plane * lats_here, -1, LANES))
     lat = box_lat0[0] - window_base() + lax.axis_index(PLANE) * (rows_here // RATIO)
     lat = jnp.clip(lat + jnp.arange(window_extent(rows_here), dtype=jnp.int32), 0, plane * lats_here - 1)
-    band, lat = lat // lats_here, lat % lats_here
-    pick = (band * count + lat % count) * turns + lat // count
-    return global_final, got, pick.astype(jnp.int32), prepared
+    finals = [shift(block, "col", step) if step else block for step, block in enumerate(pieces)]
+
+    def finish(after):
+        blocks, after = lax.optimization_barrier((finals, after))
+        return collate(jnp.stack(owners).astype(jnp.int32), blocks), after
+
+    return finish, got, lat.astype(jnp.int32), prepared
 
 
 def global_by_channel(
@@ -305,7 +385,7 @@
         windows, ((0, 0), (0, 0), (0, STRIP * group - wide), (0, PACKED - windows.shape[3]))
     )
     windows = windows.reshape(high, hours * STRIP, LANES)
-    return global_state, windows, jnp.arange(high, dtype=jnp.int32), prepared
+    return lambda after: (global_state, after), windows, jnp.arange(high, dtype=jnp.int32), prepared
 
 
 def next_to(low, high, axis):
@@ -390,7 +470,8 @@
 
 
 def silu(x):
-    return x / (1.0 + jnp.exp(-x))
+    half = 0.5 * x
+    return half + half * jnp.tanh(half)
 
 
 def denoise_kernel(
@@ -458,65 +539,69 @@
         lax.fori_loop(0, tall // 2, stack, 0)
 
         def make_first(index, carry, rim=rim):
-            row = index * 4
-            value = silu(conv(stack_ref, row, 4, width, first_w_ref)) * inside(row - rim + 1, 4)
+            row = index * 8
+            value = silu(conv(stack_ref, row, 8, width, first_w_ref)) * inside(row - rim + 1, 8)
             value = value.astype(bf16)
-            first_ref[flat(row, 4, width), :] = value
+            first_ref[flat(row, 8, width), :] = value
             value = value.astype(f32)
-            for step in range(2):
+            for step in range(4):
                 at = 2 * step * width
-                pair_ref[...] = value[at : at + width] + value[at + width : at + 2 * width]
-                even = pair_ref[pl.ds(0, half, stride=2), :]
-                odd = pair_ref[pl.ds(1, half, stride=2), :]
-                pooled_ref[flat(index * 2 + step, 1, half), :] = ((even + odd) * 0.25).astype(bf16)
+                pair_ref[step] = value[at : at + width] + value[at + width : at + 2 * width]
+                even = pair_ref[step, pl.ds(0, half, stride=2), :]
+                odd = pair_ref[step, pl.ds(1, half, stride=2), :]
+                pooled_ref[flat(index * 4 + step, 1, half), :] = ((even + odd) * 0.25).astype(bf16)
             return carry
 
-        lax.fori_loop(0, (tall - 2) // 4, make_first, 0)
+        lax.fori_loop(0, (tall - 2) // 8, make_first, 0)
 
         half_rows = (tall - 2) // 2 - 2
 
-        def make_lifted(index, carry):
-            value = silu(conv(pooled_ref, index * 2, 2, half, down_w_ref)).astype(bf16)
-            lifted_ref[flat(index * 2, 2, half), :] = jnp.dot(
+        def make_lifted(index, carry, part=half_rows // 2):
+            value = silu(conv(pooled_ref, index * part, part, half, down_w_ref)).astype(bf16)
+            lifted_ref[flat(index * part, part, half), :] = jnp.dot(
                 value, up_w_ref[...], preferred_element_type=f32
             )
             return carry
 
-        lax.fori_loop(0, half_rows // 2, make_lifted, 0)
+        lax.fori_loop(0, 2, make_lifted, 0)
 
         def make_third(index, carry, rim=rim):
-            row = index * 2
-            lifted = lifted_ref[flat(index, 1, half), :]
-            spread_ref[pl.ds(0, half, stride=2), :] = lifted
-            spread_ref[pl.ds(1, half, stride=2), :] = lifted
+            row = index * 4
+            spreads = []
+            for step in range(2):
+                lifted = lifted_ref[flat(index * 2 + step, 1, half), :]
+                spread_ref[step, pl.ds(0, half, stride=2), :] = lifted
+                spread_ref[step, pl.ds(1, half, stride=2), :] = lifted
+                spreads += [spread_ref[step]] * 2
             bridged = jnp.dot(
-                first_ref[flat(row + 2, 2, width), :], bridge_w_ref[...], preferred_element_type=f32
+                first_ref[flat(row + 2, 4, width), :], bridge_w_ref[...], preferred_element_type=f32
             )
-            spread = spread_ref[...]
-            value = silu(bridged + jnp.concatenate([spread, spread], axis=0))
-            value = value * inside(row - rim + 3, 2)
-            third_ref[flat(row, 2, width), :] = value.astype(bf16)
+            value = silu(bridged + jnp.concatenate(spreads, axis=0))
+            value = value * inside(row - rim + 3, 4)
+            third_ref[flat(row, 4, width), :] = value.astype(bf16)
             return carry
 
-        lax.fori_loop(0, half_rows, make_third, 0)
-
-        def finish(index, carry, hour=hour, rim=rim):
-            row = index * 2
+        lax.fori_loop(0, half_rows // 2, make_third, 0)
+
+        part = (rows + 2 * (rim - RIM_USED)) // 2 if hour == 0 else rows // 2
+
+        def finish(index, carry, hour=hour, rim=rim, part=part):
+            row = index * part
             skip = 1 if hour == 1 else 0
-            fresh = conv(third_ref, row + skip, 2, width, last_w_ref)
-            own = stack_ref[flat(row + RIM_USED + skip, 2, width), :].astype(f32)
+            fresh = conv(third_ref, row + skip, part, width, last_w_ref)
+            own = stack_ref[flat(row + RIM_USED + skip, part, width), :].astype(f32)
             fresh = (own + fresh).astype(bf16)
             if hour == 0:
-                noise = noise_ref[pl.ds(row, 2)].reshape(2 * width, channels).astype(f32)
-                fresh = (fresh.astype(f32) + noise_level * noise) * inside(row - rim + RIM_USED, 2)
-                stack_ref[flat(row, 2, width), :] = fresh.astype(bf16)
+                noise = noise_ref[pl.ds(row, part)].reshape(part * width, channels).astype(f32)
+                fresh = (fresh.astype(f32) + noise_level * noise) * inside(row - rim + RIM_USED, part)
+                stack_ref[flat(row, part, width), :] = fresh.astype(bf16)
             else:
-                for step in range(2):
+                for step in range(part):
                     at = step * width + pad
                     out_ref[row + step] = fresh[at : at + cols]
             return carry
 
-        lax.fori_loop(0, (tall - 2 * RIM_USED) // 2 if hour == 0 else rows // 2, finish, 0)
+        lax.fori_loop(0, 2, finish, 0)
 
 
 def denoise(rows, cols, totals, variables, conds, place, pick, noisy, noise, blend, strips, weights):
@@ -534,8 +619,8 @@
             pltpu.VMEM((tall // 2 * width // 2, channels), bf16),
             pltpu.VMEM((tall // 2 * width // 2, channels), f32),
             pltpu.VMEM((tall * width, channels), bf16),
-            pltpu.VMEM((width, channels), f32),
-            pltpu.VMEM((width, channels), f32),
+            pltpu.VMEM((4, width, channels), f32),
+            pltpu.VMEM((2, width, channels), f32),
             pltpu.VMEM((2, blend.shape[2], channels), bf16),
         ],
         compiler_params=pltpu.CompilerParams(vmem_limit_bytes=40 * 2**20),
@@ -610,8 +695,20 @@
     def prepare(after):
         lows = jnp.concatenate([mid0[rows_here - RIM :], mid1[rows_here - inner :]], axis=0)
         highs = jnp.concatenate([mid0[:RIM], mid1[:inner]], axis=0)
-        lows, highs, _ = lax.optimization_barrier((lows, highs, after))
         above, below = next_to(lows, highs, PLANE)
+
+        def rim_cols(part):
+            return jnp.concatenate(
+                [
+                    above[:RIM, part], mid0[:, part], below[:RIM, part],
+                    above[RIM:, part], mid1[:, part], below[RIM:, part],
+                ],
+                axis=0,
+            )
+
+        left, right = next_to(
+            rim_cols(slice(cols_here - RIM_COLS, cols_here)), rim_cols(slice(0, RIM_COLS)), "col"
+        )
         weights = (
             conv_weight(w_first, LANES, w_first.shape[0]),
             conv_weight(w_down, w_down.shape[2], w_down.shape[0]),
@@ -619,34 +716,20 @@
             w_bridge.T,
             conv_weight(w_last, w_last.shape[2], LANES),
         )
-        return above, below, weights
-
-    by_latitude = global_state.shape[0] % lax.axis_size("col") == 0
+        return (mid0, mid1, above, below, left, right), weights
+
+    by_latitude = lax.axis_size("col") == 4 and global_state.shape[0] % 4 == 0
     global_steps = global_by_latitude if by_latitude else global_by_channel
-    global_final, strips, pick, (above, below, weights) = global_steps(
+    finish, strips, pick, (parts, weights) = global_steps(
         hours, global_state, spec_filter, w_skip, w_mix, w_decode, box_lat0, box_lon0,
         rows_here, cols_here, prepare,
     )
-
-    def rim_cols(part):
-        return jnp.concatenate(
-            [
-                above[:RIM, part], mid0[:, part], below[:RIM, part],
-                above[RIM:, part], mid1[:, part], below[RIM:, part],
-            ],
-            axis=0,
-        )
-
-    left, right = next_to(
-        rim_cols(slice(cols_here - RIM_COLS, cols_here)), rim_cols(slice(0, RIM_COLS)), "col"
-    )
-    noisy, noise, blend = assemble(
-        rows_here, cols_here, totals, high, lanes, place, mid0, mid1, above, below, left, right
-    )
+    noisy, noise, blend = assemble(rows_here, cols_here, totals, high, lanes, place, *parts)
     regional_final = denoise(
         rows_here, cols_here, totals, variables, conds, place, pick, noisy, noise, blend, strips, weights
     )
-    return global_final, jnp.transpose(regional_final[:, :, :variables], (2, 0, 1))
+    regional_final = jnp.transpose(regional_final[:, :, :variables], (2, 0, 1))
+    return finish(regional_final)
 
 
 def solution(mesh):

time: 302 us -> 186 us (0.62)
  the two profiles are of different devices: /device:TPU:8 before, /device:TPU:0 now
where the time goes in v3:
time: 186 us; the launch traced here: 185 us
  Pallas kernels  53.9 us (29%)
  local copies, waits for them, and re-layouts  52.2 us (28%)
  waiting for transfers between devices  39.4 us (21%)
  starting transfers between devices  33.7 us (18%)
  other arithmetic  3.09 us (2%)
  between operations  2.79 us (2%)
    all_to_all x3, waiting for transfers between devices, exchange(): return lax.all_to_all(blocks, axis, split_axis=0, concat_axis=0, tiled=True)  33.4 us
    pallas_call x1, Pallas kernels, denoise(): pl.pallas_call(functools.partial(denoise_kernel, rows, cols, totals, vari...  23.5 us
    pallas_call x1, Pallas kernels, advance_latitudes(): pl.pallas_call(functools.partial(latitude_kernel, hours, turns, step), ou...  21.8 us
    unnamed x71, local copies, waits for them, and re-layouts  21 us
    all_to_all x3, starting transfers between devices, exchange(): return lax.all_to_all(blocks, axis, split_axis=0, concat_axis=0, tiled=True)  13 us
    ppermute x6, starting transfers between devices, shift(): lax.ppermute(block, axis, [(source, (source + step) % count) for source i...  11.7 us
    slice x3, local copies, waits for them, and re-layouts, sort_modes(): part = spec_filter[:, low::step].astype(jnp.bfloat16)  9.68 us
    ppermute x2, starting transfers between devices, next_to(): lax.ppermute(low, axis, forward)  6.28 us
  transfers between devices with their start and end apart: 13, of which 5 were waited for; matrix products, arithmetic and copies ran while one was open for 19% of the time, Pallas kernels for 16%

profile of v3, /device:TPU:0, one launch (start us, length us, event | category | flops | bytes accessed | tf_op | source)
XLA Modules:
  0.0 185.1 jit_solution(163635042330922847)
XLA Ops:
  0.7 2.9 %constant_dynamic-slice_fusion = (bf16[2,360,384]{2,1,0:T(8,128)(2,1)}, bf16[2,360,384]{2,1,0:T(8,128)(2,1)}, bf16[2,360,384]{2,1,0:T(8,128)(2,1)S(1)}, bf16[2,360,384]{2,1,0:T(8,128)(2,1)}) fusion(bf16[8,360,384]{2,1,0:T(8,128)(2,1)} %param.20, s32[]{:T(128)S(6)} %select_n.82, s32[]{:T(128)S(6)} %select_n.80, s32[]{:T(128)S(6)} %select_n.79, s32[]{:T(128)S(6)} %select_n.81), kind=kLoop, calls=%fused_computation.48 | loop fusion | bytes 4423696 | tf_op jit(solution)/shard_map/dynamic_slice | solution.py:330
  3.6 5.0 %collective-permute-start = (bf16[2,360,384]{2,1,0:T(8,128)(2,1)}, bf16[2,360,384]{2,1,0:T(8,128)(2,1)}, u32[]{:S(2)}, u32[]{:S(2)}) collective-permute-start(bf16[2,360,384]{2,1,0:T(8,128)(2,1)} %get-tuple-element.69), channel_id=1, source_target_pairs={{0,3},{1,0},{2,1},{3,2},{4,7},{5,4},{6,5},{7,6},{8,11},{9,8},{10,9... | collective-permute-start | bytes 1658888 | tf_op jit(solution)/shard_map/ppermute | solution.py:282
  9.7 2.5 %slice.91 = bf16[2,180,96]{1,2,0:T(8,128)(2,1)S(1)} slice(bf16[2,720,96]{1,2,0:T(8,128)(2,1)S(1)} %convert.5), slice={[0:2:1], [0:720:4], [0:96:1]} | slice | bytes 138240 | tf_op jit(solution)/shard_map/slice | solution.py:88
  12.2 2.4 %slice.92 = bf16[2,180,96]{1,2,0:T(8,128)(2,1)S(1)} slice(bf16[2,720,96]{1,2,0:T(8,128)(2,1)S(1)} %convert.5), slice={[0:2:1], [2:720:4], [0:96:1]} | slice | bytes 138240 | tf_op jit(solution)/shard_map/slice | solution.py:88
  14.6 4.8 %slice.93 = bf16[2,360,96]{1,2,0:T(8,128)(2,1)S(1)} slice(bf16[2,720,96]{1,2,0:T(8,128)(2,1)S(1)} %convert.5), slice={[0:2:1], [1:720:2], [0:96:1]} | slice | bytes 276480 | tf_op jit(solution)/shard_map/slice | solution.py:88
  21.4 4.1 %all-to-all-start = ((bf16[4,192,96]{2,1,0:T(8,128)(2,1)}), bf16[4,192,96]{2,1,0:T(8,128)(2,1)}, u32[]{:S(2)}, u32[]{:S(2)}) async-start(bf16[4,192,96]{2,1,0:T(8,128)(2,1)} %broadcast_in_dim.36), calls=%async_computation | async-start | bytes 393216 | tf_op jit(solution)/shard_map/all_to_all | solution.py:95
  28.1 3.4 %collective-permute-start.3 = (bf16[14,128,128]{2,1,0:T(8,128)(2,1)}, bf16[14,128,128]{2,1,0:T(8,128)(2,1)S(1)}, u32[]{:S(2)}, u32[]{:S(2)}) collective-permute-start(bf16[14,128,128]{2,1,0:T(8,128)(2,1)} %pad_maximum_fusion), channel_id=1, source_target_pairs={{0,4},{4,8},{8,12},{12,16},{16,20},{20,24},{24,28},{1,5},{5,9},{9,... | collective-permute-start | bytes 1376264 | tf_op jit(solution)/shard_map/ppermute | solution.py:395
  32.3 1.5 collective-permute-start.4
  40.4 2.2 %copy.60 = bf16[256,3,3,128]{0,2,3,1:T(4,128)(2,1)} copy(bf16[256,3,3,128]{3,0,2,1:T(8,128)(2,1)} %bitcast.88) | data formatting | bytes 1179648 | tf_op jit(solution)/shard_map/reshape | solution.py:636
  43.8 1.6 copy.61
  46.2 14.2 %all-to-all-done = bf16[4,192,96]{2,1,0:T(8,128)(2,1)} async-done(((bf16[4,192,96]{2,1,0:T(8,128)(2,1)}), bf16[4,192,96]{2,1,0:T(8,128)(2,1)}, u32[]{:S(2)}, u32[]{:S(2)}) %all-to-all-start) | async-done | bytes 147488 | tf_op jit(solution)/shard_map/all_to_all | solution.py:95
  60.4 1.8 copy.57
  62.2 1.8 broadcast_in_dim.37
  63.9 2.0 %broadcast_in_dim.38 = bf16[8,192,384]{2,1,0:T(8,128)(2,1)} broadcast(bf16[192,384]{1,0:T(8,128)(2,1)} %broadcast_in_dim.37), dimensions={1,2} | broadcast | bytes 1327104 | tf_op jit(solution)/shard_map/broadcast_in_dim | solution.py:99
  66.0 4.3 %all-to-all-start.1 = ((bf16[8,192,384]{2,1,0:T(8,128)(2,1)}), bf16[8,192,384]{2,1,0:T(8,128)(2,1)}, u32[]{:S(2)}, u32[]{:S(2)}) async-start(bf16[8,192,384]{2,1,0:T(8,128)(2,1)} %broadcast_in_dim.38), calls=%async_computation.1 | async-start | bytes 2359296 | tf_op jit(solution)/shard_map/all_to_all | solution.py:95
  70.4 2.9 %collective-permute-start.5 = (bf16[60,16,128]{2,1,0:T(8,128)(2,1)S(1)}, bf16[60,16,128]{2,1,0:T(8,128)(2,1)S(1)}, u32[]{:S(2)}, u32[]{:S(2)}) collective-permute-start(bf16[60,16,128]{2,1,0:T(8,128)(2,1)S(1)} %get-tuple-element.83), channel_id=1, source_target_pairs={{0,1},{1,2},{2,3},{4,5},{5,6},{6,7},{8,9},{9,10},{10,11},{12,13},{... | collective-permute-start | bytes 737288 | tf_op jit(solution)/shard_map/ppermute | solution.py:395
  74.6 2.1 %copy_bitcast_fusion = (bf16[384,384]{1,0:T(8,128)(2,1)}, bf16[384,384]{1,0:T(8,128)(2,1)}) fusion(bf16[48,8,3,128]{3,2,1,0:T(4,128)(2,1)} %bitcast.83, bf16[48,8,3,128]{3,2,1,0:T(4,128)(2,1)} %bitcast.84), kind=kLoop, calls=%fused_computation.14 | loop fusion | bytes 1179648 | tf_op jit(solution)/shard_map/reshape | solution.py:638
  76.7 2.3 %collective-permute-done.5.left_ref = bf16[60,16,128]{2,1,0:T(8,128)(2,1)S(1)} collective-permute-done((bf16[60,16,128]{2,1,0:T(8,128)(2,1)S(1)}, bf16[60,16,128]{2,1,0:T(8,128)(2,1)S(1)}, u32[]{:S(2)}, u32[]{:S(2)}) %collective-permute-start.5) | collective-permute-done | bytes 245792 | tf_op jit(solution)/shard_map/ppermute | solution.py:395
  79.7 3.7 %collective-permute-done.6.right_ref = bf16[60,16,128]{2,1,0:T(8,128)(2,1)S(1)} collective-permute-done((bf16[60,16,128]{2,1,0:T(8,128)(2,1)S(1)}, bf16[60,16,128]{2,1,0:T(8,128)(2,1)S(1)}, u32[]{:S(2)}, u32[]{:S(2)}) %collective-permute-start.6) | collective-permute-done | bytes 245792 | tf_op jit(solution)/shard_map/ppermute | solution.py:395
  84.0 2.5 %all-to-all-done.1 = bf16[8,192,384]{2,1,0:T(8,128)(2,1)} async-done(((bf16[8,192,384]{2,1,0:T(8,128)(2,1)}), bf16[8,192,384]{2,1,0:T(8,128)(2,1)}, u32[]{:S(2)}, u32[]{:S(2)}) %all-to-all-start.1) | async-done | bytes 1179680 | tf_op jit(solution)/shard_map/all_to_all | solution.py:95
  89.5 21.8 %advance_latitudes.1 = (bf16[2,360,384]{2,1,0:T(8,128)(2,1)S(1)}, bf16[2,360,384]{2,1,0:T(8,128)(2,1)S(1)}, bf16[2,360,384]{2,1,0:T(8,128)(2,1)S(1)}, bf16[2,360...) custom-call(s32[3]{0:T(128)S(1)} %pad_add_fusion.1.place_ref, bf16[2,360,384]{2,1,0:T(8,128)(2,1)S(1)} %get-tuple-element.31.refs_0_, ...), custom_call_target="tpu_custom_call" | custom-call | flops 6341787648 | bytes 12582912 | tf_op jit(solution)/shard_map/advance_latitudes/pallas_call | solution.py:226
  113.5 4.6 %all-to-all-start.2 = ((bf16[32,32,128]{2,1,0:T(8,128)(2,1)}), bf16[32,32,128]{2,1,0:T(8,128)(2,1)S(1)}, u32[]{:S(2)}, u32[]{:S(2)}) async-start(bf16[32,32,128]{2,1,0:T(8,128)(2,1)} %bitcast.85), calls=%async_computation.2 | async-start | bytes 524288 | tf_op jit(solution)/shard_map/all_to_all | solution.py:95
  119.4 1.8 collective-permute-start.7
  121.2 2.4 %collective-permute-start.8 = (bf16[2,360,384]{2,1,0:T(8,128)(2,1)}, bf16[2,360,384]{2,1,0:T(8,128)(2,1)}, u32[]{:S(2)}, u32[]{:S(2)}) collective-permute-start(bf16[2,360,384]{2,1,0:T(8,128)(2,1)} %copy-done.15), channel_id=1, source_target_pairs={{0,2},{1,3},{2,0},{3,1},{4,6},{5,7},{6,4},{7,5},{8,10},{9,11},{10,... | collective-permute-start | bytes 1658888 | tf_op jit(solution)/shard_map/ppermute | solution.py:282
  123.6 1.4 collective-permute-start.9
  126.9 5.6 %assemble.1 = (bf16[34,160,128]{2,1,0:T(8,128)(2,1)S(1)}, bf16[26,160,128]{2,1,0:T(8,128)(2,1)S(1)}, bf16[34,160,256]{2,1,0:T(8,128)(2,1)S(1)}) custom-call(s32[2]{0:T(128)S(1)} %pad_add_fusion.2.place_ref, bf16[16,128,128]{2,1,0:T(8,128)(2,1)S(1)} %get-tuple-element.40.mid0_ref, bf16[16,128,128]{2,1,0:T(8,128)(2,1)S(1)} %get-tuple-element.41.mid1_ref, ...), custom_call_target="tpu_custom_call" | custom-call | flops 200000000 | bytes 10000000 | tf_op jit(solution)/shard_map/assemble/pallas_call | solution.py:455
  132.6 1.5 copy-done.8
  136.2 16.7 %all-to-all-done.2 = bf16[32,32,128]{2,1,0:T(8,128)(2,1)S(1)} async-done(((bf16[32,32,128]{2,1,0:T(8,128)(2,1)}), bf16[32,32,128]{2,1,0:T(8,128)(2,1)S(1)}, u32[]{:S(2)}, u32[]{:S(2)}) %all-to-all-start.2) | async-done | bytes 262176 | tf_op jit(solution)/shard_map/all_to_all | solution.py:95
  152.9 1.8 copy-done.9
  154.6 1.3 copy-done.11
  157.2 23.5 %denoise.1 = bf16[16,128,128]{2,1,0:T(8,128)(2,1)S(1)} custom-call(s32[2]{0:T(128)S(1)} %pad_add_fusion.2.place_ref, s32[8]{0:T(128)S(1)} %add_clamp_fusion.pick_ref, bf16[34,160,128]{2,1,0:T(8,128)(2,1)S(1)} %copy-done.11, bf16[26,160,128]{2,1,0:T(8,128)(2,1)S(1)} %copy-done.13, bf16[34,160,256]{2,1,0:T(8,128)(2,1)S(1)} %copy-done.9, ...), custom_call_target="tpu_custom_call" | custom-call | flops 10000000000 | bytes 10000000 | tf_op jit(solution)/shard_map/denoise/pallas_call | solution.py:611
  181.9 2.9 %collate.1 = bf16[8,360,384]{2,1,0:T(8,128)(2,1)} custom-call(s32[4]{0:T(128)} %pad_add_fusion.place_ref, bf16[2,360,384]{2,1,0:T(8,128)(2,1)} %copy-done, bf16[2,360,384]{2,1,0:T(8,128)(2,1)} %collective-permute-done.7.refs_1_, bf16[2,360,384]{2,1,0:T(8,128)(2,1)} %collective-permute-done.8.refs_2_, bf16[2,360,384]{2,1,0:T(8,128)(2,1)} %collective-permute-done.9.refs_3_), custom_call_target="tpu_custom_call" | custom-call | tf_op jit(solution)/shard_map/collate/pallas_call | solution.py:269
  (112 shorter events, 29.1 us)
Async XLA Ops:
  0.7 8.9 %copy-start.22 = (f32[2,720,96]{1,2,0:T(8,128)S(1)}, f32[2,720,96]{1,2,0:T(8,128)}, u32[]{:S(2)}) copy-start(f32[2,720,96]{1,2,0:T(8,128)} %param.21) | copy-start | bytes 1658884
  3.6 73.1 %collective-permute-start = (bf16[2,360,384]{2,1,0:T(8,128)(2,1)}, bf16[2,360,384]{2,1,0:T(8,128)(2,1)}, u32[]{:S(2)}, u32[]{:S(2)}) collective-permute-start(bf16[2,360,384]{2,1,0:T(8,128)(2,1)} %get-tuple-element.69), channel_id=1, source_target_pairs={{0,3},{1,0},{2,1},{3,2},{4,7},{5,4},{6,5},{7,6},{8,11},{9,8},{10,9... | collective-permute-start | bytes 1658888 | tf_op jit(solution)/shard_map/ppermute | solution.py:282
  8.6 68.0 %collective-permute-start.1 = (bf16[2,360,384]{2,1,0:T(8,128)(2,1)}, bf16[2,360,384]{2,1,0:T(8,128)(2,1)}, u32[]{:S(2)}, u32[]{:S(2)}) collective-permute-start(bf16[2,360,384]{2,1,0:T(8,128)(2,1)} %get-tuple-element.71), channel_id=1, source_target_pairs={{0,2},{1,3},{2,0},{3,1},{4,6},{5,7},{6,4},{7,5},{8,10},{9,11},{10,... | collective-permute-start | bytes 1658888 | tf_op jit(solution)/shard_map/ppermute | solution.py:282
  8.6 68.0 %collective-permute-start.2 = (bf16[2,360,384]{2,1,0:T(8,128)(2,1)}, bf16[2,360,384]{2,1,0:T(8,128)(2,1)}, u32[]{:S(2)}, u32[]{:S(2)}) collective-permute-start(bf16[2,360,384]{2,1,0:T(8,128)(2,1)} %get-tuple-element.68), channel_id=1, source_target_pairs={{0,1},{1,2},{2,3},{3,0},{4,5},{5,6},{6,7},{7,4},{8,9},{9,10},{10,1... | collective-permute-start | bytes 1658888 | tf_op jit(solution)/shard_map/ppermute | solution.py:282
  19.6 5.8 %copy-start.21 = (bf16[2,99,16,128]{3,2,1,0:T(8,128)(2,1)S(1)}, bf16[2,99,16,128]{3,2,1,0:T(8,128)(2,1)}, u32[]{:S(2)}) copy-start(bf16[2,99,16,128]{3,2,1,0:T(8,128)(2,1)} %param.26) | copy-start | bytes 2433028
  19.6 5.8 %copy-start.23 = (bf16[99,16,128]{2,1,0:T(8,128)(2,1)S(1)}, bf16[99,16,128]{2,1,0:T(8,128)(2,1)}, u32[]{:S(2)}) copy-start(bf16[99,16,128]{2,1,0:T(8,128)(2,1)} %param.25) | copy-start | bytes 1216516
  20.3 5.3 %copy-start.25 = (s32[16,128]{1,0:T(8,128)S(1)}, s32[16,128]{1,0:T(8,128)}, u32[]{:S(2)}) copy-start(s32[16,128]{1,0:T(8,128)} %param.34) | copy-start | bytes 24580
  20.4 5.4 %copy-start.26 = (s32[16,128]{1,0:T(8,128)S(1)}, s32[16,128]{1,0:T(8,128)}, u32[]{:S(2)}) copy-start(s32[16,128]{1,0:T(8,128)} %param.35) | copy-start | bytes 24580
  21.4 39.0 %all-to-all-start = ((bf16[4,192,96]{2,1,0:T(8,128)(2,1)}), bf16[4,192,96]{2,1,0:T(8,128)(2,1)}, u32[]{:S(2)}, u32[]{:S(2)}) async-start(bf16[4,192,96]{2,1,0:T(8,128)(2,1)} %broadcast_in_dim.36), calls=%async_computation | async-start | bytes 393216 | tf_op jit(solution)/shard_map/all_to_all | solution.py:95
  26.9 7.8 %copy-start.20 = (bf16[2,128,16,128]{1,3,2,0:T(8,128)(2,1)}, bf16[2,128,16,128]{1,3,2,0:T(8,128)(2,1)S(1)}, u32[]{:S(2)}) copy-start(bf16[2,128,16,128]{1,3,2,0:T(8,128)(2,1)S(1)} %copy.58) | copy-start | bytes 3145732
  26.9 7.6 %copy-start.24 = (bf16[384,26]{0,1:T(8,128)(2,1)S(1)}, bf16[384,26]{0,1:T(8,128)(2,1)}, u32[]{:S(2)}) copy-start(bf16[384,26]{0,1:T(8,128)(2,1)} %param.24) | copy-start | bytes 59908
  28.1 42.2 %collective-permute-start.3 = (bf16[14,128,128]{2,1,0:T(8,128)(2,1)}, bf16[14,128,128]{2,1,0:T(8,128)(2,1)S(1)}, u32[]{:S(2)}, u32[]{:S(2)}) collective-permute-start(bf16[14,128,128]{2,1,0:T(8,128)(2,1)} %pad_maximum_fusion), channel_id=1, source_target_pairs={{0,4},{4,8},{8,12},{12,16},{16,20},{20,24},{24,28},{1,5},{5,9},{9,... | collective-permute-start | bytes 1376264 | tf_op jit(solution)/shard_map/ppermute | solution.py:395
  32.3 38.0 %collective-permute-start.4 = (bf16[14,128,128]{2,1,0:T(8,128)(2,1)}, bf16[14,128,128]{2,1,0:T(8,128)(2,1)S(1)}, u32[]{:S(2)}, u32[]{:S(2)}) collective-permute-start(bf16[14,128,128]{2,1,0:T(8,128)(2,1)} %pad_maximum_fusion.1), channel_id=1, source_target_pairs={{4,0},{8,4},{12,8},{16,12},{20,16},{24,20},{28,24},{5,1},{9,5},{13... | collective-permute-start | bytes 1376264 | tf_op jit(solution)/shard_map/ppermute | solution.py:395
  66.0 20.6 %all-to-all-start.1 = ((bf16[8,192,384]{2,1,0:T(8,128)(2,1)}), bf16[8,192,384]{2,1,0:T(8,128)(2,1)}, u32[]{:S(2)}, u32[]{:S(2)}) async-start(bf16[8,192,384]{2,1,0:T(8,128)(2,1)} %broadcast_in_dim.38), calls=%async_computation.1 | async-start | bytes 2359296 | tf_op jit(solution)/shard_map/all_to_all | solution.py:95
  70.4 8.6 %collective-permute-start.5 = (bf16[60,16,128]{2,1,0:T(8,128)(2,1)S(1)}, bf16[60,16,128]{2,1,0:T(8,128)(2,1)S(1)}, u32[]{:S(2)}, u32[]{:S(2)}) collective-permute-start(bf16[60,16,128]{2,1,0:T(8,128)(2,1)S(1)} %get-tuple-element.83), channel_id=1, source_target_pairs={{0,1},{1,2},{2,3},{4,5},{5,6},{6,7},{8,9},{9,10},{10,11},{12,13},{... | collective-permute-start | bytes 737288 | tf_op jit(solution)/shard_map/ppermute | solution.py:395
  73.3 10.0 %collective-permute-start.6 = (bf16[60,16,128]{2,1,0:T(8,128)(2,1)S(1)}, bf16[60,16,128]{2,1,0:T(8,128)(2,1)S(1)}, u32[]{:S(2)}, u32[]{:S(2)}) collective-permute-start(bf16[60,16,128]{2,1,0:T(8,128)(2,1)S(1)} %get-tuple-element.82), channel_id=1, source_target_pairs={{1,0},{2,1},{3,2},{5,4},{6,5},{7,6},{9,8},{10,9},{11,10},{13,12},{... | collective-permute-start | bytes 737288 | tf_op jit(solution)/shard_map/ppermute | solution.py:395
  88.5 1.1 copy-start.19
  112.2 1.1 copy-start.15
  112.2 1.3 copy-start.16
  112.2 40.7 %copy-start.7 = (bf16[128,256]{0,1:T(8,128)(2,1)S(1)}, bf16[128,256]{0,1:T(8,128)(2,1)}, u32[]{:S(2)}) copy-start(bf16[128,256]{0,1:T(8,128)(2,1)} %copy.61) | copy-start | bytes 196612
  113.4 39.4 %copy-start.1 = (bf16[384,384]{1,0:T(8,128)(2,1)S(1)}, bf16[384,384]{1,0:T(8,128)(2,1)}, u32[]{:S(2)}) copy-start(bf16[384,384]{1,0:T(8,128)(2,1)} %get-tuple-element.54.last_w_ref) | copy-start | bytes 884740
  113.4 39.4 %copy-start.2 = (bf16[384,384]{1,0:T(8,128)(2,1)S(1)}, bf16[384,384]{1,0:T(8,128)(2,1)}, u32[]{:S(2)}) copy-start(bf16[384,384]{1,0:T(8,128)(2,1)} %get-tuple-element.50.first_w_ref) | copy-start | bytes 884740
  113.5 39.4 %all-to-all-start.2 = ((bf16[32,32,128]{2,1,0:T(8,128)(2,1)}), bf16[32,32,128]{2,1,0:T(8,128)(2,1)S(1)}, u32[]{:S(2)}, u32[]{:S(2)}) async-start(bf16[32,32,128]{2,1,0:T(8,128)(2,1)} %bitcast.85), calls=%async_computation.2 | async-start | bytes 524288 | tf_op jit(solution)/shard_map/all_to_all | solution.py:95
  119.4 61.4 %collective-permute-start.7 = (bf16[2,360,384]{2,1,0:T(8,128)(2,1)}, bf16[2,360,384]{2,1,0:T(8,128)(2,1)}, u32[]{:S(2)}, u32[]{:S(2)}) collective-permute-start(bf16[2,360,384]{2,1,0:T(8,128)(2,1)} %copy-done.16), channel_id=1, source_target_pairs={{0,1},{1,2},{2,3},{3,0},{4,5},{5,6},{6,7},{7,4},{8,9},{9,10},{10,1... | collective-permute-start | bytes 1658888 | tf_op jit(solution)/shard_map/ppermute | solution.py:282
  121.2 59.6 %collective-permute-start.8 = (bf16[2,360,384]{2,1,0:T(8,128)(2,1)}, bf16[2,360,384]{2,1,0:T(8,128)(2,1)}, u32[]{:S(2)}, u32[]{:S(2)}) collective-permute-start(bf16[2,360,384]{2,1,0:T(8,128)(2,1)} %copy-done.15), channel_id=1, source_target_pairs={{0,2},{1,3},{2,0},{3,1},{4,6},{5,7},{6,4},{7,5},{8,10},{9,11},{10,... | collective-permute-start | bytes 1658888 | tf_op jit(solution)/shard_map/ppermute | solution.py:282
  123.6 57.2 %collective-permute-start.9 = (bf16[2,360,384]{2,1,0:T(8,128)(2,1)}, bf16[2,360,384]{2,1,0:T(8,128)(2,1)}, u32[]{:S(2)}, u32[]{:S(2)}) collective-permute-start(bf16[2,360,384]{2,1,0:T(8,128)(2,1)} %copy-done.14), channel_id=1, source_target_pairs={{0,3},{1,0},{2,1},{3,2},{4,7},{5,4},{6,5},{7,6},{8,11},{9,8},{10,9... | collective-permute-start | bytes 1658888 | tf_op jit(solution)/shard_map/ppermute | solution.py:282
  132.6 1.5 copy-start.8
  134.1 1.1 copy-start.10
  135.2 1.0 copy-start.12
  152.8 1.8 copy-start.9
  154.6 1.3 copy-start.11
  156.0 1.2 copy-start.13
  (8 other events, 6.9 us)

commit v4 on v3

--- a/solution.py
+++ b/solution.py
@@ -82,15 +82,6 @@
     )
 
 
-def sort_modes(spec_filter):
-    parts = []
-    for low, step, unit in ((0, 4, MODE_TILE), (2, 4, MODE_TILE), (1, 2, 2 * MODE_TILE)):
-        part = spec_filter[:, low::step].astype(jnp.bfloat16)
-        part = jnp.pad(part, ((0, 0), (0, -part.shape[1] % unit), (0, 0)))
-        parts.append(part.reshape(-1, part.shape[2]))
-    return jnp.concatenate(parts, axis=0)
-
-
 def exchange(blocks, axis):
     return lax.all_to_all(blocks, axis, split_axis=0, concat_axis=0, tiled=True)
 
@@ -99,14 +90,29 @@
     return exchange(jnp.broadcast_to(block[None], (lax.axis_size(axis),) + block.shape), axis)
 
 
-def collect_filter(spec_filter):
-    flat = sort_modes(spec_filter)
-    rows = flat.shape[0]
+def filter_share(spec_filter):
+    rows = 2 * spec_filter.shape[1]
+    flat = spec_filter.reshape(rows, spec_filter.shape[2])
     share = rows // lax.axis_size(PLANE)
     mine = lax.dynamic_slice_in_dim(flat, lax.axis_index(PLANE) * share, share, 0)
-    wide = spread(mine, "col")
-    wide = jnp.swapaxes(wide, 0, 1).reshape(share, -1)
-    return spread(wide, PLANE).reshape(rows, -1)
+    return mine.astype(jnp.bfloat16)
+
+
+def collect_filter(mine):
+    count = lax.axis_size("col")
+    me = lax.axis_index("col")
+    wide = jnp.broadcast_to(mine[None], (count,) + mine.shape)
+    for step in range(1, count):
+        block = shift(mine, "col", -step)
+        wide = lax.dynamic_update_slice_in_dim(wide, block[None], (me + step) % count, 0)
+    wide = jnp.swapaxes(wide, 0, 1).reshape(mine.shape[0], -1)
+    return spread(wide, PLANE).reshape(-1, wide.shape[1])
+
+
+def gelu(x):
+    slope = math.sqrt(2.0 / math.pi)
+    half = 0.5 * x
+    return half + half * jnp.tanh(x * (slope + (0.044715 * slope) * (x * x)))
 
 
 def latitude_kernel(hours, turns, step, place_ref, *refs):
@@ -114,7 +120,7 @@
     even_forward_ref, odd_forward_ref, even_inverse_ref, odd_inverse_ref = refs[:4]
     filter_ref, skip_ref, mix_ref, decode_ref = refs[4:8]
     out_refs, strip_ref = refs[8:12], refs[12]
-    state_ref, spectral_ref, coarse_ref, near_ref, packed_ref = refs[13:]
+    state_ref, spectral_ref, gain_ref, coarse_ref, near_ref, packed_ref = refs[13:]
     f32, bf16 = jnp.float32, jnp.bfloat16
     piece, channels = piece_refs[0].shape[1:]
     padded = state_ref.shape[0] // 4
@@ -128,13 +134,22 @@
                 index * padded : (index + 1) * padded, turn * channels : (turn + 1) * channels
             ] = jnp.concatenate([piece_refs[index][turn], spare], axis=0)
 
-    def gain(spectrum, low):
+    modes = filter_ref.shape[0] // 2
+    for index in range(channels // LANES):
+        lanes = slice(index * LANES, (index + 1) * LANES)
+        gain_ref[index, : 2 * modes, :] = filter_ref[:, lanes].astype(f32)
+        gain_ref[index, 2 * modes :, :] = jnp.zeros((gain_ref.shape[1] - 2 * modes, LANES), f32)
+
+    def gain_rows(low, count, stride):
+        rows = pl.ds(low, count, stride=stride)
+        tiles = [gain_ref[index, rows, :] for index in range(channels // LANES)]
+        return jnp.concatenate(tiles * turns, axis=1)
+
+    def gain(spectrum, low, stride):
         half = spectrum.shape[0] // 2
         real, imag = spectrum[:half], spectrum[half:]
-        gain_real = filter_ref[low : low + half, :].astype(f32)
-        gain_imag = filter_ref[low + half : low + 2 * half, :].astype(f32)
-        gain_real = jnp.concatenate([gain_real] * turns, axis=1)
-        gain_imag = jnp.concatenate([gain_imag] * turns, axis=1)
+        gain_real = gain_rows(low, half, stride)
+        gain_imag = gain_rows(modes + low, half, stride)
         return jnp.concatenate(
             [
                 (real * gain_real - imag * gain_imag).astype(bf16),
@@ -151,14 +166,12 @@
             state_ref[index * padded : (index + 1) * padded, :].astype(f32) for index in range(4)
         ]
         both, other = pieces[0] + pieces[2], pieces[1] + pieces[3]
-        low = 0
         shares = []
         for index, mixed in enumerate((both + other, both - other)):
             spectrum = dot(even_forward_ref[index], mixed.astype(bf16))
-            shares.append(dot(even_inverse_ref[index], gain(spectrum, low)))
-            low += spectrum.shape[0]
+            shares.append(dot(even_inverse_ref[index], gain(spectrum, 2 * index, 4)))
         mixed = jnp.concatenate([pieces[0] - pieces[2], pieces[1] - pieces[3]], axis=0)
-        odd = gain(dot(odd_forward_ref[...], mixed.astype(bf16)), low)
+        odd = gain(dot(odd_forward_ref[...], mixed.astype(bf16)), 1, 2)
         odd = dot(odd_inverse_ref[...], odd)
         for index in range(4):
             even = shares[0] + shares[1] if index % 2 == 0 else shares[0] - shares[1]
@@ -172,7 +185,7 @@
                 lanes = slice(turn * channels, (turn + 1) * channels)
                 state = state_ref[here, lanes]
                 summed = spectral_ref[here, lanes].astype(f32) + dot(state, skip_ref[...])
-                activated = jax.nn.gelu(summed).astype(bf16)
+                activated = gelu(summed).astype(bf16)
                 update = dot(activated, mix_ref[...])
                 state_ref[here, lanes] = (state.astype(f32) + update).astype(bf16)
             return carry
@@ -222,6 +235,7 @@
         [jnp.pad(decode, ((0, 0), (t * LANES, (turns - 1 - t) * LANES))) for t in range(turns)], axis=0
     )
     modes = gains.shape[0] // 2
+    spare = max(4 * (tables[0].shape[1] // 2), 2 * (tables[1].shape[0] // 2)) - modes
     flops = hours * turns * 8 * padded * channels * (3 * modes // 4 + 2 * channels)
     results = pl.pallas_call(
         functools.partial(latitude_kernel, hours, turns, step),
@@ -234,6 +248,7 @@
         scratch_shapes=[
             pltpu.VMEM((4 * padded, turns * channels), jnp.bfloat16),
             pltpu.VMEM((4 * padded, turns * channels), jnp.bfloat16),
+            pltpu.VMEM((channels // LANES, gains.shape[0] + spare, LANES), jnp.float32),
             pltpu.VMEM((turns, 2 * piece, LANES), jnp.float32),
             pltpu.VMEM((span, LANES), jnp.float32),
             pltpu.VMEM((turns, hours * span // group, LANES), jnp.float32),
@@ -324,33 +339,53 @@
     lats_here, piece, _ = global_state.shape
     turns = lats_here // count
     tables = split_tables(piece * count, spec_filter.shape[1])
-    owners = [(me - step) % count * turns for step in range(count)]
+    places = [[turn * count + (me - step) % count for step in range(count)] for turn in range(turns)]
+    mine = filter_share(spec_filter)
+    after = mine
     received = []
-    for step, owner in enumerate(owners):
-        own = lax.dynamic_slice_in_dim(global_state, owner, turns, 0)
-        received.append(shift(own, "col", -step) if step else own)
-    gains = collect_filter(spec_filter)
-    prepared = prepare(received[1])
-    received, gains, prepared = lax.optimization_barrier((received, gains, prepared))
+    for turn in range(turns):
+        global_state, _ = lax.optimization_barrier((global_state, after))
+        blocks = []
+        for step in range(count):
+            own = lax.dynamic_slice_in_dim(global_state, places[turn][step], 1, 0)
+            blocks.append(shift(own, "col", -step) if step else own)
+        received.append(blocks)
+        after = blocks[1]
+    gains = collect_filter(mine)
+    prepared = prepare(received[0][1])
     start = (box_lon0[0] - window_base() - me * piece) % (piece * count)
-    place = jnp.stack([start // piece, (start // piece + 1) % count, start % piece])
-    pieces, strips = advance_latitudes(
-        hours, cols_here // RATIO, place.astype(jnp.int32), received, tables, gains, w_skip, w_mix,
-        w_decode,
-    )
+    place = jnp.stack([start // piece, (start // piece + 1) % count, start % piece]).astype(jnp.int32)
+    outcome, strips = [], []
+    for turn in range(turns):
+        blocks = received[turn]
+        if turn == turns - 1:
+            blocks, prepared = lax.optimization_barrier((blocks, prepared))
+        blocks, strip = advance_latitudes(
+            hours, cols_here // RATIO, place, blocks, tables, gains, w_skip, w_mix, w_decode
+        )
+        outcome.append(blocks)
+        strips.append(strip)
     plane = lax.axis_size(PLANE)
+    strips = jnp.concatenate(strips, axis=1)
     sent = jnp.broadcast_to(strips[None], (plane,) + strips.shape)
     got = exchange(sent.reshape((plane * count,) + strips.shape[1:]), PLANE + ("col",))
+    outcome[-1], got = lax.optimization_barrier((outcome[-1], got))
     got = got.reshape((plane * lats_here, -1, LANES))
     lat = box_lat0[0] - window_base() + lax.axis_index(PLANE) * (rows_here // RATIO)
     lat = jnp.clip(lat + jnp.arange(window_extent(rows_here), dtype=jnp.int32), 0, plane * lats_here - 1)
-    finals = [shift(block, "col", step) if step else block for step, block in enumerate(pieces)]
+    band, lat = lat // lats_here, lat % lats_here
+    pick = (band * count + lat % count) * turns + lat // count
+    finals = [
+        shift(block, "col", step) if step else block
+        for blocks in outcome
+        for step, block in enumerate(blocks)
+    ]
 
     def finish(after):
         blocks, after = lax.optimization_barrier((finals, after))
-        return collate(jnp.stack(owners).astype(jnp.int32), blocks), after
-
-    return finish, got, lat.astype(jnp.int32), prepared
+        return collate(jnp.stack(sum(places, [])).astype(jnp.int32), blocks), after
+
+    return finish, got, pick.astype(jnp.int32), prepared
 
 
 def global_by_channel(
@@ -411,9 +446,14 @@
         ref[0:rim, pad : pad + cols, :] = above_ref[part : part + rim]
         ref[rim : rim + rows, pad : pad + cols, :] = mid_ref[...]
         ref[rim + rows :, pad : pad + cols, :] = below_ref[part : part + rim]
-        first = 0 if rim == RIM else rows + 2 * RIM
-        ref[:, 0:pad, :] = left_ref[first : first + rows + 2 * rim]
-        ref[:, pad + cols :, :] = right_ref[first : first + rows + 2 * rim]
+        skip = RIM - rim
+        for side_ref, low, to in (
+            (left_ref, 0, pad - rim),
+            (right_ref, pad + cols, 0),
+        ):
+            side = side_ref[skip : skip + rows + 2 * rim].astype(jnp.float32)
+            side = pltpu.roll(side, (to - part) % pad, 1)
+            ref[:, low : low + pad, :] = side.astype(jnp.bfloat16)
 
     base = window_base()
     col = lax.broadcasted_iota(jnp.int32, (width, 1), 0) - pad
@@ -697,17 +737,22 @@
         highs = jnp.concatenate([mid0[:RIM], mid1[:inner]], axis=0)
         above, below = next_to(lows, highs, PLANE)
 
-        def rim_cols(part):
+        def rim_cols(first, first_inner):
+            wide, thin = slice(first, first + RIM), slice(first_inner, first_inner + inner)
+            noise = jnp.concatenate([above[RIM:, thin], mid1[:, thin], below[RIM:, thin]], axis=0)
+            noise = jnp.pad(
+                noise, ((RIM_USED, RIM_USED), (0, RIM_COLS - RIM - inner), (0, 0))
+            )
             return jnp.concatenate(
                 [
-                    above[:RIM, part], mid0[:, part], below[:RIM, part],
-                    above[RIM:, part], mid1[:, part], below[RIM:, part],
+                    jnp.concatenate([above[:RIM, wide], mid0[:, wide], below[:RIM, wide]], axis=0),
+                    noise,
                 ],
-                axis=0,
+                axis=1,
             )
 
         left, right = next_to(
-            rim_cols(slice(cols_here - RIM_COLS, cols_here)), rim_cols(slice(0, RIM_COLS)), "col"
+            rim_cols(cols_here - RIM, cols_here - inner), rim_cols(0, 0), "col"
         )
         weights = (
             conv_weight(w_first, LANES, w_first.shape[0]),

time: 186 us -> 197 us (1.059)
  the two profiles are of different devices: /device:TPU:0 before, /device:TPU:8 now
where the time goes in v4:
time: 197 us; the launch traced here: 196 us
  Pallas kernels  61.3 us (31%)
  local copies, waits for them, and re-layouts  59.8 us (30%)
  starting transfers between devices  40.7 us (21%)
  waiting for transfers between devices  28.3 us (14%)
  between operations  2.93 us (1%)
  other arithmetic  2.77 us (1%)
    pallas_call x2, Pallas kernels, advance_latitudes(): pl.pallas_call(functools.partial(latitude_kernel, hours, turns, step), ou...  28.8 us
    unnamed x117, local copies, waits for them, and re-layouts  27.2 us
    ppermute x15, waiting for transfers between devices, shift(): lax.ppermute(block, axis, [(source, (source + step) % count) for source i...  25.4 us
    pallas_call x1, Pallas kernels, denoise(): pl.pallas_call(functools.partial(denoise_kernel, rows, cols, totals, vari...  23.9 us
    ppermute x15, starting transfers between devices, shift(): lax.ppermute(block, axis, [(source, (source + step) % count) for source i...  20 us
    dynamic_update_slice x3, local copies, waits for them, and re-layouts, collect_filter(): lax.dynamic_update_slice_in_dim(wide, block[None], (me + step) % count, 0)  9.46 us
    all_to_all x2, starting transfers between devices, exchange(): return lax.all_to_all(blocks, axis, split_axis=0, concat_axis=0, tiled=True)  8.63 us
    ppermute x2, starting transfers between devices, next_to(): lax.ppermute(high, axis, backward)  6.66 us
  transfers between devices with their start and end apart: 21, of which 6 were waited for; matrix products, arithmetic and copies ran while one was open for 19% of the time, Pallas kernels for 22%

profile of v4, /device:TPU:8, one launch (start us, length us, event | category | flops | bytes accessed | tf_op | source)
XLA Modules:
  0.0 195.9 jit_solution(2016759106265544026)
XLA Ops:
  0.6 1.5 copy.42
  3.1 3.0 %collective-permute-start.4 = (bf16[180,96]{0,1:T(8,128)(2,1)}, bf16[180,96]{0,1:T(8,128)(2,1)}, u32[]{:S(2)}, u32[]{:S(2)}) collective-permute-start(bf16[180,96]{0,1:T(8,128)(2,1)} %dynamic-slice_convert_fusion), channel_id=1, source_target_pairs={{0,2},{1,3},{2,0},{3,1},{4,6},{5,7},{6,4},{7,5},{8,10},{9,11},{10,... | collective-permute-start | bytes 103688 | tf_op jit(solution)/shard_map/ppermute | solution.py:297
  6.2 2.5 %collective-permute-start.5 = (bf16[180,96]{0,1:T(8,128)(2,1)}, bf16[180,96]{0,1:T(8,128)(2,1)}, u32[]{:S(2)}, u32[]{:S(2)}) collective-permute-start(bf16[180,96]{0,1:T(8,128)(2,1)} %dynamic-slice_convert_fusion), channel_id=1, source_target_pairs={{0,1},{1,2},{2,3},{3,0},{4,5},{5,6},{6,7},{7,4},{8,9},{9,10},{10,1... | collective-permute-start | bytes 103688 | tf_op jit(solution)/shard_map/ppermute | solution.py:297
  8.6 2.3 %constant_dynamic-slice_fusion.4 = (bf16[1,360,384]{2,1,0:T(8,128)(2,1)}, bf16[1,360,384]{2,1,0:T(8,128)(2,1)}, bf16[1,360,384]{2,1,0:T(8,128)(2,1)}, bf16[1,360,384]{2,1,0:T(8,128)(2,1)}) fusion(bf16[8,360,384]{2,1,0:T(8,128)(2,1)} %param.20, s32[]{:T(128)S(6)} %select_n.142, s32[]{:T(128)S(6)} %select_n.141, s32[]{:T(128)S(6)} %select_n.140, s32[]{:T(128)S(6)} %select_n.139), kind=kLoop, calls=%fused_computation.43 | loop fusion | bytes 2211856 | tf_op jit(solution)/shard_map/dynamic_slice | solution.py:350
  13.3 3.5 %collective-permute-start.12 = (bf16[14,128,128]{2,1,0:T(8,128)(2,1)S(1)}, bf16[14,128,128]{2,1,0:T(8,128)(2,1)S(1)}, u32[]{:S(2)}, u32[]{:S(2)}) collective-permute-start(bf16[14,128,128]{2,1,0:T(8,128)(2,1)S(1)} %pad_maximum_fusion), channel_id=1, source_target_pairs={{0,4},{4,8},{8,12},{12,16},{16,20},{20,24},{24,28},{1,5},{5,9},{9,... | collective-permute-start | bytes 1376264 | tf_op jit(solution)/shard_map/ppermute | solution.py:430
  27.8 3.2 %dynamic_update_slice.9 = bf16[4,180,96]{2,0,1:T(4,128)(2,1)S(1)} dynamic-update-slice(bf16[4,180,96]{2,0,1:T(4,128)(2,1)S(1)} %broadcast_in_dim.45, bf16[1,180,96]{2,0,1:T(2,128)(2,1)S(1)} %copy.44, s32[]{:T(128)S(6)} %select_n.144, s32[]{:T(128)} %constant.163.clone.1, s32[]{:T(128)} %constant.163.clone.1) | dynamic-update-slice | bytes 69124 | tf_op jit(solution)/shard_map/dynamic_update_slice | solution.py:107
  30.9 3.2 %dynamic_update_slice.10 = bf16[4,180,96]{2,0,1:T(4,128)(2,1)S(1)} dynamic-update-slice(bf16[4,180,96]{2,0,1:T(4,128)(2,1)S(1)} %dynamic_update_slice.9, bf16[1,180,96]{2,0,1:T(2,128)(2,1)S(1)} %copy.45, s32[]{:T(128)S(6)} %select_n.146, s32[]{:T(128)} %constant.163.clone.1, s32[]{:T(128)} %constant.163.clone.1) | dynamic-update-slice | bytes 69124 | tf_op jit(solution)/shard_map/dynamic_update_slice | solution.py:107
  34.1 3.2 %dynamic_update_slice.11 = bf16[4,180,96]{2,0,1:T(4,128)(2,1)S(1)} dynamic-update-slice(bf16[4,180,96]{2,0,1:T(4,128)(2,1)S(1)} %dynamic_update_slice.10, bf16[1,180,96]{2,0,1:T(2,128)(2,1)S(1)} %copy.47, s32[]{:T(128)S(6)} %select_n.148, s32[]{:T(128)} %constant.163.clone.1, s32[]{:T(128)} %constant.163.clone.1) | dynamic-update-slice | bytes 69124 | tf_op jit(solution)/shard_map/dynamic_update_slice | solution.py:107
  38.5 4.8 %all-to-all-start = ((bf16[8,180,384]{2,1,0:T(8,128)(2,1)}), bf16[8,180,384]{2,1,0:T(8,128)(2,1)}, u32[]{:S(2)}, u32[]{:S(2)}) async-start(bf16[8,180,384]{2,1,0:T(8,128)(2,1)} %broadcast_in_dim.50), calls=%async_computation | async-start | bytes 2260992 | tf_op jit(solution)/shard_map/all_to_all | solution.py:86
  43.5 2.4 %constant_dynamic-slice_fusion = (bf16[1,360,384]{2,1,0:T(8,128)(2,1)}, bf16[1,360,384]{2,1,0:T(8,128)(2,1)}, bf16[1,360,384]{2,1,0:T(8,128)(2,1)}, bf16[1,360,384]{2,1,0:T(8,128)(2,1)}) fusion(bf16[8,360,384]{2,1,0:T(8,128)(2,1)} %param.20, s32[]{:T(128)S(6)} %select_n.152, s32[]{:T(128)S(6)} %select_n.151, s32[]{:T(128)S(6)} %select_n.150, s32[]{:T(128)S(6)} %select_n.149), kind=kLoop, calls=%fused_computation.39 | loop fusion | bytes 2211856 | tf_op jit(solution)/shard_map/dynamic_slice | solution.py:350
  47.3 2.4 %collective-permute-start.11 = (bf16[1,360,384]{2,1,0:T(8,128)(2,1)}, bf16[1,360,384]{2,1,0:T(8,128)(2,1)S(1)}, u32[]{:S(2)}, u32[]{:S(2)}) collective-permute-start(bf16[1,360,384]{2,1,0:T(8,128)(2,1)} %get-tuple-element.96), channel_id=1, source_target_pairs={{0,1},{1,2},{2,3},{3,0},{4,5},{5,6},{6,7},{7,4},{8,9},{9,10},{10,1... | collective-permute-start | bytes 829448 | tf_op jit(solution)/shard_map/ppermute | solution.py:297
  50.5 5.4 %collective-permute-start.15 = (bf16[34,16,128]{2,1,0:T(8,128)(2,1)}, bf16[34,16,128]{2,1,0:T(8,128)(2,1)S(1)}, u32[]{:S(2)}, u32[]{:S(2)}) collective-permute-start(bf16[34,16,128]{2,1,0:T(8,128)(2,1)} %pad_maximum_fusion.3), channel_id=1, source_target_pairs={{1,0},{2,1},{3,2},{5,4},{6,5},{7,6},{9,8},{10,9},{11,10},{13,12},{... | collective-permute-start | bytes 417800 | tf_op jit(solution)/shard_map/ppermute | solution.py:430
  56.7 1.9 collective-permute-start.14
  60.2 2.2 %copy.51 = bf16[256,3,3,128]{0,2,3,1:T(4,128)(2,1)} copy(bf16[256,3,3,128]{3,0,2,1:T(8,128)(2,1)} %bitcast.86) | data formatting | bytes 1179648 | tf_op jit(solution)/shard_map/reshape | solution.py:676
  62.4 2.1 %copy.59 = bf16[48,8,3,256]{3,1,2,0:T(8,128)(2,1)} copy(bf16[48,8,3,256]{3,2,1,0:T(4,128)(2,1)} %bitcast.80) | data formatting | bytes 1179648
  66.9 11.4 %collective-permute-done.11.refs_3_ = bf16[1,360,384]{2,1,0:T(8,128)(2,1)S(1)} collective-permute-done((bf16[1,360,384]{2,1,0:T(8,128)(2,1)}, bf16[1,360,384]{2,1,0:T(8,128)(2,1)S(1)}, u32[]{:S(2)}, u32[]{:S(2)}) %collective-permute-start.11) | collective-permute-done | bytes 276512 | tf_op jit(solution)/shard_map/ppermute | solution.py:297
  79.0 2.4 %collective-permute-start.2 = (bf16[1,360,384]{2,1,0:T(8,128)(2,1)}, bf16[1,360,384]{2,1,0:T(8,128)(2,1)}, u32[]{:S(2)}, u32[]{:S(2)}) collective-permute-start(bf16[1,360,384]{2,1,0:T(8,128)(2,1)} %get-tuple-element.100), channel_id=1, source_target_pairs={{0,1},{1,2},{2,3},{3,0},{4,5},{5,6},{6,7},{7,4},{8,9},{9,10},{10,1... | collective-permute-start | bytes 829448 | tf_op jit(solution)/shard_map/ppermute | solution.py:297
  81.4 4.8 %collective-permute-done.9.refs_1_ = bf16[1,360,384]{2,1,0:T(8,128)(2,1)} collective-permute-done((bf16[1,360,384]{2,1,0:T(8,128)(2,1)}, bf16[1,360,384]{2,1,0:T(8,128)(2,1)}, u32[]{:S(2)}, u32[]{:S(2)}) %collective-permute-start.9) | collective-permute-done | bytes 276512 | tf_op jit(solution)/shard_map/ppermute | solution.py:297
  86.2 2.9 %collective-permute-done.15.right_ref = bf16[34,16,128]{2,1,0:T(8,128)(2,1)S(1)} collective-permute-done((bf16[34,16,128]{2,1,0:T(8,128)(2,1)}, bf16[34,16,128]{2,1,0:T(8,128)(2,1)S(1)}, u32[]{:S(2)}, u32[]{:S(2)}) %collective-permute-start.15) | collective-permute-done | bytes 139296 | tf_op jit(solution)/shard_map/ppermute | solution.py:430
  99.0 14.0 %advance_latitudes.3 = (bf16[1,360,384]{2,1,0:T(8,128)(2,1)S(1)}, bf16[1,360,384]{2,1,0:T(8,128)(2,1)S(1)}, bf16[1,360,384]{2,1,0:T(8,128)(2,1)S(1)}, bf16[1,360...) custom-call(s32[3]{0:T(128)S(1)} %pad_add_fusion.place_ref, bf16[1,360,384]{2,1,0:T(8,128)(2,1)S(1)} %copy-done.3, ...), custom_call_target="tpu_custom_call" | custom-call | flops 3085959168 | bytes 12582912 | tf_op jit(solution)/shard_map/advance_latitudes/pallas_call | solution.py:240
  114.6 14.8 %advance_latitudes.2 = (bf16[1,360,384]{2,1,0:T(8,128)(2,1)S(1)}, bf16[1,360,384]{2,1,0:T(8,128)(2,1)S(1)}, bf16[1,360,384]{2,1,0:T(8,128)(2,1)}, bf16[1,360,384]{2,1,0:T(8,128)(2,1)}, bf16[4,16,128]{2,1,0:T(8,128)(2,1)S(1)}) custom-call(s32[3]{0:T(128)S(1)} %pad_add_fusion.place_ref, bf16[1,360,384]{2,1,0:T(8,128)(2,1)S(1)} %copy-done.2, ...), custom_call_target="tpu_custom_call" | custom-call | flops 3085959168 | bytes 12582912 | tf_op jit(solution)/shard_map/advance_latitudes/pallas_call | solution.py:240
  130.3 3.8 %all-to-all-start.1 = ((bf16[32,32,128]{2,1,0:T(8,128)(2,1)}), bf16[32,32,128]{2,1,0:T(8,128)(2,1)}, u32[]{:S(2)}, u32[]{:S(2)}) async-start(bf16[32,32,128]{2,1,0:T(8,128)(2,1)} %bitcast.84), calls=%async_computation.1 | async-start | bytes 524288 | tf_op jit(solution)/shard_map/all_to_all | solution.py:86
  134.1 1.5 collective-permute-start.6
  138.0 5.7 %assemble.1 = (bf16[34,160,128]{2,1,0:T(8,128)(2,1)S(1)}, bf16[26,160,128]{2,1,0:T(8,128)(2,1)S(1)}, bf16[34,160,256]{2,1,0:T(8,128)(2,1)S(1)}) custom-call(s32[2]{0:T(128)S(1)} %pad_add_fusion.1.place_ref, bf16[16,128,128]{2,1,0:T(8,128)(2,1)S(1)} %get-tuple-element.66.mid0_ref, bf16[16,128,128]{2,1,0:T(8,128)(2,1)S(1)} %get-tuple-element.67.mid1_ref, ...), custom_call_target="tpu_custom_call" | custom-call | flops 200000000 | bytes 10000000 | tf_op jit(solution)/shard_map/assemble/pallas_call | solution.py:495
  143.7 1.5 copy-done.10
  148.5 1.7 collective-permute-start.8
  150.5 3.5 %collective-permute-start.17 = (bf16[1,360,384]{2,1,0:T(8,128)(2,1)}, bf16[1,360,384]{2,1,0:T(8,128)(2,1)S(1)}, u32[]{:S(2)}, u32[]{:S(2)}) collective-permute-start(bf16[1,360,384]{2,1,0:T(8,128)(2,1)} %copy-done.27), channel_id=1, source_target_pairs={{0,2},{1,3},{2,0},{3,1},{4,6},{5,7},{6,4},{7,5},{8,10},{9,11},{10,... | collective-permute-start | bytes 829448 | tf_op jit(solution)/shard_map/ppermute | solution.py:297
  154.1 1.8 copy-done.11
  158.4 23.9 %denoise.1 = bf16[16,128,128]{2,1,0:T(8,128)(2,1)S(1)} custom-call(s32[2]{0:T(128)S(1)} %pad_add_fusion.1.place_ref, s32[8]{0:T(128)S(1)} %multiply_add_fusion.pick_ref, bf16[34,160,128]{2,1,0:T(8,128)(2,1)S(1)} %copy-done.13, bf16[26,160,128]{2,1,0:T(8,128)(2,1)S(1)} %copy-done.15, bf16[34,160,256]{2,1,0:T(8,128)(2,1)S(1)} %copy-done.11, ...), custom_call_target="tpu_custom_call" | custom-call | flops 10000000000 | bytes 10000000 | tf_op jit(solution)/shard_map/denoise/pallas_call | solution.py:651
  182.4 3.0 %collective-permute-done.16.refs_5_ = bf16[1,360,384]{2,1,0:T(8,128)(2,1)S(1)} collective-permute-done((bf16[1,360,384]{2,1,0:T(8,128)(2,1)}, bf16[1,360,384]{2,1,0:T(8,128)(2,1)S(1)}, u32[]{:S(2)}, u32[]{:S(2)}) %collective-permute-start.16) | collective-permute-done | bytes 276512 | tf_op jit(solution)/shard_map/ppermute | solution.py:297
  185.5 4.8 %collective-permute-done.17.refs_6_ = bf16[1,360,384]{2,1,0:T(8,128)(2,1)S(1)} collective-permute-done((bf16[1,360,384]{2,1,0:T(8,128)(2,1)}, bf16[1,360,384]{2,1,0:T(8,128)(2,1)S(1)}, u32[]{:S(2)}, u32[]{:S(2)}) %collective-permute-start.17) | collective-permute-done | bytes 276512 | tf_op jit(solution)/shard_map/ppermute | solution.py:297
  192.7 3.0 %collate.1 = bf16[8,360,384]{2,1,0:T(8,128)(2,1)} custom-call(s32[8]{0:T(128)} %stack.56.place_ref, bf16[1,360,384]{2,1,0:T(8,128)(2,1)} %copy-done.5, bf16[1,360,384]{2,1,0:T(8,128)(2,1)} %collective-permute-done.6.refs_1_, bf16[1,360,384]{2,1,0:T(8,128)(2,1)} %copy-done.40, bf16[1,360,384]{2,1,0:T(8,128)(2,1)} %copy-done.41, ...), custom_call_target="tpu_custom_call" | custom-call | tf_op jit(solution)/shard_map/collate/pallas_call | solution.py:284
  (183 shorter events, 44.9 us)
Async XLA Ops:
  3.1 20.5 %collective-permute-start.3 = (bf16[180,96]{0,1:T(8,128)(2,1)}, bf16[180,96]{0,1:T(8,128)(2,1)}, u32[]{:S(2)}, u32[]{:S(2)}) collective-permute-start(bf16[180,96]{0,1:T(8,128)(2,1)} %dynamic-slice_convert_fusion), channel_id=1, source_target_pairs={{0,3},{1,0},{2,1},{3,2},{4,7},{5,4},{6,5},{7,6},{8,11},{9,8},{10,9... | collective-permute-start | bytes 103688 | tf_op jit(solution)/shard_map/ppermute | solution.py:297
  3.1 22.7 %collective-permute-start.4 = (bf16[180,96]{0,1:T(8,128)(2,1)}, bf16[180,96]{0,1:T(8,128)(2,1)}, u32[]{:S(2)}, u32[]{:S(2)}) collective-permute-start(bf16[180,96]{0,1:T(8,128)(2,1)} %dynamic-slice_convert_fusion), channel_id=1, source_target_pairs={{0,2},{1,3},{2,0},{3,1},{4,6},{5,7},{6,4},{7,5},{8,10},{9,11},{10,... | collective-permute-start | bytes 103688 | tf_op jit(solution)/shard_map/ppermute | solution.py:297
  6.2 20.6 %collective-permute-start.5 = (bf16[180,96]{0,1:T(8,128)(2,1)}, bf16[180,96]{0,1:T(8,128)(2,1)}, u32[]{:S(2)}, u32[]{:S(2)}) collective-permute-start(bf16[180,96]{0,1:T(8,128)(2,1)} %dynamic-slice_convert_fusion), channel_id=1, source_target_pairs={{0,1},{1,2},{2,3},{3,0},{4,5},{5,6},{6,7},{7,4},{8,9},{9,10},{10,1... | collective-permute-start | bytes 103688 | tf_op jit(solution)/shard_map/ppermute | solution.py:297
  10.9 32.5 %collective-permute-start = (bf16[1,360,384]{2,1,0:T(8,128)(2,1)}, bf16[1,360,384]{2,1,0:T(8,128)(2,1)S(1)}, u32[]{:S(2)}, u32[]{:S(2)}) collective-permute-start(bf16[1,360,384]{2,1,0:T(8,128)(2,1)} %get-tuple-element.102), channel_id=1, source_target_pairs={{0,3},{1,0},{2,1},{3,2},{4,7},{5,4},{6,5},{7,6},{8,11},{9,8},{10,9... | collective-permute-start | bytes 829448 | tf_op jit(solution)/shard_map/ppermute | solution.py:297
  13.3 36.4 %collective-permute-start.12 = (bf16[14,128,128]{2,1,0:T(8,128)(2,1)S(1)}, bf16[14,128,128]{2,1,0:T(8,128)(2,1)S(1)}, u32[]{:S(2)}, u32[]{:S(2)}) collective-permute-start(bf16[14,128,128]{2,1,0:T(8,128)(2,1)S(1)} %pad_maximum_fusion), channel_id=1, source_target_pairs={{0,4},{4,8},{8,12},{12,16},{16,20},{20,24},{24,28},{1,5},{5,9},{9,... | collective-permute-start | bytes 1376264 | tf_op jit(solution)/shard_map/ppermute | solution.py:430
  23.6 26.1 %collective-permute-start.13 = (bf16[14,128,128]{2,1,0:T(8,128)(2,1)}, bf16[14,128,128]{2,1,0:T(8,128)(2,1)S(1)}, u32[]{:S(2)}, u32[]{:S(2)}) collective-permute-start(bf16[14,128,128]{2,1,0:T(8,128)(2,1)} %pad_maximum_fusion.1), channel_id=1, source_target_pairs={{4,0},{8,4},{12,8},{16,12},{20,16},{24,20},{28,24},{5,1},{9,5},{13... | collective-permute-start | bytes 1376264 | tf_op jit(solution)/shard_map/ppermute | solution.py:430
  38.5 51.2 %all-to-all-start = ((bf16[8,180,384]{2,1,0:T(8,128)(2,1)}), bf16[8,180,384]{2,1,0:T(8,128)(2,1)}, u32[]{:S(2)}, u32[]{:S(2)}) async-start(bf16[8,180,384]{2,1,0:T(8,128)(2,1)} %broadcast_in_dim.50), calls=%async_computation | async-start | bytes 2260992 | tf_op jit(solution)/shard_map/all_to_all | solution.py:86
  43.4 15.2 %copy-start.35 = (bf16[128,3,3,128]{0,2,3,1:T(4,128)(2,1)S(1)}, bf16[128,3,3,128]{0,2,3,1:T(4,128)(2,1)}, u32[]{:S(2)}) copy-start(bf16[128,3,3,128]{0,2,3,1:T(4,128)(2,1)} %pad.24) | copy-start | bytes 884740
  43.4 15.2 %copy-start.36 = (bf16[128,3,3,128]{0,2,3,1:T(4,128)(2,1)S(1)}, bf16[128,3,3,128]{0,2,3,1:T(4,128)(2,1)}, u32[]{:S(2)}) copy-start(bf16[128,3,3,128]{0,2,3,1:T(4,128)(2,1)} %pad.23) | copy-start | bytes 884740
  45.9 20.4 %collective-permute-start.10 = (bf16[1,360,384]{2,1,0:T(8,128)(2,1)}, bf16[1,360,384]{2,1,0:T(8,128)(2,1)S(1)}, u32[]{:S(2)}, u32[]{:S(2)}) collective-permute-start(bf16[1,360,384]{2,1,0:T(8,128)(2,1)} %get-tuple-element.97), channel_id=1, source_target_pairs={{0,2},{1,3},{2,0},{3,1},{4,6},{5,7},{6,4},{7,5},{8,10},{9,11},{10,... | collective-permute-start | bytes 829448 | tf_op jit(solution)/shard_map/ppermute | solution.py:297
  47.3 31.0 %collective-permute-start.11 = (bf16[1,360,384]{2,1,0:T(8,128)(2,1)}, bf16[1,360,384]{2,1,0:T(8,128)(2,1)S(1)}, u32[]{:S(2)}, u32[]{:S(2)}) collective-permute-start(bf16[1,360,384]{2,1,0:T(8,128)(2,1)} %get-tuple-element.96), channel_id=1, source_target_pairs={{0,1},{1,2},{2,3},{3,0},{4,5},{5,6},{6,7},{7,4},{8,9},{9,10},{10,1... | collective-permute-start | bytes 829448 | tf_op jit(solution)/shard_map/ppermute | solution.py:297
  49.7 36.5 %collective-permute-start.9 = (bf16[1,360,384]{2,1,0:T(8,128)(2,1)}, bf16[1,360,384]{2,1,0:T(8,128)(2,1)}, u32[]{:S(2)}, u32[]{:S(2)}) collective-permute-start(bf16[1,360,384]{2,1,0:T(8,128)(2,1)} %get-tuple-element.98), channel_id=1, source_target_pairs={{0,3},{1,0},{2,1},{3,2},{4,7},{5,4},{6,5},{7,6},{8,11},{9,8},{10,9... | collective-permute-start | bytes 829448 | tf_op jit(solution)/shard_map/ppermute | solution.py:297
  50.5 38.6 %collective-permute-start.15 = (bf16[34,16,128]{2,1,0:T(8,128)(2,1)}, bf16[34,16,128]{2,1,0:T(8,128)(2,1)S(1)}, u32[]{:S(2)}, u32[]{:S(2)}) collective-permute-start(bf16[34,16,128]{2,1,0:T(8,128)(2,1)} %pad_maximum_fusion.3), channel_id=1, source_target_pairs={{1,0},{2,1},{3,2},{5,4},{6,5},{7,6},{9,8},{10,9},{11,10},{13,12},{... | collective-permute-start | bytes 417800 | tf_op jit(solution)/shard_map/ppermute | solution.py:430
  56.7 32.4 %collective-permute-start.14 = (bf16[34,16,128]{2,1,0:T(8,128)(2,1)}, bf16[34,16,128]{2,1,0:T(8,128)(2,1)S(1)}, u32[]{:S(2)}, u32[]{:S(2)}) collective-permute-start(bf16[34,16,128]{2,1,0:T(8,128)(2,1)} %pad_maximum_fusion.2), channel_id=1, source_target_pairs={{0,1},{1,2},{2,3},{4,5},{5,6},{6,7},{8,9},{9,10},{10,11},{12,13},{... | collective-permute-start | bytes 417800 | tf_op jit(solution)/shard_map/ppermute | solution.py:430
  66.9 46.8 %collective-permute-start.1 = (bf16[1,360,384]{2,1,0:T(8,128)(2,1)}, bf16[1,360,384]{2,1,0:T(8,128)(2,1)}, u32[]{:S(2)}, u32[]{:S(2)}) collective-permute-start(bf16[1,360,384]{2,1,0:T(8,128)(2,1)} %get-tuple-element.101), channel_id=1, source_target_pairs={{0,2},{1,3},{2,0},{3,1},{4,6},{5,7},{6,4},{7,5},{8,10},{9,11},{10,... | collective-permute-start | bytes 829448 | tf_op jit(solution)/shard_map/ppermute | solution.py:297
  79.0 34.7 %collective-permute-start.2 = (bf16[1,360,384]{2,1,0:T(8,128)(2,1)}, bf16[1,360,384]{2,1,0:T(8,128)(2,1)}, u32[]{:S(2)}, u32[]{:S(2)}) collective-permute-start(bf16[1,360,384]{2,1,0:T(8,128)(2,1)} %get-tuple-element.100), channel_id=1, source_target_pairs={{0,1},{1,2},{2,3},{3,0},{4,5},{5,6},{6,7},{7,4},{8,9},{9,10},{10,1... | collective-permute-start | bytes 829448 | tf_op jit(solution)/shard_map/ppermute | solution.py:297
  98.9 15.7 %copy-start.2 = (bf16[1,360,384]{2,1,0:T(8,128)(2,1)S(1)}, bf16[1,360,384]{2,1,0:T(8,128)(2,1)}, u32[]{:S(2)}) copy-start(bf16[1,360,384]{2,1,0:T(8,128)(2,1)} %get-tuple-element.103.refs_0_) | copy-start | bytes 829444
  98.9 15.7 %copy-start.17 = (bf16[384,384]{1,0:T(8,128)(2,1)S(1)}, bf16[384,384]{1,0:T(8,128)(2,1)}, u32[]{:S(2)}) copy-start(bf16[384,384]{1,0:T(8,128)(2,1)} %refs_9_.3) | copy-start | bytes 884740
  98.9 15.7 %copy-start.19 = (bf16[384,384]{1,0:T(8,128)(2,1)S(1)}, bf16[384,384]{1,0:T(8,128)(2,1)}, u32[]{:S(2)}) copy-start(bf16[384,384]{1,0:T(8,128)(2,1)} %refs_10_.3) | copy-start | bytes 884740
  98.9 15.7 %copy-start.21 = (bf16[1,360,384]{2,1,0:T(8,128)(2,1)S(1)}, bf16[1,360,384]{2,1,0:T(8,128)(2,1)}, u32[]{:S(2)}) copy-start(bf16[1,360,384]{2,1,0:T(8,128)(2,1)} %copy-done.20) | copy-start | bytes 829444
  99.0 15.7 %copy-start.31 = (bf16[2,384,384]{2,1,0:T(8,128)(2,1)S(1)}, bf16[2,384,384]{2,1,0:T(8,128)(2,1)}, u32[]{:S(2)}) copy-start(bf16[2,384,384]{2,1,0:T(8,128)(2,1)} %constant.186.clone.refs_4_) | copy-start | bytes 1769476
  99.0 15.7 %copy-start.33 = (bf16[2,384,384]{2,1,0:T(8,128)(2,1)S(1)}, bf16[2,384,384]{2,1,0:T(8,128)(2,1)}, u32[]{:S(2)}) copy-start(bf16[2,384,384]{2,1,0:T(8,128)(2,1)} %constant.188.clone.refs_6_) | copy-start | bytes 1769476
  129.4 24.6 %copy-start.9 = (bf16[128,256]{0,1:T(8,128)(2,1)S(1)}, bf16[128,256]{0,1:T(8,128)(2,1)}, u32[]{:S(2)}) copy-start(bf16[128,256]{0,1:T(8,128)(2,1)} %copy.52) | copy-start | bytes 196612
  130.3 23.7 %copy-start = (bf16[48,8,3,256]{3,1,2,0:T(8,128)(2,1)S(1)}, bf16[48,8,3,256]{3,1,2,0:T(8,128)(2,1)}, u32[]{:S(2)}) copy-start(bf16[48,8,3,256]{3,1,2,0:T(8,128)(2,1)} %copy.59) | copy-start | bytes 1769476
  130.3 23.7 %copy-start.1 = (bf16[384,384]{1,0:T(8,128)(2,1)S(1)}, bf16[384,384]{1,0:T(8,128)(2,1)}, u32[]{:S(2)}) copy-start(bf16[384,384]{1,0:T(8,128)(2,1)} %get-tuple-element.76.first_w_ref) | copy-start | bytes 884740
  130.3 19.9 %all-to-all-start.1 = ((bf16[32,32,128]{2,1,0:T(8,128)(2,1)}), bf16[32,32,128]{2,1,0:T(8,128)(2,1)}, u32[]{:S(2)}, u32[]{:S(2)}) async-start(bf16[32,32,128]{2,1,0:T(8,128)(2,1)} %bitcast.84), calls=%async_computation.1 | async-start | bytes 524288 | tf_op jit(solution)/shard_map/all_to_all | solution.py:86
  134.1 19.9 %collective-permute-start.6 = (bf16[1,360,384]{2,1,0:T(8,128)(2,1)}, bf16[1,360,384]{2,1,0:T(8,128)(2,1)}, u32[]{:S(2)}, u32[]{:S(2)}) collective-permute-start(bf16[1,360,384]{2,1,0:T(8,128)(2,1)} %copy-done.29), channel_id=1, source_target_pairs={{0,1},{1,2},{2,3},{3,0},{4,5},{5,6},{6,7},{7,4},{8,9},{9,10},{10,1... | collective-permute-start | bytes 829448 | tf_op jit(solution)/shard_map/ppermute | solution.py:297
  147.3 35.1 %collective-permute-start.7 = (bf16[1,360,384]{2,1,0:T(8,128)(2,1)}, bf16[1,360,384]{2,1,0:T(8,128)(2,1)S(1)}, u32[]{:S(2)}, u32[]{:S(2)}) collective-permute-start(bf16[1,360,384]{2,1,0:T(8,128)(2,1)} %get-tuple-element.49), channel_id=1, source_target_pairs={{0,2},{1,3},{2,0},{3,1},{4,6},{5,7},{6,4},{7,5},{8,10},{9,11},{10,... | collective-permute-start | bytes 829448 | tf_op jit(solution)/shard_map/ppermute | solution.py:297
  148.5 33.9 %collective-permute-start.8 = (bf16[1,360,384]{2,1,0:T(8,128)(2,1)}, bf16[1,360,384]{2,1,0:T(8,128)(2,1)S(1)}, u32[]{:S(2)}, u32[]{:S(2)}) collective-permute-start(bf16[1,360,384]{2,1,0:T(8,128)(2,1)} %get-tuple-element.50), channel_id=1, source_target_pairs={{0,3},{1,0},{2,1},{3,2},{4,7},{5,4},{6,5},{7,6},{8,11},{9,8},{10,9... | collective-permute-start | bytes 829448 | tf_op jit(solution)/shard_map/ppermute | solution.py:297
  150.3 35.2 %collective-permute-start.16 = (bf16[1,360,384]{2,1,0:T(8,128)(2,1)}, bf16[1,360,384]{2,1,0:T(8,128)(2,1)S(1)}, u32[]{:S(2)}, u32[]{:S(2)}) collective-permute-start(bf16[1,360,384]{2,1,0:T(8,128)(2,1)} %copy-done.28), channel_id=1, source_target_pairs={{0,1},{1,2},{2,3},{3,0},{4,5},{5,6},{6,7},{7,4},{8,9},{9,10},{10,1... | collective-permute-start | bytes 829448 | tf_op jit(solution)/shard_map/ppermute | solution.py:297
  150.5 39.8 %collective-permute-start.17 = (bf16[1,360,384]{2,1,0:T(8,128)(2,1)}, bf16[1,360,384]{2,1,0:T(8,128)(2,1)S(1)}, u32[]{:S(2)}, u32[]{:S(2)}) collective-permute-start(bf16[1,360,384]{2,1,0:T(8,128)(2,1)} %copy-done.27), channel_id=1, source_target_pairs={{0,2},{1,3},{2,0},{3,1},{4,6},{5,7},{6,4},{7,5},{8,10},{9,11},{10,... | collective-permute-start | bytes 829448 | tf_op jit(solution)/shard_map/ppermute | solution.py:297
  154.0 37.5 %collective-permute-start.18 = (bf16[1,360,384]{2,1,0:T(8,128)(2,1)}, bf16[1,360,384]{2,1,0:T(8,128)(2,1)}, u32[]{:S(2)}, u32[]{:S(2)}) collective-permute-start(bf16[1,360,384]{2,1,0:T(8,128)(2,1)} %copy-done.26), channel_id=1, source_target_pairs={{0,3},{1,0},{2,1},{3,2},{4,7},{5,4},{6,5},{7,6},{8,11},{9,8},{10,9... | collective-permute-start | bytes 829448 | tf_op jit(solution)/shard_map/ppermute | solution.py:297
  (43 other events, 148.3 us)

commit v5 on v4

--- a/solution.py
+++ b/solution.py
@@ -98,15 +98,13 @@
     return mine.astype(jnp.bfloat16)
 
 
-def collect_filter(mine):
+def every_channel(mine):
     count = lax.axis_size("col")
     me = lax.axis_index("col")
-    wide = jnp.broadcast_to(mine[None], (count,) + mine.shape)
-    for step in range(1, count):
-        block = shift(mine, "col", -step)
-        wide = lax.dynamic_update_slice_in_dim(wide, block[None], (me + step) % count, 0)
-    wide = jnp.swapaxes(wide, 0, 1).reshape(mine.shape[0], -1)
-    return spread(wide, PLANE).reshape(-1, wide.shape[1])
+    blocks = [shift(mine, "col", -step) if step else mine for step in range(count)]
+    ring = jnp.concatenate(blocks + blocks[:-1], axis=1)
+    width = mine.shape[1]
+    return lax.dynamic_slice_in_dim(ring, (count - me) % count * width, count * width, 1)
 
 
 def gelu(x):
@@ -225,41 +223,35 @@
             ).astype(bf16)
 
 
-def advance_latitudes(hours, step, place, pieces, tables, gains, w_skip, w_mix, w_decode):
-    turns, piece, channels = pieces[0].shape
+def advance_latitude(hours, turn, step, place, pieces, tables, gains, w_skip, w_mix, w_decode):
+    _, piece, channels = pieces[0].shape
     padded = round_up(piece, LANES)
     group = LANES // PACKED
     span = round_up(3 * step + STRIP * group, 8 * group)
     decode = jnp.pad(w_decode, ((0, 0), (0, LANES - w_decode.shape[1])))
-    decode = jnp.concatenate(
-        [jnp.pad(decode, ((0, 0), (t * LANES, (turns - 1 - t) * LANES))) for t in range(turns)], axis=0
-    )
     modes = gains.shape[0] // 2
     spare = max(4 * (tables[0].shape[1] // 2), 2 * (tables[1].shape[0] // 2)) - modes
-    flops = hours * turns * 8 * padded * channels * (3 * modes // 4 + 2 * channels)
     results = pl.pallas_call(
-        functools.partial(latitude_kernel, hours, turns, step),
-        out_shape=tuple(
-            jax.ShapeDtypeStruct((turns, piece, channels), jnp.bfloat16) for _ in pieces
-        )
-        + (jax.ShapeDtypeStruct((4, turns * hours * STRIP, LANES), jnp.bfloat16),),
+        functools.partial(latitude_kernel, hours, 1, step),
+        grid=(1,),
+        out_shape=tuple(jax.ShapeDtypeStruct((1, piece, channels), jnp.bfloat16) for _ in pieces)
+        + (jax.ShapeDtypeStruct((4, hours * STRIP, LANES), jnp.bfloat16),),
         in_specs=[pl.BlockSpec(memory_space=pltpu.SMEM)]
-        + [pl.BlockSpec(memory_space=pltpu.VMEM)] * 12,
+        + [pl.BlockSpec((1, piece, channels), lambda i: (turn, 0, 0))] * 4
+        + [pl.BlockSpec(memory_space=pltpu.VMEM)] * 8,
         scratch_shapes=[
-            pltpu.VMEM((4 * padded, turns * channels), jnp.bfloat16),
-            pltpu.VMEM((4 * padded, turns * channels), jnp.bfloat16),
+            pltpu.VMEM((4 * padded, channels), jnp.bfloat16),
+            pltpu.VMEM((4 * padded, channels), jnp.bfloat16),
             pltpu.VMEM((channels // LANES, gains.shape[0] + spare, LANES), jnp.float32),
-            pltpu.VMEM((turns, 2 * piece, LANES), jnp.float32),
+            pltpu.VMEM((1, 2 * piece, LANES), jnp.float32),
             pltpu.VMEM((span, LANES), jnp.float32),
-            pltpu.VMEM((turns, hours * span // group, LANES), jnp.float32),
+            pltpu.VMEM((1, hours * span // group, LANES), jnp.float32),
         ],
         compiler_params=pltpu.CompilerParams(vmem_limit_bytes=48 * 2**20),
         cost_estimate=pl.CostEstimate(
-            flops=flops,
-            bytes_accessed=12 * 2**20,
-            transcendentals=hours * turns * 4 * piece * channels,
+            flops=16 * 10**9, bytes_accessed=8 * 2**20, transcendentals=hours * 4 * piece * channels
         ),
-        name="advance_latitudes",
+        name="advance_latitude",
     )(place, *pieces, *tables, gains, w_skip, w_mix, decode)
     return results[:4], results[4]
 
@@ -339,29 +331,24 @@
     lats_here, piece, _ = global_state.shape
     turns = lats_here // count
     tables = split_tables(piece * count, spec_filter.shape[1])
-    places = [[turn * count + (me - step) % count for step in range(count)] for turn in range(turns)]
+    owners = [(me - step) % count * turns for step in range(count)]
     mine = filter_share(spec_filter)
-    after = mine
+    global_state, mine = lax.optimization_barrier((global_state, mine))
     received = []
-    for turn in range(turns):
-        global_state, _ = lax.optimization_barrier((global_state, after))
-        blocks = []
-        for step in range(count):
-            own = lax.dynamic_slice_in_dim(global_state, places[turn][step], 1, 0)
-            blocks.append(shift(own, "col", -step) if step else own)
-        received.append(blocks)
-        after = blocks[1]
-    gains = collect_filter(mine)
-    prepared = prepare(received[0][1])
+    for step, owner in enumerate(owners):
+        own = lax.dynamic_slice_in_dim(global_state, owner, turns, 0)
+        received.append(shift(own, "col", -step) if step else own)
+    wide = every_channel(mine)
+    gains = spread(wide, PLANE).reshape(-1, wide.shape[1])
+    prepared = prepare(wide)
     start = (box_lon0[0] - window_base() - me * piece) % (piece * count)
     place = jnp.stack([start // piece, (start // piece + 1) % count, start % piece]).astype(jnp.int32)
     outcome, strips = [], []
     for turn in range(turns):
-        blocks = received[turn]
         if turn == turns - 1:
-            blocks, prepared = lax.optimization_barrier((blocks, prepared))
-        blocks, strip = advance_latitudes(
-            hours, cols_here // RATIO, place, blocks, tables, gains, w_skip, w_mix, w_decode
+            received, prepared = lax.optimization_barrier((received, prepared))
+        blocks, strip = advance_latitude(
+            hours, turn, cols_here // RATIO, place, received, tables, gains, w_skip, w_mix, w_decode
         )
         outcome.append(blocks)
         strips.append(strip)
@@ -373,8 +360,7 @@
     got = got.reshape((plane * lats_here, -1, LANES))
     lat = box_lat0[0] - window_base() + lax.axis_index(PLANE) * (rows_here // RATIO)
     lat = jnp.clip(lat + jnp.arange(window_extent(rows_here), dtype=jnp.int32), 0, plane * lats_here - 1)
-    band, lat = lat // lats_here, lat % lats_here
-    pick = (band * count + lat % count) * turns + lat // count
+    places = [owner + turn for turn in range(turns) for owner in owners]
     finals = [
         shift(block, "col", step) if step else block
         for blocks in outcome
@@ -383,9 +369,9 @@
 
     def finish(after):
         blocks, after = lax.optimization_barrier((finals, after))
-        return collate(jnp.stack(sum(places, [])).astype(jnp.int32), blocks), after
-
-    return finish, got, pick.astype(jnp.int32), prepared
+        return collate(jnp.stack(places).astype(jnp.int32), blocks), after
+
+    return finish, got, lat.astype(jnp.int32), prepared
 
 
 def global_by_channel(
@@ -504,7 +490,7 @@
         in_specs=[pl.BlockSpec(memory_space=pltpu.SMEM)]
         + [pl.BlockSpec(memory_space=pltpu.VMEM)] * 6,
         compiler_params=pltpu.CompilerParams(vmem_limit_bytes=40 * 2**20),
-        cost_estimate=pl.CostEstimate(flops=2 * 10**8, bytes_accessed=10**7, transcendentals=0),
+        cost_estimate=pl.CostEstimate(flops=10**6, bytes_accessed=10**5, transcendentals=0),
         name="assemble",
     )(place, mid0, mid1, above, below, left, right)
 
@@ -664,9 +650,7 @@
             pltpu.VMEM((2, blend.shape[2], channels), bf16),
         ],
         compiler_params=pltpu.CompilerParams(vmem_limit_bytes=40 * 2**20),
-        cost_estimate=pl.CostEstimate(
-            flops=10**10, bytes_accessed=10**7, transcendentals=4 * 10**6
-        ),
+        cost_estimate=pl.CostEstimate(flops=10**6, bytes_accessed=10**5, transcendentals=0),
         name="denoise",
     )(place, pick, noisy, noise, blend, strips, *weights)
 
@@ -735,6 +719,7 @@
     def prepare(after):
         lows = jnp.concatenate([mid0[rows_here - RIM :], mid1[rows_here - inner :]], axis=0)
         highs = jnp.concatenate([mid0[:RIM], mid1[:inner]], axis=0)
+        lows, highs, _ = lax.optimization_barrier((lows, highs, after))
         above, below = next_to(lows, highs, PLANE)
 
         def rim_cols(first, first_inner):

time: 197 us -> 174 us (0.88); the launches traced: 196 us -> 171 us
  local copies, waits for them, and re-layouts: 59.8 us -> 32.4 us
  waiting for transfers between devices: 28.3 us -> 33.6 us
  starting transfers between devices: 40.7 us -> 37.7 us
    ppermute x15 -> x12, waiting for transfers between devices: 25.4 us -> 5.21 us  [shift(): lax.ppermute(block, axis, [(source, (source + step) % count) for source i...]
    all_to_all x2, waiting for transfers between devices: 0.01 us -> 15.2 us  [exchange(): return lax.all_to_all(blocks, axis, split_axis=0, concat_axis=0, tiled=True)]
    unnamed x117 -> x61, local copies, waits for them, and re-layouts: 27.2 us -> 16.2 us
    ppermute x2, waiting for transfers between devices: 2.88 us -> 13.2 us  [next_to(): lax.ppermute(high, axis, backward)]
    dynamic_update_slice x3 -> x0, local copies, waits for them, and re-layouts: 9.46 us -> none  [collect_filter(): lax.dynamic_update_slice_in_dim(wide, block[None], (me + step) % count, 0)]
    broadcast_in_dim x4 -> x0, local copies, waits for them, and re-layouts: 2.79 us -> none  [the longest x3 2.74 us: collect_filter(): block[None]]
    ppermute x2, starting transfers between devices: 6.66 us -> 4.62 us  [next_to(): lax.ppermute(high, axis, backward)]
    ppermute x15 -> x12, starting transfers between devices: 20 us -> 18.1 us  [shift(): lax.ppermute(block, axis, [(source, (source + step) % count) for source i...]
  transfers between devices with their start and end apart: 21 -> 18, of which waited for: 6 -> 5; matrix products, arithmetic and copies ran while one was open for 19% -> 11% of each run, Pallas kernels for 22% -> 17%
where the time goes in v5:
time: 174 us; the launch traced here: 171 us
  Pallas kernels  61.3 us (35%)
  starting transfers between devices  37.7 us (22%)
  waiting for transfers between devices  33.6 us (19%)
  local copies, waits for them, and re-layouts  32.4 us (19%)
  other arithmetic  2.93 us (2%)
  between operations  2.74 us (2%)
    pallas_call x2, Pallas kernels, advance_latitude(): pl.pallas_call(functools.partial(latitude_kernel, hours, 1, step), grid=(...  28.8 us
    pallas_call x1, Pallas kernels, denoise(): pl.pallas_call(functools.partial(denoise_kernel, rows, cols, totals, vari...  23.5 us
    ppermute x12, starting transfers between devices, shift(): lax.ppermute(block, axis, [(source, (source + step) % count) for source i...  18.1 us
    unnamed x61, local copies, waits for them, and re-layouts  16.2 us
    all_to_all x2, waiting for transfers between devices, exchange(): return lax.all_to_all(blocks, axis, split_axis=0, concat_axis=0, tiled=True)  15.2 us
    ppermute x2, waiting for transfers between devices, next_to(): lax.ppermute(high, axis, backward)  13.2 us
    all_to_all x2, starting transfers between devices, exchange(): return lax.all_to_all(blocks, axis, split_axis=0, concat_axis=0, tiled=True)  8.87 us
    ppermute x2, starting transfers between devices, next_to(): lax.ppermute(low, axis, forward)  6.1 us
  transfers between devices with their start and end apart: 18, of which 5 were waited for; matrix products, arithmetic and copies ran while one was open for 11% of the time, Pallas kernels for 17%

profile of v5, /device:TPU:8, one launch (start us, length us, event | category | flops | bytes accessed | tf_op | source)
XLA Modules:
  0.0 170.7 jit_solution(15385015526241992285)
XLA Ops:
  0.6 1.5 copy.29
  2.5 1.6 collective-permute-start.5
  5.2 1.9 %collective-permute-start.3 = (bf16[180,96]{0,1:T(8,128)(2,1)S(1)}, bf16[180,96]{0,1:T(8,128)(2,1)S(1)}, u32[]{:S(2)}, u32[]{:S(2)}) collective-permute-start(bf16[180,96]{0,1:T(8,128)(2,1)S(1)} %dynamic-slice_convert_fusion), channel_id=1, source_target_pairs={{0,3},{1,0},{2,1},{3,2},{4,7},{5,4},{6,5},{7,6},{8,11},{9,8},{10,9... | collective-permute-start | bytes 103688 | tf_op jit(solution)/shard_map/ppermute | solution.py:289
  7.2 3.1 %constant_dynamic-slice_fusion.1 = (bf16[2,360,384]{2,1,0:T(8,128)(2,1)}, bf16[2,360,384]{2,1,0:T(8,128)(2,1)}, bf16[2,360,384]{2,1,0:T(8,128)(2,1)}, bf16[2,360,384]{2,1,0:T(8,128)(2,1)}) fusion(bf16[8,360,384]{2,1,0:T(8,128)(2,1)} %param.20, s32[]{:T(128)S(6)} %select_n.90, s32[]{:T(128)S(6)} %select_n.89, s32[]{:T(128)S(6)} %select_n.88, s32[]{:T(128)S(6)} %select_n.87), kind=kLoop, calls=%fused_computation.49 | loop fusion | bytes 4423696 | tf_op jit(solution)/shard_map/dynamic_slice | solution.py:339
  10.3 3.6 %collective-permute-start.1 = (bf16[2,360,384]{2,1,0:T(8,128)(2,1)}, bf16[2,360,384]{2,1,0:T(8,128)(2,1)}, u32[]{:S(2)}, u32[]{:S(2)}) collective-permute-start(bf16[2,360,384]{2,1,0:T(8,128)(2,1)} %get-tuple-element.99), channel_id=1, source_target_pairs={{0,2},{1,3},{2,0},{3,1},{4,6},{5,7},{6,4},{7,5},{8,10},{9,11},{10,... | collective-permute-start | bytes 1658888 | tf_op jit(solution)/shard_map/ppermute | solution.py:289
  16.7 3.4 %collective-permute-start.9 = (bf16[14,128,128]{2,1,0:T(8,128)(2,1)}, bf16[14,128,128]{2,1,0:T(8,128)(2,1)S(1)}, u32[]{:S(2)}, u32[]{:S(2)}) collective-permute-start(bf16[14,128,128]{2,1,0:T(8,128)(2,1)} %get-tuple-element.54), channel_id=1, source_target_pairs={{0,4},{4,8},{8,12},{12,16},{16,20},{20,24},{24,28},{1,5},{5,9},{9,... | collective-permute-start | bytes 1376264 | tf_op jit(solution)/shard_map/ppermute | solution.py:416
  20.3 1.3 collective-permute-start.10
  21.6 1.2 copy.33
  22.9 1.2 copy.37
  26.1 1.1 broadcast_in_dim.14
  27.2 4.8 %all-to-all-start = ((bf16[8,180,384]{2,1,0:T(8,128)(2,1)}), bf16[8,180,384]{2,1,0:T(8,128)(2,1)}, u32[]{:S(2)}, u32[]{:S(2)}) async-start(bf16[8,180,384]{2,1,0:T(8,128)(2,1)} %broadcast_in_dim.14), calls=%async_computation | async-start | bytes 2260992 | tf_op jit(solution)/shard_map/all_to_all | solution.py:86
  32.1 11.0 %collective-permute-done.10.below_ref = bf16[14,128,128]{2,1,0:T(8,128)(2,1)S(1)} collective-permute-done((bf16[14,128,128]{2,1,0:T(8,128)(2,1)}, bf16[14,128,128]{2,1,0:T(8,128)(2,1)S(1)}, u32[]{:S(2)}, u32[]{:S(2)}) %collective-permute-start.10) | collective-permute-done | bytes 458784 | tf_op jit(solution)/shard_map/ppermute | solution.py:416
  43.9 3.3 %collective-permute-start.12 = (bf16[34,16,128]{2,1,0:T(8,128)(2,1)}, bf16[34,16,128]{2,1,0:T(8,128)(2,1)S(1)}, u32[]{:S(2)}, u32[]{:S(2)}) collective-permute-start(bf16[34,16,128]{2,1,0:T(8,128)(2,1)} %pad_maximum_fusion.3), channel_id=1, source_target_pairs={{1,0},{2,1},{3,2},{5,4},{6,5},{7,6},{9,8},{10,9},{11,10},{13,12},{... | collective-permute-start | bytes 417800 | tf_op jit(solution)/shard_map/ppermute | solution.py:416
  48.0 2.7 %collective-permute-start.11 = (bf16[34,16,128]{2,1,0:T(8,128)(2,1)}, bf16[34,16,128]{2,1,0:T(8,128)(2,1)}, u32[]{:S(2)}, u32[]{:S(2)}) collective-permute-start(bf16[34,16,128]{2,1,0:T(8,128)(2,1)} %pad_maximum_fusion.2), channel_id=1, source_target_pairs={{0,1},{1,2},{2,3},{4,5},{5,6},{6,7},{8,9},{9,10},{10,11},{12,13},{... | collective-permute-start | bytes 417800 | tf_op jit(solution)/shard_map/ppermute | solution.py:416
  52.7 2.2 %copy.34 = bf16[256,3,3,128]{0,2,3,1:T(4,128)(2,1)} copy(bf16[256,3,3,128]{3,0,2,1:T(8,128)(2,1)} %bitcast.82) | data formatting | bytes 1179648 | tf_op jit(solution)/shard_map/reshape | solution.py:660
  54.9 1.2 copy.40
  56.3 2.6 %collective-permute-done.1.refs_2_ = bf16[2,360,384]{2,1,0:T(8,128)(2,1)} collective-permute-done((bf16[2,360,384]{2,1,0:T(8,128)(2,1)}, bf16[2,360,384]{2,1,0:T(8,128)(2,1)}, u32[]{:S(2)}, u32[]{:S(2)}) %collective-permute-start.1) | collective-permute-done | bytes 552992 | tf_op jit(solution)/shard_map/ppermute | solution.py:289
  58.9 2.6 %collective-permute-done.refs_1_ = bf16[2,360,384]{2,1,0:T(8,128)(2,1)} collective-permute-done((bf16[2,360,384]{2,1,0:T(8,128)(2,1)}, bf16[2,360,384]{2,1,0:T(8,128)(2,1)}, u32[]{:S(2)}, u32[]{:S(2)}) %collective-permute-start) | collective-permute-done | bytes 552992 | tf_op jit(solution)/shard_map/ppermute | solution.py:289
  61.5 2.2 %collective-permute-done.12.right_ref = bf16[34,16,128]{2,1,0:T(8,128)(2,1)S(1)} collective-permute-done((bf16[34,16,128]{2,1,0:T(8,128)(2,1)}, bf16[34,16,128]{2,1,0:T(8,128)(2,1)S(1)}, u32[]{:S(2)}, u32[]{:S(2)}) %collective-permute-start.12) | collective-permute-done | bytes 139296 | tf_op jit(solution)/shard_map/ppermute | solution.py:416
  63.7 2.2 %reshape.125.refs_8_ = bf16[1440,384]{1,0:T(8,128)(2,1)} reshape(bf16[8,180,384]{2,1,0:T(8,128)(2,1)} %all-to-all-done) | data formatting | bytes 2211840 | tf_op jit(solution)/shard_map/reshape | solution.py:342
  71.0 14.4 %advance_latitude.3 = (bf16[1,360,384]{2,1,0:T(8,128)(2,1)S(1)}, bf16[1,360,384]{2,1,0:T(8,128)(2,1)S(1)}, bf16[1,360,384]{2,1,0:T(8,128)(2,1)S(1)}, bf16[1,360,...) custom-call(s32[3]{0:T(128)S(1)} %pad_add_fusion.place_ref, bf16[2,360,384]{2,1,0:T(8,128)(2,1)S(1)} %copy-done, ...), custom_call_target="tpu_custom_call" | custom-call | flops 16000000000 | bytes 8388608 | tf_op jit(solution)/shard_map/advance_latitude/pallas_call | solution.py:234
  88.2 14.4 %advance_latitude.2 = (bf16[1,360,384]{2,1,0:T(8,128)(2,1)S(1)}, bf16[1,360,384]{2,1,0:T(8,128)(2,1)S(1)}, bf16[1,360,384]{2,1,0:T(8,128)(2,1)S(1)}, bf16[1,360,...) custom-call(s32[3]{0:T(128)S(1)} %pad_add_fusion.place_ref, bf16[2,360,384]{2,1,0:T(8,128)(2,1)S(1)} %copy-done, ...), custom_call_target="tpu_custom_call" | custom-call | flops 16000000000 | bytes 8388608 | tf_op jit(solution)/shard_map/advance_latitude/pallas_call | solution.py:234
  105.5 4.0 %all-to-all-start.1 = ((bf16[32,32,128]{2,1,0:T(8,128)(2,1)}), bf16[32,32,128]{2,1,0:T(8,128)(2,1)S(1)}, u32[]{:S(2)}, u32[]{:S(2)}) async-start(bf16[32,32,128]{2,1,0:T(8,128)(2,1)} %bitcast.81), calls=%async_computation.1 | async-start | bytes 524288 | tf_op jit(solution)/shard_map/all_to_all | solution.py:86
  109.5 1.5 collective-permute-start.6
  111.7 1.2 collective-permute-start.7
  112.9 1.8 %collective-permute-start.8 = (bf16[1,360,384]{2,1,0:T(8,128)(2,1)}, bf16[1,360,384]{2,1,0:T(8,128)(2,1)}, u32[]{:S(2)}, u32[]{:S(2)}) collective-permute-start(bf16[1,360,384]{2,1,0:T(8,128)(2,1)} %copy-done.10), channel_id=1, source_target_pairs={{0,3},{1,0},{2,1},{3,2},{4,7},{5,4},{6,5},{7,6},{8,11},{9,8},{10,9... | collective-permute-start | bytes 829448 | tf_op jit(solution)/shard_map/ppermute | solution.py:289
  114.8 15.2 %all-to-all-done.1 = bf16[32,32,128]{2,1,0:T(8,128)(2,1)S(1)} async-done(((bf16[32,32,128]{2,1,0:T(8,128)(2,1)}), bf16[32,32,128]{2,1,0:T(8,128)(2,1)S(1)}, u32[]{:S(2)}, u32[]{:S(2)}) %all-to-all-start.1) | async-done | bytes 262176 | tf_op jit(solution)/shard_map/all_to_all | solution.py:86
  130.0 5.1 %collective-permute-start.14 = (bf16[1,360,384]{2,1,0:T(8,128)(2,1)}, bf16[1,360,384]{2,1,0:T(8,128)(2,1)}, u32[]{:S(2)}, u32[]{:S(2)}) collective-permute-start(bf16[1,360,384]{2,1,0:T(8,128)(2,1)} %copy-done.8), channel_id=1, source_target_pairs={{0,2},{1,3},{2,0},{3,1},{4,6},{5,7},{6,4},{7,5},{8,10},{9,11},{10,... | collective-permute-start | bytes 829448 | tf_op jit(solution)/shard_map/ppermute | solution.py:289
  136.7 6.1 %assemble.1 = (bf16[34,160,128]{2,1,0:T(8,128)(2,1)S(1)}, bf16[26,160,128]{2,1,0:T(8,128)(2,1)S(1)}, bf16[34,160,256]{2,1,0:T(8,128)(2,1)S(1)}) custom-call(s32[2]{0:T(128)S(1)} %pad_add_fusion.1.place_ref, bf16[16,128,128]{2,1,0:T(8,128)(2,1)S(1)} %get-tuple-element.70.mid0_ref, bf16[16,128,128]{2,1,0:T(8,128)(2,1)S(1)} %get-tuple-element.71.mid1_ref, ...), custom_call_target="tpu_custom_call" | custom-call | flops 1000000 | bytes 100000 | tf_op jit(solution)/shard_map/assemble/pallas_call | solution.py:481
  142.8 23.5 %denoise.1 = bf16[16,128,128]{2,1,0:T(8,128)(2,1)S(1)} custom-call(s32[2]{0:T(128)S(1)} %pad_add_fusion.1.place_ref, s32[8]{0:T(128)S(1)} %add_clamp_fusion.pick_ref, bf16[34,160,128]{2,1,0:T(8,128)(2,1)S(1)} %get-tuple-element.76.noisy_ref, bf16[26,160,128]{2,1,0:T(8,128)(2,1)S(1)} %get-tuple-element.77.noise_ref, ...), custom_call_target="tpu_custom_call" | custom-call | flops 1000000 | bytes 100000 | tf_op jit(solution)/shard_map/denoise/pallas_call | solution.py:637
  166.4 1.1 copy.38
  167.5 3.0 %collate.1 = bf16[8,360,384]{2,1,0:T(8,128)(2,1)} custom-call(s32[8]{0:T(128)} %stack.56.place_ref, bf16[1,360,384]{2,1,0:T(8,128)(2,1)} %copy-done.2, bf16[1,360,384]{2,1,0:T(8,128)(2,1)} %collective-permute-done.6.refs_1_, bf16[1,360,384]{2,1,0:T(8,128)(2,1)} %collective-permute-done.7.refs_2_, bf16[1,360,384]{2,1,0:T(8,128)(2,1)} %collective-permute-done.8.refs_3_, ...), custom_call_target="tpu_custom_call" | custom-call | tf_op jit(solution)/shard_map/collate/pallas_call | solution.py:276
  (113 shorter events, 21.7 us)
Async XLA Ops:
  2.5 14.2 %collective-permute-start.5 = (bf16[180,96]{0,1:T(8,128)(2,1)S(1)}, bf16[180,96]{0,1:T(8,128)(2,1)S(1)}, u32[]{:S(2)}, u32[]{:S(2)}) collective-permute-start(bf16[180,96]{0,1:T(8,128)(2,1)S(1)} %dynamic-slice_convert_fusion), channel_id=1, source_target_pairs={{0,1},{1,2},{2,3},{3,0},{4,5},{5,6},{6,7},{7,4},{8,9},{9,10},{10,1... | collective-permute-start | bytes 103688 | tf_op jit(solution)/shard_map/ppermute | solution.py:289
  4.1 12.5 %collective-permute-start.4 = (bf16[180,96]{0,1:T(8,128)(2,1)S(1)}, bf16[180,96]{0,1:T(8,128)(2,1)S(1)}, u32[]{:S(2)}, u32[]{:S(2)}) collective-permute-start(bf16[180,96]{0,1:T(8,128)(2,1)S(1)} %dynamic-slice_convert_fusion), channel_id=1, source_target_pairs={{0,2},{1,3},{2,0},{3,1},{4,6},{5,7},{6,4},{7,5},{8,10},{9,11},{10,... | collective-permute-start | bytes 103688 | tf_op jit(solution)/shard_map/ppermute | solution.py:289
  5.2 11.3 %collective-permute-start.3 = (bf16[180,96]{0,1:T(8,128)(2,1)S(1)}, bf16[180,96]{0,1:T(8,128)(2,1)S(1)}, u32[]{:S(2)}, u32[]{:S(2)}) collective-permute-start(bf16[180,96]{0,1:T(8,128)(2,1)S(1)} %dynamic-slice_convert_fusion), channel_id=1, source_target_pairs={{0,3},{1,0},{2,1},{3,2},{4,7},{5,4},{6,5},{7,6},{8,11},{9,8},{10,9... | collective-permute-start | bytes 103688 | tf_op jit(solution)/shard_map/ppermute | solution.py:289
  7.2 6.8 %copy-start.17 = (bf16[2,99,16,128]{3,2,1,0:T(8,128)(2,1)S(1)}, bf16[2,99,16,128]{3,2,1,0:T(8,128)(2,1)}, u32[]{:S(2)}) copy-start(bf16[2,99,16,128]{3,2,1,0:T(8,128)(2,1)} %param.26) | copy-start | bytes 2433028
  7.2 6.8 %copy-start.18 = (bf16[99,16,128]{2,1,0:T(8,128)(2,1)S(1)}, bf16[99,16,128]{2,1,0:T(8,128)(2,1)}, u32[]{:S(2)}) copy-start(bf16[99,16,128]{2,1,0:T(8,128)(2,1)} %param.25) | copy-start | bytes 1216516
  10.2 3.9 %copy-start.21 = (s32[16,128]{1,0:T(8,128)S(1)}, s32[16,128]{1,0:T(8,128)}, u32[]{:S(2)}) copy-start(s32[16,128]{1,0:T(8,128)} %param.34) | copy-start | bytes 24580
  10.2 4.0 %copy-start.22 = (s32[16,128]{1,0:T(8,128)S(1)}, s32[16,128]{1,0:T(8,128)}, u32[]{:S(2)}) copy-start(s32[16,128]{1,0:T(8,128)} %param.35) | copy-start | bytes 24580
  10.2 46.1 %collective-permute-start.2 = (bf16[2,360,384]{2,1,0:T(8,128)(2,1)}, bf16[2,360,384]{2,1,0:T(8,128)(2,1)}, u32[]{:S(2)}, u32[]{:S(2)}) collective-permute-start(bf16[2,360,384]{2,1,0:T(8,128)(2,1)} %get-tuple-element.98), channel_id=1, source_target_pairs={{0,1},{1,2},{2,3},{3,0},{4,5},{5,6},{6,7},{7,4},{8,9},{9,10},{10,1... | collective-permute-start | bytes 1658888 | tf_op jit(solution)/shard_map/ppermute | solution.py:289
  10.3 48.6 %collective-permute-start.1 = (bf16[2,360,384]{2,1,0:T(8,128)(2,1)}, bf16[2,360,384]{2,1,0:T(8,128)(2,1)}, u32[]{:S(2)}, u32[]{:S(2)}) collective-permute-start(bf16[2,360,384]{2,1,0:T(8,128)(2,1)} %get-tuple-element.99), channel_id=1, source_target_pairs={{0,2},{1,3},{2,0},{3,1},{4,6},{5,7},{6,4},{7,5},{8,10},{9,11},{10,... | collective-permute-start | bytes 1658888 | tf_op jit(solution)/shard_map/ppermute | solution.py:289
  16.5 44.9 %collective-permute-start = (bf16[2,360,384]{2,1,0:T(8,128)(2,1)}, bf16[2,360,384]{2,1,0:T(8,128)(2,1)}, u32[]{:S(2)}, u32[]{:S(2)}) collective-permute-start(bf16[2,360,384]{2,1,0:T(8,128)(2,1)} %get-tuple-element.100), channel_id=1, source_target_pairs={{0,3},{1,0},{2,1},{3,2},{4,7},{5,4},{6,5},{7,6},{8,11},{9,8},{10,9... | collective-permute-start | bytes 1658888 | tf_op jit(solution)/shard_map/ppermute | solution.py:289
  16.7 15.3 %collective-permute-start.9 = (bf16[14,128,128]{2,1,0:T(8,128)(2,1)}, bf16[14,128,128]{2,1,0:T(8,128)(2,1)S(1)}, u32[]{:S(2)}, u32[]{:S(2)}) collective-permute-start(bf16[14,128,128]{2,1,0:T(8,128)(2,1)} %get-tuple-element.54), channel_id=1, source_target_pairs={{0,4},{4,8},{8,12},{12,16},{16,20},{20,24},{24,28},{1,5},{5,9},{9,... | collective-permute-start | bytes 1376264 | tf_op jit(solution)/shard_map/ppermute | solution.py:416
  20.3 22.8 %collective-permute-start.10 = (bf16[14,128,128]{2,1,0:T(8,128)(2,1)}, bf16[14,128,128]{2,1,0:T(8,128)(2,1)S(1)}, u32[]{:S(2)}, u32[]{:S(2)}) collective-permute-start(bf16[14,128,128]{2,1,0:T(8,128)(2,1)} %get-tuple-element.55), channel_id=1, source_target_pairs={{4,0},{8,4},{12,8},{16,12},{20,16},{24,20},{28,24},{5,1},{9,5},{13... | collective-permute-start | bytes 1376264 | tf_op jit(solution)/shard_map/ppermute | solution.py:416
  27.2 36.5 %all-to-all-start = ((bf16[8,180,384]{2,1,0:T(8,128)(2,1)}), bf16[8,180,384]{2,1,0:T(8,128)(2,1)}, u32[]{:S(2)}, u32[]{:S(2)}) async-start(bf16[8,180,384]{2,1,0:T(8,128)(2,1)} %broadcast_in_dim.14), calls=%async_computation | async-start | bytes 2260992 | tf_op jit(solution)/shard_map/all_to_all | solution.py:86
  32.0 18.6 %copy-start.15 = (bf16[128,3,3,128]{0,2,3,1:T(4,128)(2,1)S(1)}, bf16[128,3,3,128]{0,2,3,1:T(4,128)(2,1)}, u32[]{:S(2)}) copy-start(bf16[128,3,3,128]{0,2,3,1:T(4,128)(2,1)} %pad.23) | copy-start | bytes 884740
  32.0 18.6 %copy-start.16 = (bf16[128,3,3,128]{0,2,3,1:T(4,128)(2,1)S(1)}, bf16[128,3,3,128]{0,2,3,1:T(4,128)(2,1)}, u32[]{:S(2)}) copy-start(bf16[128,3,3,128]{0,2,3,1:T(4,128)(2,1)} %pad.24) | copy-start | bytes 884740
  43.1 8.3 %copy-start.19 = (bf16[128,128]{1,0:T(8,128)(2,1)S(1)}, bf16[128,128]{1,0:T(8,128)(2,1)}, u32[]{:S(2)}) copy-start(bf16[128,128]{1,0:T(8,128)(2,1)} %param.30) | copy-start | bytes 98308
  43.2 9.4 %copy-start.20 = (bf16[384,26]{0,1:T(8,128)(2,1)S(1)}, bf16[384,26]{0,1:T(8,128)(2,1)}, u32[]{:S(2)}) copy-start(bf16[384,26]{0,1:T(8,128)(2,1)} %param.24) | copy-start | bytes 59908
  43.9 19.8 %collective-permute-start.12 = (bf16[34,16,128]{2,1,0:T(8,128)(2,1)}, bf16[34,16,128]{2,1,0:T(8,128)(2,1)S(1)}, u32[]{:S(2)}, u32[]{:S(2)}) collective-permute-start(bf16[34,16,128]{2,1,0:T(8,128)(2,1)} %pad_maximum_fusion.3), channel_id=1, source_target_pairs={{1,0},{2,1},{3,2},{5,4},{6,5},{7,6},{9,8},{10,9},{11,10},{13,12},{... | collective-permute-start | bytes 417800 | tf_op jit(solution)/shard_map/ppermute | solution.py:416
  48.0 15.7 %collective-permute-start.11 = (bf16[34,16,128]{2,1,0:T(8,128)(2,1)}, bf16[34,16,128]{2,1,0:T(8,128)(2,1)}, u32[]{:S(2)}, u32[]{:S(2)}) collective-permute-start(bf16[34,16,128]{2,1,0:T(8,128)(2,1)} %pad_maximum_fusion.2), channel_id=1, source_target_pairs={{0,1},{1,2},{2,3},{4,5},{5,6},{6,7},{8,9},{9,10},{10,11},{12,13},{... | collective-permute-start | bytes 417800 | tf_op jit(solution)/shard_map/ppermute | solution.py:416
  63.7 21.7 %copy-start.3 = (bf16[34,16,128]{2,1,0:T(8,128)(2,1)}, bf16[34,16,128]{2,1,0:T(8,128)(2,1)S(1)}, u32[]{:S(2)}) copy-start(bf16[34,16,128]{2,1,0:T(8,128)(2,1)S(1)} %collective-permute-done.12.right_ref) | copy-start | bytes 417796
  65.9 1.1 copy-start
  66.9 1.0 copy-start.5
  68.9 1.1 copy-start.13
  69.9 1.1 copy-start.14
  104.0 1.5 copy-start.11
  105.5 24.5 %all-to-all-start.1 = ((bf16[32,32,128]{2,1,0:T(8,128)(2,1)}), bf16[32,32,128]{2,1,0:T(8,128)(2,1)S(1)}, u32[]{:S(2)}, u32[]{:S(2)}) async-start(bf16[32,32,128]{2,1,0:T(8,128)(2,1)} %bitcast.81), calls=%async_computation.1 | async-start | bytes 524288 | tf_op jit(solution)/shard_map/all_to_all | solution.py:86
  109.5 25.5 %collective-permute-start.6 = (bf16[1,360,384]{2,1,0:T(8,128)(2,1)}, bf16[1,360,384]{2,1,0:T(8,128)(2,1)}, u32[]{:S(2)}, u32[]{:S(2)}) collective-permute-start(bf16[1,360,384]{2,1,0:T(8,128)(2,1)} %copy-done.12), channel_id=1, source_target_pairs={{0,1},{1,2},{2,3},{3,0},{4,5},{5,6},{6,7},{7,4},{8,9},{9,10},{10,1... | collective-permute-start | bytes 829448 | tf_op jit(solution)/shard_map/ppermute | solution.py:289
  111.7 54.6 %collective-permute-start.7 = (bf16[1,360,384]{2,1,0:T(8,128)(2,1)}, bf16[1,360,384]{2,1,0:T(8,128)(2,1)}, u32[]{:S(2)}, u32[]{:S(2)}) collective-permute-start(bf16[1,360,384]{2,1,0:T(8,128)(2,1)} %copy-done.11), channel_id=1, source_target_pairs={{0,2},{1,3},{2,0},{3,1},{4,6},{5,7},{6,4},{7,5},{8,10},{9,11},{10,... | collective-permute-start | bytes 829448 | tf_op jit(solution)/shard_map/ppermute | solution.py:289
  112.9 53.4 %collective-permute-start.8 = (bf16[1,360,384]{2,1,0:T(8,128)(2,1)}, bf16[1,360,384]{2,1,0:T(8,128)(2,1)}, u32[]{:S(2)}, u32[]{:S(2)}) collective-permute-start(bf16[1,360,384]{2,1,0:T(8,128)(2,1)} %copy-done.10), channel_id=1, source_target_pairs={{0,3},{1,0},{2,1},{3,2},{4,7},{5,4},{6,5},{7,6},{8,11},{9,8},{10,9... | collective-permute-start | bytes 829448 | tf_op jit(solution)/shard_map/ppermute | solution.py:289
  130.0 36.4 %collective-permute-start.13 = (bf16[1,360,384]{2,1,0:T(8,128)(2,1)}, bf16[1,360,384]{2,1,0:T(8,128)(2,1)}, u32[]{:S(2)}, u32[]{:S(2)}) collective-permute-start(bf16[1,360,384]{2,1,0:T(8,128)(2,1)} %copy-done.9), channel_id=1, source_target_pairs={{0,1},{1,2},{2,3},{3,0},{4,5},{5,6},{6,7},{7,4},{8,9},{9,10},{10,1... | collective-permute-start | bytes 829448 | tf_op jit(solution)/shard_map/ppermute | solution.py:289
  130.0 36.4 %collective-permute-start.14 = (bf16[1,360,384]{2,1,0:T(8,128)(2,1)}, bf16[1,360,384]{2,1,0:T(8,128)(2,1)}, u32[]{:S(2)}, u32[]{:S(2)}) collective-permute-start(bf16[1,360,384]{2,1,0:T(8,128)(2,1)} %copy-done.8), channel_id=1, source_target_pairs={{0,2},{1,3},{2,0},{3,1},{4,6},{5,7},{6,4},{7,5},{8,10},{9,11},{10,... | collective-permute-start | bytes 829448 | tf_op jit(solution)/shard_map/ppermute | solution.py:289
  135.1 31.3 %collective-permute-start.15 = (bf16[1,360,384]{2,1,0:T(8,128)(2,1)}, bf16[1,360,384]{2,1,0:T(8,128)(2,1)}, u32[]{:S(2)}, u32[]{:S(2)}) collective-permute-start(bf16[1,360,384]{2,1,0:T(8,128)(2,1)} %copy-done.7), channel_id=1, source_target_pairs={{0,3},{1,0},{2,1},{3,2},{4,7},{5,4},{6,5},{7,6},{8,11},{9,8},{10,9... | collective-permute-start | bytes 829448 | tf_op jit(solution)/shard_map/ppermute | solution.py:289
  (9 other events, 6.8 us)

commit v6 on v5

--- a/solution.py
+++ b/solution.py
@@ -16,6 +16,7 @@
 RIM = 9
 RIM_USED = 4
 LANES = 128
+VMEM = 60 * 2**20
 PACKED = 32
 MODE_TILE = 64
 STRIP = 8
@@ -247,7 +248,7 @@
             pltpu.VMEM((span, LANES), jnp.float32),
             pltpu.VMEM((1, hours * span // group, LANES), jnp.float32),
         ],
-        compiler_params=pltpu.CompilerParams(vmem_limit_bytes=48 * 2**20),
+        compiler_params=pltpu.CompilerParams(vmem_limit_bytes=VMEM),
         cost_estimate=pl.CostEstimate(
             flops=16 * 10**9, bytes_accessed=8 * 2**20, transcendentals=hours * 4 * piece * channels
         ),
@@ -343,17 +344,18 @@
     prepared = prepare(wide)
     start = (box_lon0[0] - window_base() - me * piece) % (piece * count)
     place = jnp.stack([start // piece, (start // piece + 1) % count, start % piece]).astype(jnp.int32)
+    received, prepared = lax.optimization_barrier((received, prepared))
     outcome, strips = [], []
     for turn in range(turns):
-        if turn == turns - 1:
-            received, prepared = lax.optimization_barrier((received, prepared))
         blocks, strip = advance_latitude(
             hours, turn, cols_here // RATIO, place, received, tables, gains, w_skip, w_mix, w_decode
         )
+        if turn < turns - 1:
+            blocks = [shift(block, "col", step) if step else block for step, block in enumerate(blocks)]
         outcome.append(blocks)
         strips.append(strip)
     plane = lax.axis_size(PLANE)
-    strips = jnp.concatenate(strips, axis=1)
+    strips, outcome[:-1] = lax.optimization_barrier((jnp.concatenate(strips, axis=1), outcome[:-1]))
     sent = jnp.broadcast_to(strips[None], (plane,) + strips.shape)
     got = exchange(sent.reshape((plane * count,) + strips.shape[1:]), PLANE + ("col",))
     outcome[-1], got = lax.optimization_barrier((outcome[-1], got))
@@ -361,11 +363,10 @@
     lat = box_lat0[0] - window_base() + lax.axis_index(PLANE) * (rows_here // RATIO)
     lat = jnp.clip(lat + jnp.arange(window_extent(rows_here), dtype=jnp.int32), 0, plane * lats_here - 1)
     places = [owner + turn for turn in range(turns) for owner in owners]
-    finals = [
-        shift(block, "col", step) if step else block
-        for blocks in outcome
-        for step, block in enumerate(blocks)
+    outcome[-1] = [
+        shift(block, "col", step) if step else block for step, block in enumerate(outcome[-1])
     ]
+    finals = sum(outcome, [])
 
     def finish(after):
         blocks, after = lax.optimization_barrier((finals, after))
@@ -489,7 +490,7 @@
         ),
         in_specs=[pl.BlockSpec(memory_space=pltpu.SMEM)]
         + [pl.BlockSpec(memory_space=pltpu.VMEM)] * 6,
-        compiler_params=pltpu.CompilerParams(vmem_limit_bytes=40 * 2**20),
+        compiler_params=pltpu.CompilerParams(vmem_limit_bytes=VMEM),
         cost_estimate=pl.CostEstimate(flops=10**6, bytes_accessed=10**5, transcendentals=0),
         name="assemble",
     )(place, mid0, mid1, above, below, left, right)
@@ -649,7 +650,7 @@
             pltpu.VMEM((2, width, channels), f32),
             pltpu.VMEM((2, blend.shape[2], channels), bf16),
         ],
-        compiler_params=pltpu.CompilerParams(vmem_limit_bytes=40 * 2**20),
+        compiler_params=pltpu.CompilerParams(vmem_limit_bytes=VMEM),
         cost_estimate=pl.CostEstimate(flops=10**6, bytes_accessed=10**5, transcendentals=0),
         name="denoise",
     )(place, pick, noisy, noise, blend, strips, *weights)
@@ -746,17 +747,17 @@
             w_bridge.T,
             conv_weight(w_last, w_last.shape[2], LANES),
         )
-        return (mid0, mid1, above, below, left, right), weights
+        parts = (mid0, mid1, above, below, left, right)
+        return assemble(rows_here, cols_here, totals, high, lanes, place, *parts), weights
 
     by_latitude = lax.axis_size("col") == 4 and global_state.shape[0] % 4 == 0
     global_steps = global_by_latitude if by_latitude else global_by_channel
-    finish, strips, pick, (parts, weights) = global_steps(
+    finish, strips, pick, (fields, weights) = global_steps(
         hours, global_state, spec_filter, w_skip, w_mix, w_decode, box_lat0, box_lon0,
         rows_here, cols_here, prepare,
     )
-    noisy, noise, blend = assemble(rows_here, cols_here, totals, high, lanes, place, *parts)
     regional_final = denoise(
-        rows_here, cols_here, totals, variables, conds, place, pick, noisy, noise, blend, strips, weights
+        rows_here, cols_here, totals, variables, conds, place, pick, *fields, strips, weights
     )
     regional_final = jnp.transpose(regional_final[:, :, :variables], (2, 0, 1))
     return finish(regional_final)

time: 174 us -> 171 us (0.983)
  local copies, waits for them, and re-layouts: 32.4 us -> 18.3 us
  Pallas kernels: 61.3 us -> 70.3 us
  other arithmetic: 2.93 us -> 5.32 us
  waiting for transfers between devices: 33.6 us -> 35.7 us
  starting transfers between devices: 37.7 us -> 35.7 us
    unnamed x61 -> x59, local copies, waits for them, and re-layouts: 16.2 us -> 5.59 us
    all_to_all x2, waiting for transfers between devices: 15.2 us -> 8.88 us  [exchange(): return lax.all_to_all(blocks, axis, split_axis=0, concat_axis=0, tiled=True)]
    ppermute x2, waiting for transfers between devices: 13.2 us -> 17.8 us  [next_to(): lax.ppermute(high, axis, backward)]
    ppermute x12, starting transfers between devices: 18.1 us -> 14.5 us  [shift(): lax.ppermute(block, axis, [(source, (source + step) % count) for source i...]
    reshape x3, local copies, waits for them, and re-layouts: 4.62 us -> 1.2 us  [conv_weight(): weight = weight.reshape(out, 3, 3, given)]
    pallas_call x1, Pallas kernels: 23.5 us -> 26.7 us  [denoise(): pl.pallas_call(functools.partial(denoise_kernel, rows, cols, totals, vari...]
    pallas_call x2, Pallas kernels: 28.8 us -> 31.7 us  [advance_latitude(): pl.pallas_call(functools.partial(latitude_kernel, hours, 1, step), grid=(...]
    ppermute x2, waiting for transfers between devices: 0.01 us -> 2.85 us  [next_to(): lax.ppermute(low, axis, forward)]
  transfers between devices with their start and end apart: 18 -> 18, of which waited for: 5 -> 6; matrix products, arithmetic and copies ran while one was open for 11% -> 11% of each run, Pallas kernels for 17% -> 31%
where the time goes in v6:
time: 171 us; the launch traced here: 168 us
  Pallas kernels  70.3 us (41%)
  starting transfers between devices  35.7 us (21%)
  waiting for transfers between devices  35.7 us (21%)
  local copies, waits for them, and re-layouts  18.3 us (11%)
  other arithmetic  5.32 us (3%)
  between operations  2.71 us (2%)
    pallas_call x2, Pallas kernels, advance_latitude(): pl.pallas_call(functools.partial(latitude_kernel, hours, 1, step), grid=(...  31.7 us
    pallas_call x1, Pallas kernels, denoise(): pl.pallas_call(functools.partial(denoise_kernel, rows, cols, totals, vari...  26.7 us
    ppermute x2, waiting for transfers between devices, next_to(): lax.ppermute(high, axis, backward)  17.8 us
    ppermute x12, starting transfers between devices, shift(): lax.ppermute(block, axis, [(source, (source + step) % count) for source i...  14.5 us
    all_to_all x2, starting transfers between devices, exchange(): return lax.all_to_all(blocks, axis, split_axis=0, concat_axis=0, tiled=True)  10.7 us
    pallas_call x1, Pallas kernels, assemble(): pl.pallas_call(functools.partial(assemble_kernel, rows, cols, totals, hig...  8.92 us
    all_to_all x2, waiting for transfers between devices, exchange(): return lax.all_to_all(blocks, axis, split_axis=0, concat_axis=0, tiled=True)  8.88 us
    ppermute x12, waiting for transfers between devices, shift(): lax.ppermute(block, axis, [(source, (source + step) % count) for source i...  6.18 us
  transfers between devices with their start and end apart: 18, of which 6 were waited for; matrix products, arithmetic and copies ran while one was open for 11% of the time, Pallas kernels for 31%

profile of v6, /device:TPU:8, one launch (start us, length us, event | category | flops | bytes accessed | tf_op | source)
XLA Modules:
  0.0 168.0 jit_solution(15523186882565806474)
XLA Ops:
  0.6 1.5 copy.29
  2.5 1.6 collective-permute-start.5
  4.1 1.1 collective-permute-start.4
  5.2 1.9 %collective-permute-start.3 = (bf16[180,96]{0,1:T(8,128)(2,1)S(1)}, bf16[180,96]{0,1:T(8,128)(2,1)S(1)}, u32[]{:S(2)}, u32[]{:S(2)}) collective-permute-start(bf16[180,96]{0,1:T(8,128)(2,1)S(1)} %dynamic-slice_convert_fusion), channel_id=1, source_target_pairs={{0,3},{1,0},{2,1},{3,2},{4,7},{5,4},{6,5},{7,6},{8,11},{9,8},{10,9... | collective-permute-start | bytes 103688 | tf_op jit(solution)/shard_map/ppermute | solution.py:290
  7.2 3.1 %constant_dynamic-slice_fusion.1 = (bf16[2,360,384]{2,1,0:T(8,128)(2,1)}, bf16[2,360,384]{2,1,0:T(8,128)(2,1)}, bf16[2,360,384]{2,1,0:T(8,128)(2,1)}, bf16[2,360,384]{2,1,0:T(8,128)(2,1)}) fusion(bf16[8,360,384]{2,1,0:T(8,128)(2,1)} %param.20, s32[]{:T(128)S(6)} %select_n.90, s32[]{:T(128)S(6)} %select_n.89, s32[]{:T(128)S(6)} %select_n.88, s32[]{:T(128)S(6)} %select_n.87), kind=kLoop, calls=%fused_computation.49 | loop fusion | bytes 4423696 | tf_op jit(solution)/shard_map/dynamic_slice | solution.py:340
  10.4 3.6 %collective-permute-start.1 = (bf16[2,360,384]{2,1,0:T(8,128)(2,1)}, bf16[2,360,384]{2,1,0:T(8,128)(2,1)}, u32[]{:S(2)}, u32[]{:S(2)}) collective-permute-start(bf16[2,360,384]{2,1,0:T(8,128)(2,1)} %get-tuple-element.103), channel_id=1, source_target_pairs={{0,2},{1,3},{2,0},{3,1},{4,6},{5,7},{6,4},{7,5},{8,10},{9,11},{10,... | collective-permute-start | bytes 1658888 | tf_op jit(solution)/shard_map/ppermute | solution.py:290
  14.4 1.0 copy.30
  15.7 1.0 pad_maximum_fusion
  18.0 3.4 %collective-permute-start.6 = (bf16[14,128,128]{2,1,0:T(8,128)(2,1)}, bf16[14,128,128]{2,1,0:T(8,128)(2,1)S(1)}, u32[]{:S(2)}, u32[]{:S(2)}) collective-permute-start(bf16[14,128,128]{2,1,0:T(8,128)(2,1)} %get-tuple-element.52), channel_id=1, source_target_pairs={{0,4},{4,8},{8,12},{12,16},{16,20},{20,24},{24,28},{1,5},{5,9},{9,... | collective-permute-start | bytes 1376264 | tf_op jit(solution)/shard_map/ppermute | solution.py:417
  22.4 1.3 collective-permute-start.7
  23.9 1.1 broadcast_in_dim.34
  25.0 4.8 %all-to-all-start = ((bf16[8,180,384]{2,1,0:T(8,128)(2,1)}), bf16[8,180,384]{2,1,0:T(8,128)(2,1)S(1)}, u32[]{:S(2)}, u32[]{:S(2)}) async-start(bf16[8,180,384]{2,1,0:T(8,128)(2,1)} %broadcast_in_dim.34), calls=%async_computation | async-start | bytes 2260992 | tf_op jit(solution)/shard_map/all_to_all | solution.py:87
  29.9 2.8 %collective-permute-done.6.above_ref = bf16[14,128,128]{2,1,0:T(8,128)(2,1)S(1)} collective-permute-done((bf16[14,128,128]{2,1,0:T(8,128)(2,1)}, bf16[14,128,128]{2,1,0:T(8,128)(2,1)S(1)}, u32[]{:S(2)}, u32[]{:S(2)}) %collective-permute-start.6) | collective-permute-done | bytes 458784 | tf_op jit(solution)/shard_map/ppermute | solution.py:417
  32.8 11.6 %collective-permute-done.7.below_ref = bf16[14,128,128]{2,1,0:T(8,128)(2,1)S(1)} collective-permute-done((bf16[14,128,128]{2,1,0:T(8,128)(2,1)}, bf16[14,128,128]{2,1,0:T(8,128)(2,1)S(1)}, u32[]{:S(2)}, u32[]{:S(2)}) %collective-permute-start.7) | collective-permute-done | bytes 458784 | tf_op jit(solution)/shard_map/ppermute | solution.py:417
  45.2 3.3 %collective-permute-start.9 = (bf16[34,16,128]{2,1,0:T(8,128)(2,1)}, bf16[34,16,128]{2,1,0:T(8,128)(2,1)}, u32[]{:S(2)}, u32[]{:S(2)}) collective-permute-start(bf16[34,16,128]{2,1,0:T(8,128)(2,1)} %pad_maximum_fusion.3), channel_id=1, source_target_pairs={{1,0},{2,1},{3,2},{5,4},{6,5},{7,6},{9,8},{10,9},{11,10},{13,12},{... | collective-permute-start | bytes 417800 | tf_op jit(solution)/shard_map/ppermute | solution.py:417
  49.3 2.5 %collective-permute-start.8 = (bf16[34,16,128]{2,1,0:T(8,128)(2,1)}, bf16[34,16,128]{2,1,0:T(8,128)(2,1)}, u32[]{:S(2)}, u32[]{:S(2)}) collective-permute-start(bf16[34,16,128]{2,1,0:T(8,128)(2,1)} %pad_maximum_fusion.2), channel_id=1, source_target_pairs={{0,1},{1,2},{2,3},{4,5},{5,6},{6,7},{8,9},{9,10},{10,11},{12,13},{... | collective-permute-start | bytes 417800 | tf_op jit(solution)/shard_map/ppermute | solution.py:417
  57.7 6.2 %collective-permute-done.9.right_ref = bf16[34,16,128]{2,1,0:T(8,128)(2,1)} collective-permute-done((bf16[34,16,128]{2,1,0:T(8,128)(2,1)}, bf16[34,16,128]{2,1,0:T(8,128)(2,1)}, u32[]{:S(2)}, u32[]{:S(2)}) %collective-permute-start.9) | collective-permute-done | bytes 139296 | tf_op jit(solution)/shard_map/ppermute | solution.py:417
  63.8 8.9 %assemble.1 = (bf16[34,160,128]{2,1,0:T(8,128)(2,1)}, bf16[26,160,128]{2,1,0:T(8,128)(2,1)}, bf16[34,160,256]{2,1,0:T(8,128)(2,1)}) custom-call(s32[2]{0:T(128)} %pad_add_fusion.1.place_ref, bf16[16,128,128]{2,1,0:T(8,128)(2,1)} %copy-done, bf16[16,128,128]{2,1,0:T(8,128)(2,1)} %copy-done.1, bf16[14,128,128]{2,1,0:T(8,128)(2,1)} %copy-done.4, ...), custom_call_target="tpu_custom_call" | custom-call | flops 1000000 | bytes 100000 | tf_op jit(solution)/shard_map/assemble/pallas_call | solution.py:482
  72.8 1.1 reshape.132.refs_8_
  73.9 15.9 %advance_latitude.2 = (bf16[1,360,384]{2,1,0:T(8,128)(2,1)}, bf16[1,360,384]{2,1,0:T(8,128)(2,1)}, bf16[1,360,384]{2,1,0:T(8,128)(2,1)}, bf16[1,360,384]{2,1,0:T(8,128)(2,1)}, bf16[4,16,128]{2,1,0:T(8,128)(2,1)}) custom-call(s32[3]{0:T(128)} %pad_add_fusion.place_ref, bf16[2,360,384]{2,1,0:T(8,128)(2,1)} %get-tuple-element.57.refs_0_, ...), custom_call_target="tpu_custom_call" | custom-call | flops 16000000000 | bytes 8388608 | tf_op jit(solution)/shard_map/advance_latitude/pallas_call | solution.py:235
  89.9 1.9 %collective-permute-start.12 = (bf16[1,360,384]{2,1,0:T(8,128)(2,1)}, bf16[1,360,384]{2,1,0:T(8,128)(2,1)S(1)}, u32[]{:S(2)}, u32[]{:S(2)}) collective-permute-start(bf16[1,360,384]{2,1,0:T(8,128)(2,1)} %get-tuple-element.66), channel_id=1, source_target_pairs={{0,3},{1,0},{2,1},{3,2},{4,7},{5,4},{6,5},{7,6},{8,11},{9,8},{10,9... | collective-permute-start | bytes 829448 | tf_op jit(solution)/shard_map/ppermute | solution.py:290
  91.8 15.9 %advance_latitude.3 = (bf16[1,360,384]{2,1,0:T(8,128)(2,1)}, bf16[1,360,384]{2,1,0:T(8,128)(2,1)}, bf16[1,360,384]{2,1,0:T(8,128)(2,1)}, bf16[1,360,384]{2,1,0:T(8,128)(2,1)}, bf16[4,16,128]{2,1,0:T(8,128)(2,1)}) custom-call(s32[3]{0:T(128)} %pad_add_fusion.place_ref, bf16[2,360,384]{2,1,0:T(8,128)(2,1)} %get-tuple-element.57.refs_0_, ...), custom_call_target="tpu_custom_call" | custom-call | flops 16000000000 | bytes 8388608 | tf_op jit(solution)/shard_map/advance_latitude/pallas_call | solution.py:235
  108.4 5.2 %collective-permute-done.11.refs_2_ = bf16[1,360,384]{2,1,0:T(8,128)(2,1)S(1)} collective-permute-done((bf16[1,360,384]{2,1,0:T(8,128)(2,1)}, bf16[1,360,384]{2,1,0:T(8,128)(2,1)S(1)}, u32[]{:S(2)}, u32[]{:S(2)}) %collective-permute-start.11) | collective-permute-done | bytes 276512 | tf_op jit(solution)/shard_map/ppermute | solution.py:290
  113.6 0.9 collective-permute-done.12.refs_3_
  115.4 5.8 %all-to-all-start.1 = ((bf16[32,32,128]{2,1,0:T(8,128)(2,1)}), bf16[32,32,128]{2,1,0:T(8,128)(2,1)S(1)}, u32[]{:S(2)}, u32[]{:S(2)}) async-start(bf16[32,32,128]{2,1,0:T(8,128)(2,1)} %bitcast.34), calls=%async_computation.1 | async-start | bytes 524288 | tf_op jit(solution)/shard_map/all_to_all | solution.py:87
  121.8 8.9 %all-to-all-done.1 = bf16[32,32,128]{2,1,0:T(8,128)(2,1)S(1)} async-done(((bf16[32,32,128]{2,1,0:T(8,128)(2,1)}), bf16[32,32,128]{2,1,0:T(8,128)(2,1)S(1)}, u32[]{:S(2)}, u32[]{:S(2)}) %all-to-all-start.1) | async-done | bytes 262176 | tf_op jit(solution)/shard_map/all_to_all | solution.py:87
  130.7 1.0 collective-permute-start.13
  131.7 3.0 %collective-permute-start.14 = (bf16[1,360,384]{2,1,0:T(8,128)(2,1)}, bf16[1,360,384]{2,1,0:T(8,128)(2,1)S(1)}, u32[]{:S(2)}, u32[]{:S(2)}) collective-permute-start(bf16[1,360,384]{2,1,0:T(8,128)(2,1)} %get-tuple-element.78), channel_id=1, source_target_pairs={{0,2},{1,3},{2,0},{3,1},{4,6},{5,7},{6,4},{7,5},{8,10},{9,11},{10,... | collective-permute-start | bytes 829448 | tf_op jit(solution)/shard_map/ppermute | solution.py:290
  135.9 26.7 %denoise.1 = bf16[16,128,128]{2,1,0:T(8,128)(2,1)} custom-call(s32[2]{0:T(128)} %pad_add_fusion.1.place_ref, s32[8]{0:T(128)} %add_clamp_fusion.pick_ref, bf16[34,160,128]{2,1,0:T(8,128)(2,1)} %get-tuple-element.80.noisy_ref, bf16[26,160,128]{2,1,0:T(8,128)(2,1)} %get-tuple-element.81.noise_ref, bf16[34,160,256]{2,1,0:T(8,128)(2,1)} %get-tuple-element.82.blend_ref, ...), custom_call_target="tpu_custom_call" | custom-call | flops 1000000 | bytes 100000 | tf_op jit(solution)/shard_map/denoise/pallas_call | solution.py:638
  162.6 1.1 slice_bitcast_fusion
  163.7 1.1 copy.38
  164.9 3.0 %collate.1 = bf16[8,360,384]{2,1,0:T(8,128)(2,1)} custom-call(s32[8]{0:T(128)} %stack.56.place_ref, bf16[1,360,384]{2,1,0:T(8,128)(2,1)} %get-tuple-element.89.refs_0_, bf16[1,360,384]{2,1,0:T(8,128)(2,1)} %copy-done.9, bf16[1,360,384]{2,1,0:T(8,128)(2,1)} %copy-done.10, bf16[1,360,384]{2,1,0:T(8,128)(2,1)} %copy-done.11, ...), custom_call_target="tpu_custom_call" | custom-call | tf_op jit(solution)/shard_map/collate/pallas_call | solution.py:277
  (111 shorter events, 12.8 us)
Async XLA Ops:
  2.5 15.5 %collective-permute-start.5 = (bf16[180,96]{0,1:T(8,128)(2,1)S(1)}, bf16[180,96]{0,1:T(8,128)(2,1)S(1)}, u32[]{:S(2)}, u32[]{:S(2)}) collective-permute-start(bf16[180,96]{0,1:T(8,128)(2,1)S(1)} %dynamic-slice_convert_fusion), channel_id=1, source_target_pairs={{0,1},{1,2},{2,3},{3,0},{4,5},{5,6},{6,7},{7,4},{8,9},{9,10},{10,1... | collective-permute-start | bytes 103688 | tf_op jit(solution)/shard_map/ppermute | solution.py:290
  4.1 13.8 %collective-permute-start.4 = (bf16[180,96]{0,1:T(8,128)(2,1)S(1)}, bf16[180,96]{0,1:T(8,128)(2,1)S(1)}, u32[]{:S(2)}, u32[]{:S(2)}) collective-permute-start(bf16[180,96]{0,1:T(8,128)(2,1)S(1)} %dynamic-slice_convert_fusion), channel_id=1, source_target_pairs={{0,2},{1,3},{2,0},{3,1},{4,6},{5,7},{6,4},{7,5},{8,10},{9,11},{10,... | collective-permute-start | bytes 103688 | tf_op jit(solution)/shard_map/ppermute | solution.py:290
  5.2 12.6 %collective-permute-start.3 = (bf16[180,96]{0,1:T(8,128)(2,1)S(1)}, bf16[180,96]{0,1:T(8,128)(2,1)S(1)}, u32[]{:S(2)}, u32[]{:S(2)}) collective-permute-start(bf16[180,96]{0,1:T(8,128)(2,1)S(1)} %dynamic-slice_convert_fusion), channel_id=1, source_target_pairs={{0,3},{1,0},{2,1},{3,2},{4,7},{5,4},{6,5},{7,6},{8,11},{9,8},{10,9... | collective-permute-start | bytes 103688 | tf_op jit(solution)/shard_map/ppermute | solution.py:290
  7.2 6.9 %copy-start.3 = (bf16[2,99,16,128]{3,2,1,0:T(8,128)(2,1)S(1)}, bf16[2,99,16,128]{3,2,1,0:T(8,128)(2,1)}, u32[]{:S(2)}) copy-start(bf16[2,99,16,128]{3,2,1,0:T(8,128)(2,1)} %param.26) | copy-start | bytes 2433028
  7.2 6.9 %copy-start.7 = (bf16[99,16,128]{2,1,0:T(8,128)(2,1)S(1)}, bf16[99,16,128]{2,1,0:T(8,128)(2,1)}, u32[]{:S(2)}) copy-start(bf16[99,16,128]{2,1,0:T(8,128)(2,1)} %param.25) | copy-start | bytes 1216516
  10.3 62.5 %collective-permute-start.2 = (bf16[2,360,384]{2,1,0:T(8,128)(2,1)}, bf16[2,360,384]{2,1,0:T(8,128)(2,1)}, u32[]{:S(2)}, u32[]{:S(2)}) collective-permute-start(bf16[2,360,384]{2,1,0:T(8,128)(2,1)} %get-tuple-element.102), channel_id=1, source_target_pairs={{0,1},{1,2},{2,3},{3,0},{4,5},{5,6},{6,7},{7,4},{8,9},{9,10},{10,1... | collective-permute-start | bytes 1658888 | tf_op jit(solution)/shard_map/ppermute | solution.py:290
  10.4 62.4 %collective-permute-start.1 = (bf16[2,360,384]{2,1,0:T(8,128)(2,1)}, bf16[2,360,384]{2,1,0:T(8,128)(2,1)}, u32[]{:S(2)}, u32[]{:S(2)}) collective-permute-start(bf16[2,360,384]{2,1,0:T(8,128)(2,1)} %get-tuple-element.103), channel_id=1, source_target_pairs={{0,2},{1,3},{2,0},{3,1},{4,6},{5,7},{6,4},{7,5},{8,10},{9,11},{10,... | collective-permute-start | bytes 1658888 | tf_op jit(solution)/shard_map/ppermute | solution.py:290
  15.6 6.8 %copy-start = (bf16[16,128,128]{2,1,0:T(8,128)(2,1)}, bf16[16,128,128]{2,1,0:T(8,128)(2,1)S(1)}, u32[]{:S(2)}) copy-start(bf16[16,128,128]{2,1,0:T(8,128)(2,1)S(1)} %get-tuple-element.111.mid0_ref) | copy-start | bytes 1572868
  15.6 8.1 %copy-start.1 = (bf16[16,128,128]{2,1,0:T(8,128)(2,1)}, bf16[16,128,128]{2,1,0:T(8,128)(2,1)S(1)}, u32[]{:S(2)}) copy-start(bf16[16,128,128]{2,1,0:T(8,128)(2,1)S(1)} %get-tuple-element.110.mid1_ref) | copy-start | bytes 1572868
  17.8 54.9 %collective-permute-start = (bf16[2,360,384]{2,1,0:T(8,128)(2,1)}, bf16[2,360,384]{2,1,0:T(8,128)(2,1)}, u32[]{:S(2)}, u32[]{:S(2)}) collective-permute-start(bf16[2,360,384]{2,1,0:T(8,128)(2,1)} %get-tuple-element.104), channel_id=1, source_target_pairs={{0,3},{1,0},{2,1},{3,2},{4,7},{5,4},{6,5},{7,6},{8,11},{9,8},{10,9... | collective-permute-start | bytes 1658888 | tf_op jit(solution)/shard_map/ppermute | solution.py:290
  18.0 14.7 %collective-permute-start.6 = (bf16[14,128,128]{2,1,0:T(8,128)(2,1)}, bf16[14,128,128]{2,1,0:T(8,128)(2,1)S(1)}, u32[]{:S(2)}, u32[]{:S(2)}) collective-permute-start(bf16[14,128,128]{2,1,0:T(8,128)(2,1)} %get-tuple-element.52), channel_id=1, source_target_pairs={{0,4},{4,8},{8,12},{12,16},{16,20},{20,24},{24,28},{1,5},{5,9},{9,... | collective-permute-start | bytes 1376264 | tf_op jit(solution)/shard_map/ppermute | solution.py:417
  22.4 22.0 %collective-permute-start.7 = (bf16[14,128,128]{2,1,0:T(8,128)(2,1)}, bf16[14,128,128]{2,1,0:T(8,128)(2,1)S(1)}, u32[]{:S(2)}, u32[]{:S(2)}) collective-permute-start(bf16[14,128,128]{2,1,0:T(8,128)(2,1)} %get-tuple-element.53), channel_id=1, source_target_pairs={{4,0},{8,4},{12,8},{16,12},{20,16},{24,20},{28,24},{5,1},{9,5},{13... | collective-permute-start | bytes 1376264 | tf_op jit(solution)/shard_map/ppermute | solution.py:417
  25.0 47.8 %all-to-all-start = ((bf16[8,180,384]{2,1,0:T(8,128)(2,1)}), bf16[8,180,384]{2,1,0:T(8,128)(2,1)S(1)}, u32[]{:S(2)}, u32[]{:S(2)}) async-start(bf16[8,180,384]{2,1,0:T(8,128)(2,1)} %broadcast_in_dim.34), calls=%async_computation | async-start | bytes 2260992 | tf_op jit(solution)/shard_map/all_to_all | solution.py:87
  29.8 23.4 %copy-start.17 = (bf16[128,128]{1,0:T(8,128)(2,1)S(1)}, bf16[128,128]{1,0:T(8,128)(2,1)}, u32[]{:S(2)}) copy-start(bf16[128,128]{1,0:T(8,128)(2,1)} %param.30) | copy-start | bytes 98308
  29.8 24.1 %copy-start.16 = (bf16[128,256]{1,0:T(8,128)(2,1)S(1)}, bf16[128,256]{1,0:T(8,128)(2,1)}, u32[]{:S(2)}) copy-start(bf16[128,256]{1,0:T(8,128)(2,1)} %param.29) | copy-start | bytes 196612
  29.9 24.8 %copy-start.18 = (bf16[384,26]{0,1:T(8,128)(2,1)S(1)}, bf16[384,26]{0,1:T(8,128)(2,1)}, u32[]{:S(2)}) copy-start(bf16[384,26]{0,1:T(8,128)(2,1)} %param.24) | copy-start | bytes 59908
  29.9 25.6 %copy-start.6 = (bf16[256,9,128]{2,0,1:T(8,128)(2,1)S(1)}, bf16[256,9,128]{2,0,1:T(8,128)(2,1)}, u32[]{:S(2)}) copy-start(bf16[256,9,128]{2,0,1:T(8,128)(2,1)} %param.28) | copy-start | bytes 1769476
  32.7 23.4 %copy-start.4 = (bf16[14,128,128]{2,1,0:T(8,128)(2,1)}, bf16[14,128,128]{2,1,0:T(8,128)(2,1)S(1)}, u32[]{:S(2)}) copy-start(bf16[14,128,128]{2,1,0:T(8,128)(2,1)S(1)} %collective-permute-done.6.above_ref) | copy-start | bytes 1376260
  44.4 11.8 %copy-start.5 = (bf16[14,128,128]{2,1,0:T(8,128)(2,1)}, bf16[14,128,128]{2,1,0:T(8,128)(2,1)S(1)}, u32[]{:S(2)}) copy-start(bf16[14,128,128]{2,1,0:T(8,128)(2,1)S(1)} %collective-permute-done.7.below_ref) | copy-start | bytes 1376260
  45.2 18.6 %collective-permute-start.9 = (bf16[34,16,128]{2,1,0:T(8,128)(2,1)}, bf16[34,16,128]{2,1,0:T(8,128)(2,1)}, u32[]{:S(2)}, u32[]{:S(2)}) collective-permute-start(bf16[34,16,128]{2,1,0:T(8,128)(2,1)} %pad_maximum_fusion.3), channel_id=1, source_target_pairs={{1,0},{2,1},{3,2},{5,4},{6,5},{7,6},{9,8},{10,9},{11,10},{13,12},{... | collective-permute-start | bytes 417800 | tf_op jit(solution)/shard_map/ppermute | solution.py:417
  49.3 14.5 %collective-permute-start.8 = (bf16[34,16,128]{2,1,0:T(8,128)(2,1)}, bf16[34,16,128]{2,1,0:T(8,128)(2,1)}, u32[]{:S(2)}, u32[]{:S(2)}) collective-permute-start(bf16[34,16,128]{2,1,0:T(8,128)(2,1)} %pad_maximum_fusion.2), channel_id=1, source_target_pairs={{0,1},{1,2},{2,3},{4,5},{5,6},{6,7},{8,9},{9,10},{10,11},{12,13},{... | collective-permute-start | bytes 417800 | tf_op jit(solution)/shard_map/ppermute | solution.py:417
  89.8 18.6 %collective-permute-start.10 = (bf16[1,360,384]{2,1,0:T(8,128)(2,1)}, bf16[1,360,384]{2,1,0:T(8,128)(2,1)S(1)}, u32[]{:S(2)}, u32[]{:S(2)}) collective-permute-start(bf16[1,360,384]{2,1,0:T(8,128)(2,1)} %get-tuple-element.64), channel_id=1, source_target_pairs={{0,1},{1,2},{2,3},{3,0},{4,5},{5,6},{6,7},{7,4},{8,9},{9,10},{10,1... | collective-permute-start | bytes 829448 | tf_op jit(solution)/shard_map/ppermute | solution.py:290
  89.8 23.9 %collective-permute-start.11 = (bf16[1,360,384]{2,1,0:T(8,128)(2,1)}, bf16[1,360,384]{2,1,0:T(8,128)(2,1)S(1)}, u32[]{:S(2)}, u32[]{:S(2)}) collective-permute-start(bf16[1,360,384]{2,1,0:T(8,128)(2,1)} %get-tuple-element.65), channel_id=1, source_target_pairs={{0,2},{1,3},{2,0},{3,1},{4,6},{5,7},{6,4},{7,5},{8,10},{9,11},{10,... | collective-permute-start | bytes 829448 | tf_op jit(solution)/shard_map/ppermute | solution.py:290
  89.9 17.8 %copy-start.19 = (bf16[4,16,128]{2,1,0:T(8,128)(2,1)S(1)}, bf16[4,16,128]{2,1,0:T(8,128)(2,1)}, u32[]{:S(2)}) copy-start(bf16[4,16,128]{2,1,0:T(8,128)(2,1)} %get-tuple-element.61) | copy-start | bytes 49156
  89.9 24.7 %collective-permute-start.12 = (bf16[1,360,384]{2,1,0:T(8,128)(2,1)}, bf16[1,360,384]{2,1,0:T(8,128)(2,1)S(1)}, u32[]{:S(2)}, u32[]{:S(2)}) collective-permute-start(bf16[1,360,384]{2,1,0:T(8,128)(2,1)} %get-tuple-element.66), channel_id=1, source_target_pairs={{0,3},{1,0},{2,1},{3,2},{4,7},{5,4},{6,5},{7,6},{8,11},{9,8},{10,9... | collective-permute-start | bytes 829448 | tf_op jit(solution)/shard_map/ppermute | solution.py:290
  108.4 54.2 %copy-start.9 = (bf16[1,360,384]{2,1,0:T(8,128)(2,1)}, bf16[1,360,384]{2,1,0:T(8,128)(2,1)S(1)}, u32[]{:S(2)}) copy-start(bf16[1,360,384]{2,1,0:T(8,128)(2,1)S(1)} %collective-permute-done.10.refs_1_) | copy-start | bytes 829444
  113.6 49.0 %copy-start.10 = (bf16[1,360,384]{2,1,0:T(8,128)(2,1)}, bf16[1,360,384]{2,1,0:T(8,128)(2,1)S(1)}, u32[]{:S(2)}) copy-start(bf16[1,360,384]{2,1,0:T(8,128)(2,1)S(1)} %collective-permute-done.11.refs_2_) | copy-start | bytes 829444
  114.6 48.0 %copy-start.11 = (bf16[1,360,384]{2,1,0:T(8,128)(2,1)}, bf16[1,360,384]{2,1,0:T(8,128)(2,1)S(1)}, u32[]{:S(2)}) copy-start(bf16[1,360,384]{2,1,0:T(8,128)(2,1)S(1)} %collective-permute-done.12.refs_3_) | copy-start | bytes 829444
  115.4 15.3 %all-to-all-start.1 = ((bf16[32,32,128]{2,1,0:T(8,128)(2,1)}), bf16[32,32,128]{2,1,0:T(8,128)(2,1)S(1)}, u32[]{:S(2)}, u32[]{:S(2)}) async-start(bf16[32,32,128]{2,1,0:T(8,128)(2,1)} %bitcast.34), calls=%async_computation.1 | async-start | bytes 524288 | tf_op jit(solution)/shard_map/all_to_all | solution.py:87
  130.7 33.0 %collective-permute-start.13 = (bf16[1,360,384]{2,1,0:T(8,128)(2,1)}, bf16[1,360,384]{2,1,0:T(8,128)(2,1)S(1)}, u32[]{:S(2)}, u32[]{:S(2)}) collective-permute-start(bf16[1,360,384]{2,1,0:T(8,128)(2,1)} %get-tuple-element.77), channel_id=1, source_target_pairs={{0,1},{1,2},{2,3},{3,0},{4,5},{5,6},{6,7},{7,4},{8,9},{9,10},{10,1... | collective-permute-start | bytes 829448 | tf_op jit(solution)/shard_map/ppermute | solution.py:290
  131.7 32.0 %collective-permute-start.14 = (bf16[1,360,384]{2,1,0:T(8,128)(2,1)}, bf16[1,360,384]{2,1,0:T(8,128)(2,1)S(1)}, u32[]{:S(2)}, u32[]{:S(2)}) collective-permute-start(bf16[1,360,384]{2,1,0:T(8,128)(2,1)} %get-tuple-element.78), channel_id=1, source_target_pairs={{0,2},{1,3},{2,0},{3,1},{4,6},{5,7},{6,4},{7,5},{8,10},{9,11},{10,... | collective-permute-start | bytes 829448 | tf_op jit(solution)/shard_map/ppermute | solution.py:290
  134.8 29.0 %collective-permute-start.15 = (bf16[1,360,384]{2,1,0:T(8,128)(2,1)}, bf16[1,360,384]{2,1,0:T(8,128)(2,1)S(1)}, u32[]{:S(2)}, u32[]{:S(2)}) collective-permute-start(bf16[1,360,384]{2,1,0:T(8,128)(2,1)} %get-tuple-element.79), channel_id=1, source_target_pairs={{0,3},{1,0},{2,1},{3,2},{4,7},{5,4},{6,5},{7,6},{8,11},{9,8},{10,9... | collective-permute-start | bytes 829448 | tf_op jit(solution)/shard_map/ppermute | solution.py:290
  (8 other events, 19.4 us)

commit v7 on v6

--- a/solution.py
+++ b/solution.py
@@ -334,11 +334,9 @@
     tables = split_tables(piece * count, spec_filter.shape[1])
     owners = [(me - step) % count * turns for step in range(count)]
     mine = filter_share(spec_filter)
-    global_state, mine = lax.optimization_barrier((global_state, mine))
-    received = []
-    for step, owner in enumerate(owners):
-        own = lax.dynamic_slice_in_dim(global_state, owner, turns, 0)
-        received.append(shift(own, "col", -step) if step else own)
+    bands = [lax.dynamic_slice_in_dim(global_state, owner, turns, 0) for owner in owners]
+    bands, mine = lax.optimization_barrier((bands, mine))
+    received = [shift(band, "col", -step) if step else band for step, band in enumerate(bands)]
     wide = every_channel(mine)
     gains = spread(wide, PLANE).reshape(-1, wide.shape[1])
     prepared = prepare(wide)
@@ -354,15 +352,19 @@
             blocks = [shift(block, "col", step) if step else block for step, block in enumerate(blocks)]
         outcome.append(blocks)
         strips.append(strip)
+    strips, outcome[:-1] = lax.optimization_barrier((jnp.concatenate(strips, axis=1), outcome[:-1]))
+    near = []
+    for step in range(count):
+        strip = lax.dynamic_index_in_dim(strips, (me - step) % count, 0, keepdims=False)
+        near.append(shift(strip, "col", -step) if step else strip)
+    got = spread(jnp.stack(near), PLANE)
     plane = lax.axis_size(PLANE)
-    strips, outcome[:-1] = lax.optimization_barrier((jnp.concatenate(strips, axis=1), outcome[:-1]))
-    sent = jnp.broadcast_to(strips[None], (plane,) + strips.shape)
-    got = exchange(sent.reshape((plane * count,) + strips.shape[1:]), PLANE + ("col",))
-    outcome[-1], got = lax.optimization_barrier((outcome[-1], got))
     got = got.reshape((plane * lats_here, -1, LANES))
     lat = box_lat0[0] - window_base() + lax.axis_index(PLANE) * (rows_here // RATIO)
     lat = jnp.clip(lat + jnp.arange(window_extent(rows_here), dtype=jnp.int32), 0, plane * lats_here - 1)
     places = [owner + turn for turn in range(turns) for owner in owners]
+    band, lat = lat // lats_here, lat % lats_here
+    pick = (band * count + (lat // turns - me) % count) * turns + lat % turns
     outcome[-1] = [
         shift(block, "col", step) if step else block for step, block in enumerate(outcome[-1])
     ]
@@ -372,7 +374,7 @@
         blocks, after = lax.optimization_barrier((finals, after))
         return collate(jnp.stack(places).astype(jnp.int32), blocks), after
 
-    return finish, got, lat.astype(jnp.int32), prepared
+    return finish, got, pick.astype(jnp.int32), prepared
 
 
 def global_by_channel(
@@ -503,8 +505,8 @@
 
 def denoise_kernel(
     rows, cols, totals, variables, conds, place_ref, pick_ref, noisy_ref, noise_ref, blend_ref,
-    strip_ref, first_w_ref, down_w_ref, up_w_ref, bridge_w_ref, last_w_ref, out_ref, stack_ref, first_ref, pooled_ref,
-    lifted_ref, third_ref, pair_ref, spread_ref, window_ref,
+    strip_ref, first_w_ref, down_w_ref, up_w_ref, bridge_w_ref, last_w_ref, out_ref, own_ref,
+    stack_ref, first_ref, pooled_ref, lifted_ref, third_ref, pair_ref, spread_ref, window_ref,
 ):
     width = noisy_ref.shape[1]
     half = width // 2
@@ -528,25 +530,30 @@
     def flat(start, count, unit):
         return pl.ds(pl.multiple_of(start * unit, 16), count * unit)
 
-    def inside(row, count):
+    def inside(row):
         marks = []
-        for step in range(count):
+        for step in range(2):
             there = place_ref[0] + row + step
-            marks.append(col_in * jnp.where((there >= 0) & (there < totals[0]), 1.0, 0.0))
-        return jnp.concatenate(marks, axis=0)
-
-    def conv(source_ref, row, count, unit, weight_ref):
-        lhs = jnp.concatenate(
-            [source_ref[flat(row + step, count, unit), :] for step in range(3)], axis=1
-        )
-        wide = jnp.dot(lhs, weight_ref[...], preferred_element_type=f32)
-        size = weight_ref.shape[1] // 3
-        span = count * unit
-        return (
-            pltpu.roll(wide[:, :size], 1, 0)
-            + wide[:, size : 2 * size]
-            + pltpu.roll(wide[:, 2 * size :], span - 1, 0)
-        )
+            mark = col_in * jnp.where((there >= 0) & (there < totals[0]), 1.0, 0.0)
+            marks.append(jnp.broadcast_to(mark, (width, channels)))
+        return jnp.concatenate(marks, axis=1)
+
+    def keep(ref, where, value):
+        size = value.shape[0]
+        ref[0, where, :] = pltpu.roll(value, 1, 0).astype(bf16)
+        ref[1, where, :] = value.astype(bf16)
+        ref[2, where, :] = pltpu.roll(value, size - 1, 0).astype(bf16)
+
+    def pairs(ref, row, count):
+        blocks = []
+        for pair in range(count):
+            taps = [
+                ref[shift, flat(row + 2 * pair + step, 1, width), :]
+                for step in range(4)
+                for shift in range(3)
+            ]
+            blocks.append(jnp.concatenate(taps, axis=1))
+        return jnp.concatenate(blocks, axis=0)
 
     for hour in range(2):
         rim = RIM - RIM_USED * hour
@@ -555,85 +562,102 @@
         def stack(index, carry, hour=hour, rim=rim):
             here = flat(index * 2, 2, width)
             weights = blend_ref[pl.ds(index * 2 + RIM - rim, 2)].reshape(2 * width, -1)
-            cond = jnp.dot(weights, window_ref[hour], preferred_element_type=f32).astype(bf16)
+            cond = jnp.dot(weights, window_ref[hour], preferred_element_type=f32)
             if hour == 0:
-                own = noisy_ref[pl.ds(index * 2, 2)].reshape(2 * width, channels)
+                own = noisy_ref[pl.ds(index * 2, 2)].reshape(2 * width, channels).astype(f32)
+                own_ref[here, :] = own
             else:
-                own = stack_ref[here, :]
-            stack_ref[here, :] = jnp.where(is_state, own, cond)
+                own = own_ref[here, :]
+            keep(stack_ref, here, jnp.where(is_state, own, cond))
             return carry
 
         lax.fori_loop(0, tall // 2, stack, 0)
 
         def make_first(index, carry, rim=rim):
             row = index * 8
-            value = silu(conv(stack_ref, row, 8, width, first_w_ref)) * inside(row - rim + 1, 8)
-            value = value.astype(bf16)
-            first_ref[flat(row, 8, width), :] = value
-            value = value.astype(f32)
-            for step in range(4):
-                at = 2 * step * width
-                pair_ref[step] = value[at : at + width] + value[at + width : at + 2 * width]
-                even = pair_ref[step, pl.ds(0, half, stride=2), :]
-                odd = pair_ref[step, pl.ds(1, half, stride=2), :]
-                pooled_ref[flat(index * 4 + step, 1, half), :] = ((even + odd) * 0.25).astype(bf16)
+            value = jnp.dot(
+                pairs(stack_ref, row, 4), first_w_ref[...], preferred_element_type=f32
+            )
+            for pair in range(4):
+                top = row + 2 * pair
+                part = silu(value[pair * width : (pair + 1) * width]) * inside(top - rim + 1)
+                part = part.astype(bf16)
+                first_ref[flat(index * 4 + pair, 1, width), :] = part
+                part = part.astype(f32)
+                pair_ref[pair] = part[:, :channels] + part[:, channels:]
+                even = pair_ref[pair, pl.ds(0, half, stride=2), :]
+                odd = pair_ref[pair, pl.ds(1, half, stride=2), :]
+                keep(pooled_ref, flat(index * 4 + pair, 1, half), (even + odd) * 0.25)
             return carry
 
         lax.fori_loop(0, (tall - 2) // 8, make_first, 0)
 
         half_rows = (tall - 2) // 2 - 2
 
-        def make_lifted(index, carry, part=half_rows // 2):
-            value = silu(conv(pooled_ref, index * part, part, half, down_w_ref)).astype(bf16)
-            lifted_ref[flat(index * part, part, half), :] = jnp.dot(
-                value, up_w_ref[...], preferred_element_type=f32
+        def make_third(index, carry, part=half_rows // 2, rim=rim):
+            row = index * part
+            taps = [
+                pooled_ref[shift, flat(row + step, part, half), :]
+                for step in range(3)
+                for shift in range(3)
+            ]
+            second = jnp.dot(
+                jnp.concatenate(taps, axis=1), down_w_ref[...], preferred_element_type=f32
             )
-            return carry
-
-        lax.fori_loop(0, 2, make_lifted, 0)
-
-        def make_third(index, carry, rim=rim):
-            row = index * 4
-            spreads = []
-            for step in range(2):
-                lifted = lifted_ref[flat(index * 2 + step, 1, half), :]
+            lifted_ref[: part * half, :] = jnp.dot(
+                silu(second).astype(bf16), up_w_ref[...], preferred_element_type=f32
+            )
+            bridged = jnp.dot(
+                first_ref[flat(row + 1, part, width), :], bridge_w_ref[...], preferred_element_type=f32
+            )
+            for step in range(part):
+                lifted = lifted_ref[step * half : (step + 1) * half, :]
                 spread_ref[step, pl.ds(0, half, stride=2), :] = lifted
                 spread_ref[step, pl.ds(1, half, stride=2), :] = lifted
-                spreads += [spread_ref[step]] * 2
-            bridged = jnp.dot(
-                first_ref[flat(row + 2, 4, width), :], bridge_w_ref[...], preferred_element_type=f32
+                spread = spread_ref[step]
+                value = bridged[step * width : (step + 1) * width]
+                value = silu(value + jnp.concatenate([spread, spread], axis=1))
+                top = 2 * (row + step)
+                value = value * inside(top - rim + 3)
+                keep(third_ref, flat(top, 1, width), value[:, :channels])
+                keep(third_ref, flat(top + 1, 1, width), value[:, channels:])
+            return carry
+
+        lax.fori_loop(0, 2, make_third, 0)
+
+        part = (rows + 2 * (rim - RIM_USED)) // 2 if hour == 0 else rows // 4
+        skip = 1 if hour == 1 else 0
+
+        def finish(index, carry, hour=hour, rim=rim, part=part, skip=skip):
+            start = index * 2 * part
+            value = jnp.dot(
+                pairs(third_ref, start + skip, part), last_w_ref[...], preferred_element_type=f32
             )
-            value = silu(bridged + jnp.concatenate(spreads, axis=0))
-            value = value * inside(row - rim + 3, 4)
-            third_ref[flat(row, 4, width), :] = value.astype(bf16)
+            for pair in range(part):
+                for step in range(2):
+                    row = start + 2 * pair + step
+                    fresh = value[
+                        pair * width : (pair + 1) * width, step * channels : (step + 1) * channels
+                    ]
+                    own = own_ref[flat(row + RIM_USED + skip, 1, width), :]
+                    fresh = (own + fresh).astype(bf16)
+                    if hour == 0:
+                        there = place_ref[0] + row - rim + RIM_USED
+                        mark = col_in * jnp.where((there >= 0) & (there < totals[0]), 1.0, 0.0)
+                        noise = noise_ref[row].astype(f32)
+                        fresh = (fresh.astype(f32) + noise_level * noise) * mark
+                        own_ref[flat(row, 1, width), :] = fresh.astype(bf16).astype(f32)
+                    else:
+                        out_ref[row] = fresh[pad : pad + cols]
             return carry
 
-        lax.fori_loop(0, half_rows // 2, make_third, 0)
-
-        part = (rows + 2 * (rim - RIM_USED)) // 2 if hour == 0 else rows // 2
-
-        def finish(index, carry, hour=hour, rim=rim, part=part):
-            row = index * part
-            skip = 1 if hour == 1 else 0
-            fresh = conv(third_ref, row + skip, part, width, last_w_ref)
-            own = stack_ref[flat(row + RIM_USED + skip, part, width), :].astype(f32)
-            fresh = (own + fresh).astype(bf16)
-            if hour == 0:
-                noise = noise_ref[pl.ds(row, part)].reshape(part * width, channels).astype(f32)
-                fresh = (fresh.astype(f32) + noise_level * noise) * inside(row - rim + RIM_USED, part)
-                stack_ref[flat(row, part, width), :] = fresh.astype(bf16)
-            else:
-                for step in range(part):
-                    at = step * width + pad
-                    out_ref[row + step] = fresh[at : at + cols]
-            return carry
-
-        lax.fori_loop(0, 2, finish, 0)
+        lax.fori_loop(0, 1 if hour == 0 else 2, finish, 0)
 
 
 def denoise(rows, cols, totals, variables, conds, place, pick, noisy, noise, blend, strips, weights):
     width, channels = noisy.shape[1:]
     tall = rows + 2 * RIM
+    most = (tall - 2) // 4 - 1
     bf16, f32 = jnp.bfloat16, jnp.float32
     return pl.pallas_call(
         functools.partial(denoise_kernel, rows, cols, totals, variables, conds),
@@ -641,13 +665,14 @@
         in_specs=[pl.BlockSpec(memory_space=pltpu.SMEM)] * 2
         + [pl.BlockSpec(memory_space=pltpu.VMEM)] * 9,
         scratch_shapes=[
-            pltpu.VMEM((tall * width, channels), bf16),
-            pltpu.VMEM((tall * width, channels), bf16),
-            pltpu.VMEM((tall // 2 * width // 2, channels), bf16),
-            pltpu.VMEM((tall // 2 * width // 2, channels), f32),
-            pltpu.VMEM((tall * width, channels), bf16),
+            pltpu.VMEM((tall * width, channels), f32),
+            pltpu.VMEM((3, tall * width, channels), bf16),
+            pltpu.VMEM((tall // 2 * width, 2 * channels), bf16),
+            pltpu.VMEM((3, tall // 2 * width // 2, channels), bf16),
+            pltpu.VMEM((most * width // 2, channels), f32),
+            pltpu.VMEM((3, tall * width, channels), bf16),
             pltpu.VMEM((4, width, channels), f32),
-            pltpu.VMEM((2, width, channels), f32),
+            pltpu.VMEM((most, width, channels), f32),
             pltpu.VMEM((2, blend.shape[2], channels), bf16),
         ],
         compiler_params=pltpu.CompilerParams(vmem_limit_bytes=VMEM),
@@ -658,9 +683,15 @@
 
 def conv_weight(weight, depth, width):
     out, _, given = weight.shape
-    weight = weight.reshape(out, 3, 3, given)
-    weight = jnp.pad(weight, ((0, width - out), (0, 0), (0, 0), (0, depth - given)))
-    return jnp.transpose(weight, (1, 3, 2, 0)).reshape(3 * depth, 3 * width)
+    weight = jnp.pad(weight, ((0, width - out), (0, 0), (0, depth - given)))
+    return jnp.transpose(weight, (1, 2, 0)).reshape(9 * depth, width)
+
+
+def pair_weight(weight):
+    row = weight.shape[0] // 3
+    return jnp.concatenate(
+        [jnp.pad(weight, ((0, row), (0, 0))), jnp.pad(weight, ((row, 0), (0, 0)))], axis=1
+    )
 
 
 def shards(
@@ -741,11 +772,14 @@
             rim_cols(cols_here - RIM, cols_here - inner), rim_cols(0, 0), "col"
         )
         weights = (
-            conv_weight(w_first, LANES, w_first.shape[0]),
+            pair_weight(conv_weight(w_first, LANES, w_first.shape[0])),
             conv_weight(w_down, w_down.shape[2], w_down.shape[0]),
             w_up.T,
-            w_bridge.T,
-            conv_weight(w_last, w_last.shape[2], LANES),
+            jnp.concatenate(
+                [jnp.pad(w_bridge.T, ((0, 0), (0, LANES))), jnp.pad(w_bridge.T, ((0, 0), (LANES, 0)))],
+                axis=0,
+            ),
+            pair_weight(conv_weight(w_last, w_last.shape[2], LANES)),
         )
         parts = (mid0, mid1, above, below, left, right)
         return assemble(rows_here, cols_here, totals, high, lanes, place, *parts), weights

time: 171 us -> 168 us (0.982)
  waiting for transfers between devices: 35.7 us -> 28 us
  starting transfers between devices: 35.7 us -> 39.2 us
  other arithmetic: 5.32 us -> 7.33 us
    all_to_all x2, waiting for transfers between devices: 8.88 us -> 0.01 us  [exchange(): return lax.all_to_all(blocks, axis, split_axis=0, concat_axis=0, tiled=True)]
    ppermute x12 -> x15, starting transfers between devices: 14.5 us -> 20 us  [shift(): lax.ppermute(block, axis, [(source, (source + step) % count) for source i...]
    ppermute x12 -> x15, waiting for transfers between devices: 6.18 us -> 8.83 us  [shift(): lax.ppermute(block, axis, [(source, (source + step) % count) for source i...]
    reshape x4 -> x0, local copies, waits for them, and re-layouts: 2.09 us -> none  [the longest x3 1.2 us: conv_weight(): weight = weight.reshape(out, 3, 3, given)]
    ppermute x2, waiting for transfers between devices: 2.85 us -> 0.76 us  [next_to(): lax.ppermute(low, axis, forward)]
    all_to_all x2, starting transfers between devices: 10.7 us -> 8.64 us  [exchange(): return lax.all_to_all(blocks, axis, split_axis=0, concat_axis=0, tiled=True)]
    concatenate x0 -> x2, other arithmetic: none -> 1.99 us  [the longest x1 1.33 us: pair_weight(): jnp.concatenate([jnp.pad(weight, ((0, row), (0, 0))), jnp.pad(weight, ((r...]
    unnamed x59 -> x56, local copies, waits for them, and re-layouts: 5.59 us -> 7.51 us
  transfers between devices with their start and end apart: 18 -> 21, of which waited for: 6 -> 8; matrix products, arithmetic and copies ran while one was open for 11% -> 10% of each run, Pallas kernels for 31% -> 30%
where the time goes in v7:
time: 168 us; the launch traced here: 165 us
  Pallas kernels  68.7 us (41%)
  starting transfers between devices  39.2 us (23%)
  waiting for transfers between devices  28 us (17%)
  local copies, waits for them, and re-layouts  19.2 us (11%)
  other arithmetic  7.33 us (4%)
  between operations  2.76 us (2%)
    pallas_call x2, Pallas kernels, advance_latitude(): pl.pallas_call(functools.partial(latitude_kernel, hours, 1, step), grid=(...  31.7 us
    pallas_call x1, Pallas kernels, denoise(): pl.pallas_call(functools.partial(denoise_kernel, rows, cols, totals, vari...  25.1 us
    ppermute x15, starting transfers between devices, shift(): lax.ppermute(block, axis, [(source, (source + step) % count) for source i...  20 us
    ppermute x2, waiting for transfers between devices, next_to(): lax.ppermute(high, axis, backward)  18.4 us
    pallas_call x1, Pallas kernels, assemble(): pl.pallas_call(functools.partial(assemble_kernel, rows, cols, totals, hig...  8.92 us
    ppermute x15, waiting for transfers between devices, shift(): lax.ppermute(block, axis, [(source, (source + step) % count) for source i...  8.83 us
    all_to_all x2, starting transfers between devices, exchange(): return lax.all_to_all(blocks, axis, split_axis=0, concat_axis=0, tiled=True)  8.64 us
    unnamed x56, local copies, waits for them, and re-layouts  7.51 us
  transfers between devices with their start and end apart: 21, of which 8 were waited for; matrix products, arithmetic and copies ran while one was open for 10% of the time, Pallas kernels for 30%

profile of v7, /device:TPU:8, one launch (start us, length us, event | category | flops | bytes accessed | tf_op | source)
XLA Modules:
  0.0 165.1 jit_solution(11192692798764722613)
XLA Ops:
  0.7 1.5 copy.29
  2.6 2.9 %constant_dynamic-slice_fusion.2 = (bf16[2,360,384]{2,1,0:T(8,128)(2,1)S(1)}, bf16[2,360,384]{2,1,0:T(8,128)(2,1)}, bf16[2,360,384]{2,1,0:T(8,128)(2,1)}, bf16[2,360,384]{2,1,0:T(8,128)(2,1)}) fusion(bf16[8,360,384]{2,1,0:T(8,128)(2,1)} %param.20, s32[]{:T(128)S(6)} %select_n.132, s32[]{:T(128)S(6)} %select_n.130, s32[]{:T(128)S(6)} %select_n.129, ...), kind=kLoop, calls=%fused_computation.65 | loop fusion | bytes 4423696 | tf_op jit(solution)/shard_map/dynamic_slice | solution.py:337
  5.5 1.6 collective-permute-start.5
  8.1 2.0 %collective-permute-start.3 = (bf16[180,96]{0,1:T(8,128)(2,1)S(1)}, bf16[180,96]{0,1:T(8,128)(2,1)S(1)}, u32[]{:S(2)}, u32[]{:S(2)}) collective-permute-start(bf16[180,96]{0,1:T(8,128)(2,1)S(1)} %dynamic-slice_convert_fusion), channel_id=1, source_target_pairs={{0,3},{1,0},{2,1},{3,2},{4,7},{5,4},{6,5},{7,6},{8,11},{9,8},{10,9... | collective-permute-start | bytes 103688 | tf_op jit(solution)/shard_map/ppermute | solution.py:290
  10.2 1.3 collective-permute-start
  15.4 1.8 %collective-permute-start.2 = (bf16[2,360,384]{2,1,0:T(8,128)(2,1)S(1)}, bf16[2,360,384]{2,1,0:T(8,128)(2,1)}, u32[]{:S(2)}, u32[]{:S(2)}) collective-permute-start(bf16[2,360,384]{2,1,0:T(8,128)(2,1)S(1)} %get-tuple-element.51), channel_id=1, source_target_pairs={{0,1},{1,2},{2,3},{3,0},{4,5},{5,6},{6,7},{7,4},{8,9},{9,10},{10,1... | collective-permute-start | bytes 1658888 | tf_op jit(solution)/shard_map/ppermute | solution.py:290
  17.4 3.4 %collective-permute-start.6 = (bf16[14,128,128]{2,1,0:T(8,128)(2,1)}, bf16[14,128,128]{2,1,0:T(8,128)(2,1)S(1)}, u32[]{:S(2)}, u32[]{:S(2)}) collective-permute-start(bf16[14,128,128]{2,1,0:T(8,128)(2,1)} %get-tuple-element.53), channel_id=1, source_target_pairs={{0,4},{4,8},{8,12},{12,16},{16,20},{20,24},{24,28},{1,5},{5,9},{9,... | collective-permute-start | bytes 1376264 | tf_op jit(solution)/shard_map/ppermute | solution.py:419
  21.1 1.3 fusion.5
  22.4 1.3 collective-permute-start.7
  25.2 1.1 broadcast_in_dim.34
  26.3 5.0 %all-to-all-start = ((bf16[8,180,384]{2,1,0:T(8,128)(2,1)}), bf16[8,180,384]{2,1,0:T(8,128)(2,1)S(1)}, u32[]{:S(2)}, u32[]{:S(2)}) async-start(bf16[8,180,384]{2,1,0:T(8,128)(2,1)} %broadcast_in_dim.34), calls=%async_computation | async-start | bytes 2260992 | tf_op jit(solution)/shard_map/all_to_all | solution.py:87
  32.1 11.6 %collective-permute-done.7.below_ref = bf16[14,128,128]{2,1,0:T(8,128)(2,1)S(1)} collective-permute-done((bf16[14,128,128]{2,1,0:T(8,128)(2,1)}, bf16[14,128,128]{2,1,0:T(8,128)(2,1)S(1)}, u32[]{:S(2)}, u32[]{:S(2)}) %collective-permute-start.7) | collective-permute-done | bytes 458784 | tf_op jit(solution)/shard_map/ppermute | solution.py:419
  44.6 2.3 %collective-permute-start.9 = (bf16[34,16,128]{2,1,0:T(8,128)(2,1)}, bf16[34,16,128]{2,1,0:T(8,128)(2,1)S(1)}, u32[]{:S(2)}, u32[]{:S(2)}) collective-permute-start(bf16[34,16,128]{2,1,0:T(8,128)(2,1)} %pad_maximum_fusion.3), channel_id=1, source_target_pairs={{1,0},{2,1},{3,2},{5,4},{6,5},{7,6},{9,8},{10,9},{11,10},{13,12},{... | collective-permute-start | bytes 417800 | tf_op jit(solution)/shard_map/ppermute | solution.py:419
  47.7 3.5 %collective-permute-start.8 = (bf16[34,16,128]{2,1,0:T(8,128)(2,1)}, bf16[34,16,128]{2,1,0:T(8,128)(2,1)}, u32[]{:S(2)}, u32[]{:S(2)}) collective-permute-start(bf16[34,16,128]{2,1,0:T(8,128)(2,1)} %pad_maximum_fusion.2), channel_id=1, source_target_pairs={{0,1},{1,2},{2,3},{4,5},{5,6},{6,7},{8,9},{9,10},{10,11},{12,13},{... | collective-permute-start | bytes 417800 | tf_op jit(solution)/shard_map/ppermute | solution.py:419
  51.9 1.6 copy.33
  56.7 6.7 %collective-permute-done.9.right_ref = bf16[34,16,128]{2,1,0:T(8,128)(2,1)S(1)} collective-permute-done((bf16[34,16,128]{2,1,0:T(8,128)(2,1)}, bf16[34,16,128]{2,1,0:T(8,128)(2,1)S(1)}, u32[]{:S(2)}, u32[]{:S(2)}) %collective-permute-start.9) | collective-permute-done | bytes 139296 | tf_op jit(solution)/shard_map/ppermute | solution.py:419
  64.1 8.9 %assemble.1 = (bf16[34,160,128]{2,1,0:T(8,128)(2,1)}, bf16[26,160,128]{2,1,0:T(8,128)(2,1)}, bf16[34,160,256]{2,1,0:T(8,128)(2,1)}) custom-call(s32[2]{0:T(128)} %pad_add_fusion.1.place_ref, bf16[16,128,128]{2,1,0:T(8,128)(2,1)} %copy-done, bf16[16,128,128]{2,1,0:T(8,128)(2,1)} %copy-done.1, bf16[14,128,128]{2,1,0:T(8,128)(2,1)} %copy-done.4, ...), custom_call_target="tpu_custom_call" | custom-call | flops 1000000 | bytes 100000 | tf_op jit(solution)/shard_map/assemble/pallas_call | solution.py:484
  73.1 1.1 reshape.117.refs_8_
  74.2 15.8 %advance_latitude.2 = (bf16[1,360,384]{2,1,0:T(8,128)(2,1)}, bf16[1,360,384]{2,1,0:T(8,128)(2,1)}, bf16[1,360,384]{2,1,0:T(8,128)(2,1)}, bf16[1,360,384]{2,1,0:T(8,128)(2,1)}, bf16[4,16,128]{2,1,0:T(8,128)(2,1)}) custom-call(s32[3]{0:T(128)} %pad_add_fusion.place_ref, bf16[2,360,384]{2,1,0:T(8,128)(2,1)} %get-tuple-element.58.refs_0_, ...), custom_call_target="tpu_custom_call" | custom-call | flops 16000000000 | bytes 8388608 | tf_op jit(solution)/shard_map/advance_latitude/pallas_call | solution.py:235
  90.9 2.3 %collective-permute-start.11 = (bf16[1,360,384]{2,1,0:T(8,128)(2,1)}, bf16[1,360,384]{2,1,0:T(8,128)(2,1)S(1)}, u32[]{:S(2)}, u32[]{:S(2)}) collective-permute-start(bf16[1,360,384]{2,1,0:T(8,128)(2,1)} %get-tuple-element.66), channel_id=1, source_target_pairs={{0,2},{1,3},{2,0},{3,1},{4,6},{5,7},{6,4},{7,5},{8,10},{9,11},{10,... | collective-permute-start | bytes 829448 | tf_op jit(solution)/shard_map/ppermute | solution.py:290
  93.2 15.9 %advance_latitude.3 = (bf16[1,360,384]{2,1,0:T(8,128)(2,1)}, bf16[1,360,384]{2,1,0:T(8,128)(2,1)}, bf16[1,360,384]{2,1,0:T(8,128)(2,1)}, bf16[1,360,384]{2,1,0:T(8,128)(2,1)}, bf16[4,16,128]{2,1,0:T(8,128)(2,1)}) custom-call(s32[3]{0:T(128)} %pad_add_fusion.place_ref, bf16[2,360,384]{2,1,0:T(8,128)(2,1)} %get-tuple-element.58.refs_0_, ...), custom_call_target="tpu_custom_call" | custom-call | flops 16000000000 | bytes 8388608 | tf_op jit(solution)/shard_map/advance_latitude/pallas_call | solution.py:235
  110.0 5.1 %collective-permute-done.11.refs_2_ = bf16[1,360,384]{2,1,0:T(8,128)(2,1)S(1)} collective-permute-done((bf16[1,360,384]{2,1,0:T(8,128)(2,1)}, bf16[1,360,384]{2,1,0:T(8,128)(2,1)S(1)}, u32[]{:S(2)}, u32[]{:S(2)}) %collective-permute-start.11) | collective-permute-done | bytes 276512 | tf_op jit(solution)/shard_map/ppermute | solution.py:290
  115.1 1.8 %collective-permute-done.12.refs_3_ = bf16[1,360,384]{2,1,0:T(8,128)(2,1)S(1)} collective-permute-done((bf16[1,360,384]{2,1,0:T(8,128)(2,1)}, bf16[1,360,384]{2,1,0:T(8,128)(2,1)S(1)}, u32[]{:S(2)}, u32[]{:S(2)}) %collective-permute-start.12) | collective-permute-done | bytes 276512 | tf_op jit(solution)/shard_map/ppermute | solution.py:290
  116.9 1.6 collective-permute-start.17
  118.6 1.9 %collective-permute-start.16 = (bf16[32,128]{1,0:T(8,128)(2,1)S(1)}, bf16[32,128]{1,0:T(8,128)(2,1)S(1)}, u32[]{:S(2)}, u32[]{:S(2)}) collective-permute-start(bf16[32,128]{1,0:T(8,128)(2,1)S(1)} %get-tuple-element.123), channel_id=1, source_target_pairs={{0,3},{1,0},{2,1},{3,2},{4,7},{5,4},{6,5},{7,6},{8,11},{9,8},{10,9... | collective-permute-start | bytes 24584 | tf_op jit(solution)/shard_map/ppermute | solution.py:290
  123.0 3.7 %all-to-all-start.1 = ((bf16[8,4,32,128]{3,2,1,0:T(8,128)(2,1)}), bf16[8,4,32,128]{3,2,1,0:T(8,128)(2,1)S(1)}, u32[]{:S(2)}, u32[]{:S(2)}) async-start(bf16[8,4,32,128]{3,2,1,0:T(8,128)(2,1)} %broadcast_in_dim.35), calls=%async_computation.1 | async-start | bytes 524288 | tf_op jit(solution)/shard_map/all_to_all | solution.py:87
  127.3 2.0 %collective-permute-start.13 = (bf16[1,360,384]{2,1,0:T(8,128)(2,1)}, bf16[1,360,384]{2,1,0:T(8,128)(2,1)S(1)}, u32[]{:S(2)}, u32[]{:S(2)}) collective-permute-start(bf16[1,360,384]{2,1,0:T(8,128)(2,1)} %get-tuple-element.73), channel_id=1, source_target_pairs={{0,1},{1,2},{2,3},{3,0},{4,5},{5,6},{6,7},{7,4},{8,9},{9,10},{10,1... | collective-permute-start | bytes 829448 | tf_op jit(solution)/shard_map/ppermute | solution.py:290
  129.3 2.3 %collective-permute-start.14 = (bf16[1,360,384]{2,1,0:T(8,128)(2,1)}, bf16[1,360,384]{2,1,0:T(8,128)(2,1)S(1)}, u32[]{:S(2)}, u32[]{:S(2)}) collective-permute-start(bf16[1,360,384]{2,1,0:T(8,128)(2,1)} %get-tuple-element.74), channel_id=1, source_target_pairs={{0,2},{1,3},{2,0},{3,1},{4,6},{5,7},{6,4},{7,5},{8,10},{9,11},{10,... | collective-permute-start | bytes 829448 | tf_op jit(solution)/shard_map/ppermute | solution.py:290
  134.6 25.1 %denoise.1 = bf16[16,128,128]{2,1,0:T(8,128)(2,1)} custom-call(s32[2]{0:T(128)} %pad_add_fusion.1.place_ref, s32[8]{0:T(128)} %fusion.18.pick_ref, bf16[34,160,128]{2,1,0:T(8,128)(2,1)} %get-tuple-element.76.noisy_ref, bf16[26,160,128]{2,1,0:T(8,128)(2,1)} %get-tuple-element.77.noise_ref, bf16[34,160,256]{2,1,0:T(8,128)(2,1)} %get-tuple-element.78.blend_ref, ...), custom_call_target="tpu_custom_call" | custom-call | flops 1000000 | bytes 100000 | tf_op jit(solution)/shard_map/denoise/pallas_call | solution.py:662
  159.7 1.1 slice_bitcast_fusion
  160.9 1.1 copy.38
  162.0 3.0 %collate.1 = bf16[8,360,384]{2,1,0:T(8,128)(2,1)} custom-call(s32[8]{0:T(128)} %stack.69.place_ref, bf16[1,360,384]{2,1,0:T(8,128)(2,1)} %get-tuple-element.85.refs_0_, bf16[1,360,384]{2,1,0:T(8,128)(2,1)} %copy-done.9, bf16[1,360,384]{2,1,0:T(8,128)(2,1)} %copy-done.10, bf16[1,360,384]{2,1,0:T(8,128)(2,1)} %copy-done.11, ...), custom_call_target="tpu_custom_call" | custom-call | tf_op jit(solution)/shard_map/collate/pallas_call | solution.py:277
  (117 shorter events, 20.5 us)
Async XLA Ops:
  2.6 9.1 %copy-start.3 = (bf16[2,99,16,128]{3,2,1,0:T(8,128)(2,1)S(1)}, bf16[2,99,16,128]{3,2,1,0:T(8,128)(2,1)}, u32[]{:S(2)}) copy-start(bf16[2,99,16,128]{3,2,1,0:T(8,128)(2,1)} %param.26) | copy-start | bytes 2433028
  2.6 9.2 %copy-start.19 = (s32[16,128]{1,0:T(8,128)S(1)}, s32[16,128]{1,0:T(8,128)}, u32[]{:S(2)}) copy-start(s32[16,128]{1,0:T(8,128)} %param.34) | copy-start | bytes 24580
  2.6 9.3 %copy-start.20 = (s32[16,128]{1,0:T(8,128)S(1)}, s32[16,128]{1,0:T(8,128)}, u32[]{:S(2)}) copy-start(s32[16,128]{1,0:T(8,128)} %param.35) | copy-start | bytes 24580
  5.5 11.8 %collective-permute-start.5 = (bf16[180,96]{0,1:T(8,128)(2,1)S(1)}, bf16[180,96]{0,1:T(8,128)(2,1)S(1)}, u32[]{:S(2)}, u32[]{:S(2)}) collective-permute-start(bf16[180,96]{0,1:T(8,128)(2,1)S(1)} %dynamic-slice_convert_fusion), channel_id=1, source_target_pairs={{0,1},{1,2},{2,3},{3,0},{4,5},{5,6},{6,7},{7,4},{8,9},{9,10},{10,1... | collective-permute-start | bytes 103688 | tf_op jit(solution)/shard_map/ppermute | solution.py:290
  7.1 10.2 %collective-permute-start.4 = (bf16[180,96]{0,1:T(8,128)(2,1)S(1)}, bf16[180,96]{0,1:T(8,128)(2,1)S(1)}, u32[]{:S(2)}, u32[]{:S(2)}) collective-permute-start(bf16[180,96]{0,1:T(8,128)(2,1)S(1)} %dynamic-slice_convert_fusion), channel_id=1, source_target_pairs={{0,2},{1,3},{2,0},{3,1},{4,6},{5,7},{6,4},{7,5},{8,10},{9,11},{10,... | collective-permute-start | bytes 103688 | tf_op jit(solution)/shard_map/ppermute | solution.py:290
  8.1 7.3 %collective-permute-start.3 = (bf16[180,96]{0,1:T(8,128)(2,1)S(1)}, bf16[180,96]{0,1:T(8,128)(2,1)S(1)}, u32[]{:S(2)}, u32[]{:S(2)}) collective-permute-start(bf16[180,96]{0,1:T(8,128)(2,1)S(1)} %dynamic-slice_convert_fusion), channel_id=1, source_target_pairs={{0,3},{1,0},{2,1},{3,2},{4,7},{5,4},{6,5},{7,6},{8,11},{9,8},{10,9... | collective-permute-start | bytes 103688 | tf_op jit(solution)/shard_map/ppermute | solution.py:290
  10.2 62.9 %collective-permute-start = (bf16[2,360,384]{2,1,0:T(8,128)(2,1)}, bf16[2,360,384]{2,1,0:T(8,128)(2,1)}, u32[]{:S(2)}, u32[]{:S(2)}) collective-permute-start(bf16[2,360,384]{2,1,0:T(8,128)(2,1)} %get-tuple-element.49), channel_id=1, source_target_pairs={{0,3},{1,0},{2,1},{3,2},{4,7},{5,4},{6,5},{7,6},{8,11},{9,8},{10,9... | collective-permute-start | bytes 1658888 | tf_op jit(solution)/shard_map/ppermute | solution.py:290
  11.5 61.5 %collective-permute-start.1 = (bf16[2,360,384]{2,1,0:T(8,128)(2,1)}, bf16[2,360,384]{2,1,0:T(8,128)(2,1)}, u32[]{:S(2)}, u32[]{:S(2)}) collective-permute-start(bf16[2,360,384]{2,1,0:T(8,128)(2,1)} %get-tuple-element.50), channel_id=1, source_target_pairs={{0,2},{1,3},{2,0},{3,1},{4,6},{5,7},{6,4},{7,5},{8,10},{9,11},{10,... | collective-permute-start | bytes 1658888 | tf_op jit(solution)/shard_map/ppermute | solution.py:290
  15.4 57.6 %collective-permute-start.2 = (bf16[2,360,384]{2,1,0:T(8,128)(2,1)S(1)}, bf16[2,360,384]{2,1,0:T(8,128)(2,1)}, u32[]{:S(2)}, u32[]{:S(2)}) collective-permute-start(bf16[2,360,384]{2,1,0:T(8,128)(2,1)S(1)} %get-tuple-element.51), channel_id=1, source_target_pairs={{0,1},{1,2},{2,3},{3,0},{4,5},{5,6},{6,7},{7,4},{8,9},{9,10},{10,1... | collective-permute-start | bytes 1658888 | tf_op jit(solution)/shard_map/ppermute | solution.py:290
  17.4 14.7 %collective-permute-start.6 = (bf16[14,128,128]{2,1,0:T(8,128)(2,1)}, bf16[14,128,128]{2,1,0:T(8,128)(2,1)S(1)}, u32[]{:S(2)}, u32[]{:S(2)}) collective-permute-start(bf16[14,128,128]{2,1,0:T(8,128)(2,1)} %get-tuple-element.53), channel_id=1, source_target_pairs={{0,4},{4,8},{8,12},{12,16},{16,20},{20,24},{24,28},{1,5},{5,9},{9,... | collective-permute-start | bytes 1376264 | tf_op jit(solution)/shard_map/ppermute | solution.py:419
  22.4 21.3 %collective-permute-start.7 = (bf16[14,128,128]{2,1,0:T(8,128)(2,1)}, bf16[14,128,128]{2,1,0:T(8,128)(2,1)S(1)}, u32[]{:S(2)}, u32[]{:S(2)}) collective-permute-start(bf16[14,128,128]{2,1,0:T(8,128)(2,1)} %get-tuple-element.54), channel_id=1, source_target_pairs={{4,0},{8,4},{12,8},{16,12},{20,16},{24,20},{28,24},{5,1},{9,5},{13... | collective-permute-start | bytes 1376264 | tf_op jit(solution)/shard_map/ppermute | solution.py:419
  26.3 25.4 %copy-start.17 = (bf16[128,128]{1,0:T(8,128)(2,1)S(1)}, bf16[128,128]{1,0:T(8,128)(2,1)}, u32[]{:S(2)}) copy-start(bf16[128,128]{1,0:T(8,128)(2,1)} %param.30) | copy-start | bytes 98308
  26.3 28.0 %copy-start.6 = (bf16[256,9,128]{2,0,1:T(8,128)(2,1)S(1)}, bf16[256,9,128]{2,0,1:T(8,128)(2,1)}, u32[]{:S(2)}) copy-start(bf16[256,9,128]{2,0,1:T(8,128)(2,1)} %param.28) | copy-start | bytes 1769476
  26.3 46.7 %all-to-all-start = ((bf16[8,180,384]{2,1,0:T(8,128)(2,1)}), bf16[8,180,384]{2,1,0:T(8,128)(2,1)S(1)}, u32[]{:S(2)}, u32[]{:S(2)}) async-start(bf16[8,180,384]{2,1,0:T(8,128)(2,1)} %broadcast_in_dim.34), calls=%async_computation | async-start | bytes 2260992 | tf_op jit(solution)/shard_map/all_to_all | solution.py:87
  32.1 24.6 %copy-start.4 = (bf16[14,128,128]{2,1,0:T(8,128)(2,1)}, bf16[14,128,128]{2,1,0:T(8,128)(2,1)S(1)}, u32[]{:S(2)}) copy-start(bf16[14,128,128]{2,1,0:T(8,128)(2,1)S(1)} %collective-permute-done.6.above_ref) | copy-start | bytes 1376260
  43.8 19.7 %copy-start.5 = (bf16[14,128,128]{2,1,0:T(8,128)(2,1)}, bf16[14,128,128]{2,1,0:T(8,128)(2,1)S(1)}, u32[]{:S(2)}) copy-start(bf16[14,128,128]{2,1,0:T(8,128)(2,1)S(1)} %collective-permute-done.7.below_ref) | copy-start | bytes 1376260
  44.6 18.9 %collective-permute-start.9 = (bf16[34,16,128]{2,1,0:T(8,128)(2,1)}, bf16[34,16,128]{2,1,0:T(8,128)(2,1)S(1)}, u32[]{:S(2)}, u32[]{:S(2)}) collective-permute-start(bf16[34,16,128]{2,1,0:T(8,128)(2,1)} %pad_maximum_fusion.3), channel_id=1, source_target_pairs={{1,0},{2,1},{3,2},{5,4},{6,5},{7,6},{9,8},{10,9},{11,10},{13,12},{... | collective-permute-start | bytes 417800 | tf_op jit(solution)/shard_map/ppermute | solution.py:419
  47.7 15.8 %collective-permute-start.8 = (bf16[34,16,128]{2,1,0:T(8,128)(2,1)}, bf16[34,16,128]{2,1,0:T(8,128)(2,1)}, u32[]{:S(2)}, u32[]{:S(2)}) collective-permute-start(bf16[34,16,128]{2,1,0:T(8,128)(2,1)} %pad_maximum_fusion.2), channel_id=1, source_target_pairs={{0,1},{1,2},{2,3},{4,5},{5,6},{6,7},{8,9},{9,10},{10,11},{12,13},{... | collective-permute-start | bytes 417800 | tf_op jit(solution)/shard_map/ppermute | solution.py:419
  90.0 20.0 %collective-permute-start.10 = (bf16[1,360,384]{2,1,0:T(8,128)(2,1)}, bf16[1,360,384]{2,1,0:T(8,128)(2,1)S(1)}, u32[]{:S(2)}, u32[]{:S(2)}) collective-permute-start(bf16[1,360,384]{2,1,0:T(8,128)(2,1)} %get-tuple-element.65), channel_id=1, source_target_pairs={{0,1},{1,2},{2,3},{3,0},{4,5},{5,6},{6,7},{7,4},{8,9},{9,10},{10,1... | collective-permute-start | bytes 829448 | tf_op jit(solution)/shard_map/ppermute | solution.py:290
  90.9 24.2 %collective-permute-start.11 = (bf16[1,360,384]{2,1,0:T(8,128)(2,1)}, bf16[1,360,384]{2,1,0:T(8,128)(2,1)S(1)}, u32[]{:S(2)}, u32[]{:S(2)}) collective-permute-start(bf16[1,360,384]{2,1,0:T(8,128)(2,1)} %get-tuple-element.66), channel_id=1, source_target_pairs={{0,2},{1,3},{2,0},{3,1},{4,6},{5,7},{6,4},{7,5},{8,10},{9,11},{10,... | collective-permute-start | bytes 829448 | tf_op jit(solution)/shard_map/ppermute | solution.py:290
  93.2 15.9 %copy-start.18 = (bf16[4,16,128]{2,1,0:T(8,128)(2,1)S(1)}, bf16[4,16,128]{2,1,0:T(8,128)(2,1)}, u32[]{:S(2)}) copy-start(bf16[4,16,128]{2,1,0:T(8,128)(2,1)} %get-tuple-element.62) | copy-start | bytes 49156
  93.2 23.7 %collective-permute-start.12 = (bf16[1,360,384]{2,1,0:T(8,128)(2,1)}, bf16[1,360,384]{2,1,0:T(8,128)(2,1)S(1)}, u32[]{:S(2)}, u32[]{:S(2)}) collective-permute-start(bf16[1,360,384]{2,1,0:T(8,128)(2,1)} %get-tuple-element.67), channel_id=1, source_target_pairs={{0,3},{1,0},{2,1},{3,2},{4,7},{5,4},{6,5},{7,6},{8,11},{9,8},{10,9... | collective-permute-start | bytes 829448 | tf_op jit(solution)/shard_map/ppermute | solution.py:290
  110.0 49.7 %copy-start.9 = (bf16[1,360,384]{2,1,0:T(8,128)(2,1)}, bf16[1,360,384]{2,1,0:T(8,128)(2,1)S(1)}, u32[]{:S(2)}) copy-start(bf16[1,360,384]{2,1,0:T(8,128)(2,1)S(1)} %collective-permute-done.10.refs_1_) | copy-start | bytes 829444
  115.1 44.6 %copy-start.10 = (bf16[1,360,384]{2,1,0:T(8,128)(2,1)}, bf16[1,360,384]{2,1,0:T(8,128)(2,1)S(1)}, u32[]{:S(2)}) copy-start(bf16[1,360,384]{2,1,0:T(8,128)(2,1)S(1)} %collective-permute-done.11.refs_2_) | copy-start | bytes 829444
  116.9 42.8 %copy-start.11 = (bf16[1,360,384]{2,1,0:T(8,128)(2,1)}, bf16[1,360,384]{2,1,0:T(8,128)(2,1)S(1)}, u32[]{:S(2)}) copy-start(bf16[1,360,384]{2,1,0:T(8,128)(2,1)S(1)} %collective-permute-done.12.refs_3_) | copy-start | bytes 829444
  116.9 3.7 %collective-permute-start.18 = (bf16[32,128]{1,0:T(8,128)(2,1)S(1)}, bf16[32,128]{1,0:T(8,128)(2,1)S(1)}, u32[]{:S(2)}, u32[]{:S(2)}) collective-permute-start(bf16[32,128]{1,0:T(8,128)(2,1)S(1)} %get-tuple-element.121), channel_id=1, source_target_pairs={{0,1},{1,2},{2,3},{3,0},{4,5},{5,6},{6,7},{7,4},{8,9},{9,10},{10,1... | collective-permute-start | bytes 24584 | tf_op jit(solution)/shard_map/ppermute | solution.py:290
  116.9 4.7 %collective-permute-start.17 = (bf16[32,128]{1,0:T(8,128)(2,1)S(1)}, bf16[32,128]{1,0:T(8,128)(2,1)S(1)}, u32[]{:S(2)}, u32[]{:S(2)}) collective-permute-start(bf16[32,128]{1,0:T(8,128)(2,1)S(1)} %get-tuple-element.122), channel_id=1, source_target_pairs={{0,2},{1,3},{2,0},{3,1},{4,6},{5,7},{6,4},{7,5},{8,10},{9,11},{10,... | collective-permute-start | bytes 24584 | tf_op jit(solution)/shard_map/ppermute | solution.py:290
  118.6 3.7 %collective-permute-start.16 = (bf16[32,128]{1,0:T(8,128)(2,1)S(1)}, bf16[32,128]{1,0:T(8,128)(2,1)S(1)}, u32[]{:S(2)}, u32[]{:S(2)}) collective-permute-start(bf16[32,128]{1,0:T(8,128)(2,1)S(1)} %get-tuple-element.123), channel_id=1, source_target_pairs={{0,3},{1,0},{2,1},{3,2},{4,7},{5,4},{6,5},{7,6},{8,11},{9,8},{10,9... | collective-permute-start | bytes 24584 | tf_op jit(solution)/shard_map/ppermute | solution.py:290
  123.0 10.9 %all-to-all-start.1 = ((bf16[8,4,32,128]{3,2,1,0:T(8,128)(2,1)}), bf16[8,4,32,128]{3,2,1,0:T(8,128)(2,1)S(1)}, u32[]{:S(2)}, u32[]{:S(2)}) async-start(bf16[8,4,32,128]{3,2,1,0:T(8,128)(2,1)} %broadcast_in_dim.35), calls=%async_computation.1 | async-start | bytes 524288 | tf_op jit(solution)/shard_map/all_to_all | solution.py:87
  127.3 33.5 %collective-permute-start.13 = (bf16[1,360,384]{2,1,0:T(8,128)(2,1)}, bf16[1,360,384]{2,1,0:T(8,128)(2,1)S(1)}, u32[]{:S(2)}, u32[]{:S(2)}) collective-permute-start(bf16[1,360,384]{2,1,0:T(8,128)(2,1)} %get-tuple-element.73), channel_id=1, source_target_pairs={{0,1},{1,2},{2,3},{3,0},{4,5},{5,6},{6,7},{7,4},{8,9},{9,10},{10,1... | collective-permute-start | bytes 829448 | tf_op jit(solution)/shard_map/ppermute | solution.py:290
  129.3 31.5 %collective-permute-start.14 = (bf16[1,360,384]{2,1,0:T(8,128)(2,1)}, bf16[1,360,384]{2,1,0:T(8,128)(2,1)S(1)}, u32[]{:S(2)}, u32[]{:S(2)}) collective-permute-start(bf16[1,360,384]{2,1,0:T(8,128)(2,1)} %get-tuple-element.74), channel_id=1, source_target_pairs={{0,2},{1,3},{2,0},{3,1},{4,6},{5,7},{6,4},{7,5},{8,10},{9,11},{10,... | collective-permute-start | bytes 829448 | tf_op jit(solution)/shard_map/ppermute | solution.py:290
  131.6 29.2 %collective-permute-start.15 = (bf16[1,360,384]{2,1,0:T(8,128)(2,1)}, bf16[1,360,384]{2,1,0:T(8,128)(2,1)S(1)}, u32[]{:S(2)}, u32[]{:S(2)}) collective-permute-start(bf16[1,360,384]{2,1,0:T(8,128)(2,1)} %get-tuple-element.75), channel_id=1, source_target_pairs={{0,3},{1,0},{2,1},{3,2},{4,7},{5,4},{6,5},{7,6},{8,11},{9,8},{10,9... | collective-permute-start | bytes 829448 | tf_op jit(solution)/shard_map/ppermute | solution.py:290
  (10 other events, 24.2 us)

commit v8 on v7

--- a/solution.py
+++ b/solution.py
@@ -116,10 +116,17 @@
 
 def latitude_kernel(hours, turns, step, place_ref, *refs):
     piece_refs, refs = refs[:4], refs[4:]
-    even_forward_ref, odd_forward_ref, even_inverse_ref, odd_inverse_ref = refs[:4]
-    filter_ref, skip_ref, mix_ref, decode_ref = refs[4:8]
-    out_refs, strip_ref = refs[8:12], refs[12]
-    state_ref, spectral_ref, gain_ref, coarse_ref, near_ref, packed_ref = refs[13:]
+    even_forward_ref, odd_forward_ref = refs[:2]
+    far_refs, out_refs, strip_ref, refs = refs[2:8], refs[8:12], refs[12], refs[13:]
+    near_refs, sems, refs = refs[:6], refs[6], refs[7:]
+    filter_ref, even_inverse_ref, odd_inverse_ref, skip_ref, mix_ref, decode_ref = near_refs
+    state_ref, gain_ref, coarse_ref, near_ref, packed_ref = refs
+    copies = [
+        pltpu.make_async_copy(far, near, sems.at[index])
+        for index, (far, near) in enumerate(zip(far_refs, near_refs))
+    ]
+    for copy in copies:
+        copy.start()
     f32, bf16 = jnp.float32, jnp.bfloat16
     piece, channels = piece_refs[0].shape[1:]
     padded = state_ref.shape[0] // 4
@@ -134,10 +141,12 @@
             ] = jnp.concatenate([piece_refs[index][turn], spare], axis=0)
 
     modes = filter_ref.shape[0] // 2
-    for index in range(channels // LANES):
-        lanes = slice(index * LANES, (index + 1) * LANES)
-        gain_ref[index, : 2 * modes, :] = filter_ref[:, lanes].astype(f32)
-        gain_ref[index, 2 * modes :, :] = jnp.zeros((gain_ref.shape[1] - 2 * modes, LANES), f32)
+
+    def spread_gains():
+        for index in range(channels // LANES):
+            lanes = slice(index * LANES, (index + 1) * LANES)
+            gain_ref[index, : 2 * modes, :] = filter_ref[:, lanes].astype(f32)
+            gain_ref[index, 2 * modes :, :] = jnp.zeros((gain_ref.shape[1] - 2 * modes, LANES), f32)
 
     def gain_rows(low, count, stride):
         rows = pl.ds(low, count, stride=stride)
@@ -160,36 +169,37 @@
     def dot(left, right):
         return jnp.dot(left, right, preferred_element_type=f32)
 
-    def advance(hour, carry):
+    for hour in range(hours):
         pieces = [
             state_ref[index * padded : (index + 1) * padded, :].astype(f32) for index in range(4)
         ]
         both, other = pieces[0] + pieces[2], pieces[1] + pieces[3]
-        shares = []
-        for index, mixed in enumerate((both + other, both - other)):
-            spectrum = dot(even_forward_ref[index], mixed.astype(bf16))
-            shares.append(dot(even_inverse_ref[index], gain(spectrum, 2 * index, 4)))
+        spectra = [
+            dot(even_forward_ref[index], mixed.astype(bf16))
+            for index, mixed in enumerate((both + other, both - other))
+        ]
         mixed = jnp.concatenate([pieces[0] - pieces[2], pieces[1] - pieces[3]], axis=0)
-        odd = gain(dot(odd_forward_ref[...], mixed.astype(bf16)), 1, 2)
-        odd = dot(odd_inverse_ref[...], odd)
+        spectra.append(dot(odd_forward_ref[...], mixed.astype(bf16)))
+        if hour == 0:
+            copies[0].wait()
+            spread_gains()
+            for copy in copies[1:]:
+                copy.wait()
+        shares = [
+            dot(even_inverse_ref[index], gain(spectra[index], 2 * index, 4)) for index in range(2)
+        ]
+        odd = dot(odd_inverse_ref[...], gain(spectra[2], 1, 2))
         for index in range(4):
+            here = slice(index * padded, (index + 1) * padded)
             even = shares[0] + shares[1] if index % 2 == 0 else shares[0] - shares[1]
             part = odd[:padded] if index % 2 == 0 else odd[padded:]
-            total = even + part if index < 2 else even - part
-            spectral_ref[index * padded : (index + 1) * padded, :] = total.astype(bf16)
-
-        def mix(index, carry):
-            here = pl.ds(pl.multiple_of(index * padded, LANES), padded)
+            spectral = even + part if index < 2 else even - part
             for turn in range(turns):
                 lanes = slice(turn * channels, (turn + 1) * channels)
                 state = state_ref[here, lanes]
-                summed = spectral_ref[here, lanes].astype(f32) + dot(state, skip_ref[...])
-                activated = gelu(summed).astype(bf16)
+                activated = gelu(spectral[:, lanes] + dot(state, skip_ref[...])).astype(bf16)
                 update = dot(activated, mix_ref[...])
                 state_ref[here, lanes] = (state.astype(f32) + update).astype(bf16)
-            return carry
-
-        lax.fori_loop(0, 4, mix, 0)
 
         for index in range(2):
             here = pl.ds(pl.multiple_of(place_ref[index] * padded, LANES), padded)
@@ -203,10 +213,8 @@
             packed = near_ref[pl.ds(0, rows, stride=group), :]
             for sub in range(1, group):
                 packed += pltpu.roll(near_ref[pl.ds(sub, rows, stride=group), :], sub * PACKED, 1)
-            packed_ref[turn, pl.ds(pl.multiple_of(hour * rows, 8), rows), :] = packed
-        return carry
-
-    lax.fori_loop(0, hours, advance, 0)
+            packed_ref[turn, hour * rows : (hour + 1) * rows, :] = packed
+
     for index in range(4):
         for turn in range(turns):
             out_refs[index][turn] = state_ref[
@@ -231,6 +239,7 @@
     span = round_up(3 * step + STRIP * group, 8 * group)
     decode = jnp.pad(w_decode, ((0, 0), (0, LANES - w_decode.shape[1])))
     modes = gains.shape[0] // 2
+    late = (gains,) + tables[2:] + (w_skip, w_mix, decode)
     spare = max(4 * (tables[0].shape[1] // 2), 2 * (tables[1].shape[0] // 2)) - modes
     results = pl.pallas_call(
         functools.partial(latitude_kernel, hours, 1, step),
@@ -239,9 +248,11 @@
         + (jax.ShapeDtypeStruct((4, hours * STRIP, LANES), jnp.bfloat16),),
         in_specs=[pl.BlockSpec(memory_space=pltpu.SMEM)]
         + [pl.BlockSpec((1, piece, channels), lambda i: (turn, 0, 0))] * 4
-        + [pl.BlockSpec(memory_space=pltpu.VMEM)] * 8,
-        scratch_shapes=[
-            pltpu.VMEM((4 * padded, channels), jnp.bfloat16),
+        + [pl.BlockSpec(memory_space=pltpu.VMEM)] * 2
+        + [pl.BlockSpec(memory_space=pl.ANY)] * len(late),
+        scratch_shapes=[pltpu.VMEM(array.shape, array.dtype) for array in late]
+        + [
+            pltpu.SemaphoreType.DMA((len(late),)),
             pltpu.VMEM((4 * padded, channels), jnp.bfloat16),
             pltpu.VMEM((channels // LANES, gains.shape[0] + spare, LANES), jnp.float32),
             pltpu.VMEM((1, 2 * piece, LANES), jnp.float32),
@@ -253,7 +264,7 @@
             flops=16 * 10**9, bytes_accessed=8 * 2**20, transcendentals=hours * 4 * piece * channels
         ),
         name="advance_latitude",
-    )(place, *pieces, *tables, gains, w_skip, w_mix, decode)
+    )(place, *pieces, *tables[:2], *late)
     return results[:4], results[4]
 
 
@@ -325,7 +336,7 @@
 
 def global_by_latitude(
     hours, global_state, spec_filter, w_skip, w_mix, w_decode, box_lat0, box_lon0, rows_here,
-    cols_here, prepare,
+    cols_here, first, prepare,
 ):
     count = lax.axis_size("col")
     me = lax.axis_index("col")
@@ -335,29 +346,30 @@
     owners = [(me - step) % count * turns for step in range(count)]
     mine = filter_share(spec_filter)
     bands = [lax.dynamic_slice_in_dim(global_state, owner, turns, 0) for owner in owners]
-    bands, mine = lax.optimization_barrier((bands, mine))
+    mine, _ = lax.optimization_barrier((mine, (bands, first)))
     received = [shift(band, "col", -step) if step else band for step, band in enumerate(bands)]
     wide = every_channel(mine)
+    parts, weights = prepare()
     gains = spread(wide, PLANE).reshape(-1, wide.shape[1])
-    prepared = prepare(wide)
     start = (box_lon0[0] - window_base() - me * piece) % (piece * count)
     place = jnp.stack([start // piece, (start // piece + 1) % count, start % piece]).astype(jnp.int32)
-    received, prepared = lax.optimization_barrier((received, prepared))
+    received, weights = lax.optimization_barrier((received, weights))
     outcome, strips = [], []
     for turn in range(turns):
         blocks, strip = advance_latitude(
             hours, turn, cols_here // RATIO, place, received, tables, gains, w_skip, w_mix, w_decode
         )
-        if turn < turns - 1:
-            blocks = [shift(block, "col", step) if step else block for step, block in enumerate(blocks)]
         outcome.append(blocks)
         strips.append(strip)
-    strips, outcome[:-1] = lax.optimization_barrier((jnp.concatenate(strips, axis=1), outcome[:-1]))
+    outcome = [list(blocks) for blocks in outcome]
+    early = [shift(outcome[0][step], "col", step) for step in (1, 3)]
+    strips, early = lax.optimization_barrier((jnp.concatenate(strips, axis=1), early))
     near = []
     for step in range(count):
         strip = lax.dynamic_index_in_dim(strips, (me - step) % count, 0, keepdims=False)
         near.append(shift(strip, "col", -step) if step else strip)
-    got = spread(jnp.stack(near), PLANE)
+    near, outcome, parts = lax.optimization_barrier((jnp.stack(near), outcome, parts))
+    got = spread(near, PLANE)
     plane = lax.axis_size(PLANE)
     got = got.reshape((plane * lats_here, -1, LANES))
     lat = box_lat0[0] - window_base() + lax.axis_index(PLANE) * (rows_here // RATIO)
@@ -365,24 +377,28 @@
     places = [owner + turn for turn in range(turns) for owner in owners]
     band, lat = lat // lats_here, lat % lats_here
     pick = (band * count + (lat // turns - me) % count) * turns + lat % turns
-    outcome[-1] = [
-        shift(block, "col", step) if step else block for step, block in enumerate(outcome[-1])
-    ]
-    finals = sum(outcome, [])
+    finals = []
+    for turn, blocks in enumerate(outcome):
+        for step, block in enumerate(blocks):
+            if turn == 0 and step % 2 == 1:
+                block = early[step // 2]
+            elif step:
+                block = shift(block, "col", step)
+            finals.append(block)
 
     def finish(after):
         blocks, after = lax.optimization_barrier((finals, after))
         return collate(jnp.stack(places).astype(jnp.int32), blocks), after
 
-    return finish, got, pick.astype(jnp.int32), prepared
+    return finish, got, pick.astype(jnp.int32), (parts, weights)
 
 
 def global_by_channel(
     hours, global_state, spec_filter, w_skip, w_mix, w_decode, box_lat0, box_lon0, rows_here,
-    cols_here, prepare,
+    cols_here, first, prepare,
 ):
     count = lax.axis_size("col")
-    prepared = prepare(global_state)
+    prepared = prepare()
     forward, inverse = fourier_tables(global_state.shape[1] * count, spec_filter.shape[1])
     base = window_base()
     high, wide = window_extent(rows_here), window_extent(cols_here)
@@ -461,16 +477,10 @@
         there = place_ref[0] + row
         row_base = jnp.where((there >= 0) & (there < totals[0]), whole + base, FAR)
         shifts = noisy_ref[index, :, :].astype(jnp.float32)
-        lat = row_base.astype(jnp.float32) + shifts[:, lanes : lanes + 1]
-        lon = col_base.astype(jnp.float32) + shifts[:, lanes + 1 : lanes + 2]
-        from_lat = point_lat - lat
-        from_lon = point_lon - lon
-        weight_lat = jnp.where(
-            from_lat == 0.0, 1.0 - frac_row, jnp.where(from_lat == 1.0, frac_row, 0.0)
-        )
-        weight_lon = jnp.where(
-            from_lon == 0.0, 1.0 - frac_col, jnp.where(from_lon == 1.0, frac_col, 0.0)
-        )
+        lat = row_base.astype(jnp.float32) + frac_row + shifts[:, lanes : lanes + 1]
+        lon = col_base.astype(jnp.float32) + frac_col + shifts[:, lanes + 1 : lanes + 2]
+        weight_lat = jnp.maximum(1.0 - jnp.abs(point_lat - lat), 0.0)
+        weight_lon = jnp.maximum(1.0 - jnp.abs(point_lon - lon), 0.0)
         blend_ref[index, :, :] = (weight_lat * weight_lon).astype(jnp.bfloat16)
         return carry
 
@@ -493,27 +503,31 @@
         in_specs=[pl.BlockSpec(memory_space=pltpu.SMEM)]
         + [pl.BlockSpec(memory_space=pltpu.VMEM)] * 6,
         compiler_params=pltpu.CompilerParams(vmem_limit_bytes=VMEM),
-        cost_estimate=pl.CostEstimate(flops=10**6, bytes_accessed=10**5, transcendentals=0),
+        cost_estimate=pl.CostEstimate(flops=10**10, bytes_accessed=10**7, transcendentals=0),
         name="assemble",
     )(place, mid0, mid1, above, below, left, right)
 
 
-def silu(x):
-    half = 0.5 * x
-    return half + half * jnp.tanh(half)
-
-
 def denoise_kernel(
-    rows, cols, totals, variables, conds, place_ref, pick_ref, noisy_ref, noise_ref, blend_ref,
-    strip_ref, first_w_ref, down_w_ref, up_w_ref, bridge_w_ref, last_w_ref, out_ref, own_ref,
-    stack_ref, first_ref, pooled_ref, lifted_ref, third_ref, pair_ref, spread_ref, window_ref,
+    rows, cols, totals, variables, conds, place_ref, pick_ref, noisy_ref, blend_ref, strip_ref, *refs
 ):
+    far_refs, out_ref, refs = refs[:6], refs[6], refs[7:]
+    near_refs, sems, refs = refs[:6], refs[6], refs[7:]
+    noise_ref, first_w_ref, down_w_ref, up_w_ref, bridge_w_ref, last_w_ref = near_refs
+    own_ref, stack_ref, first_ref, pooled_ref, third_ref, pair_ref, spread_ref, window_ref = refs
+    copies = [
+        pltpu.make_async_copy(far, near, sems.at[index])
+        for index, (far, near) in enumerate(zip(far_refs, near_refs))
+    ]
+    for copy in copies:
+        copy.start()
     width = noisy_ref.shape[1]
     half = width // 2
     pad = (width - cols) // 2
     channels = noisy_ref.shape[2]
     f32, bf16 = jnp.float32, jnp.bfloat16
     col_in = grid_place(place_ref[1], totals[1], -pad, width).astype(f32)
+    edges = [jnp.broadcast_to(col_in[low : low + pad], (pad, channels)) for low in (0, pad + cols)]
     lane = lax.broadcasted_iota(jnp.int32, (1, channels), 1)
     is_state = lane < variables
     is_cond = (lane >= variables) & (lane < variables + conds)
@@ -528,15 +542,15 @@
             ).astype(bf16)
 
     def flat(start, count, unit):
-        return pl.ds(pl.multiple_of(start * unit, 16), count * unit)
-
-    def inside(row):
-        marks = []
-        for step in range(2):
-            there = place_ref[0] + row + step
-            mark = col_in * jnp.where((there >= 0) & (there < totals[0]), 1.0, 0.0)
-            marks.append(jnp.broadcast_to(mark, (width, channels)))
-        return jnp.concatenate(marks, axis=1)
+        return slice(start * unit, (start + count) * unit)
+
+    def mask(value, row):
+        low, mid, high = value[:pad], value[pad : pad + cols], value[pad + cols :]
+        value = jnp.concatenate([low * edges[0], mid, high * edges[1]], axis=0)
+        if 0 <= row < rows:
+            return value
+        there = place_ref[0] + row
+        return value * jnp.where((there >= 0) & (there < totals[0]), 1.0, 0.0)
 
     def keep(ref, where, value):
         size = value.shape[0]
@@ -555,47 +569,49 @@
             blocks.append(jnp.concatenate(taps, axis=1))
         return jnp.concatenate(blocks, axis=0)
 
+    def silu_of_half(half_value):
+        return half_value + half_value * jnp.tanh(half_value)
+
     for hour in range(2):
         rim = RIM - RIM_USED * hour
         tall = rows + 2 * rim
 
-        def stack(index, carry, hour=hour, rim=rim):
-            here = flat(index * 2, 2, width)
-            weights = blend_ref[pl.ds(index * 2 + RIM - rim, 2)].reshape(2 * width, -1)
+        for row in range(0, tall, 2):
+            here = flat(row, 2, width)
+            weights = blend_ref[row + RIM - rim : row + RIM - rim + 2].reshape(2 * width, -1)
             cond = jnp.dot(weights, window_ref[hour], preferred_element_type=f32)
             if hour == 0:
-                own = noisy_ref[pl.ds(index * 2, 2)].reshape(2 * width, channels).astype(f32)
+                own = noisy_ref[row : row + 2].reshape(2 * width, channels).astype(f32)
                 own_ref[here, :] = own
             else:
                 own = own_ref[here, :]
             keep(stack_ref, here, jnp.where(is_state, own, cond))
-            return carry
-
-        lax.fori_loop(0, tall // 2, stack, 0)
-
-        def make_first(index, carry, rim=rim):
-            row = index * 8
+
+        if hour == 0:
+            copies[1].wait()
+        for row in range(0, tall - 2, 8):
             value = jnp.dot(
                 pairs(stack_ref, row, 4), first_w_ref[...], preferred_element_type=f32
             )
             for pair in range(4):
                 top = row + 2 * pair
-                part = silu(value[pair * width : (pair + 1) * width]) * inside(top - rim + 1)
-                part = part.astype(bf16)
-                first_ref[flat(index * 4 + pair, 1, width), :] = part
-                part = part.astype(f32)
-                pair_ref[pair] = part[:, :channels] + part[:, channels:]
-                even = pair_ref[pair, pl.ds(0, half, stride=2), :]
-                odd = pair_ref[pair, pl.ds(1, half, stride=2), :]
-                keep(pooled_ref, flat(index * 4 + pair, 1, half), (even + odd) * 0.25)
-            return carry
-
-        lax.fori_loop(0, (tall - 2) // 8, make_first, 0)
-
+                here = flat(top // 2, 1, width)
+                part = silu_of_half(value[pair * width : (pair + 1) * width])
+                upper = mask(part[:, :channels], top - rim + 1)
+                lower = mask(part[:, channels:], top - rim + 2)
+                first_ref[here, :channels] = upper.astype(bf16)
+                first_ref[here, channels:] = lower.astype(bf16)
+                pair_ref[top // 2] = upper + lower
+                even = pair_ref[top // 2, pl.ds(0, half, stride=2), :]
+                odd = pair_ref[top // 2, pl.ds(1, half, stride=2), :]
+                keep(pooled_ref, flat(top // 2, 1, half), even + odd)
+
+        if hour == 0:
+            for copy in copies[2:5]:
+                copy.wait()
         half_rows = (tall - 2) // 2 - 2
-
-        def make_third(index, carry, part=half_rows // 2, rim=rim):
-            row = index * part
+        part = half_rows // 2
+        for row in (0, part):
             taps = [
                 pooled_ref[shift, flat(row + step, part, half), :]
                 for step in range(3)
@@ -604,81 +620,77 @@
             second = jnp.dot(
                 jnp.concatenate(taps, axis=1), down_w_ref[...], preferred_element_type=f32
             )
-            lifted_ref[: part * half, :] = jnp.dot(
-                silu(second).astype(bf16), up_w_ref[...], preferred_element_type=f32
+            lifted = jnp.dot(
+                silu_of_half(second).astype(bf16), up_w_ref[...], preferred_element_type=f32
             )
             bridged = jnp.dot(
                 first_ref[flat(row + 1, part, width), :], bridge_w_ref[...], preferred_element_type=f32
             )
             for step in range(part):
-                lifted = lifted_ref[step * half : (step + 1) * half, :]
-                spread_ref[step, pl.ds(0, half, stride=2), :] = lifted
-                spread_ref[step, pl.ds(1, half, stride=2), :] = lifted
-                spread = spread_ref[step]
-                value = bridged[step * width : (step + 1) * width]
-                value = silu(value + jnp.concatenate([spread, spread], axis=1))
+                own = lifted[step * half : (step + 1) * half]
+                spread_ref[row + step, pl.ds(0, half, stride=2), :] = own
+                spread_ref[row + step, pl.ds(1, half, stride=2), :] = own
+                own = spread_ref[row + step]
                 top = 2 * (row + step)
-                value = value * inside(top - rim + 3)
-                keep(third_ref, flat(top, 1, width), value[:, :channels])
-                keep(third_ref, flat(top + 1, 1, width), value[:, channels:])
-            return carry
-
-        lax.fori_loop(0, 2, make_third, 0)
-
-        part = (rows + 2 * (rim - RIM_USED)) // 2 if hour == 0 else rows // 4
+                for side in range(2):
+                    value = bridged[
+                        step * width : (step + 1) * width, side * channels : (side + 1) * channels
+                    ]
+                    value = mask(silu_of_half(value + own), top + side - rim + 3)
+                    keep(third_ref, flat(top + side, 1, width), value)
+
+        if hour == 0:
+            copies[5].wait()
+            copies[0].wait()
         skip = 1 if hour == 1 else 0
-
-        def finish(index, carry, hour=hour, rim=rim, part=part, skip=skip):
-            start = index * 2 * part
-            value = jnp.dot(
-                pairs(third_ref, start + skip, part), last_w_ref[...], preferred_element_type=f32
+        count = (rows + 2 * (rim - RIM_USED)) // 2 if hour == 0 else rows // 2
+        for first in range(0, count, 4):
+            size = min(4, count - first)
+            values = jnp.dot(
+                pairs(third_ref, 2 * first + skip, size), last_w_ref[...], preferred_element_type=f32
             )
-            for pair in range(part):
-                for step in range(2):
-                    row = start + 2 * pair + step
-                    fresh = value[
-                        pair * width : (pair + 1) * width, step * channels : (step + 1) * channels
-                    ]
-                    own = own_ref[flat(row + RIM_USED + skip, 1, width), :]
-                    fresh = (own + fresh).astype(bf16)
-                    if hour == 0:
-                        there = place_ref[0] + row - rim + RIM_USED
-                        mark = col_in * jnp.where((there >= 0) & (there < totals[0]), 1.0, 0.0)
-                        noise = noise_ref[row].astype(f32)
-                        fresh = (fresh.astype(f32) + noise_level * noise) * mark
-                        own_ref[flat(row, 1, width), :] = fresh.astype(bf16).astype(f32)
-                    else:
-                        out_ref[row] = fresh[pad : pad + cols]
-            return carry
-
-        lax.fori_loop(0, 1 if hour == 0 else 2, finish, 0)
+            for index in range(2 * size):
+                pair, side = divmod(index, 2)
+                row = 2 * first + index
+                fresh = values[
+                    pair * width : (pair + 1) * width, side * channels : (side + 1) * channels
+                ]
+                fresh = own_ref[flat(row + RIM_USED + skip, 1, width), :] + fresh
+                if hour == 0:
+                    fresh = fresh + noise_level * noise_ref[row].astype(f32)
+                    own_ref[flat(row, 1, width), :] = mask(fresh, row - rim + RIM_USED)
+                else:
+                    out_ref[row] = fresh[pad : pad + cols].astype(bf16)
 
 
 def denoise(rows, cols, totals, variables, conds, place, pick, noisy, noise, blend, strips, weights):
     width, channels = noisy.shape[1:]
     tall = rows + 2 * RIM
-    most = (tall - 2) // 4 - 1
+    most = (tall - 2) // 2
     bf16, f32 = jnp.bfloat16, jnp.float32
+    late = (noise,) + weights
     return pl.pallas_call(
         functools.partial(denoise_kernel, rows, cols, totals, variables, conds),
         out_shape=jax.ShapeDtypeStruct((rows, cols, channels), bf16),
         in_specs=[pl.BlockSpec(memory_space=pltpu.SMEM)] * 2
-        + [pl.BlockSpec(memory_space=pltpu.VMEM)] * 9,
-        scratch_shapes=[
+        + [pl.BlockSpec(memory_space=pltpu.VMEM)] * 3
+        + [pl.BlockSpec(memory_space=pl.ANY)] * len(late),
+        scratch_shapes=[pltpu.VMEM(array.shape, array.dtype) for array in late]
+        + [
+            pltpu.SemaphoreType.DMA((len(late),)),
             pltpu.VMEM((tall * width, channels), f32),
             pltpu.VMEM((3, tall * width, channels), bf16),
-            pltpu.VMEM((tall // 2 * width, 2 * channels), bf16),
-            pltpu.VMEM((3, tall // 2 * width // 2, channels), bf16),
-            pltpu.VMEM((most * width // 2, channels), f32),
+            pltpu.VMEM((most * width, 2 * channels), bf16),
+            pltpu.VMEM((3, most * width // 2, channels), bf16),
             pltpu.VMEM((3, tall * width, channels), bf16),
-            pltpu.VMEM((4, width, channels), f32),
+            pltpu.VMEM((most, width, channels), f32),
             pltpu.VMEM((most, width, channels), f32),
             pltpu.VMEM((2, blend.shape[2], channels), bf16),
         ],
         compiler_params=pltpu.CompilerParams(vmem_limit_bytes=VMEM),
         cost_estimate=pl.CostEstimate(flops=10**6, bytes_accessed=10**5, transcendentals=0),
         name="denoise",
-    )(place, pick, noisy, noise, blend, strips, *weights)
+    )(place, pick, noisy, blend, strips, *late)
 
 
 def conv_weight(weight, depth, width):
@@ -748,10 +760,9 @@
     place = jnp.stack([row_start, col_start]).astype(jnp.int32)
     totals = (total_rows, total_cols)
 
-    def prepare(after):
+    def prepare():
         lows = jnp.concatenate([mid0[rows_here - RIM :], mid1[rows_here - inner :]], axis=0)
         highs = jnp.concatenate([mid0[:RIM], mid1[:inner]], axis=0)
-        lows, highs, _ = lax.optimization_barrier((lows, highs, after))
         above, below = next_to(lows, highs, PLANE)
 
         def rim_cols(first, first_inner):
@@ -772,24 +783,25 @@
             rim_cols(cols_here - RIM, cols_here - inner), rim_cols(0, 0), "col"
         )
         weights = (
-            pair_weight(conv_weight(w_first, LANES, w_first.shape[0])),
-            conv_weight(w_down, w_down.shape[2], w_down.shape[0]),
-            w_up.T,
-            jnp.concatenate(
+            pair_weight(conv_weight(0.5 * w_first, LANES, w_first.shape[0])),
+            conv_weight(0.125 * w_down, w_down.shape[2], w_down.shape[0]),
+            0.5 * w_up.T,
+            0.5
+            * jnp.concatenate(
                 [jnp.pad(w_bridge.T, ((0, 0), (0, LANES))), jnp.pad(w_bridge.T, ((0, 0), (LANES, 0)))],
                 axis=0,
             ),
             pair_weight(conv_weight(w_last, w_last.shape[2], LANES)),
         )
-        parts = (mid0, mid1, above, below, left, right)
-        return assemble(rows_here, cols_here, totals, high, lanes, place, *parts), weights
+        return (mid0, mid1, above, below, left, right), weights
 
     by_latitude = lax.axis_size("col") == 4 and global_state.shape[0] % 4 == 0
     global_steps = global_by_latitude if by_latitude else global_by_channel
-    finish, strips, pick, (fields, weights) = global_steps(
+    finish, strips, pick, (parts, weights) = global_steps(
         hours, global_state, spec_filter, w_skip, w_mix, w_decode, box_lat0, box_lon0,
-        rows_here, cols_here, prepare,
-    )
+        rows_here, cols_here, mids, prepare,
+    )
+    fields = assemble(rows_here, cols_here, totals, high, lanes, place, *parts)
     regional_final = denoise(
         rows_here, cols_here, totals, variables, conds, place, pick, *fields, strips, weights
     )

time: 168 us -> 185 us (1.10)
  waiting for transfers between devices: 28 us -> 59.1 us
  Pallas kernels: 68.7 us -> 54.6 us
    ppermute x15, waiting for transfers between devices: 8.83 us -> 44.1 us  [shift(): lax.ppermute(block, axis, [(source, (source + step) % count) for source i...]
    pallas_call x1, Pallas kernels: 25.1 us -> 17 us  [denoise(): pl.pallas_call(functools.partial(denoise_kernel, rows, cols, totals, vari...]
    pallas_call x2, Pallas kernels: 31.7 us -> 25.9 us  [advance_latitude(): pl.pallas_call(functools.partial(latitude_kernel, hours, 1, step), grid=(...]
    ppermute x2, waiting for transfers between devices: 18.4 us -> 15 us  [next_to(): lax.ppermute(high, axis, backward)]
    unnamed x56 -> x62, local copies, waits for them, and re-layouts: 7.51 us -> 4.35 us
  transfers between devices with their start and end apart: 21 -> 21, of which waited for: 8 -> 5; matrix products, arithmetic and copies ran while one was open for 10% -> 11% of each run, Pallas kernels for 30% -> 28%
where the time goes in v8:
time: 185 us; the launch traced here: 183 us
  waiting for transfers between devices  59.1 us (32%)
  Pallas kernels  54.6 us (30%)
  starting transfers between devices  40.5 us (22%)
  local copies, waits for them, and re-layouts  19.2 us (10%)
  other arithmetic  6.93 us (4%)
  between operations  2.93 us (2%)
    ppermute x15, waiting for transfers between devices, shift(): lax.ppermute(block, axis, [(source, (source + step) % count) for source i...  44.1 us
    pallas_call x2, Pallas kernels, advance_latitude(): pl.pallas_call(functools.partial(latitude_kernel, hours, 1, step), grid=(...  25.9 us
    ppermute x15, starting transfers between devices, shift(): lax.ppermute(block, axis, [(source, (source + step) % count) for source i...  19.7 us
    pallas_call x1, Pallas kernels, denoise(): pl.pallas_call(functools.partial(denoise_kernel, rows, cols, totals, vari...  17 us
    ppermute x2, waiting for transfers between devices, next_to(): lax.ppermute(high, axis, backward)  15 us
    all_to_all x2, starting transfers between devices, exchange(): return lax.all_to_all(blocks, axis, split_axis=0, concat_axis=0, tiled=True)  9.31 us
    pallas_call x1, Pallas kernels, assemble(): pl.pallas_call(functools.partial(assemble_kernel, rows, cols, totals, hig...  8.63 us
    ppermute x2, starting transfers between devices, next_to(): lax.ppermute(low, axis, forward)  6.1 us
  transfers between devices with their start and end apart: 21, of which 5 were waited for; matrix products, arithmetic and copies ran while one was open for 11% of the time, Pallas kernels for 28%

profile of v8, /device:TPU:8, one launch (start us, length us, event | category | flops | bytes accessed | tf_op | source)
XLA Modules:
  0.0 183.2 jit_solution(28795170987131009)
XLA Ops:
  0.7 3.1 %constant_dynamic-slice_fusion.2 = (bf16[2,360,384]{2,1,0:T(8,128)(2,1)}, bf16[2,360,384]{2,1,0:T(8,128)(2,1)}, bf16[2,360,384]{2,1,0:T(8,128)(2,1)}, bf16[2,360,384]{2,1,0:T(8,128)(2,1)}) fusion(bf16[8,360,384]{2,1,0:T(8,128)(2,1)} %param.20, s32[]{:T(128)S(6)} %select_n.132, s32[]{:T(128)S(6)} %select_n.130, s32[]{:T(128)S(6)} %select_n.129, s32[]{:T(128)S(6)} %select_n.131), kind=kLoop, calls=%fused_computation.69 | loop fusion | bytes 4423696 | tf_op jit(solution)/shard_map/dynamic_slice | solution.py:348
  3.9 3.0 %collective-permute-start.1 = (bf16[2,360,384]{2,1,0:T(8,128)(2,1)}, bf16[2,360,384]{2,1,0:T(8,128)(2,1)}, u32[]{:S(2)}, u32[]{:S(2)}) collective-permute-start(bf16[2,360,384]{2,1,0:T(8,128)(2,1)} %get-tuple-element.105), channel_id=1, source_target_pairs={{0,2},{1,3},{2,0},{3,1},{4,6},{5,7},{6,4},{7,5},{8,10},{9,11},{10,... | collective-permute-start | bytes 1658888 | tf_op jit(solution)/shard_map/ppermute | solution.py:301
  6.9 2.5 %collective-permute-start.2 = (bf16[2,360,384]{2,1,0:T(8,128)(2,1)}, bf16[2,360,384]{2,1,0:T(8,128)(2,1)}, u32[]{:S(2)}, u32[]{:S(2)}) collective-permute-start(bf16[2,360,384]{2,1,0:T(8,128)(2,1)} %get-tuple-element.102), channel_id=1, source_target_pairs={{0,1},{1,2},{2,3},{3,0},{4,5},{5,6},{6,7},{7,4},{8,9},{9,10},{10,1... | collective-permute-start | bytes 1658888 | tf_op jit(solution)/shard_map/ppermute | solution.py:301
  10.6 1.0 copy.35
  11.7 1.5 collective-permute-start.4
  16.2 1.1 multiply_bitcast_fusion
  20.2 1.4 fusion.5
  22.3 1.1 copy.30
  24.2 33.4 %collective-permute-done.3 = bf16[180,96]{0,1:T(8,128)(2,1)S(1)} collective-permute-done((bf16[180,96]{0,1:T(8,128)(2,1)S(1)}, bf16[180,96]{0,1:T(8,128)(2,1)S(1)}, u32[]{:S(2)}, u32[]{:S(2)}) %collective-permute-start.3) | collective-permute-done | bytes 34592 | tf_op jit(solution)/shard_map/ppermute | solution.py:301
  58.0 4.2 %collective-permute-start.11 = (bf16[14,128,128]{2,1,0:T(8,128)(2,1)S(1)}, bf16[14,128,128]{2,1,0:T(8,128)(2,1)}, u32[]{:S(2)}, u32[]{:S(2)}) collective-permute-start(bf16[14,128,128]{2,1,0:T(8,128)(2,1)S(1)} %pad_maximum_fusion), channel_id=1, source_target_pairs={{0,4},{4,8},{8,12},{12,16},{16,20},{20,24},{24,28},{1,5},{5,9},{9,... | collective-permute-start | bytes 1376264 | tf_op jit(solution)/shard_map/ppermute | solution.py:435
  62.1 1.3 collective-permute-start.12
  63.7 1.1 broadcast_in_dim.34
  64.7 4.5 %all-to-all-start = ((bf16[8,180,384]{2,1,0:T(8,128)(2,1)}), bf16[8,180,384]{2,1,0:T(8,128)(2,1)S(1)}, u32[]{:S(2)}, u32[]{:S(2)}) async-start(bf16[8,180,384]{2,1,0:T(8,128)(2,1)} %broadcast_in_dim.34), calls=%async_computation | async-start | bytes 2260992 | tf_op jit(solution)/shard_map/all_to_all | solution.py:87
  69.2 15.0 %collective-permute-done.12.below_ref = bf16[14,128,128]{2,1,0:T(8,128)(2,1)} collective-permute-done((bf16[14,128,128]{2,1,0:T(8,128)(2,1)S(1)}, bf16[14,128,128]{2,1,0:T(8,128)(2,1)}, u32[]{:S(2)}, u32[]{:S(2)}) %collective-permute-start.12) | collective-permute-done | bytes 458784 | tf_op jit(solution)/shard_map/ppermute | solution.py:435
  85.7 0.8 fusion.24
  87.4 1.9 %collective-permute-start.13 = (bf16[34,16,128]{2,1,0:T(8,128)(2,1)S(1)}, bf16[34,16,128]{2,1,0:T(8,128)(2,1)S(1)}, u32[]{:S(2)}, u32[]{:S(2)}) collective-permute-start(bf16[34,16,128]{2,1,0:T(8,128)(2,1)S(1)} %pad_maximum_fusion.2), channel_id=1, source_target_pairs={{0,1},{1,2},{2,3},{4,5},{5,6},{6,7},{8,9},{9,10},{10,11},{12,13},{... | collective-permute-start | bytes 417800 | tf_op jit(solution)/shard_map/ppermute | solution.py:435
  89.4 4.1 %collective-permute-start.14 = (bf16[34,16,128]{2,1,0:T(8,128)(2,1)S(1)}, bf16[34,16,128]{2,1,0:T(8,128)(2,1)S(1)}, u32[]{:S(2)}, u32[]{:S(2)}) collective-permute-start(bf16[34,16,128]{2,1,0:T(8,128)(2,1)S(1)} %pad_maximum_fusion.3), channel_id=1, source_target_pairs={{1,0},{2,1},{3,2},{5,4},{6,5},{7,6},{9,8},{10,9},{11,10},{13,12},{... | collective-permute-start | bytes 417800 | tf_op jit(solution)/shard_map/ppermute | solution.py:435
  93.5 1.1 reshape.117.refs_6_
  94.6 13.0 %advance_latitude.2 = (bf16[1,360,384]{2,1,0:T(8,128)(2,1)}, bf16[1,360,384]{2,1,0:T(8,128)(2,1)}, bf16[1,360,384]{2,1,0:T(8,128)(2,1)}, bf16[1,360,384]{2,1,0:T(8,128)(2,1)}, bf16[4,16,128]{2,1,0:T(8,128)(2,1)}) custom-call(s32[3]{0:T(128)} %pad_add_fusion.place_ref, bf16[2,360,384]{2,1,0:T(8,128)(2,1)} %get-tuple-element.50.refs_0_, ...), custom_call_target="tpu_custom_call" | custom-call | flops 16000000000 | bytes 8388608 | tf_op jit(solution)/shard_map/advance_latitude/pallas_call | solution.py:244
  107.6 2.0 %collective-permute-start.6 = (bf16[1,360,384]{2,1,0:T(8,128)(2,1)}, bf16[1,360,384]{2,1,0:T(8,128)(2,1)S(1)}, u32[]{:S(2)}, u32[]{:S(2)}) collective-permute-start(bf16[1,360,384]{2,1,0:T(8,128)(2,1)} %get-tuple-element.57), channel_id=1, source_target_pairs={{0,1},{1,2},{2,3},{3,0},{4,5},{5,6},{6,7},{7,4},{8,9},{9,10},{10,1... | collective-permute-start | bytes 829448 | tf_op jit(solution)/shard_map/ppermute | solution.py:301
  109.7 13.0 %advance_latitude.3 = (bf16[1,360,384]{2,1,0:T(8,128)(2,1)}, bf16[1,360,384]{2,1,0:T(8,128)(2,1)}, bf16[1,360,384]{2,1,0:T(8,128)(2,1)}, bf16[1,360,384]{2,1,0:T(8,128)(2,1)}, bf16[4,16,128]{2,1,0:T(8,128)(2,1)}) custom-call(s32[3]{0:T(128)} %pad_add_fusion.place_ref, bf16[2,360,384]{2,1,0:T(8,128)(2,1)} %get-tuple-element.50.refs_0_, ...), custom_call_target="tpu_custom_call" | custom-call | flops 16000000000 | bytes 8388608 | tf_op jit(solution)/shard_map/advance_latitude/pallas_call | solution.py:244
  123.5 2.0 %collective-permute-start.10 = (bf16[32,128]{1,0:T(8,128)(2,1)S(1)}, bf16[32,128]{1,0:T(8,128)(2,1)S(1)}, u32[]{:S(2)}, u32[]{:S(2)}) collective-permute-start(bf16[32,128]{1,0:T(8,128)(2,1)S(1)} %get-tuple-element.125), channel_id=1, source_target_pairs={{0,1},{1,2},{2,3},{3,0},{4,5},{5,6},{6,7},{7,4},{8,9},{9,10},{10,1... | collective-permute-start | bytes 24584 | tf_op jit(solution)/shard_map/ppermute | solution.py:301
  125.5 3.5 %collective-permute-start.9 = (bf16[32,128]{1,0:T(8,128)(2,1)S(1)}, bf16[32,128]{1,0:T(8,128)(2,1)S(1)}, u32[]{:S(2)}, u32[]{:S(2)}) collective-permute-start(bf16[32,128]{1,0:T(8,128)(2,1)S(1)} %get-tuple-element.126), channel_id=1, source_target_pairs={{0,2},{1,3},{2,0},{3,1},{4,6},{5,7},{6,4},{7,5},{8,10},{9,11},{10,... | collective-permute-start | bytes 24584 | tf_op jit(solution)/shard_map/ppermute | solution.py:301
  130.8 9.8 %collective-permute-done.8 = bf16[32,128]{1,0:T(8,128)(2,1)S(1)} collective-permute-done((bf16[32,128]{1,0:T(8,128)(2,1)S(1)}, bf16[32,128]{1,0:T(8,128)(2,1)S(1)}, u32[]{:S(2)}, u32[]{:S(2)}) %collective-permute-start.8) | collective-permute-done | bytes 8224 | tf_op jit(solution)/shard_map/ppermute | solution.py:301
  140.8 2.8 %collective-permute-start.17 = (bf16[1,360,384]{2,1,0:T(8,128)(2,1)}, bf16[1,360,384]{2,1,0:T(8,128)(2,1)S(1)}, u32[]{:S(2)}, u32[]{:S(2)}) collective-permute-start(bf16[1,360,384]{2,1,0:T(8,128)(2,1)} %get-tuple-element.72), channel_id=1, source_target_pairs={{0,2},{1,3},{2,0},{3,1},{4,6},{5,7},{6,4},{7,5},{8,10},{9,11},{10,... | collective-permute-start | bytes 829448 | tf_op jit(solution)/shard_map/ppermute | solution.py:301
  143.7 2.0 %collective-permute-start.18 = (bf16[1,360,384]{2,1,0:T(8,128)(2,1)}, bf16[1,360,384]{2,1,0:T(8,128)(2,1)S(1)}, u32[]{:S(2)}, u32[]{:S(2)}) collective-permute-start(bf16[1,360,384]{2,1,0:T(8,128)(2,1)} %get-tuple-element.73), channel_id=1, source_target_pairs={{0,3},{1,0},{2,1},{3,2},{4,7},{5,4},{6,5},{7,6},{8,11},{9,8},{10,9... | collective-permute-start | bytes 829448 | tf_op jit(solution)/shard_map/ppermute | solution.py:301
  146.5 4.9 %all-to-all-start.1 = ((bf16[8,4,32,128]{3,2,1,0:T(8,128)(2,1)}), bf16[8,4,32,128]{3,2,1,0:T(8,128)(2,1)S(1)}, u32[]{:S(2)}, u32[]{:S(2)}) async-start(bf16[8,4,32,128]{3,2,1,0:T(8,128)(2,1)} %broadcast_in_dim.35), calls=%async_computation.1 | async-start | bytes 524288 | tf_op jit(solution)/shard_map/all_to_all | solution.py:87
  151.3 8.6 %assemble.1 = (bf16[34,160,128]{2,1,0:T(8,128)(2,1)}, bf16[26,160,128]{2,1,0:T(8,128)(2,1)}, bf16[34,160,256]{2,1,0:T(8,128)(2,1)}) custom-call(s32[2]{0:T(128)} %pad_add_fusion.1.place_ref, bf16[16,128,128]{2,1,0:T(8,128)(2,1)} %copy-done.1, bf16[16,128,128]{2,1,0:T(8,128)(2,1)} %copy-done.3, bf16[14,128,128]{2,1,0:T(8,128)(2,1)} %collective-permute-done.11.above_ref, ...), custom_call_target="tpu_custom_call" | custom-call | flops 10000000000 | bytes 10000000 | tf_op jit(solution)/shard_map/assemble/pallas_call | solution.py:494
  160.7 17.0 %denoise.1 = bf16[16,128,128]{2,1,0:T(8,128)(2,1)} custom-call(s32[2]{0:T(128)} %pad_add_fusion.1.place_ref, s32[8]{0:T(128)} %fusion.19.pick_ref, bf16[34,160,128]{2,1,0:T(8,128)(2,1)} %get-tuple-element.80.noisy_ref, bf16[34,160,256]{2,1,0:T(8,128)(2,1)} %get-tuple-element.81.blend_ref, bf16[64,16,128]{2,1,0:T(8,128)(2,1)} %bitcast.78, ...), custom_call_target="tpu_custom_call" | custom-call | flops 1000000 | bytes 100000 | tf_op jit(solution)/shard_map/denoise/pallas_call | solution.py:672
  177.7 1.1 slice_bitcast_fusion
  178.9 1.1 copy.38
  180.0 3.0 %collate.1 = bf16[8,360,384]{2,1,0:T(8,128)(2,1)} custom-call(s32[8]{0:T(128)} %stack.69.place_ref, bf16[1,360,384]{2,1,0:T(8,128)(2,1)} %get-tuple-element.89.refs_0_, bf16[1,360,384]{2,1,0:T(8,128)(2,1)} %copy-done.7, bf16[1,360,384]{2,1,0:T(8,128)(2,1)} %copy-done.9, bf16[1,360,384]{2,1,0:T(8,128)(2,1)} %copy-done.8, ...), custom_call_target="tpu_custom_call" | custom-call | tf_op jit(solution)/shard_map/collate/pallas_call | solution.py:288
  (127 shorter events, 14.5 us)
Async XLA Ops:
  0.7 8.7 %copy-start.4 = (f32[2,720,96]{1,2,0:T(8,128)S(1)}, f32[2,720,96]{1,2,0:T(8,128)}, u32[]{:S(2)}) copy-start(f32[2,720,96]{1,2,0:T(8,128)} %param.21) | copy-start | bytes 1658884
  3.8 6.3 %copy-start.5 = (bf16[99,16,128]{2,1,0:T(8,128)(2,1)S(1)}, bf16[99,16,128]{2,1,0:T(8,128)(2,1)}, u32[]{:S(2)}) copy-start(bf16[99,16,128]{2,1,0:T(8,128)(2,1)} %param.25) | copy-start | bytes 1216516
  3.8 6.5 %copy-start.19 = (s32[16,128]{1,0:T(8,128)S(1)}, s32[16,128]{1,0:T(8,128)}, u32[]{:S(2)}) copy-start(s32[16,128]{1,0:T(8,128)} %param.34) | copy-start | bytes 24580
  3.8 6.6 %copy-start.20 = (s32[16,128]{1,0:T(8,128)S(1)}, s32[16,128]{1,0:T(8,128)}, u32[]{:S(2)}) copy-start(s32[16,128]{1,0:T(8,128)} %param.35) | copy-start | bytes 24580
  3.9 89.6 %collective-permute-start = (bf16[2,360,384]{2,1,0:T(8,128)(2,1)}, bf16[2,360,384]{2,1,0:T(8,128)(2,1)}, u32[]{:S(2)}, u32[]{:S(2)}) collective-permute-start(bf16[2,360,384]{2,1,0:T(8,128)(2,1)} %get-tuple-element.103), channel_id=1, source_target_pairs={{0,3},{1,0},{2,1},{3,2},{4,7},{5,4},{6,5},{7,6},{8,11},{9,8},{10,9... | collective-permute-start | bytes 1658888 | tf_op jit(solution)/shard_map/ppermute | solution.py:301
  3.9 89.6 %collective-permute-start.1 = (bf16[2,360,384]{2,1,0:T(8,128)(2,1)}, bf16[2,360,384]{2,1,0:T(8,128)(2,1)}, u32[]{:S(2)}, u32[]{:S(2)}) collective-permute-start(bf16[2,360,384]{2,1,0:T(8,128)(2,1)} %get-tuple-element.105), channel_id=1, source_target_pairs={{0,2},{1,3},{2,0},{3,1},{4,6},{5,7},{6,4},{7,5},{8,10},{9,11},{10,... | collective-permute-start | bytes 1658888 | tf_op jit(solution)/shard_map/ppermute | solution.py:301
  6.9 86.6 %collective-permute-start.2 = (bf16[2,360,384]{2,1,0:T(8,128)(2,1)}, bf16[2,360,384]{2,1,0:T(8,128)(2,1)}, u32[]{:S(2)}, u32[]{:S(2)}) collective-permute-start(bf16[2,360,384]{2,1,0:T(8,128)(2,1)} %get-tuple-element.102), channel_id=1, source_target_pairs={{0,1},{1,2},{2,3},{3,0},{4,5},{5,6},{6,7},{7,4},{8,9},{9,10},{10,1... | collective-permute-start | bytes 1658888 | tf_op jit(solution)/shard_map/ppermute | solution.py:301
  11.7 46.0 %collective-permute-start.3 = (bf16[180,96]{0,1:T(8,128)(2,1)S(1)}, bf16[180,96]{0,1:T(8,128)(2,1)S(1)}, u32[]{:S(2)}, u32[]{:S(2)}) collective-permute-start(bf16[180,96]{0,1:T(8,128)(2,1)S(1)} %dynamic-slice_convert_fusion), channel_id=1, source_target_pairs={{0,3},{1,0},{2,1},{3,2},{4,7},{5,4},{6,5},{7,6},{8,11},{9,8},{10,9... | collective-permute-start | bytes 103688 | tf_op jit(solution)/shard_map/ppermute | solution.py:301
  11.7 46.2 %collective-permute-start.4 = (bf16[180,96]{0,1:T(8,128)(2,1)S(1)}, bf16[180,96]{0,1:T(8,128)(2,1)S(1)}, u32[]{:S(2)}, u32[]{:S(2)}) collective-permute-start(bf16[180,96]{0,1:T(8,128)(2,1)S(1)} %dynamic-slice_convert_fusion), channel_id=1, source_target_pairs={{0,2},{1,3},{2,0},{3,1},{4,6},{5,7},{6,4},{7,5},{8,10},{9,11},{10,... | collective-permute-start | bytes 103688 | tf_op jit(solution)/shard_map/ppermute | solution.py:301
  21.6 36.1 %copy-start.14 = (bf16[180,672]{0,1:T(8,128)(2,1)S(1)}, bf16[180,672]{0,1:T(8,128)(2,1)}, u32[]{:S(2)}) copy-start(bf16[180,672]{0,1:T(8,128)(2,1)} %constant_dynamic-update-slice_fusion.9) | copy-start | bytes 725764
  57.6 4.5 %collective-permute-start.5 = (bf16[180,96]{0,1:T(8,128)(2,1)S(1)}, bf16[180,96]{0,1:T(8,128)(2,1)S(1)}, u32[]{:S(2)}, u32[]{:S(2)}) collective-permute-start(bf16[180,96]{0,1:T(8,128)(2,1)S(1)} %dynamic-slice_convert_fusion), channel_id=1, source_target_pairs={{0,1},{1,2},{2,3},{3,0},{4,5},{5,6},{6,7},{7,4},{8,9},{9,10},{10,1... | collective-permute-start | bytes 103688 | tf_op jit(solution)/shard_map/ppermute | solution.py:301
  58.0 27.0 %collective-permute-start.11 = (bf16[14,128,128]{2,1,0:T(8,128)(2,1)S(1)}, bf16[14,128,128]{2,1,0:T(8,128)(2,1)}, u32[]{:S(2)}, u32[]{:S(2)}) collective-permute-start(bf16[14,128,128]{2,1,0:T(8,128)(2,1)S(1)} %pad_maximum_fusion), channel_id=1, source_target_pairs={{0,4},{4,8},{8,12},{12,16},{16,20},{20,24},{24,28},{1,5},{5,9},{9,... | collective-permute-start | bytes 1376264 | tf_op jit(solution)/shard_map/ppermute | solution.py:435
  62.1 22.0 %collective-permute-start.12 = (bf16[14,128,128]{2,1,0:T(8,128)(2,1)S(1)}, bf16[14,128,128]{2,1,0:T(8,128)(2,1)}, u32[]{:S(2)}, u32[]{:S(2)}) collective-permute-start(bf16[14,128,128]{2,1,0:T(8,128)(2,1)S(1)} %pad_maximum_fusion.1), channel_id=1, source_target_pairs={{4,0},{8,4},{12,8},{16,12},{20,16},{24,20},{28,24},{5,1},{9,5},{13... | collective-permute-start | bytes 1376264 | tf_op jit(solution)/shard_map/ppermute | solution.py:435
  64.7 28.8 %all-to-all-start = ((bf16[8,180,384]{2,1,0:T(8,128)(2,1)}), bf16[8,180,384]{2,1,0:T(8,128)(2,1)S(1)}, u32[]{:S(2)}, u32[]{:S(2)}) async-start(bf16[8,180,384]{2,1,0:T(8,128)(2,1)} %broadcast_in_dim.34), calls=%async_computation | async-start | bytes 2260992 | tf_op jit(solution)/shard_map/all_to_all | solution.py:87
  87.4 53.3 %collective-permute-start.13 = (bf16[34,16,128]{2,1,0:T(8,128)(2,1)S(1)}, bf16[34,16,128]{2,1,0:T(8,128)(2,1)S(1)}, u32[]{:S(2)}, u32[]{:S(2)}) collective-permute-start(bf16[34,16,128]{2,1,0:T(8,128)(2,1)S(1)} %pad_maximum_fusion.2), channel_id=1, source_target_pairs={{0,1},{1,2},{2,3},{4,5},{5,6},{6,7},{8,9},{9,10},{10,11},{12,13},{... | collective-permute-start | bytes 417800 | tf_op jit(solution)/shard_map/ppermute | solution.py:435
  89.4 51.3 %collective-permute-start.14 = (bf16[34,16,128]{2,1,0:T(8,128)(2,1)S(1)}, bf16[34,16,128]{2,1,0:T(8,128)(2,1)S(1)}, u32[]{:S(2)}, u32[]{:S(2)}) collective-permute-start(bf16[34,16,128]{2,1,0:T(8,128)(2,1)S(1)} %pad_maximum_fusion.3), channel_id=1, source_target_pairs={{1,0},{2,1},{3,2},{5,4},{6,5},{7,6},{9,8},{10,9},{11,10},{13,12},{... | collective-permute-start | bytes 417800 | tf_op jit(solution)/shard_map/ppermute | solution.py:435
  107.6 15.8 %collective-permute-start.6 = (bf16[1,360,384]{2,1,0:T(8,128)(2,1)}, bf16[1,360,384]{2,1,0:T(8,128)(2,1)S(1)}, u32[]{:S(2)}, u32[]{:S(2)}) collective-permute-start(bf16[1,360,384]{2,1,0:T(8,128)(2,1)} %get-tuple-element.57), channel_id=1, source_target_pairs={{0,1},{1,2},{2,3},{3,0},{4,5},{5,6},{6,7},{7,4},{8,9},{9,10},{10,1... | collective-permute-start | bytes 829448 | tf_op jit(solution)/shard_map/ppermute | solution.py:301
  109.6 13.1 %copy-start.18 = (bf16[4,16,128]{2,1,0:T(8,128)(2,1)S(1)}, bf16[4,16,128]{2,1,0:T(8,128)(2,1)}, u32[]{:S(2)}) copy-start(bf16[4,16,128]{2,1,0:T(8,128)(2,1)} %get-tuple-element.55) | copy-start | bytes 49156
  109.6 31.1 %copy-start.21 = (bf16[1,360,384]{2,1,0:T(8,128)(2,1)S(1)}, bf16[1,360,384]{2,1,0:T(8,128)(2,1)}, u32[]{:S(2)}) copy-start(bf16[1,360,384]{2,1,0:T(8,128)(2,1)} %get-tuple-element.68) | copy-start | bytes 829444
  109.6 13.8 %collective-permute-start.7 = (bf16[1,360,384]{2,1,0:T(8,128)(2,1)}, bf16[1,360,384]{2,1,0:T(8,128)(2,1)S(1)}, u32[]{:S(2)}, u32[]{:S(2)}) collective-permute-start(bf16[1,360,384]{2,1,0:T(8,128)(2,1)} %get-tuple-element.58), channel_id=1, source_target_pairs={{0,3},{1,0},{2,1},{3,2},{4,7},{5,4},{6,5},{7,6},{8,11},{9,8},{10,9... | collective-permute-start | bytes 829448 | tf_op jit(solution)/shard_map/ppermute | solution.py:301
  123.4 36.5 %copy-start.7 = (bf16[1,360,384]{2,1,0:T(8,128)(2,1)}, bf16[1,360,384]{2,1,0:T(8,128)(2,1)S(1)}, u32[]{:S(2)}) copy-start(bf16[1,360,384]{2,1,0:T(8,128)(2,1)S(1)} %collective-permute-done.6.refs_1_) | copy-start | bytes 829444
  123.4 36.5 %copy-start.8 = (bf16[1,360,384]{2,1,0:T(8,128)(2,1)}, bf16[1,360,384]{2,1,0:T(8,128)(2,1)S(1)}, u32[]{:S(2)}) copy-start(bf16[1,360,384]{2,1,0:T(8,128)(2,1)S(1)} %collective-permute-done.7.refs_3_) | copy-start | bytes 829444
  123.5 6.8 %collective-permute-start.10 = (bf16[32,128]{1,0:T(8,128)(2,1)S(1)}, bf16[32,128]{1,0:T(8,128)(2,1)S(1)}, u32[]{:S(2)}, u32[]{:S(2)}) collective-permute-start(bf16[32,128]{1,0:T(8,128)(2,1)S(1)} %get-tuple-element.125), channel_id=1, source_target_pairs={{0,1},{1,2},{2,3},{3,0},{4,5},{5,6},{6,7},{7,4},{8,9},{9,10},{10,1... | collective-permute-start | bytes 24584 | tf_op jit(solution)/shard_map/ppermute | solution.py:301
  125.5 5.3 %collective-permute-start.9 = (bf16[32,128]{1,0:T(8,128)(2,1)S(1)}, bf16[32,128]{1,0:T(8,128)(2,1)S(1)}, u32[]{:S(2)}, u32[]{:S(2)}) collective-permute-start(bf16[32,128]{1,0:T(8,128)(2,1)S(1)} %get-tuple-element.126), channel_id=1, source_target_pairs={{0,2},{1,3},{2,0},{3,1},{4,6},{5,7},{6,4},{7,5},{8,10},{9,11},{10,... | collective-permute-start | bytes 24584 | tf_op jit(solution)/shard_map/ppermute | solution.py:301
  129.0 11.6 %collective-permute-start.8 = (bf16[32,128]{1,0:T(8,128)(2,1)S(1)}, bf16[32,128]{1,0:T(8,128)(2,1)S(1)}, u32[]{:S(2)}, u32[]{:S(2)}) collective-permute-start(bf16[32,128]{1,0:T(8,128)(2,1)S(1)} %get-tuple-element.127), channel_id=1, source_target_pairs={{0,3},{1,0},{2,1},{3,2},{4,7},{5,4},{6,5},{7,6},{8,11},{9,8},{10,9... | collective-permute-start | bytes 24584 | tf_op jit(solution)/shard_map/ppermute | solution.py:301
  140.6 10.7 %copy-start.22 = (bf16[34,16,128]{2,1,0:T(8,128)(2,1)}, bf16[34,16,128]{2,1,0:T(8,128)(2,1)S(1)}, u32[]{:S(2)}) copy-start(bf16[34,16,128]{2,1,0:T(8,128)(2,1)S(1)} %collective-permute-done.13.left_ref) | copy-start | bytes 417796
  140.7 10.6 %copy-start.23 = (bf16[34,16,128]{2,1,0:T(8,128)(2,1)}, bf16[34,16,128]{2,1,0:T(8,128)(2,1)S(1)}, u32[]{:S(2)}) copy-start(bf16[34,16,128]{2,1,0:T(8,128)(2,1)S(1)} %collective-permute-done.14.right_ref) | copy-start | bytes 417796
  140.7 38.1 %collective-permute-start.15 = (bf16[1,360,384]{2,1,0:T(8,128)(2,1)S(1)}, bf16[1,360,384]{2,1,0:T(8,128)(2,1)S(1)}, u32[]{:S(2)}, u32[]{:S(2)}) collective-permute-start(bf16[1,360,384]{2,1,0:T(8,128)(2,1)S(1)} %copy-done.21), channel_id=1, source_target_pairs={{0,2},{1,3},{2,0},{3,1},{4,6},{5,7},{6,4},{7,5},{8,10},{9,11},{10,... | collective-permute-start | bytes 829448 | tf_op jit(solution)/shard_map/ppermute | solution.py:301
  140.8 38.1 %collective-permute-start.16 = (bf16[1,360,384]{2,1,0:T(8,128)(2,1)}, bf16[1,360,384]{2,1,0:T(8,128)(2,1)S(1)}, u32[]{:S(2)}, u32[]{:S(2)}) collective-permute-start(bf16[1,360,384]{2,1,0:T(8,128)(2,1)} %get-tuple-element.71), channel_id=1, source_target_pairs={{0,1},{1,2},{2,3},{3,0},{4,5},{5,6},{6,7},{7,4},{8,9},{9,10},{10,1... | collective-permute-start | bytes 829448 | tf_op jit(solution)/shard_map/ppermute | solution.py:301
  140.8 38.0 %collective-permute-start.17 = (bf16[1,360,384]{2,1,0:T(8,128)(2,1)}, bf16[1,360,384]{2,1,0:T(8,128)(2,1)S(1)}, u32[]{:S(2)}, u32[]{:S(2)}) collective-permute-start(bf16[1,360,384]{2,1,0:T(8,128)(2,1)} %get-tuple-element.72), channel_id=1, source_target_pairs={{0,2},{1,3},{2,0},{3,1},{4,6},{5,7},{6,4},{7,5},{8,10},{9,11},{10,... | collective-permute-start | bytes 829448 | tf_op jit(solution)/shard_map/ppermute | solution.py:301
  143.7 35.2 %collective-permute-start.18 = (bf16[1,360,384]{2,1,0:T(8,128)(2,1)}, bf16[1,360,384]{2,1,0:T(8,128)(2,1)S(1)}, u32[]{:S(2)}, u32[]{:S(2)}) collective-permute-start(bf16[1,360,384]{2,1,0:T(8,128)(2,1)} %get-tuple-element.73), channel_id=1, source_target_pairs={{0,3},{1,0},{2,1},{3,2},{4,7},{5,4},{6,5},{7,6},{8,11},{9,8},{10,9... | collective-permute-start | bytes 829448 | tf_op jit(solution)/shard_map/ppermute | solution.py:301
  146.5 13.5 %all-to-all-start.1 = ((bf16[8,4,32,128]{3,2,1,0:T(8,128)(2,1)}), bf16[8,4,32,128]{3,2,1,0:T(8,128)(2,1)S(1)}, u32[]{:S(2)}, u32[]{:S(2)}) async-start(bf16[8,4,32,128]{3,2,1,0:T(8,128)(2,1)} %broadcast_in_dim.35), calls=%async_computation.1 | async-start | bytes 524288 | tf_op jit(solution)/shard_map/all_to_all | solution.py:87
  (13 other events, 28.6 us)
